TPU v7x, 32 devices: a whole 2x2x4 slice. The times are simulated.
32 devices in a mesh: lat: 8 (over z, x), tp: 4 (over y, core).
Axes of the slice: x: 2, y: 2, z: 4, core: 2. Of those that a mesh axis runs over, the one named last changes fastest.
Arguments:
- features: bfloat16 [42, 2, 96, 1024], P(None, None, 'lat', 'tp'), may hold values from -6 to 6
- target: bfloat16 [42, 2, 96, 1024], P(None, None, 'lat', 'tp'), may hold values from -6 to 6
- w_qkv: bfloat16 [1024, 3, 1024], P(None, None, 'tp'), may hold values from -1 to 1
- w_proj: bfloat16 [1024, 1024], P('tp'), may hold values from -0.1875 to 0.1875
- qkv_clip: float32 [2, 3, 1024], P(None, None, 'tp'), may hold values from 0.5 to 3
- proj_clip: float32 [2, 1024], replicated, may hold values from 0.5 to 3
- shift_offset: int32 [1], replicated, may hold values from 0 to 5
- region_ids: int32 [42, 2, 96], replicated, may hold values from 0 to 1
Outputs:
- mixed: bfloat16 [42, 2, 96, 1024], P(None, None, 'lat', 'tp')
- qkv_clip_grad: float32 [2, 3, 1024], P(None, None, 'tp')
- proj_clip_grad: float32 [2, 1024], replicated
All inputs are finite; a program needn't handle non-finite values.
Results may differ from a plain program's by a relative error of at most 0.0058.
Values may be sent and summed in bfloat16 or wider, within the bound.
No kernel may reach another device: no remote copies, remote signals or barrier semaphores. Data moves between devices by JAX's collectives and lax.ppermute only.
A program may use at most 128 MiB of HBM per device.

v0:
```python
import jax
import jax.numpy as jnp
from jax import lax
from jax.experimental import pallas as pl
from jax.experimental.pallas import tpu as pltpu
from jax.sharding import PartitionSpec as P

HD = 64
WLAT = 6
EPS = 1e-05
NEG = -1e30
F32 = jnp.float32
BF = jnp.bfloat16
SCALE = HD ** (-0.5)
NT = (((1,), (1,)), ((), ()))
TN = (((0,), (0,)), ((), ()))


def spec(n):
    return [pl.BlockSpec(memory_space=pltpu.VMEM)] * n


def params(mib):
    return pltpu.CompilerParams(vmem_limit_bytes=mib * 1024 * 1024)


def bounds_of(weight, logits_hi, logits_lo):
    top = jnp.max(weight, axis=0, keepdims=True)
    low = jnp.min(weight, axis=0, keepdims=True)
    hi = 1.0 / (1.0 + jnp.exp(-logits_hi))
    lo = 1.0 / (1.0 + jnp.exp(-logits_lo))
    return hi * top, lo * low, hi * (1.0 - hi) * top, lo * (1.0 - lo) * low


def clip_qkv_kernel(w_ref, c_ref, wc_ref, b_ref):
    def body(i, carry):
        w = w_ref[i].astype(F32)
        up, lw, fh, fl = bounds_of(w, c_ref[i, 0:1], c_ref[i, 1:2])
        wc_ref[i] = jnp.minimum(jnp.maximum(w, lw), up).astype(BF)
        b_ref[i, 0:1] = up
        b_ref[i, 1:2] = lw
        b_ref[i, 2:3] = fh
        b_ref[i, 3:4] = fl
        return carry

    lax.fori_loop(0, 3, body, 0)


def clip_qkv(w, clips):
    n, d, e = w.shape
    return pl.pallas_call(
        clip_qkv_kernel,
        out_shape=(
            jax.ShapeDtypeStruct((n, d, e), BF),
            jax.ShapeDtypeStruct((n, 8, e), F32),
        ),
        in_specs=spec(2),
        out_specs=tuple(spec(2)),
        compiler_params=params(24),
        cost_estimate=pl.CostEstimate(flops=10 * n * d * e, bytes_accessed=4 * n * d * e, transcendentals=0),
    )(w, clips)


def clip_proj_kernel(w0, w1, w2, w3, c_ref, wc_ref, b_ref):
    shards = (w0, w1, w2, w3)
    size = w0.shape[0]

    def body(i, carry):
        cols = pl.ds(pl.multiple_of(i * 256, 256), 256)
        w = jnp.concatenate([s[:, cols].astype(F32) for s in shards], axis=0)
        up, lw, fh, fl = bounds_of(w, c_ref[0:1, cols], c_ref[1:2, cols])
        wc = jnp.minimum(jnp.maximum(w, lw), up).astype(BF)
        wc_ref[:, cols] = wc
        b_ref[0:1, cols] = up
        b_ref[1:2, cols] = lw
        b_ref[2:3, cols] = fh
        b_ref[3:4, cols] = fl
        return carry

    lax.fori_loop(0, w0.shape[1] // 256, body, 0)


def clip_proj(shards, clips):
    e, d = shards[0].shape
    return pl.pallas_call(
        clip_proj_kernel,
        out_shape=(
            jax.ShapeDtypeStruct((4 * e, d), BF),
            jax.ShapeDtypeStruct((8, d), F32),
        ),
        in_specs=spec(5),
        out_specs=tuple(spec(2)),
        compiler_params=params(24),
        cost_estimate=pl.CostEstimate(flops=40 * e * d, bytes_accessed=16 * e * d, transcendentals=0),
    )(*shards, clips)


def stacked(block, mask_a, mask_b):
    return jnp.concatenate([block * mask_a, block * mask_b], axis=0)


def head_masks():
    lane = lax.broadcasted_iota(jnp.int32, (1, 2 * HD), 1)
    mask_a = jnp.where(lane < HD, 1.0, 0.0).astype(BF)
    mask_b = jnp.where(lane < HD, 0.0, 1.0).astype(BF)
    return mask_a, mask_b


def probs_t(k, q2, allowed):
    st = lax.dot_general(k, q2, NT, preferred_element_type=F32) * SCALE
    st = jnp.where(allowed, st, NEG)
    e = jnp.exp(st - jnp.max(st, axis=0, keepdims=True))
    return e * (1.0 / jnp.sum(e, axis=0, keepdims=True))


def merge_heads(t_block):
    both = t_block.T
    n = both.shape[0] // 2
    lane = lax.broadcasted_iota(jnp.int32, (n, 2 * HD), 1)
    return jnp.where(lane < HD, both[:n], both[n:])


def allowed_t(idk_ref, idq_ref, w, cells):
    rows = pl.ds(pl.multiple_of(w * cells, 16), cells)
    idk = idk_ref[rows, :]
    return (idk == idq_ref[w]) & (idk >= 0)


def forward_kernel(t_ref, *refs):
    pieces = refs[:8]
    wo_ref, wp_ref, idk_ref, idq_ref, normed_ref, qkv_ref, attn_ref, xs = refs[8:]
    t = t_ref[0]
    half = pieces[0].shape[0] // 4
    cells = 2 * half
    width = pieces[0].shape[1]
    for k in range(4):
        cols = pl.ds(pl.multiple_of((t ^ k) * width, width), width)
        for s in range(2):
            for p in range(2):
                block = pieces[4 * s + k][cells * p : cells * (p + 1), :].astype(F32)
                for i in range(2):
                    first = cells * (2 * p + i) + half * s
                    xs[first : first + half, cols] = block[half * i : half * (i + 1)]

    def norm(w, carry):
        rows = pl.ds(pl.multiple_of(w * 48, 16), 48)
        x = xs[rows, :]
        mean = jnp.mean(x, axis=-1, keepdims=True)
        x = x - mean
        var = jnp.mean(x * x, axis=-1, keepdims=True)
        normed_ref[rows, :] = (x * lax.rsqrt(var + EPS)).astype(BF)
        return carry

    lax.fori_loop(0, 12, norm, 0)

    def project(i, carry):
        for g, w_ref in enumerate((wo_ref, wp_ref)):
            qkv_ref[3 * g + i] = jnp.dot(
                normed_ref[...], w_ref[i], preferred_element_type=F32
            ).astype(BF)
        return carry

    lax.fori_loop(0, 3, project, 0)
    mask_a, mask_b = head_masks()

    def window(w, carry):
        rows = pl.ds(pl.multiple_of(w * cells, 16), cells)
        allowed = allowed_t(idk_ref, idq_ref, w, cells)
        for hp in range(4):
            g, lanes = hp // 2, slice(128 * (hp % 2), 128 * (hp % 2) + 128)
            q2 = stacked(qkv_ref[3 * g, rows, lanes], mask_a, mask_b)
            pt = probs_t(qkv_ref[3 * g + 1, rows, lanes], q2, allowed)
            ot = lax.dot_general(
                qkv_ref[3 * g + 2, rows, lanes], pt.astype(BF), TN, preferred_element_type=F32
            )
            attn_ref[rows, 128 * hp : 128 * hp + 128] = merge_heads(ot).astype(BF)
        return carry

    lax.fori_loop(0, 4, window, 0)


def forward(t, pieces, wo, wp, idk, idq):
    n, width = pieces[0].shape
    d = 4 * width
    return pl.pallas_call(
        forward_kernel,
        out_shape=(
            jax.ShapeDtypeStruct((2 * n, d), BF),
            jax.ShapeDtypeStruct((6, 2 * n, width), BF),
            jax.ShapeDtypeStruct((2 * n, 2 * width), BF),
        ),
        in_specs=[pl.BlockSpec(memory_space=pltpu.SMEM)] + spec(12),
        out_specs=tuple(spec(3)),
        scratch_shapes=[pltpu.VMEM((2 * n, d), F32)],
        compiler_params=params(40),
        cost_estimate=pl.CostEstimate(flops=8 * 10**9, bytes_accessed=10 * 10**6, transcendentals=10**6),
    )(t, *pieces, wo, wp, idk, idq)


def turn_kernel(normed_ref, attn_ref, normed_t, attn_t):
    d = normed_ref.shape[1]

    def body(i, carry):
        cols = pl.ds(pl.multiple_of(i * 256, 256), 256)
        normed_t[cols, :] = normed_ref[:, cols].T
        return carry

    lax.fori_loop(0, d // 256, body, 0)

    def body2(i, carry):
        cols = pl.ds(pl.multiple_of(i * 256, 256), 256)
        attn_t[cols, :] = attn_ref[:, cols].T
        return carry

    lax.fori_loop(0, attn_ref.shape[1] // 256, body2, 0)


def turn(normed, attn):
    n, d = normed.shape
    e = attn.shape[1]
    return pl.pallas_call(
        turn_kernel,
        out_shape=(jax.ShapeDtypeStruct((d, n), BF), jax.ShapeDtypeStruct((e, n), BF)),
        in_specs=spec(2),
        out_specs=tuple(spec(2)),
        compiler_params=params(24),
        cost_estimate=pl.CostEstimate(flops=10**9, bytes_accessed=4 * n * (d + e), transcendentals=0),
    )(normed, attn)


def output_kernel(t_ref, *refs):
    pieces, targets = refs[:8], refs[8:16]
    own_ref, other_ref, wc_ref, idk_ref = refs[16:20]
    mixed, err_ref, y_ref = refs[20:24], refs[24], refs[25]
    t = t_ref[0]
    half = pieces[0].shape[0] // 4
    cells = 2 * half
    width = pieces[0].shape[1]
    e = own_ref.shape[1]
    for k in range(4):
        cols = pl.ds(pl.multiple_of((t ^ k) * width, width), width)
        y_ref[...] = jnp.dot(own_ref[...], wc_ref[:e, cols], preferred_element_type=F32) + jnp.dot(
            other_ref[...], wc_ref[e:, cols], preferred_element_type=F32
        )
        for p in range(2):
            errs = [[None, None], [None, None]]
            for s in range(2):
                block = pieces[4 * s + k][cells * p : cells * (p + 1), :].astype(F32)
                wanted = targets[4 * s + k][cells * p : cells * (p + 1), :].astype(F32)
                ys = []
                for i in range(2):
                    first = cells * (2 * p + i) + half * s
                    part = slice(half * i, half * (i + 1))
                    y = block[part] + y_ref[first : first + half, :]
                    ys.append(y)
                    valid = idk_ref[first : first + half, :] >= 0
                    errs[i][s] = jnp.where(valid, y - wanted[part], 0.0)
                if k < 2:
                    mixed[2 * s + k][cells * p : cells * (p + 1), :] = jnp.concatenate(
                        ys, axis=0
                    ).astype(BF)
            for i in range(2):
                first = cells * (2 * p + i)
                err_ref[first : first + cells, cols] = jnp.concatenate(errs[i], axis=0).astype(BF)


def output(t, pieces, targets, own, other, wc, idk):
    n, width = pieces[0].shape
    d = 4 * width
    piece = jax.ShapeDtypeStruct((n, width), BF)
    return pl.pallas_call(
        output_kernel,
        out_shape=(piece, piece, piece, piece, jax.ShapeDtypeStruct((2 * n, d), BF)),
        in_specs=[pl.BlockSpec(memory_space=pltpu.SMEM)] + spec(20),
        out_specs=tuple(spec(5)),
        scratch_shapes=[pltpu.VMEM((2 * n, width), F32)],
        compiler_params=params(40),
        cost_estimate=pl.CostEstimate(flops=2 * 10**9, bytes_accessed=8 * 10**6, transcendentals=0),
    )(t, *pieces, *targets, own, other, wc, idk)


def masked_sums(grad, w, bounds):
    g_hi = jnp.sum(jnp.where(w > bounds[0:1], grad, 0.0), axis=0, keepdims=True) * bounds[2:3]
    g_lo = jnp.sum(jnp.where(w < bounds[1:2], grad, 0.0), axis=0, keepdims=True) * bounds[3:4]
    return g_hi, g_lo


def backward_kernel(
    err_ref, wc_ref, attn_t, qkv_ref, normed_t, wo_ref, wp_ref, bo_ref, bp_ref, po_ref, pp_ref, pb_ref,
    idk_ref, idq_ref, gq_ref, gp_ref, d_ref, g_ref
):
    e = attn_t.shape[0]
    cells = idk_ref.shape[0] // 4
    d_ref[...] = lax.dot_general(err_ref[...], wc_ref[:e], NT, preferred_element_type=F32).astype(BF)
    mask_a, mask_b = head_masks()

    def window(w, carry):
        rows = pl.ds(pl.multiple_of(w * cells, 16), cells)
        allowed = allowed_t(idk_ref, idq_ref, w, cells)
        for hp in range(4):
            g, lanes = hp // 2, slice(128 * (hp % 2), 128 * (hp % 2) + 128)
            q2 = stacked(qkv_ref[3 * g, rows, lanes], mask_a, mask_b)
            k = qkv_ref[3 * g + 1, rows, lanes]
            v = qkv_ref[3 * g + 2, rows, lanes]
            pt = probs_t(k, q2, allowed)
            d2 = stacked(d_ref[rows, 128 * hp : 128 * hp + 128], mask_a, mask_b)
            g_ref[3 * g + 2, rows, lanes] = jnp.dot(
                pt.astype(BF), d2, preferred_element_type=F32
            ).astype(BF)
            dpt = lax.dot_general(v, d2, NT, preferred_element_type=F32)
            gst = (pt * (dpt - jnp.sum(pt * dpt, axis=0, keepdims=True))).astype(BF)
            g_ref[3 * g + 1, rows, lanes] = (
                jnp.dot(gst, q2, preferred_element_type=F32) * SCALE
            ).astype(BF)
            gqt = lax.dot_general(k, gst, TN, preferred_element_type=F32) * SCALE
            g_ref[3 * g, rows, lanes] = merge_heads(gqt).astype(BF)
        return carry

    lax.fori_loop(0, 4, window, 0)

    def proj_part(i, carry):
        cols = pl.ds(pl.multiple_of(i * 256, 256), 256)
        grad = jnp.dot(attn_t[...], err_ref[:, cols], preferred_element_type=F32)
        n = po_ref.shape[0]
        b = pb_ref[:, cols]
        h0, l0 = masked_sums(grad[:n], po_ref[:, cols].astype(F32), b)
        h1, l1 = masked_sums(grad[n:], pp_ref[:, cols].astype(F32), b)
        gp_ref[0:1, cols] = h0 + h1
        gp_ref[1:2, cols] = l0 + l1
        return carry

    lax.fori_loop(0, err_ref.shape[1] // 256, proj_part, 0)

    def qkv_part(i, carry):
        for g, (w_ref, b_ref) in enumerate(((wo_ref, bo_ref), (wp_ref, bp_ref))):
            grad = jnp.dot(normed_t[...], g_ref[3 * g + i], preferred_element_type=F32)
            hi, lo = masked_sums(grad, w_ref[i].astype(F32), b_ref[i])
            gq_ref[3 * g + i, 0:1] = hi
            gq_ref[3 * g + i, 1:2] = lo
        return carry

    lax.fori_loop(0, 3, qkv_part, 0)


def backward(err, wc, attn_t, qkv, normed_t, wo, wp, bo, bp, po, pp, pb, idk, idq):
    n, d = err.shape
    width = qkv.shape[2]
    return pl.pallas_call(
        backward_kernel,
        out_shape=(jax.ShapeDtypeStruct((6, 2, width), F32), jax.ShapeDtypeStruct((2, d), F32)),
        in_specs=spec(14),
        out_specs=tuple(spec(2)),
        scratch_shapes=[pltpu.VMEM((n, attn_t.shape[0]), BF), pltpu.VMEM((6, n, width), BF)],
        compiler_params=params(40),
        cost_estimate=pl.CostEstimate(flops=8 * 10**9, bytes_accessed=10 * 10**6, transcendentals=10**6),
    )(err, wc, attn_t, qkv, normed_t, wo, wp, bo, bp, po, pp, pb, idk, idq)


def send(block, shift, flip):
    count, tp = lax.axis_size("lat"), lax.axis_size("tp")
    route = [
        (u * tp + t, ((u + shift) % count) * tp + (t ^ flip)) for u in range(count) for t in range(tp)
    ]
    return lax.ppermute(block, ("lat", "tp"), route)


def after(block, *others):
    return lax.optimization_barrier((block, *others))[0]


def local(features, target, w_qkv, w_proj, qkv_clip, proj_clip, shift_offset, region_ids):
    rows, lev, lon, width = features.shape
    half = lon // 2
    many = (rows + WLAT) // 2
    sector = lax.axis_index("lat")
    t = lax.axis_index("tp")
    core = t % 2
    offset = shift_offset[0]
    t_arr = jnp.reshape(t, (1,)).astype(jnp.int32)

    def row_parts(block):
        block = jnp.transpose(block, (0, 2, 1, 3))
        padded = jnp.pad(block, ((WLAT, WLAT), (0, 0), (0, 0), (0, 0)))
        parts = []
        for flip in range(2):
            first = WLAT - offset + many * (core ^ flip)
            part = lax.dynamic_slice_in_dim(padded, first, many, 0)
            parts.append(
                [
                    part[:, half:].reshape(many * half * lev, width),
                    part[:, :half].reshape(many * half * lev, width),
                ]
            )
        return parts

    def spread(parts):
        own = [parts[0][0]] + [send(parts[k % 2][0], 0, k) for k in range(1, 4)]
        nxt = [send(parts[k % 2][1], -1, k) for k in range(4)]
        return own + nxt

    w3 = jnp.transpose(w_qkv, (1, 0, 2))
    c3 = jnp.transpose(qkv_clip, (1, 0, 2))
    parts = row_parts(features)
    pieces = spread(parts)
    w3_peer = send(w3, 0, 1)
    c3_peer = send(c3, 0, 1)
    wc_own, b_own = clip_qkv(w3, c3)
    wc_peer, b_peer = clip_qkv(w3_peer, c3_peer)

    doubled = jnp.concatenate([region_ids, region_ids[:, :, :lon]], 2)
    ids = lax.dynamic_slice_in_dim(doubled, sector * lon + half, lon, 2)
    ids = jnp.pad(ids, ((WLAT, WLAT), (0, 0), (0, 0)), constant_values=-1)
    ids = lax.dynamic_slice_in_dim(ids, WLAT - offset + many * core, many, 0)
    ids = ids.reshape(many // WLAT, WLAT, lev, 2, half).transpose(0, 3, 1, 4, 2)
    ids = ids.reshape(many // WLAT, 1, WLAT * lev * lon)
    idk = ids.reshape(many * lev * lon, 1)
    idq = jnp.concatenate([ids, ids], axis=2)

    normed, qkv, attn = forward(t_arr, pieces, wc_own, wc_peer, idk, idq)
    attn_other = send(attn, 0, 2)

    first_in = after(target, pieces[2], pieces[3], pieces[6], pieces[7])
    targets = spread(row_parts(first_in))
    p1 = send(w_proj, 0, 1)
    p2 = send(after(w_proj, pieces[2], pieces[3], pieces[6], pieces[7]), 0, 2)
    p3 = send(p2, 0, 1)
    pc, pb = clip_proj([w_proj, p1, p2, p3], proj_clip)
    normed_t, attn_t = turn(normed, attn)

    m00, m01, m10, m11, err = output(t_arr, pieces, targets, attn, attn_other, pc, idk)
    m01 = send(m01, 0, 1)
    m10 = send(m10, 1, 0)
    m11 = send(m11, 1, 1)

    gq, gp = backward(
        err, pc, attn_t, qkv, normed_t, w3, w3_peer, b_own, b_peer, w_proj, p1, pb, idk, idq
    )

    def grid(block):
        return block.reshape(many, half, lev, width)

    own = jnp.concatenate([grid(m10), grid(m00)], axis=1)
    peer = jnp.concatenate([grid(m11), grid(m01)], axis=1)
    mixed = jnp.concatenate([own, peer, own], axis=0)
    mixed = lax.dynamic_slice_in_dim(mixed, many * core + offset, rows, 0)
    mixed = jnp.transpose(mixed, (0, 2, 1, 3))

    gq_own = gq[:3] + send(gq[3:], 0, 1)
    gp = gp + send(gp, 0, 1)
    gp = gp + send(gp, 0, 2)
    both = jnp.concatenate([gq_own.reshape(-1), gp.reshape(-1)])
    both = lax.psum(both, "lat")
    qkv_sum = jnp.transpose(both[: gq_own.size].reshape(gq_own.shape), (1, 0, 2))
    proj_sum = both[gq_own.size :].reshape(gp.shape)
    return (mixed, qkv_sum, proj_sum)


def solution(mesh):
    placed = (
        P(None, None, "lat", "tp"),
        P(None, None, "lat", "tp"),
        P(None, None, "tp"),
        P("tp", None),
        P(None, None, "tp"),
        P(),
        P(),
        P(),
    )
    return jax.shard_map(
        local,
        mesh=mesh,
        in_specs=placed,
        out_specs=(P(None, None, "lat", "tp"), P(None, None, "tp"), P()),
        check_vma=False,
    )
```

profile of v0, /device:TPU:0, one launch (start us, length us, event | category | flops | bytes accessed | tf_op | source)
XLA Modules:
  0.0 165.1 jit_solution(2082764465135641431)
XLA Ops:
  0.7 0.5 collective-permute-start.14
  1.8 2.5 %constant_dynamic-slice_fusion.6 = (bf16[24,6,2,256]{3,2,1,0:T(2,128)(2,1)}, bf16[24,6,2,256]{3,2,1,0:T(2,128)(2,1)S(1)}, bf16[24,6,2,256]{3,2,1,0:T(2,128)(2,1)}, bf16[24,6,2,256]{3,2,1,0:T(2,128)(2,1)}) fusion(s32[]{:T(128)S(6)} %select_n.24, bf16[42,12,2,256]{3,2,1,0:T(2,128)(2,1)} %bitcast.28, s32[]{:T(128)S(6)} %select_n.23, s32[]{:T(128)S(6)} %add.67), kind=kLoop, calls=%fused_computation.23 | loop fusion | bytes 1105932 | tf_op jit(solution)/shard_map/slice | solution.py:391
  4.4 2.6 %collective-permute-start.1 = (bf16[288,256]{1,0:T(8,128)(2,1)S(1)}, bf16[288,256]{1,0:T(8,128)(2,1)S(1)}, u32[]{:S(2)}, u32[]{:S(2)}) collective-permute-start(bf16[288,256]{1,0:T(8,128)(2,1)S(1)} %reshape.70.refs_0_), channel_id=1, source_target_pairs={{0,2},{1,3},{2,0},{3,1},{4,6},{5,7},{6,4},{7,5},{8,10},{9,11},{10,... | collective-permute-start | bytes 442376 | tf_op jit(solution)/shard_map/ppermute | solution.py:364
  7.0 1.6 reshape.71
  8.7 0.1 collective-permute-start.2
  8.8 1.6 reshape.72
  10.4 5.7 %collective-permute-start.5 = (bf16[288,256]{1,0:T(8,128)(2,1)}, bf16[288,256]{1,0:T(8,128)(2,1)}, u32[]{:S(2)}, u32[]{:S(2)}) collective-permute-start(bf16[288,256]{1,0:T(8,128)(2,1)} %reshape.72), channel_id=1, source_target_pairs={{0,30},{1,31},{2,28},{3,29},{4,2},{5,3},{6,0},{7,1},{8,6},{9,7},{1... | collective-permute-start | bytes 442376 | tf_op jit(solution)/shard_map/ppermute | solution.py:364
  16.1 1.6 reshape.73
  17.7 0.1 collective-permute-start.6
  17.8 0.2 collective-permute-done.2.refs_3_
  18.0 2.6 %collective-permute-done.5.refs_6_ = bf16[288,256]{1,0:T(8,128)(2,1)} collective-permute-done((bf16[288,256]{1,0:T(8,128)(2,1)}, bf16[288,256]{1,0:T(8,128)(2,1)}, u32[]{:S(2)}, u32[]{:S(2)}) %collective-permute-start.5) | collective-permute-done | bytes 147488 | tf_op jit(solution)/shard_map/ppermute | solution.py:364
  20.6 4.2 %collective-permute-done.6.refs_7_ = bf16[288,256]{1,0:T(8,128)(2,1)S(1)} collective-permute-done((bf16[288,256]{1,0:T(8,128)(2,1)}, bf16[288,256]{1,0:T(8,128)(2,1)S(1)}, u32[]{:S(2)}, u32[]{:S(2)}) %collective-permute-start.6) | collective-permute-done | bytes 147488 | tf_op jit(solution)/shard_map/ppermute | solution.py:364
  24.8 0.7 copy-done.11
  25.4 0.5 collective-permute-start.18
  25.9 3.9 %collective-permute-start.3 = (bf16[288,256]{1,0:T(8,128)(2,1)}, bf16[288,256]{1,0:T(8,128)(2,1)}, u32[]{:S(2)}, u32[]{:S(2)}) collective-permute-start(bf16[288,256]{1,0:T(8,128)(2,1)} %reshape.72), channel_id=1, source_target_pairs={{0,28},{1,29},{2,30},{3,31},{4,0},{5,1},{6,2},{7,3},{8,4},{9,5},{1... | collective-permute-start | bytes 442376 | tf_op jit(solution)/shard_map/ppermute | solution.py:364
  29.9 0.1 collective-permute-start.15
  29.9 0.2 dynamic-slice_add_fusion
  30.1 0.9 collective-permute-done.15.c_ref
  31.1 0.1 copy.11
  31.2 0.1 reshape.78
  31.3 1.2 copy.12
  32.5 0.9 copy.13
  33.4 1.0 reshape_reshape.4.refs_10_.refs_19_.idk_ref
  34.4 1.0 copy.14
  35.4 0.7 shard_map.103
  36.1 0.1 pad_add_fusion.refs_11_.idq_ref
  36.2 3.5 %collective-permute-done.18.w2 = bf16[256,1024]{1,0:T(8,128)(2,1)} collective-permute-done((bf16[256,1024]{1,0:T(8,128)(2,1)}, bf16[256,1024]{1,0:T(8,128)(2,1)}, u32[]{:S(2)}, u32[]{:S(2)}) %collective-permute-start.18) | collective-permute-done | bytes 524320 | tf_op jit(solution)/shard_map/ppermute | solution.py:364
  39.7 0.5 collective-permute-start.19
  40.2 0.7 shard_map.104
  41.0 12.2 %shard_map.105 = (bf16[576,1024]{1,0:T(8,128)(2,1)S(1)}, bf16[6,576,256]{2,1,0:T(8,128)(2,1)S(1)}, bf16[576,512]{1,0:T(8,128)(2,1)}) custom-call(s32[1]{0:T(128)} %bitcast.t_ref, bf16[288,256]{1,0:T(8,128)(2,1)S(1)} %copy-done.2, bf16[288,256]{1,0:T(8,128)(2,1)} %collective-permute-done.refs_1_, bf16[288,256]{1,0:T(8,128)(2,1)S(1)} %copy-done.9, ...), custom_call_target="tpu_custom_call" | custom-call | flops 8000000000 | bytes 10000000 | tf_op jit(solution)/shard_map/pallas_call | solution.py:185
  53.2 1.0 copy-done.17
  54.2 1.2 copy-done.19
  55.5 0.5 collective-permute-start.16
  56.0 1.3 constant_dynamic-slice_fusion.4
  57.3 1.6 reshape.75
  59.0 1.6 reshape.74.refs_8_
  60.6 1.5 collective-permute-start.8
  62.1 0.3 collective-permute-start.9
  62.5 1.6 reshape.76
  64.1 1.6 reshape.77
  65.7 9.4 %collective-permute-done.8.refs_10_ = bf16[288,256]{1,0:T(8,128)(2,1)} collective-permute-done((bf16[288,256]{1,0:T(8,128)(2,1)}, bf16[288,256]{1,0:T(8,128)(2,1)}, u32[]{:S(2)}, u32[]{:S(2)}) %collective-permute-start.8) | collective-permute-done | bytes 147488 | tf_op jit(solution)/shard_map/ppermute | solution.py:364
  75.1 3.2 %collective-permute-start.10 = (bf16[288,256]{1,0:T(8,128)(2,1)}, bf16[288,256]{1,0:T(8,128)(2,1)S(1)}, u32[]{:S(2)}, u32[]{:S(2)}) collective-permute-start(bf16[288,256]{1,0:T(8,128)(2,1)} %reshape.76), channel_id=1, source_target_pairs={{0,28},{1,29},{2,30},{3,31},{4,0},{5,1},{6,2},{7,3},{8,4},{9,5},{1... | collective-permute-start | bytes 442376 | tf_op jit(solution)/shard_map/ppermute | solution.py:364
  78.4 2.1 %collective-permute-start.12 = (bf16[288,256]{1,0:T(8,128)(2,1)}, bf16[288,256]{1,0:T(8,128)(2,1)S(1)}, u32[]{:S(2)}, u32[]{:S(2)}) collective-permute-start(bf16[288,256]{1,0:T(8,128)(2,1)} %reshape.76), channel_id=1, source_target_pairs={{0,30},{1,31},{2,28},{3,29},{4,2},{5,3},{6,0},{7,1},{8,6},{9,7},{1... | collective-permute-start | bytes 442376 | tf_op jit(solution)/shard_map/ppermute | solution.py:364
  80.4 0.6 collective-permute-start.13
  81.1 2.4 %shard_map.106 = (bf16[1024,1024]{1,0:T(8,128)(2,1)S(1)}, f32[8,1024]{1,0:T(8,128)S(1)}) custom-call(bf16[256,1024]{1,0:T(8,128)(2,1)} %po_ref.1, bf16[256,1024]{1,0:T(8,128)(2,1)} %collective-permute-done.17.w1.pp_ref, bf16[256,1024]{1,0:T(8,128)(2,1)} %collective-permute-done.18.w2, bf16[256,1024]{1,0:T(8,128)(2,1)} %collective-permute-done.19.w3, ...), custom_call_target="tpu_custom_call" | custom-call | flops 10485760 | bytes 4194304 | tf_op jit(solution)/shard_map/pallas_call | solution.py:85
  83.6 2.0 %shard_map.108 = (bf16[1024,576]{1,0:T(8,128)(2,1)S(1)}, bf16[512,576]{1,0:T(8,128)(2,1)S(1)}) custom-call(bf16[576,1024]{1,0:T(8,128)(2,1)S(1)} %copy-done.18, bf16[576,512]{1,0:T(8,128)(2,1)} %get-tuple-element.26.refs_16_.attn_ref), custom_call_target="tpu_custom_call" | custom-call | flops 1000000000 | bytes 3538944 | tf_op jit(solution)/shard_map/pallas_call | solution.py:221
  85.5 2.6 %collective-permute-done.11.refs_13_ = bf16[288,256]{1,0:T(8,128)(2,1)S(1)} collective-permute-done((bf16[288,256]{1,0:T(8,128)(2,1)}, bf16[288,256]{1,0:T(8,128)(2,1)S(1)}, u32[]{:S(2)}, u32[]{:S(2)}) %collective-permute-start.11) | collective-permute-done | bytes 147488 | tf_op jit(solution)/shard_map/ppermute | solution.py:364
  88.1 3.0 %collective-permute-done.13.refs_15_ = bf16[288,256]{1,0:T(8,128)(2,1)S(1)} collective-permute-done((bf16[288,256]{1,0:T(8,128)(2,1)}, bf16[288,256]{1,0:T(8,128)(2,1)S(1)}, u32[]{:S(2)}, u32[]{:S(2)}) %collective-permute-start.13) | collective-permute-done | bytes 147488 | tf_op jit(solution)/shard_map/ppermute | solution.py:364
  91.1 3.5 %shard_map.107 = (bf16[288,256]{1,0:T(8,128)(2,1)S(1)}, bf16[288,256]{1,0:T(8,128)(2,1)S(1)}, bf16[288,256]{1,0:T(8,128)(2,1)S(1)}, bf16[288,256]{1,0:T(8,128)(2,1)S(1)}, bf16[576,1024]{1,0:T(8,128)(2,1)S(1)}) custom-call(s32[1]{0:T(128)} %bitcast.t_ref, bf16[288,256]{1,0:T(8,128)(2,1)S(1)} %copy-done.3, bf16[288,256]{1,0:T(8,128)(2,1)} %collective-permute-done.refs_1_, ...), custom_call_target="tpu_custom_call" | custom-call | flops 2000000000 | bytes 8000000 | tf_op jit(solution)/shard_map/pallas_call | solution.py:271
  94.7 0.7 copy-done.5
  95.3 0.7 copy-done.14
  96.0 0.7 copy-done.15
  96.7 0.7 copy-done.16
  97.3 16.3 %shard_map.109 = (f32[6,2,256]{2,1,0:T(2,128)S(1)}, f32[2,1024]{1,0:T(2,128)S(1)}) custom-call(bf16[576,1024]{1,0:T(8,128)(2,1)S(1)} %get-tuple-element.33.err_ref, bf16[1024,1024]{1,0:T(8,128)(2,1)S(1)} %get-tuple-element.28.refs_18_.wc_ref, bf16[512,576]{1,0:T(8,128)(2,1)S(1)} %get-tuple-element.35.attn_t, bf16[6,576,256]{2,1,0:T(8,128)(2,1)S(1)} %copy-done.20, ...), custom_call_target="tpu_custom_call" | custom-call | flops 8000000000 | bytes 10000000 | tf_op jit(solution)/shard_map/pallas_call | solution.py:348
  113.7 0.1 collective-permute-start.24
  113.7 0.5 collective-permute-start.23
  114.2 1.0 reshape.81
  115.3 0.2 collective-permute-start.22
  115.4 1.2 collective-permute-start.25
  116.6 2.5 %collective-permute-done.25 = f32[2,1024]{1,0:T(2,128)S(1)} collective-permute-done((f32[2,1024]{1,0:T(2,128)S(1)}, f32[2,1024]{1,0:T(2,128)S(1)}, u32[]{:S(2)}, u32[]{:S(2)}) %collective-permute-start.25) | collective-permute-done | bytes 8224 | tf_op jit(solution)/shard_map/ppermute | solution.py:364
  119.2 38.2 %psum.7 = f32[3584]{0:T(1024)S(1)} all-reduce(f32[3584]{0:T(1024)S(1)} %pad_maximum_fusion), channel_id=1, replica_groups=mesh['lat'=8,'tp'=4] {'lat'}, use_global_device_ids=true, to_apply=%region_0.1 | all-reduce | flops 3584 | bytes 28672 | tf_op jit(solution)/shard_map/psum | solution.py:452
  157.4 0.6 slice.61
  158.0 0.6 reshape.86
  158.8 6.3 %maximum_bitcast_fusion = bf16[42,2,12,256]{3,1,2,0:T(2,128)(2,1)} fusion(s32[]{:T(128)S(6)} %select_n.26, bf16[24,6,2,256]{3,2,1,0:T(2,128)(2,1)S(1)} %reshape.81, bf16[24,6,2,256]{3,2,1,0:T(2,128)(2,1)S(1)} %reshape.80, bf16[24,6,2,256]{3,2,1,0:T(2,128)(2,1)S(1)} %reshape.83, bf16[24,6,2,256]{3,2,1,0:T(2,128)(2,1)S(1)} %reshape.82), kind=kLoop, calls=%fused_computation.9 | loop fusion | flops 1290240 | bytes 1105924 | tf_op jit(solution)/shard_map/transpose | solution.py:446
  (77 shorter events, 0.5 us)
Async XLA Ops:
  0.6 29.2 %copy-start.7 = (f32[2,3,256]{2,0,1:T(2,128)S(1)}, f32[2,3,256]{2,0,1:T(2,128)}, u32[]{:S(2)}) copy-start(f32[2,3,256]{2,0,1:T(2,128)} %param.12) | copy-start | bytes 18436
  0.6 29.3 %copy-start.22 = (s32[42,2,96]{2,1,0:T(2,128)S(1)}, s32[42,2,96]{2,1,0:T(2,128)}, u32[]{:S(2)}) copy-start(s32[42,2,96]{2,1,0:T(2,128)} %param.15) | copy-start | bytes 96772
  0.7 39.0 %collective-permute-start.14 = (bf16[3,1024,256]{2,1,0:T(8,128)(2,1)}, bf16[3,1024,256]{2,1,0:T(8,128)(2,1)S(1)}, u32[]{:S(2)}, u32[]{:S(2)}) collective-permute-start(bf16[3,1024,256]{2,1,0:T(8,128)(2,1)} %bitcast.23), channel_id=1, source_target_pairs={{0,1},{1,0},{2,3},{3,2},{4,5},{5,4},{6,7},{7,6},{8,9},{9,8},{10,11... | collective-permute-start | bytes 4718600 | tf_op jit(solution)/shard_map/ppermute | solution.py:364
  1.8 33.5 %copy-start = (bf16[1024,3,256]{2,0,1:T(8,128)(2,1)S(1)}, bf16[1024,3,256]{2,0,1:T(8,128)(2,1)}, u32[]{:S(2)}) copy-start(bf16[1024,3,256]{2,0,1:T(8,128)(2,1)} %param.10) | copy-start | bytes 4718596
  4.4 28.1 %copy-start.1 = (bf16[288,256]{1,0:T(8,128)(2,1)}, bf16[288,256]{1,0:T(8,128)(2,1)S(1)}, u32[]{:S(2)}) copy-start(bf16[288,256]{1,0:T(8,128)(2,1)S(1)} %reshape.70.refs_0_) | copy-start | bytes 442372
  4.4 13.4 %collective-permute-start.1 = (bf16[288,256]{1,0:T(8,128)(2,1)S(1)}, bf16[288,256]{1,0:T(8,128)(2,1)S(1)}, u32[]{:S(2)}, u32[]{:S(2)}) collective-permute-start(bf16[288,256]{1,0:T(8,128)(2,1)S(1)} %reshape.70.refs_0_), channel_id=1, source_target_pairs={{0,2},{1,3},{2,0},{3,1},{4,6},{5,7},{6,4},{7,5},{8,10},{9,11},{10,... | collective-permute-start | bytes 442376 | tf_op jit(solution)/shard_map/ppermute | solution.py:364
  8.7 9.3 %collective-permute-start.2 = (bf16[288,256]{1,0:T(8,128)(2,1)}, bf16[288,256]{1,0:T(8,128)(2,1)}, u32[]{:S(2)}, u32[]{:S(2)}) collective-permute-start(bf16[288,256]{1,0:T(8,128)(2,1)} %reshape.71), channel_id=1, source_target_pairs={{0,3},{1,2},{2,1},{3,0},{4,7},{5,6},{6,5},{7,4},{8,11},{9,10},{10,... | collective-permute-start | bytes 442376 | tf_op jit(solution)/shard_map/ppermute | solution.py:364
  10.4 10.2 %collective-permute-start.5 = (bf16[288,256]{1,0:T(8,128)(2,1)}, bf16[288,256]{1,0:T(8,128)(2,1)}, u32[]{:S(2)}, u32[]{:S(2)}) collective-permute-start(bf16[288,256]{1,0:T(8,128)(2,1)} %reshape.72), channel_id=1, source_target_pairs={{0,30},{1,31},{2,28},{3,29},{4,2},{5,3},{6,0},{7,1},{8,6},{9,7},{1... | collective-permute-start | bytes 442376 | tf_op jit(solution)/shard_map/ppermute | solution.py:364
  17.7 7.1 %collective-permute-start.6 = (bf16[288,256]{1,0:T(8,128)(2,1)}, bf16[288,256]{1,0:T(8,128)(2,1)S(1)}, u32[]{:S(2)}, u32[]{:S(2)}) collective-permute-start(bf16[288,256]{1,0:T(8,128)(2,1)} %reshape.73), channel_id=1, source_target_pairs={{0,31},{1,30},{2,29},{3,28},{4,3},{5,2},{6,1},{7,0},{8,7},{9,6},{1... | collective-permute-start | bytes 442376 | tf_op jit(solution)/shard_map/ppermute | solution.py:364
  17.8 14.7 %copy-start.8 = (bf16[288,256]{1,0:T(8,128)(2,1)}, bf16[288,256]{1,0:T(8,128)(2,1)S(1)}, u32[]{:S(2)}) copy-start(bf16[288,256]{1,0:T(8,128)(2,1)S(1)} %collective-permute-done.1.refs_2_) | copy-start | bytes 442372
  24.8 0.7 copy-start.11
  25.4 14.3 %collective-permute-start.18 = (bf16[256,1024]{1,0:T(8,128)(2,1)}, bf16[256,1024]{1,0:T(8,128)(2,1)}, u32[]{:S(2)}, u32[]{:S(2)}) collective-permute-start(bf16[256,1024]{1,0:T(8,128)(2,1)} %po_ref.1), channel_id=1, source_target_pairs={{0,2},{1,3},{2,0},{3,1},{4,6},{5,7},{6,4},{7,5},{8,10},{9,11},{10,... | collective-permute-start | bytes 1572872 | tf_op jit(solution)/shard_map/ppermute | solution.py:364
  25.9 15.0 %collective-permute-start = (bf16[288,256]{1,0:T(8,128)(2,1)}, bf16[288,256]{1,0:T(8,128)(2,1)}, u32[]{:S(2)}, u32[]{:S(2)}) collective-permute-start(bf16[288,256]{1,0:T(8,128)(2,1)} %reshape.71), channel_id=1, source_target_pairs={{0,1},{1,0},{2,3},{3,2},{4,5},{5,4},{6,7},{7,6},{8,9},{9,8},{10,11... | collective-permute-start | bytes 442376 | tf_op jit(solution)/shard_map/ppermute | solution.py:364
  25.9 15.0 %collective-permute-start.3 = (bf16[288,256]{1,0:T(8,128)(2,1)}, bf16[288,256]{1,0:T(8,128)(2,1)}, u32[]{:S(2)}, u32[]{:S(2)}) collective-permute-start(bf16[288,256]{1,0:T(8,128)(2,1)} %reshape.72), channel_id=1, source_target_pairs={{0,28},{1,29},{2,30},{3,31},{4,0},{5,1},{6,2},{7,3},{8,4},{9,5},{1... | collective-permute-start | bytes 442376 | tf_op jit(solution)/shard_map/ppermute | solution.py:364
  29.9 1.2 collective-permute-start.15
  31.0 9.9 %collective-permute-start.4 = (bf16[288,256]{1,0:T(8,128)(2,1)}, bf16[288,256]{1,0:T(8,128)(2,1)}, u32[]{:S(2)}, u32[]{:S(2)}) collective-permute-start(bf16[288,256]{1,0:T(8,128)(2,1)} %reshape.73), channel_id=1, source_target_pairs={{0,29},{1,28},{2,31},{3,30},{4,1},{5,0},{6,3},{7,2},{8,5},{9,4},{1... | collective-permute-start | bytes 442376 | tf_op jit(solution)/shard_map/ppermute | solution.py:364
  35.4 5.6 %copy-start.2 = (bf16[288,256]{1,0:T(8,128)(2,1)S(1)}, bf16[288,256]{1,0:T(8,128)(2,1)}, u32[]{:S(2)}) copy-start(bf16[288,256]{1,0:T(8,128)(2,1)} %copy-done.1) | copy-start | bytes 442372
  35.4 5.6 %copy-start.9 = (bf16[288,256]{1,0:T(8,128)(2,1)S(1)}, bf16[288,256]{1,0:T(8,128)(2,1)}, u32[]{:S(2)}) copy-start(bf16[288,256]{1,0:T(8,128)(2,1)} %copy-done.8) | copy-start | bytes 442372
  35.4 5.6 %copy-start.12 = (bf16[288,256]{1,0:T(8,128)(2,1)S(1)}, bf16[288,256]{1,0:T(8,128)(2,1)}, u32[]{:S(2)}) copy-start(bf16[288,256]{1,0:T(8,128)(2,1)} %copy-done.11) | copy-start | bytes 442372
  39.7 40.7 %collective-permute-start.17 = (bf16[256,1024]{1,0:T(8,128)(2,1)}, bf16[256,1024]{1,0:T(8,128)(2,1)}, u32[]{:S(2)}, u32[]{:S(2)}) collective-permute-start(bf16[256,1024]{1,0:T(8,128)(2,1)} %po_ref.1), channel_id=1, source_target_pairs={{0,1},{1,0},{2,3},{3,2},{4,5},{5,4},{6,7},{7,6},{8,9},{9,8},{10,11... | collective-permute-start | bytes 1572872 | tf_op jit(solution)/shard_map/ppermute | solution.py:364
  39.7 40.7 %collective-permute-start.19 = (bf16[256,1024]{1,0:T(8,128)(2,1)}, bf16[256,1024]{1,0:T(8,128)(2,1)}, u32[]{:S(2)}, u32[]{:S(2)}) collective-permute-start(bf16[256,1024]{1,0:T(8,128)(2,1)} %collective-permute-done.18.w2), channel_id=1, source_target_pairs={{0,1},{1,0},{2,3},{3,2},{4,5},{5,4},{6,7},{7,6},{8,9},{9,8},{10,11... | collective-permute-start | bytes 1572872 | tf_op jit(solution)/shard_map/ppermute | solution.py:364
  41.0 15.0 %copy-start.21 = (bf16[42,2,12,256]{3,1,2,0:T(2,128)(2,1)S(1)}, bf16[42,2,12,256]{3,1,2,0:T(2,128)(2,1)}, u32[]{:S(2)}) copy-start(bf16[42,2,12,256]{3,1,2,0:T(2,128)(2,1)} %param.9) | copy-start | bytes 1548292
  53.2 1.0 copy-start.17
  54.2 1.2 copy-start.19
  55.5 25.6 %copy-start.6 = (f32[2,1024]{1,0:T(2,128)S(1)}, f32[2,1024]{1,0:T(2,128)}, u32[]{:S(2)}) copy-start(f32[2,1024]{1,0:T(2,128)} %c_ref.1) | copy-start | bytes 24580
  55.5 35.7 %collective-permute-start.16 = (bf16[576,512]{1,0:T(8,128)(2,1)}, bf16[576,512]{1,0:T(8,128)(2,1)}, u32[]{:S(2)}, u32[]{:S(2)}) collective-permute-start(bf16[576,512]{1,0:T(8,128)(2,1)} %get-tuple-element.26.refs_16_.attn_ref), channel_id=1, source_target_pairs={{0,2},{1,3},{2,0},{3,1},{4,6},{5,7},{6,4},{7,5},{8,10},{9,11},{10,... | collective-permute-start | bytes 1769480 | tf_op jit(solution)/shard_map/ppermute | solution.py:364
  59.0 3.2 %collective-permute-start.7 = (bf16[288,256]{1,0:T(8,128)(2,1)}, bf16[288,256]{1,0:T(8,128)(2,1)}, u32[]{:S(2)}, u32[]{:S(2)}) collective-permute-start(bf16[288,256]{1,0:T(8,128)(2,1)} %reshape.75), channel_id=1, source_target_pairs={{0,1},{1,0},{2,3},{3,2},{4,5},{5,4},{6,7},{7,6},{8,9},{9,8},{10,11... | collective-permute-start | bytes 442376 | tf_op jit(solution)/shard_map/ppermute | solution.py:364
  60.6 14.5 %collective-permute-start.8 = (bf16[288,256]{1,0:T(8,128)(2,1)}, bf16[288,256]{1,0:T(8,128)(2,1)}, u32[]{:S(2)}, u32[]{:S(2)}) collective-permute-start(bf16[288,256]{1,0:T(8,128)(2,1)} %reshape.74.refs_8_), channel_id=1, source_target_pairs={{0,2},{1,3},{2,0},{3,1},{4,6},{5,7},{6,4},{7,5},{8,10},{9,11},{10,... | collective-permute-start | bytes 442376 | tf_op jit(solution)/shard_map/ppermute | solution.py:364
  62.1 16.2 %collective-permute-start.9 = (bf16[288,256]{1,0:T(8,128)(2,1)}, bf16[288,256]{1,0:T(8,128)(2,1)}, u32[]{:S(2)}, u32[]{:S(2)}) collective-permute-start(bf16[288,256]{1,0:T(8,128)(2,1)} %reshape.75), channel_id=1, source_target_pairs={{0,3},{1,2},{2,1},{3,0},{4,7},{5,6},{6,5},{7,4},{8,11},{9,10},{10,... | collective-permute-start | bytes 442376 | tf_op jit(solution)/shard_map/ppermute | solution.py:364
  65.7 17.8 %copy-start.18 = (bf16[576,1024]{1,0:T(8,128)(2,1)S(1)}, bf16[576,1024]{1,0:T(8,128)(2,1)}, u32[]{:S(2)}) copy-start(bf16[576,1024]{1,0:T(8,128)(2,1)} %copy-done.17) | copy-start | bytes 3538948
  75.1 10.4 %collective-permute-start.10 = (bf16[288,256]{1,0:T(8,128)(2,1)}, bf16[288,256]{1,0:T(8,128)(2,1)S(1)}, u32[]{:S(2)}, u32[]{:S(2)}) collective-permute-start(bf16[288,256]{1,0:T(8,128)(2,1)} %reshape.76), channel_id=1, source_target_pairs={{0,28},{1,29},{2,30},{3,31},{4,0},{5,1},{6,2},{7,3},{8,4},{9,5},{1... | collective-permute-start | bytes 442376 | tf_op jit(solution)/shard_map/ppermute | solution.py:364
  78.4 9.8 %collective-permute-start.12 = (bf16[288,256]{1,0:T(8,128)(2,1)}, bf16[288,256]{1,0:T(8,128)(2,1)S(1)}, u32[]{:S(2)}, u32[]{:S(2)}) collective-permute-start(bf16[288,256]{1,0:T(8,128)(2,1)} %reshape.76), channel_id=1, source_target_pairs={{0,30},{1,31},{2,28},{3,29},{4,2},{5,3},{6,0},{7,1},{8,6},{9,7},{1... | collective-permute-start | bytes 442376 | tf_op jit(solution)/shard_map/ppermute | solution.py:364
  80.4 7.7 %collective-permute-start.11 = (bf16[288,256]{1,0:T(8,128)(2,1)}, bf16[288,256]{1,0:T(8,128)(2,1)S(1)}, u32[]{:S(2)}, u32[]{:S(2)}) collective-permute-start(bf16[288,256]{1,0:T(8,128)(2,1)} %reshape.77), channel_id=1, source_target_pairs={{0,29},{1,28},{2,31},{3,30},{4,1},{5,0},{6,3},{7,2},{8,5},{9,4},{1... | collective-permute-start | bytes 442376 | tf_op jit(solution)/shard_map/ppermute | solution.py:364
  80.4 10.7 %collective-permute-start.13 = (bf16[288,256]{1,0:T(8,128)(2,1)}, bf16[288,256]{1,0:T(8,128)(2,1)S(1)}, u32[]{:S(2)}, u32[]{:S(2)}) collective-permute-start(bf16[288,256]{1,0:T(8,128)(2,1)} %reshape.77), channel_id=1, source_target_pairs={{0,31},{1,30},{2,29},{3,28},{4,3},{5,2},{6,1},{7,0},{8,7},{9,6},{1... | collective-permute-start | bytes 442376 | tf_op jit(solution)/shard_map/ppermute | solution.py:364
  83.5 7.6 %copy-start.3 = (bf16[288,256]{1,0:T(8,128)(2,1)S(1)}, bf16[288,256]{1,0:T(8,128)(2,1)}, u32[]{:S(2)}) copy-start(bf16[288,256]{1,0:T(8,128)(2,1)} %copy-done.1) | copy-start | bytes 442372
  83.5 7.6 %copy-start.4 = (bf16[288,256]{1,0:T(8,128)(2,1)S(1)}, bf16[288,256]{1,0:T(8,128)(2,1)}, u32[]{:S(2)}) copy-start(bf16[288,256]{1,0:T(8,128)(2,1)} %reshape.74.refs_8_) | copy-start | bytes 442372
  83.5 7.6 %copy-start.10 = (bf16[288,256]{1,0:T(8,128)(2,1)S(1)}, bf16[288,256]{1,0:T(8,128)(2,1)}, u32[]{:S(2)}) copy-start(bf16[288,256]{1,0:T(8,128)(2,1)} %copy-done.8) | copy-start | bytes 442372
  83.6 7.6 %copy-start.13 = (bf16[288,256]{1,0:T(8,128)(2,1)S(1)}, bf16[288,256]{1,0:T(8,128)(2,1)}, u32[]{:S(2)}) copy-start(bf16[288,256]{1,0:T(8,128)(2,1)} %copy-done.11) | copy-start | bytes 442372
  91.1 6.2 %copy-start.20 = (bf16[6,576,256]{2,1,0:T(8,128)(2,1)S(1)}, bf16[6,576,256]{2,1,0:T(8,128)(2,1)}, u32[]{:S(2)}) copy-start(bf16[6,576,256]{2,1,0:T(8,128)(2,1)} %copy-done.19) | copy-start | bytes 5308420
  94.7 0.7 copy-start.5
  95.3 0.7 copy-start.14
  96.0 0.7 copy-start.15
  96.7 0.7 copy-start.16
  113.7 1.8 %collective-permute-start.24 = (f32[2,1024]{1,0:T(2,128)S(1)}, f32[2,1024]{1,0:T(2,128)S(1)}, u32[]{:S(2)}, u32[]{:S(2)}) collective-permute-start(f32[2,1024]{1,0:T(2,128)S(1)} %get-tuple-element.42), channel_id=1, source_target_pairs={{0,1},{1,0},{2,3},{3,2},{4,5},{5,4},{6,7},{7,6},{8,9},{9,8},{10,11... | collective-permute-start | bytes 24584 | tf_op jit(solution)/shard_map/ppermute | solution.py:364
  113.7 2.9 %collective-permute-start.23 = (f32[3,2,256]{2,1,0:T(2,128)S(1)}, f32[3,2,256]{2,1,0:T(2,128)S(1)}, u32[]{:S(2)}, u32[]{:S(2)}) collective-permute-start(f32[3,2,256]{2,1,0:T(2,128)S(1)} %slice.59), channel_id=1, source_target_pairs={{0,1},{1,0},{2,3},{3,2},{4,5},{5,4},{6,7},{7,6},{8,9},{9,8},{10,11... | collective-permute-start | bytes 18440 | tf_op jit(solution)/shard_map/ppermute | solution.py:364
  115.2 43.4 %collective-permute-start.20 = (bf16[288,256]{1,0:T(8,128)(2,1)}, bf16[288,256]{1,0:T(8,128)(2,1)S(1)}, u32[]{:S(2)}, u32[]{:S(2)}) collective-permute-start(bf16[288,256]{1,0:T(8,128)(2,1)} %copy-done.16), channel_id=1, source_target_pairs={{0,4},{1,5},{2,6},{3,7},{4,8},{5,9},{6,10},{7,11},{8,12},{9,13},{1... | collective-permute-start | bytes 442376 | tf_op jit(solution)/shard_map/ppermute | solution.py:364
  115.3 43.4 %collective-permute-start.22 = (bf16[288,256]{1,0:T(8,128)(2,1)}, bf16[288,256]{1,0:T(8,128)(2,1)S(1)}, u32[]{:S(2)}, u32[]{:S(2)}) collective-permute-start(bf16[288,256]{1,0:T(8,128)(2,1)} %copy-done.15), channel_id=1, source_target_pairs={{0,1},{1,0},{2,3},{3,2},{4,5},{5,4},{6,7},{7,6},{8,9},{9,8},{10,11... | collective-permute-start | bytes 442376 | tf_op jit(solution)/shard_map/ppermute | solution.py:364
  115.4 43.3 %collective-permute-start.21 = (bf16[288,256]{1,0:T(8,128)(2,1)}, bf16[288,256]{1,0:T(8,128)(2,1)S(1)}, u32[]{:S(2)}, u32[]{:S(2)}) collective-permute-start(bf16[288,256]{1,0:T(8,128)(2,1)} %copy-done.14), channel_id=1, source_target_pairs={{0,5},{1,4},{2,7},{3,6},{4,9},{5,8},{6,11},{7,10},{8,13},{9,12},{1... | collective-permute-start | bytes 442376 | tf_op jit(solution)/shard_map/ppermute | solution.py:364
  115.4 3.7 %collective-permute-start.25 = (f32[2,1024]{1,0:T(2,128)S(1)}, f32[2,1024]{1,0:T(2,128)S(1)}, u32[]{:S(2)}, u32[]{:S(2)}) collective-permute-start(f32[2,1024]{1,0:T(2,128)S(1)} %add.63), channel_id=1, source_target_pairs={{0,2},{1,3},{2,0},{3,1},{4,6},{5,7},{6,4},{7,5},{8,10},{9,11},{10,... | collective-permute-start | bytes 24584 | tf_op jit(solution)/shard_map/ppermute | solution.py:364
where the time goes:
time: 166 us; the launch traced here: 165 us
  blocking collectives  38.2 us (23%)
  Pallas kernels  37.8 us (23%)
  waiting for transfers between devices  28.9 us (17%)
  local copies, waits for them, and re-layouts  27.6 us (17%)
  starting transfers between devices  24.3 us (15%)
  other arithmetic  6.53 us (4%)
    psum x1, blocking collectives, local(): both = lax.psum(both, 'lat')  38.2 us
    ppermute x26, waiting for transfers between devices, send(): return lax.ppermute(block, ('lat', 'tp'), route)  28.9 us
    ppermute x26, starting transfers between devices, send(): return lax.ppermute(block, ('lat', 'tp'), route)  24.3 us
    pallas_call x1, Pallas kernels, backward(): pl.pallas_call(backward_kernel, out_shape=(jax.ShapeDtypeStruct((6, 2, wi...  16.3 us
    pallas_call x1, Pallas kernels, forward(): pl.pallas_call(forward_kernel, out_shape=(jax.ShapeDtypeStruct((2 * n, d)...  12.2 us
    reshape x4, local copies, waits for them, and re-layouts, row_parts(): part[:, :half].reshape(many * half * lev, width)  6.51 us
    transpose x1, other arithmetic, local(): mixed = jnp.transpose(mixed, (0, 2, 1, 3))  6.26 us
    unnamed x47, local copies, waits for them, and re-layouts  5.64 us
  transfers between devices with their start and end apart: 26, of which 9 were waited for; matrix products, arithmetic and copies ran while one was open for 13% of the time, Pallas kernels for 11%

commit v1 on v0

--- a/solution.py
+++ b/solution.py
@@ -161,10 +161,16 @@
         return carry
 
     lax.fori_loop(0, 3, project, 0)
+    attend(qkv_ref, idk_ref, idq_ref, attn_ref, 0, 3)
+
+
+def attend(qkv_ref, idk_ref, idq_ref, attn_ref, first, last):
     mask_a, mask_b = head_masks()
+    cells = idk_ref.shape[0] // 4
 
     def window(w, carry):
         rows = pl.ds(pl.multiple_of(w * cells, 16), cells)
+        to = pl.ds(pl.multiple_of((w - first) * cells, 16), cells)
         allowed = allowed_t(idk_ref, idq_ref, w, cells)
         for hp in range(4):
             g, lanes = hp // 2, slice(128 * (hp % 2), 128 * (hp % 2) + 128)
@@ -173,10 +179,26 @@
             ot = lax.dot_general(
                 qkv_ref[3 * g + 2, rows, lanes], pt.astype(BF), TN, preferred_element_type=F32
             )
-            attn_ref[rows, 128 * hp : 128 * hp + 128] = merge_heads(ot).astype(BF)
-        return carry
-
-    lax.fori_loop(0, 4, window, 0)
+            attn_ref[to, 128 * hp : 128 * hp + 128] = merge_heads(ot).astype(BF)
+        return carry
+
+    lax.fori_loop(first, last, window, 0)
+
+
+def last_kernel(qkv_ref, idk_ref, idq_ref, attn_ref):
+    attend(qkv_ref, idk_ref, idq_ref, attn_ref, 3, 4)
+
+
+def last_window(qkv, idk, idq):
+    n, width = qkv.shape[1:]
+    return pl.pallas_call(
+        last_kernel,
+        out_shape=jax.ShapeDtypeStruct((n // 4, 2 * width), BF),
+        in_specs=spec(3),
+        out_specs=spec(1)[0],
+        compiler_params=params(16),
+        cost_estimate=pl.CostEstimate(flops=10**9, bytes_accessed=2 * 10**6, transcendentals=10**6),
+    )(qkv, idk, idq)
 
 
 def forward(t, pieces, wo, wp, idk, idq):
@@ -187,17 +209,17 @@
         out_shape=(
             jax.ShapeDtypeStruct((2 * n, d), BF),
             jax.ShapeDtypeStruct((6, 2 * n, width), BF),
-            jax.ShapeDtypeStruct((2 * n, 2 * width), BF),
+            jax.ShapeDtypeStruct((2 * n // 4 * 3, 2 * width), BF),
         ),
         in_specs=[pl.BlockSpec(memory_space=pltpu.SMEM)] + spec(12),
         out_specs=tuple(spec(3)),
         scratch_shapes=[pltpu.VMEM((2 * n, d), F32)],
-        compiler_params=params(40),
+        compiler_params=params(24),
         cost_estimate=pl.CostEstimate(flops=8 * 10**9, bytes_accessed=10 * 10**6, transcendentals=10**6),
     )(t, *pieces, wo, wp, idk, idq)
 
 
-def turn_kernel(normed_ref, attn_ref, normed_t, attn_t):
+def turn_kernel(normed_ref, a_ref, b_ref, normed_t, attn_t):
     d = normed_ref.shape[1]
 
     def body(i, carry):
@@ -209,38 +231,40 @@
 
     def body2(i, carry):
         cols = pl.ds(pl.multiple_of(i * 256, 256), 256)
-        attn_t[cols, :] = attn_ref[:, cols].T
-        return carry
-
-    lax.fori_loop(0, attn_ref.shape[1] // 256, body2, 0)
+        attn_t[cols, :] = jnp.concatenate([a_ref[:, cols], b_ref[:, cols]], axis=0).T
+        return carry
+
+    lax.fori_loop(0, a_ref.shape[1] // 256, body2, 0)
 
 
 def turn(normed, attn):
     n, d = normed.shape
-    e = attn.shape[1]
+    e = attn[0].shape[1]
     return pl.pallas_call(
         turn_kernel,
         out_shape=(jax.ShapeDtypeStruct((d, n), BF), jax.ShapeDtypeStruct((e, n), BF)),
-        in_specs=spec(2),
+        in_specs=spec(3),
         out_specs=tuple(spec(2)),
-        compiler_params=params(24),
+        compiler_params=params(16),
         cost_estimate=pl.CostEstimate(flops=10**9, bytes_accessed=4 * n * (d + e), transcendentals=0),
-    )(normed, attn)
+    )(normed, *attn)
 
 
 def output_kernel(t_ref, *refs):
     pieces, targets = refs[:8], refs[8:16]
-    own_ref, other_ref, wc_ref, idk_ref = refs[16:20]
-    mixed, err_ref, y_ref = refs[20:24], refs[24], refs[25]
+    attns, wc_ref, idk_ref = refs[16:20], refs[20], refs[21]
+    mixed, err_ref, y_ref = refs[22:26], refs[26], refs[27]
     t = t_ref[0]
     half = pieces[0].shape[0] // 4
     cells = 2 * half
     width = pieces[0].shape[1]
-    e = own_ref.shape[1]
+    e = attns[0].shape[1]
     for k in range(4):
         cols = pl.ds(pl.multiple_of((t ^ k) * width, width), width)
-        y_ref[...] = jnp.dot(own_ref[...], wc_ref[:e, cols], preferred_element_type=F32) + jnp.dot(
-            other_ref[...], wc_ref[e:, cols], preferred_element_type=F32
+        own = jnp.concatenate([attns[0][...], attns[1][...]], axis=0)
+        other = jnp.concatenate([attns[2][...], attns[3][...]], axis=0)
+        y_ref[...] = jnp.dot(own, wc_ref[:e, cols], preferred_element_type=F32) + jnp.dot(
+            other, wc_ref[e:, cols], preferred_element_type=F32
         )
         for p in range(2):
             errs = [[None, None], [None, None]]
@@ -271,12 +295,12 @@
     return pl.pallas_call(
         output_kernel,
         out_shape=(piece, piece, piece, piece, jax.ShapeDtypeStruct((2 * n, d), BF)),
-        in_specs=[pl.BlockSpec(memory_space=pltpu.SMEM)] + spec(20),
+        in_specs=[pl.BlockSpec(memory_space=pltpu.SMEM)] + spec(22),
         out_specs=tuple(spec(5)),
         scratch_shapes=[pltpu.VMEM((2 * n, width), F32)],
-        compiler_params=params(40),
+        compiler_params=params(24),
         cost_estimate=pl.CostEstimate(flops=2 * 10**9, bytes_accessed=8 * 10**6, transcendentals=0),
-    )(t, *pieces, *targets, own, other, wc, idk)
+    )(t, *pieces, *targets, *own, *other, wc, idk)
 
 
 def masked_sums(grad, w, bounds):
@@ -286,8 +310,7 @@
 
 
 def backward_kernel(
-    err_ref, wc_ref, attn_t, qkv_ref, normed_t, wo_ref, wp_ref, bo_ref, bp_ref, po_ref, pp_ref, pb_ref,
-    idk_ref, idq_ref, gq_ref, gp_ref, d_ref, g_ref
+    err_ref, wc_ref, attn_t, qkv_ref, po_ref, pp_ref, pb_ref, idk_ref, idq_ref, g_ref, proj_ref, d_ref
 ):
     e = attn_t.shape[0]
     cells = idk_ref.shape[0] // 4
@@ -325,35 +348,126 @@
         b = pb_ref[:, cols]
         h0, l0 = masked_sums(grad[:n], po_ref[:, cols].astype(F32), b)
         h1, l1 = masked_sums(grad[n:], pp_ref[:, cols].astype(F32), b)
-        gp_ref[0:1, cols] = h0 + h1
-        gp_ref[1:2, cols] = l0 + l1
+        proj_ref[pl.ds(i, 1), :] = h0 + h1
+        proj_ref[pl.ds(4 + i, 1), :] = l0 + l1
         return carry
 
     lax.fori_loop(0, err_ref.shape[1] // 256, proj_part, 0)
 
+
+def backward(err, wc, attn_t, qkv, po, pp, pb, idk, idq):
+    n, width = qkv.shape[1:]
+    return pl.pallas_call(
+        backward_kernel,
+        out_shape=(jax.ShapeDtypeStruct((6, n, width), BF), jax.ShapeDtypeStruct((8, width), F32)),
+        in_specs=spec(9),
+        out_specs=tuple(spec(2)),
+        scratch_shapes=[pltpu.VMEM((n, attn_t.shape[0]), BF)],
+        compiler_params=params(20),
+        cost_estimate=pl.CostEstimate(flops=8 * 10**9, bytes_accessed=10 * 10**6, transcendentals=10**6),
+    )(err, wc, attn_t, qkv, po, pp, pb, idk, idq)
+
+
+def qkv_sums_kernel(g_ref, normed_t, wo_ref, wp_ref, bo_ref, bp_ref, own_ref, peer_ref):
     def qkv_part(i, carry):
-        for g, (w_ref, b_ref) in enumerate(((wo_ref, bo_ref), (wp_ref, bp_ref))):
+        for g, (w_ref, b_ref, to_ref) in enumerate(
+            ((wo_ref, bo_ref, own_ref), (wp_ref, bp_ref, peer_ref))
+        ):
             grad = jnp.dot(normed_t[...], g_ref[3 * g + i], preferred_element_type=F32)
             hi, lo = masked_sums(grad, w_ref[i].astype(F32), b_ref[i])
-            gq_ref[3 * g + i, 0:1] = hi
-            gq_ref[3 * g + i, 1:2] = lo
+            to_ref[pl.ds(2 * i, 1), :] = hi
+            to_ref[pl.ds(2 * i + 1, 1), :] = lo
         return carry
 
     lax.fori_loop(0, 3, qkv_part, 0)
 
 
-def backward(err, wc, attn_t, qkv, normed_t, wo, wp, bo, bp, po, pp, pb, idk, idq):
-    n, d = err.shape
-    width = qkv.shape[2]
-    return pl.pallas_call(
-        backward_kernel,
-        out_shape=(jax.ShapeDtypeStruct((6, 2, width), F32), jax.ShapeDtypeStruct((2, d), F32)),
-        in_specs=spec(14),
+def qkv_sums(g, normed_t, wo, wp, bo, bp):
+    width = g.shape[2]
+    return pl.pallas_call(
+        qkv_sums_kernel,
+        out_shape=(jax.ShapeDtypeStruct((6, width), F32),) * 2,
+        in_specs=spec(6),
         out_specs=tuple(spec(2)),
-        scratch_shapes=[pltpu.VMEM((n, attn_t.shape[0]), BF), pltpu.VMEM((6, n, width), BF)],
-        compiler_params=params(40),
-        cost_estimate=pl.CostEstimate(flops=8 * 10**9, bytes_accessed=10 * 10**6, transcendentals=10**6),
-    )(err, wc, attn_t, qkv, normed_t, wo, wp, bo, bp, po, pp, pb, idk, idq)
+        compiler_params=params(20),
+        cost_estimate=pl.CostEstimate(flops=4 * 10**9, bytes_accessed=8 * 10**6, transcendentals=0),
+    )(g, normed_t, wo, wp, bo, bp)
+
+
+def split_kernel(s_ref, x_ref, m0, m1, p0, p1):
+    offset, core = s_ref[0], s_ref[1]
+    rows, lon, lev, width = x_ref.shape
+    many = (rows + WLAT) // 2
+    half = lon * lev // 2
+    for rel, outs in ((0, (m0, m1)), (1, (p0, p1))):
+        base = many * (core ^ rel) - offset
+
+        def body(i, carry):
+            parts = [[], []]
+            for j in range(4):
+                r = base + 4 * i + j
+                v = x_ref[jnp.clip(r, 0, rows - 1)].astype(F32).reshape(lon * lev, width)
+                v = jnp.where((r >= 0) & (r < rows), v, 0.0)
+                parts[0].append(v[half:])
+                parts[1].append(v[:half])
+            at = pl.ds(pl.multiple_of(4 * half * i, 16), 4 * half)
+            for s in range(2):
+                outs[s][at, :] = jnp.concatenate(parts[s], axis=0).astype(BF)
+            return carry
+
+        lax.fori_loop(0, many // 4, body, 0)
+
+
+def split(place, block):
+    rows, lev, lon, width = block.shape
+    block = jnp.transpose(block, (0, 2, 1, 3))
+    piece = jax.ShapeDtypeStruct(((rows + WLAT) // 2 * lon * lev // 2, width), BF)
+    return pl.pallas_call(
+        split_kernel,
+        out_shape=(piece,) * 4,
+        in_specs=[pl.BlockSpec(memory_space=pltpu.SMEM)] + spec(1),
+        out_specs=tuple(spec(4)),
+        compiler_params=params(16),
+        cost_estimate=pl.CostEstimate(flops=10**6, bytes_accessed=2 * 10**6, transcendentals=0),
+    )(place, block)
+
+
+def join_kernel(s_ref, a0, a1, b0, b1, out_ref, grid_ref):
+    offset, core = s_ref[0], s_ref[1]
+    rows, lon, lev, width = out_ref.shape
+    many = (rows + WLAT) // 2
+    half = lon * lev // 2
+    for rel, ins in ((0, (a0, a1)), (1, (b0, b1))):
+        base = many * (core ^ rel)
+        for s in range(2):
+            for i in range(many // 4):
+                v = ins[s][4 * half * i : 4 * half * (i + 1), :].astype(F32)
+                for j in range(4):
+                    grid_ref[base + 4 * i + j, half * (1 - s) : half * (2 - s), :] = v[
+                        half * j : half * (j + 1)
+                    ]
+
+    def body(i, carry):
+        for j in range(2):
+            r = 2 * i + j
+            out_ref[r] = grid_ref[r + offset].reshape(lon, lev, width).astype(BF)
+        return carry
+
+    lax.fori_loop(0, rows // 2, body, 0)
+
+
+def join(place, parts, rows, lon, lev):
+    n, width = parts[0].shape
+    out = pl.pallas_call(
+        join_kernel,
+        out_shape=jax.ShapeDtypeStruct((rows, lon, lev, width), BF),
+        in_specs=[pl.BlockSpec(memory_space=pltpu.SMEM)] + spec(4),
+        out_specs=spec(1)[0],
+        scratch_shapes=[pltpu.VMEM((rows + WLAT, lon * lev, width), F32)],
+        compiler_params=params(16),
+        cost_estimate=pl.CostEstimate(flops=10**6, bytes_accessed=2 * 10**6, transcendentals=0),
+    )(place, *parts)
+    return jnp.transpose(out, (0, 2, 1, 3))
 
 
 def send(block, shift, flip):
@@ -373,35 +487,21 @@
     half = lon // 2
     many = (rows + WLAT) // 2
     sector = lax.axis_index("lat")
+    count = lax.axis_size("lat")
     t = lax.axis_index("tp")
     core = t % 2
     offset = shift_offset[0]
     t_arr = jnp.reshape(t, (1,)).astype(jnp.int32)
-
-    def row_parts(block):
-        block = jnp.transpose(block, (0, 2, 1, 3))
-        padded = jnp.pad(block, ((WLAT, WLAT), (0, 0), (0, 0), (0, 0)))
-        parts = []
-        for flip in range(2):
-            first = WLAT - offset + many * (core ^ flip)
-            part = lax.dynamic_slice_in_dim(padded, first, many, 0)
-            parts.append(
-                [
-                    part[:, half:].reshape(many * half * lev, width),
-                    part[:, :half].reshape(many * half * lev, width),
-                ]
-            )
-        return parts
-
-    def spread(parts):
-        own = [parts[0][0]] + [send(parts[k % 2][0], 0, k) for k in range(1, 4)]
-        nxt = [send(parts[k % 2][1], -1, k) for k in range(4)]
-        return own + nxt
+    place = jnp.stack([offset, core]).astype(jnp.int32)
+
+    m0, m1, p0, p1 = split(place, features)
+    f02, f03 = send(m0, 0, 2), send(p0, 0, 3)
+    f10, f11 = send(m1, -1, 0), send(p1, -1, 1)
+    f01 = send(p0, 0, 1)
+    f12, f13 = send(f10, 0, 2), send(f11, 0, 2)
 
     w3 = jnp.transpose(w_qkv, (1, 0, 2))
     c3 = jnp.transpose(qkv_clip, (1, 0, 2))
-    parts = row_parts(features)
-    pieces = spread(parts)
     w3_peer = send(w3, 0, 1)
     c3_peer = send(c3, 0, 1)
     wc_own, b_own = clip_qkv(w3, c3)
@@ -416,15 +516,28 @@
     idk = ids.reshape(many * lev * lon, 1)
     idq = jnp.concatenate([ids, ids], axis=2)
 
-    normed, qkv, attn = forward(t_arr, pieces, wc_own, wc_peer, idk, idq)
-    attn_other = send(attn, 0, 2)
-
-    first_in = after(target, pieces[2], pieces[3], pieces[6], pieces[7])
-    targets = spread(row_parts(first_in))
-    p1 = send(w_proj, 0, 1)
-    p2 = send(after(w_proj, pieces[2], pieces[3], pieces[6], pieces[7]), 0, 2)
-    p3 = send(p2, 0, 1)
-    pc, pb = clip_proj([w_proj, p1, p2, p3], proj_clip)
+    g0, g1, q0, q1 = split(place, target)
+    g1, q1, q0 = lax.optimization_barrier((g1, q1, q0, f02, f03, f10, f11))[:3]
+    t10, t11 = send(g1, -1, 0), send(q1, -1, 1)
+    t01 = send(q0, 0, 1)
+    share = w_proj.shape[0] // count
+    slab = send(lax.dynamic_slice_in_dim(w_proj, sector * share, share, 0), 0, 2)
+    w2 = lax.all_gather(slab, "lat", axis=0, tiled=True)
+    w1 = send(after(w_proj, f10, f11), 0, 1)
+
+    ya, yb, yc, yd = lax.optimization_barrier((g0, t01, t10, t11, f12, f13))[:4]
+    t02, t03, t12, t13 = send(ya, 0, 2), send(yb, 0, 2), send(yc, 0, 2), send(yd, 0, 2)
+    targets = [g0, t01, t02, t03, t10, t11, t12, t13]
+    f12, f13 = lax.optimization_barrier((f12, f13, t01, t10, t11))[:2]
+    pieces = [m0, f01, f02, f03, f10, f11, f12, f13]
+    normed, qkv, attn_a = forward(t_arr, pieces, wc_own, wc_peer, idk, idq)
+    other_a = send(attn_a, 0, 2)
+    attn_b = last_window(after(qkv, t02, t03, t12, t13), idk, idq)
+    other_b = send(attn_b, 0, 2)
+    attn, attn_other = (attn_a, attn_b), (other_a, other_b)
+    w2 = after(w2, attn_b)
+    w_3 = send(w2, 0, 1)
+    pc, pb = clip_proj([w_proj, w1, w2, w_3], proj_clip)
     normed_t, attn_t = turn(normed, attn)
 
     m00, m01, m10, m11, err = output(t_arr, pieces, targets, attn, attn_other, pc, idk)
@@ -432,26 +545,18 @@
     m10 = send(m10, 1, 0)
     m11 = send(m11, 1, 1)
 
-    gq, gp = backward(
-        err, pc, attn_t, qkv, normed_t, w3, w3_peer, b_own, b_peer, w_proj, p1, pb, idk, idq
-    )
-
-    def grid(block):
-        return block.reshape(many, half, lev, width)
-
-    own = jnp.concatenate([grid(m10), grid(m00)], axis=1)
-    peer = jnp.concatenate([grid(m11), grid(m01)], axis=1)
-    mixed = jnp.concatenate([own, peer, own], axis=0)
-    mixed = lax.dynamic_slice_in_dim(mixed, many * core + offset, rows, 0)
-    mixed = jnp.transpose(mixed, (0, 2, 1, 3))
-
-    gq_own = gq[:3] + send(gq[3:], 0, 1)
-    gp = gp + send(gp, 0, 1)
-    gp = gp + send(gp, 0, 2)
-    both = jnp.concatenate([gq_own.reshape(-1), gp.reshape(-1)])
-    both = lax.psum(both, "lat")
-    qkv_sum = jnp.transpose(both[: gq_own.size].reshape(gq_own.shape), (1, 0, 2))
-    proj_sum = both[gq_own.size :].reshape(gp.shape)
+    grads, proj = backward(err, pc, attn_t, qkv, w_proj, w1, pb, idk, idq)
+    proj_peer = send(proj, 0, 1)
+    grads = after(grads, m01, m10, m11)
+    own, peer = qkv_sums(grads, normed_t, w3, w3_peer, b_own, b_peer)
+    proj = proj + proj_peer
+    proj_other = send(proj, 0, 2)
+    peer = send(peer, 0, 1)
+    sums = jnp.concatenate([own + peer, proj + proj_other], axis=0)
+    sums = jnp.sum(lax.all_gather(sums, "lat", axis=0), axis=0)
+    mixed = join(place, [m00, m10, m01, m11], rows, lon, lev)
+    qkv_sum = jnp.transpose(sums[:6].reshape(3, 2, width), (1, 0, 2))
+    proj_sum = sums[6:].reshape(2, 4 * width)
     return (mixed, qkv_sum, proj_sum)
 
 

time: 166 us -> 156 us (0.940)
  blocking collectives: 38.2 us -> 62.2 us
  local copies, waits for them, and re-layouts: 27.6 us -> 11.1 us
  waiting for transfers between devices: 28.9 us -> 15.5 us
  other arithmetic: 6.53 us -> 1.2 us
    all_gather x0 -> x2, blocking collectives: none -> 62.2 us  [the longest x1 31.6 us: local(): w2 = lax.all_gather(slab, 'lat', axis=0, tiled=True)]
    psum x1 -> x0, blocking collectives: 38.2 us -> none  [local(): both = lax.psum(both, 'lat')]
    ppermute x26 -> x27, waiting for transfers between devices: 28.9 us -> 15.5 us  [send(): return lax.ppermute(block, ('lat', 'tp'), route)]
    reshape x14 -> x2, local copies, waits for them, and re-layouts: 13.3 us -> 1.21 us  [the longest x1 0.61 us: local(): proj_sum = sums[6:].reshape(2, 4 * width)]
    transpose x1 -> x0, other arithmetic: 6.26 us -> none  [local(): mixed = jnp.transpose(mixed, (0, 2, 1, 3))]
    pallas_call x1 -> x6, Pallas kernels: 16.3 us -> 21.8 us  [the longest x1 11.3 us: backward(): pl.pallas_call(backward_kernel, out_shape=(jax.ShapeDtypeStruct((6, n, wi...]
    slice x6 -> x2, local copies, waits for them, and re-layouts: 4.45 us -> 0.01 us  [the longest x1 0.01 us: local(): proj_sum = sums[6:].reshape(2, 4 * width)]
    pallas_call x1, Pallas kernels: 12.2 us -> 10 us  [forward(): pl.pallas_call(forward_kernel, out_shape=(jax.ShapeDtypeStruct((2 * n, d)...]
  transfers between devices with their start and end apart: 26 -> 27, of which waited for: 9 -> 4; matrix products, arithmetic and copies ran while one was open for 13% -> 4% of each run, Pallas kernels for 11% -> 23%
where the time goes in v1:
time: 156 us; the launch traced here: 155 us
  blocking collectives  62.2 us (40%)
  Pallas kernels  37.9 us (24%)
  starting transfers between devices  25.9 us (17%)
  waiting for transfers between devices  15.5 us (10%)
  local copies, waits for them, and re-layouts  11.1 us (7%)
  between operations  1.61 us (1%)
    all_gather x1, blocking collectives, local(): w2 = lax.all_gather(slab, 'lat', axis=0, tiled=True)  31.6 us
    all_gather x1, blocking collectives, local(): sums = jnp.sum(lax.all_gather(sums, 'lat', axis=0), axis=0)  30.6 us
    ppermute x27, starting transfers between devices, send(): return lax.ppermute(block, ('lat', 'tp'), route)  25.9 us
    ppermute x27, waiting for transfers between devices, send(): return lax.ppermute(block, ('lat', 'tp'), route)  15.5 us
    pallas_call x1, Pallas kernels, backward(): pl.pallas_call(backward_kernel, out_shape=(jax.ShapeDtypeStruct((6, n, wi...  11.3 us
    pallas_call x1, Pallas kernels, forward(): pl.pallas_call(forward_kernel, out_shape=(jax.ShapeDtypeStruct((2 * n, d)...  10 us
    unnamed x32, local copies, waits for them, and re-layouts  4.09 us
    pallas_call x1, Pallas kernels, qkv_sums(): pl.pallas_call(qkv_sums_kernel, out_shape=(jax.ShapeDtypeStruct((6, width...  3.85 us
  transfers between devices with their start and end apart: 27, of which 4 were waited for; matrix products, arithmetic and copies ran while one was open for 4% of the time, Pallas kernels for 23%

profile of v1, /device:TPU:0, one launch (start us, length us, event | category | flops | bytes accessed | tf_op | source)
XLA Modules:
  0.0 155.4 jit_solution(3743820073591451166)
XLA Ops:
  0.6 0.5 collective-permute-start.14
  1.8 0.1 pad_add_fusion.1.s_ref
  1.9 1.0 copy-done.2
  2.9 1.7 %shard_map.103 = (bf16[288,256]{1,0:T(8,128)(2,1)S(1)}, bf16[288,256]{1,0:T(8,128)(2,1)}, bf16[288,256]{1,0:T(8,128)(2,1)}, bf16[288,256]{1,0:T(8,128)(2,1)}) custom-call(s32[2]{0:T(128)S(1)} %pad_add_fusion.1.s_ref, bf16[42,12,2,256]{3,2,1,0:T(2,128)(2,1)S(1)} %bitcast.19), custom_call_target="tpu_custom_call" | custom-call | flops 1000000 | bytes 2000000 | tf_op jit(solution)/shard_map/pallas_call | solution.py:425
  4.6 2.7 %collective-permute-start.1 = (bf16[288,256]{1,0:T(8,128)(2,1)S(1)}, bf16[288,256]{1,0:T(8,128)(2,1)S(1)}, u32[]{:S(2)}, u32[]{:S(2)}) collective-permute-start(bf16[288,256]{1,0:T(8,128)(2,1)S(1)} %get-tuple-element.44.refs_0_), channel_id=1, source_target_pairs={{0,2},{1,3},{2,0},{3,1},{4,6},{5,7},{6,4},{7,5},{8,10},{9,11},{10,... | collective-permute-start | bytes 442376 | tf_op jit(solution)/shard_map/ppermute | solution.py:478
  7.3 0.0 collective-permute-start.2
  7.3 4.7 %collective-permute-start.3 = (bf16[288,256]{1,0:T(8,128)(2,1)}, bf16[288,256]{1,0:T(8,128)(2,1)}, u32[]{:S(2)}, u32[]{:S(2)}) collective-permute-start(bf16[288,256]{1,0:T(8,128)(2,1)} %get-tuple-element.46), channel_id=1, source_target_pairs={{0,28},{1,29},{2,30},{3,31},{4,0},{5,1},{6,2},{7,3},{8,4},{9,5},{1... | collective-permute-start | bytes 442376 | tf_op jit(solution)/shard_map/ppermute | solution.py:478
  12.0 0.3 collective-permute-start.4
  12.3 1.0 dynamic-slice_add_fusion
  13.4 0.0 copy-start.3
  13.4 1.0 copy-done.3
  14.4 1.6 %shard_map.104 = (bf16[288,256]{1,0:T(8,128)(2,1)S(1)}, bf16[288,256]{1,0:T(8,128)(2,1)S(1)}, bf16[288,256]{1,0:T(8,128)(2,1)}, bf16[288,256]{1,0:T(8,128)(2,1)S(1)}) custom-call(s32[2]{0:T(128)S(1)} %pad_add_fusion.1.s_ref, bf16[42,12,2,256]{3,2,1,0:T(2,128)(2,1)S(1)} %bitcast.20), custom_call_target="tpu_custom_call" | custom-call | flops 1000000 | bytes 2000000 | tf_op jit(solution)/shard_map/pallas_call | solution.py:425
  16.0 0.7 copy-done.10
  16.7 0.7 copy-done.12
  17.4 0.6 copy-done.14
  18.0 1.5 constant_dynamic-slice_fusion
  19.5 0.0 collective-permute-done.1.refs_2_
  19.5 1.5 collective-permute-start.19
  21.0 0.0 collective-permute-done.3.refs_4_
  21.0 0.1 collective-permute-start.7
  21.1 0.5 collective-permute-start.5
  21.7 1.5 collective-permute-start.6
  23.2 0.1 copy.20
  23.3 0.1 reshape.24
  23.4 1.2 copy.21
  24.6 0.9 copy.22
  25.5 1.0 reshape_reshape.4.refs_10_.idk_ref.refs_21_
  26.5 1.0 copy.23
  27.5 0.0 copy-start.11
  27.6 0.7 shard_map.105
  28.3 0.1 pad_add_fusion.refs_11_.idq_ref
  28.3 0.0 collective-permute-start
  28.4 0.5 collective-permute-start.15
  28.9 1.9 %collective-permute-done.6.refs_7_ = bf16[288,256]{1,0:T(8,128)(2,1)} collective-permute-done((bf16[288,256]{1,0:T(8,128)(2,1)}, bf16[288,256]{1,0:T(8,128)(2,1)}, u32[]{:S(2)}, u32[]{:S(2)}) %collective-permute-start.6) | collective-permute-done | bytes 147488 | tf_op jit(solution)/shard_map/ppermute | solution.py:478
  30.8 2.8 %collective-permute-start.8 = (bf16[288,256]{1,0:T(8,128)(2,1)S(1)}, bf16[288,256]{1,0:T(8,128)(2,1)S(1)}, u32[]{:S(2)}, u32[]{:S(2)}) collective-permute-start(bf16[288,256]{1,0:T(8,128)(2,1)S(1)} %copy-done.15), channel_id=1, source_target_pairs={{0,28},{1,29},{2,30},{3,31},{4,0},{5,1},{6,2},{7,3},{8,4},{9,5},{1... | collective-permute-start | bytes 442376 | tf_op jit(solution)/shard_map/ppermute | solution.py:478
  33.7 31.6 %all_gather.9.w2 = bf16[256,1024]{1,0:T(8,128)(2,1)S(1)} all-gather(bf16[32,1024]{1,0:T(8,128)(2,1)} %collective-permute-done.19), channel_id=1, replica_groups=mesh['lat'=8,'tp'=4] {'lat'}, dimensions={0}, use_global_device_ids=true | all-gather | bytes 589824 | tf_op jit(solution)/shard_map/all_gather | solution.py:525
  65.3 0.1 collective-permute-start.18
  65.4 1.8 %collective-permute-start.10 = (bf16[288,256]{1,0:T(8,128)(2,1)S(1)}, bf16[288,256]{1,0:T(8,128)(2,1)S(1)}, u32[]{:S(2)}, u32[]{:S(2)}) collective-permute-start(bf16[288,256]{1,0:T(8,128)(2,1)S(1)} %copy-done.11), channel_id=1, source_target_pairs={{0,2},{1,3},{2,0},{3,1},{4,6},{5,7},{6,4},{7,5},{8,10},{9,11},{10,... | collective-permute-start | bytes 442376 | tf_op jit(solution)/shard_map/ppermute | solution.py:478
  67.1 0.3 collective-permute-start.11
  67.5 1.7 %collective-permute-start.12 = (bf16[288,256]{1,0:T(8,128)(2,1)S(1)}, bf16[288,256]{1,0:T(8,128)(2,1)S(1)}, u32[]{:S(2)}, u32[]{:S(2)}) collective-permute-start(bf16[288,256]{1,0:T(8,128)(2,1)S(1)} %collective-permute-done.8.refs_12_), channel_id=1, source_target_pairs={{0,2},{1,3},{2,0},{3,1},{4,6},{5,7},{6,4},{7,5},{8,10},{9,11},{10,... | collective-permute-start | bytes 442376 | tf_op jit(solution)/shard_map/ppermute | solution.py:478
  69.2 0.7 shard_map.106
  69.9 0.4 collective-permute-start.13
  70.3 10.0 %shard_map.107 = (bf16[576,1024]{1,0:T(8,128)(2,1)S(1)}, bf16[6,576,256]{2,1,0:T(8,128)(2,1)S(1)}, bf16[432,512]{1,0:T(8,128)(2,1)S(1)}) custom-call(s32[1]{0:T(128)} %bitcast.1.t_ref, bf16[288,256]{1,0:T(8,128)(2,1)S(1)} %copy-done.7, bf16[288,256]{1,0:T(8,128)(2,1)S(1)} %collective-permute-done.refs_1_, bf16[288,256]{1,0:T(8,128)(2,1)S(1)} %copy-done.9, ...), custom_call_target="tpu_custom_call" | custom-call | flops 8000000000 | bytes 10000000 | tf_op jit(solution)/shard_map/pallas_call | solution.py:207
  80.3 0.8 collective-permute-done.13.refs_15_
  81.1 1.3 shard_map.108.refs_17_.b_ref
  82.4 0.1 collective-permute-start.20
  82.5 1.8 %collective-permute-start.16 = (bf16[432,512]{1,0:T(8,128)(2,1)S(1)}, bf16[432,512]{1,0:T(8,128)(2,1)S(1)}, u32[]{:S(2)}, u32[]{:S(2)}) collective-permute-start(bf16[432,512]{1,0:T(8,128)(2,1)S(1)} %get-tuple-element.63.refs_16_.a_ref), channel_id=1, source_target_pairs={{0,2},{1,3},{2,0},{3,1},{4,6},{5,7},{6,4},{7,5},{8,10},{9,11},{10,... | collective-permute-start | bytes 1327112 | tf_op jit(solution)/shard_map/ppermute | solution.py:478
  84.3 0.3 collective-permute-start.17
  84.6 0.8 shard_map.112
  85.5 0.9 shard_map.109
  86.4 11.8 %collective-permute-done.17.refs_19_ = bf16[144,512]{1,0:T(8,128)(2,1)S(1)} collective-permute-done((bf16[144,512]{1,0:T(8,128)(2,1)S(1)}, bf16[144,512]{1,0:T(8,128)(2,1)S(1)}, u32[]{:S(2)}, u32[]{:S(2)}) %collective-permute-start.17) | collective-permute-done | bytes 147488 | tf_op jit(solution)/shard_map/ppermute | solution.py:478
  98.3 2.9 %shard_map.110 = (bf16[288,256]{1,0:T(8,128)(2,1)S(1)}, bf16[288,256]{1,0:T(8,128)(2,1)S(1)}, bf16[288,256]{1,0:T(8,128)(2,1)S(1)}, bf16[288,256]{1,0:T(8,128)(2,1)S(1)}, bf16[576,1024]{1,0:T(8,128)(2,1)S(1)}) custom-call(s32[1]{0:T(128)} %bitcast.1.t_ref, bf16[288,256]{1,0:T(8,128)(2,1)S(1)} %copy-done.7, ...), custom_call_target="tpu_custom_call" | custom-call | flops 2000000000 | bytes 8000000 | tf_op jit(solution)/shard_map/pallas_call | solution.py:295
  101.2 1.9 %collective-permute-start.21 = (bf16[288,256]{1,0:T(8,128)(2,1)S(1)}, bf16[288,256]{1,0:T(8,128)(2,1)S(1)}, u32[]{:S(2)}, u32[]{:S(2)}) collective-permute-start(bf16[288,256]{1,0:T(8,128)(2,1)S(1)} %get-tuple-element.70), channel_id=1, source_target_pairs={{0,4},{1,5},{2,6},{3,7},{4,8},{5,9},{6,10},{7,11},{8,12},{9,13},{1... | collective-permute-start | bytes 442376 | tf_op jit(solution)/shard_map/ppermute | solution.py:478
  103.1 0.2 collective-permute-start.23
  103.3 11.3 %shard_map.113 = (bf16[6,576,256]{2,1,0:T(8,128)(2,1)S(1)}, f32[8,256]{1,0:T(8,128)S(1)}) custom-call(bf16[576,1024]{1,0:T(8,128)(2,1)S(1)} %get-tuple-element.73.err_ref, bf16[1024,1024]{1,0:T(8,128)(2,1)S(1)} %get-tuple-element.68.refs_20_.wc_ref, bf16[512,576]{1,0:T(8,128)(2,1)S(1)} %get-tuple-element.75.attn_t, ...), custom_call_target="tpu_custom_call" | custom-call | flops 8000000000 | bytes 10000000 | tf_op jit(solution)/shard_map/pallas_call | solution.py:360
  114.7 0.4 collective-permute-start.25
  115.0 0.9 collective-permute-done.25
  115.9 1.7 %collective-permute-start.26 = (f32[8,256]{1,0:T(8,128)S(1)}, f32[8,256]{1,0:T(8,128)S(1)}, u32[]{:S(2)}, u32[]{:S(2)}) collective-permute-start(f32[8,256]{1,0:T(8,128)S(1)} %add.39), channel_id=1, source_target_pairs={{0,2},{1,3},{2,0},{3,1},{4,6},{5,7},{6,4},{7,5},{8,10},{9,11},{10,... | collective-permute-start | bytes 24584 | tf_op jit(solution)/shard_map/ppermute | solution.py:478
  117.6 3.8 %shard_map.114 = (f32[6,256]{1,0:T(8,128)S(1)}, f32[6,256]{1,0:T(8,128)S(1)}) custom-call(bf16[6,576,256]{2,1,0:T(8,128)(2,1)S(1)} %get-tuple-element.78.g_ref, bf16[1024,576]{1,0:T(8,128)(2,1)S(1)} %get-tuple-element.79.normed_t, bf16[3,1024,256]{2,1,0:T(8,128)(2,1)S(1)} %bitcast.18, bf16[3,1024,256]{2,1,0:T(8,128)(2,1)S(1)} %collective-permute-done.14.w_ref.wp_ref, ...), custom_call_target="tpu_custom_call" | custom-call | flops 4000000000 | bytes 8000000 | tf_op jit(solution)/shard_map/pallas_call | solution.py:387
  121.5 0.1 collective-permute-start.24
  121.6 2.0 %shard_map.111 = bf16[42,12,2,256]{3,2,1,0:T(2,128)(2,1)} custom-call(s32[2]{0:T(128)S(1)} %pad_add_fusion.1.s_ref, bf16[288,256]{1,0:T(8,128)(2,1)S(1)} %get-tuple-element.69.a0, bf16[288,256]{1,0:T(8,128)(2,1)S(1)} %collective-permute-done.21.a1, bf16[288,256]{1,0:T(8,128)(2,1)S(1)} %collective-permute-done.22.b0, ...), custom_call_target="tpu_custom_call" | custom-call | flops 1000000 | bytes 2000000 | tf_op jit(solution)/shard_map/pallas_call | solution.py:461
  123.5 30.6 %all-gather.1 = f32[8,14,256]{2,1,0:T(8,128)S(1)} all-gather(f32[1,14,256]{2,1,0:T(8,128)S(1)} %maximum_bitcast_fusion), channel_id=2, replica_groups=mesh['lat'=8,'tp'=4] {'lat'}, dimensions={0}, use_global_device_ids=true | all-gather | bytes 129024 | tf_op jit(solution)/shard_map/all_gather | solution.py:556
  154.2 0.6 reshape.26
  154.8 0.6 reshape.27
  (56 shorter events, 0.2 us)
Async XLA Ops:
  0.6 26.9 %copy-start = (bf16[1024,3,256]{2,0,1:T(8,128)(2,1)S(1)}, bf16[1024,3,256]{2,0,1:T(8,128)(2,1)}, u32[]{:S(2)}) copy-start(bf16[1024,3,256]{2,0,1:T(8,128)(2,1)} %param.10) | copy-start | bytes 4718596
  0.6 66.8 %collective-permute-start.14 = (bf16[3,1024,256]{2,1,0:T(8,128)(2,1)}, bf16[3,1024,256]{2,1,0:T(8,128)(2,1)S(1)}, u32[]{:S(2)}, u32[]{:S(2)}) collective-permute-start(bf16[3,1024,256]{2,1,0:T(8,128)(2,1)} %bitcast.16), channel_id=1, source_target_pairs={{0,1},{1,0},{2,3},{3,2},{4,5},{5,4},{6,7},{7,6},{8,9},{9,8},{10,11... | collective-permute-start | bytes 4718600 | tf_op jit(solution)/shard_map/ppermute | solution.py:478
  1.9 1.0 copy-start.2
  4.6 20.0 %copy-start.6 = (bf16[288,256]{1,0:T(8,128)(2,1)}, bf16[288,256]{1,0:T(8,128)(2,1)S(1)}, u32[]{:S(2)}) copy-start(bf16[288,256]{1,0:T(8,128)(2,1)S(1)} %get-tuple-element.44.refs_0_) | copy-start | bytes 442372
  4.6 14.8 %collective-permute-start.1 = (bf16[288,256]{1,0:T(8,128)(2,1)S(1)}, bf16[288,256]{1,0:T(8,128)(2,1)S(1)}, u32[]{:S(2)}, u32[]{:S(2)}) collective-permute-start(bf16[288,256]{1,0:T(8,128)(2,1)S(1)} %get-tuple-element.44.refs_0_), channel_id=1, source_target_pairs={{0,2},{1,3},{2,0},{3,1},{4,6},{5,7},{6,4},{7,5},{8,10},{9,11},{10,... | collective-permute-start | bytes 442376 | tf_op jit(solution)/shard_map/ppermute | solution.py:478
  7.3 13.7 %collective-permute-start.2 = (bf16[288,256]{1,0:T(8,128)(2,1)}, bf16[288,256]{1,0:T(8,128)(2,1)}, u32[]{:S(2)}, u32[]{:S(2)}) collective-permute-start(bf16[288,256]{1,0:T(8,128)(2,1)} %get-tuple-element.45), channel_id=1, source_target_pairs={{0,3},{1,2},{2,1},{3,0},{4,7},{5,6},{6,5},{7,4},{8,11},{9,10},{10,... | collective-permute-start | bytes 442376 | tf_op jit(solution)/shard_map/ppermute | solution.py:478
  7.3 13.7 %collective-permute-start.3 = (bf16[288,256]{1,0:T(8,128)(2,1)}, bf16[288,256]{1,0:T(8,128)(2,1)}, u32[]{:S(2)}, u32[]{:S(2)}) collective-permute-start(bf16[288,256]{1,0:T(8,128)(2,1)} %get-tuple-element.46), channel_id=1, source_target_pairs={{0,28},{1,29},{2,30},{3,31},{4,0},{5,1},{6,2},{7,3},{8,4},{9,5},{1... | collective-permute-start | bytes 442376 | tf_op jit(solution)/shard_map/ppermute | solution.py:478
  12.0 9.0 %collective-permute-start.4 = (bf16[288,256]{1,0:T(8,128)(2,1)}, bf16[288,256]{1,0:T(8,128)(2,1)}, u32[]{:S(2)}, u32[]{:S(2)}) collective-permute-start(bf16[288,256]{1,0:T(8,128)(2,1)} %get-tuple-element.47), channel_id=1, source_target_pairs={{0,29},{1,28},{2,31},{3,30},{4,1},{5,0},{6,3},{7,2},{8,5},{9,4},{1... | collective-permute-start | bytes 442376 | tf_op jit(solution)/shard_map/ppermute | solution.py:478
  13.4 1.0 copy-start.3
  14.4 13.1 %copy-start.5 = (f32[2,3,256]{2,0,1:T(2,128)S(1)}, f32[2,3,256]{2,0,1:T(2,128)}, u32[]{:S(2)}) copy-start(f32[2,3,256]{2,0,1:T(2,128)} %param.12) | copy-start | bytes 18436
  16.0 0.7 copy-start.10
  16.7 0.7 copy-start.12
  17.4 0.6 copy-start.14
  19.5 5.1 %copy-start.8 = (bf16[288,256]{1,0:T(8,128)(2,1)}, bf16[288,256]{1,0:T(8,128)(2,1)S(1)}, u32[]{:S(2)}) copy-start(bf16[288,256]{1,0:T(8,128)(2,1)S(1)} %collective-permute-done.1.refs_2_) | copy-start | bytes 442372
  19.5 8.9 %collective-permute-start.19 = (bf16[32,1024]{1,0:T(8,128)(2,1)}, bf16[32,1024]{1,0:T(8,128)(2,1)}, u32[]{:S(2)}, u32[]{:S(2)}) collective-permute-start(bf16[32,1024]{1,0:T(8,128)(2,1)} %constant_dynamic-slice_fusion), channel_id=1, source_target_pairs={{0,2},{1,3},{2,0},{3,1},{4,6},{5,7},{6,4},{7,5},{8,10},{9,11},{10,... | collective-permute-start | bytes 196616 | tf_op jit(solution)/shard_map/ppermute | solution.py:478
  21.0 12.7 %collective-permute-start.7 = (bf16[288,256]{1,0:T(8,128)(2,1)}, bf16[288,256]{1,0:T(8,128)(2,1)}, u32[]{:S(2)}, u32[]{:S(2)}) collective-permute-start(bf16[288,256]{1,0:T(8,128)(2,1)} %get-tuple-element.51), channel_id=1, source_target_pairs={{0,1},{1,0},{2,3},{3,2},{4,5},{5,4},{6,7},{7,6},{8,9},{9,8},{10,11... | collective-permute-start | bytes 442376 | tf_op jit(solution)/shard_map/ppermute | solution.py:478
  21.1 7.2 %collective-permute-start.5 = (bf16[288,256]{1,0:T(8,128)(2,1)}, bf16[288,256]{1,0:T(8,128)(2,1)}, u32[]{:S(2)}, u32[]{:S(2)}) collective-permute-start(bf16[288,256]{1,0:T(8,128)(2,1)} %collective-permute-done.3.refs_4_), channel_id=1, source_target_pairs={{0,2},{1,3},{2,0},{3,1},{4,6},{5,7},{6,4},{7,5},{8,10},{9,11},{10,... | collective-permute-start | bytes 442376 | tf_op jit(solution)/shard_map/ppermute | solution.py:478
  21.7 9.2 %collective-permute-start.6 = (bf16[288,256]{1,0:T(8,128)(2,1)}, bf16[288,256]{1,0:T(8,128)(2,1)}, u32[]{:S(2)}, u32[]{:S(2)}) collective-permute-start(bf16[288,256]{1,0:T(8,128)(2,1)} %collective-permute-done.4.refs_5_), channel_id=1, source_target_pairs={{0,2},{1,3},{2,0},{3,1},{4,6},{5,7},{6,4},{7,5},{8,10},{9,11},{10,... | collective-permute-start | bytes 442376 | tf_op jit(solution)/shard_map/ppermute | solution.py:478
  27.5 3.3 %copy-start.15 = (bf16[288,256]{1,0:T(8,128)(2,1)S(1)}, bf16[288,256]{1,0:T(8,128)(2,1)}, u32[]{:S(2)}) copy-start(bf16[288,256]{1,0:T(8,128)(2,1)} %copy-done.14) | copy-start | bytes 442372
  27.5 6.2 %copy-start.13 = (bf16[288,256]{1,0:T(8,128)(2,1)S(1)}, bf16[288,256]{1,0:T(8,128)(2,1)}, u32[]{:S(2)}) copy-start(bf16[288,256]{1,0:T(8,128)(2,1)} %copy-done.12) | copy-start | bytes 442372
  27.5 37.8 %copy-start.1 = (bf16[256,1024]{1,0:T(8,128)(2,1)S(1)}, bf16[256,1024]{1,0:T(8,128)(2,1)}, u32[]{:S(2)}) copy-start(bf16[256,1024]{1,0:T(8,128)(2,1)} %po_ref.1) | copy-start | bytes 1572868
  27.5 37.9 %copy-start.11 = (bf16[288,256]{1,0:T(8,128)(2,1)S(1)}, bf16[288,256]{1,0:T(8,128)(2,1)}, u32[]{:S(2)}) copy-start(bf16[288,256]{1,0:T(8,128)(2,1)} %copy-done.10) | copy-start | bytes 442372
  27.5 42.7 %copy-start.7 = (bf16[288,256]{1,0:T(8,128)(2,1)S(1)}, bf16[288,256]{1,0:T(8,128)(2,1)}, u32[]{:S(2)}) copy-start(bf16[288,256]{1,0:T(8,128)(2,1)} %copy-done.6) | copy-start | bytes 442372
  27.5 42.7 %copy-start.9 = (bf16[288,256]{1,0:T(8,128)(2,1)S(1)}, bf16[288,256]{1,0:T(8,128)(2,1)}, u32[]{:S(2)}) copy-start(bf16[288,256]{1,0:T(8,128)(2,1)} %copy-done.8) | copy-start | bytes 442372
  28.3 41.5 %collective-permute-start = (bf16[288,256]{1,0:T(8,128)(2,1)}, bf16[288,256]{1,0:T(8,128)(2,1)S(1)}, u32[]{:S(2)}, u32[]{:S(2)}) collective-permute-start(bf16[288,256]{1,0:T(8,128)(2,1)} %get-tuple-element.45), channel_id=1, source_target_pairs={{0,1},{1,0},{2,3},{3,2},{4,5},{5,4},{6,7},{7,6},{8,9},{9,8},{10,11... | collective-permute-start | bytes 442376 | tf_op jit(solution)/shard_map/ppermute | solution.py:478
  28.4 38.7 %collective-permute-start.15 = (f32[3,2,256]{2,1,0:T(2,128)S(1)}, f32[3,2,256]{2,1,0:T(2,128)S(1)}, u32[]{:S(2)}, u32[]{:S(2)}) collective-permute-start(f32[3,2,256]{2,1,0:T(2,128)S(1)} %bitcast.22), channel_id=1, source_target_pairs={{0,1},{1,0},{2,3},{3,2},{4,5},{5,4},{6,7},{7,6},{8,9},{9,8},{10,11... | collective-permute-start | bytes 18440 | tf_op jit(solution)/shard_map/ppermute | solution.py:478
  30.8 34.4 %collective-permute-start.8 = (bf16[288,256]{1,0:T(8,128)(2,1)S(1)}, bf16[288,256]{1,0:T(8,128)(2,1)S(1)}, u32[]{:S(2)}, u32[]{:S(2)}) collective-permute-start(bf16[288,256]{1,0:T(8,128)(2,1)S(1)} %copy-done.15), channel_id=1, source_target_pairs={{0,28},{1,29},{2,30},{3,31},{4,0},{5,1},{6,2},{7,3},{8,4},{9,5},{1... | collective-permute-start | bytes 442376 | tf_op jit(solution)/shard_map/ppermute | solution.py:478
  33.7 31.7 %collective-permute-start.9 = (bf16[288,256]{1,0:T(8,128)(2,1)S(1)}, bf16[288,256]{1,0:T(8,128)(2,1)S(1)}, u32[]{:S(2)}, u32[]{:S(2)}) collective-permute-start(bf16[288,256]{1,0:T(8,128)(2,1)S(1)} %copy-done.13), channel_id=1, source_target_pairs={{0,29},{1,28},{2,31},{3,30},{4,1},{5,0},{6,3},{7,2},{8,5},{9,4},{1... | collective-permute-start | bytes 442376 | tf_op jit(solution)/shard_map/ppermute | solution.py:478
  65.3 20.2 %collective-permute-start.18 = (bf16[256,1024]{1,0:T(8,128)(2,1)S(1)}, bf16[256,1024]{1,0:T(8,128)(2,1)S(1)}, u32[]{:S(2)}, u32[]{:S(2)}) collective-permute-start(bf16[256,1024]{1,0:T(8,128)(2,1)S(1)} %copy-done.1), channel_id=1, source_target_pairs={{0,1},{1,0},{2,3},{3,2},{4,5},{5,4},{6,7},{7,6},{8,9},{9,8},{10,11... | collective-permute-start | bytes 1572872 | tf_op jit(solution)/shard_map/ppermute | solution.py:478
  65.4 14.9 %collective-permute-start.10 = (bf16[288,256]{1,0:T(8,128)(2,1)S(1)}, bf16[288,256]{1,0:T(8,128)(2,1)S(1)}, u32[]{:S(2)}, u32[]{:S(2)}) collective-permute-start(bf16[288,256]{1,0:T(8,128)(2,1)S(1)} %copy-done.11), channel_id=1, source_target_pairs={{0,2},{1,3},{2,0},{3,1},{4,6},{5,7},{6,4},{7,5},{8,10},{9,11},{10,... | collective-permute-start | bytes 442376 | tf_op jit(solution)/shard_map/ppermute | solution.py:478
  67.1 13.2 %collective-permute-start.11 = (bf16[288,256]{1,0:T(8,128)(2,1)}, bf16[288,256]{1,0:T(8,128)(2,1)S(1)}, u32[]{:S(2)}, u32[]{:S(2)}) collective-permute-start(bf16[288,256]{1,0:T(8,128)(2,1)} %collective-permute-done.7.refs_9_), channel_id=1, source_target_pairs={{0,2},{1,3},{2,0},{3,1},{4,6},{5,7},{6,4},{7,5},{8,10},{9,11},{10,... | collective-permute-start | bytes 442376 | tf_op jit(solution)/shard_map/ppermute | solution.py:478
  67.5 12.8 %collective-permute-start.12 = (bf16[288,256]{1,0:T(8,128)(2,1)S(1)}, bf16[288,256]{1,0:T(8,128)(2,1)S(1)}, u32[]{:S(2)}, u32[]{:S(2)}) collective-permute-start(bf16[288,256]{1,0:T(8,128)(2,1)S(1)} %collective-permute-done.8.refs_12_), channel_id=1, source_target_pairs={{0,2},{1,3},{2,0},{3,1},{4,6},{5,7},{6,4},{7,5},{8,10},{9,11},{10,... | collective-permute-start | bytes 442376 | tf_op jit(solution)/shard_map/ppermute | solution.py:478
  69.9 11.2 %collective-permute-start.13 = (bf16[288,256]{1,0:T(8,128)(2,1)S(1)}, bf16[288,256]{1,0:T(8,128)(2,1)S(1)}, u32[]{:S(2)}, u32[]{:S(2)}) collective-permute-start(bf16[288,256]{1,0:T(8,128)(2,1)S(1)} %collective-permute-done.9.refs_13_), channel_id=1, source_target_pairs={{0,2},{1,3},{2,0},{3,1},{4,6},{5,7},{6,4},{7,5},{8,10},{9,11},{10,... | collective-permute-start | bytes 442376 | tf_op jit(solution)/shard_map/ppermute | solution.py:478
  82.4 3.0 %collective-permute-start.20 = (bf16[256,1024]{1,0:T(8,128)(2,1)S(1)}, bf16[256,1024]{1,0:T(8,128)(2,1)S(1)}, u32[]{:S(2)}, u32[]{:S(2)}) collective-permute-start(bf16[256,1024]{1,0:T(8,128)(2,1)S(1)} %all_gather.9.w2), channel_id=1, source_target_pairs={{0,1},{1,0},{2,3},{3,2},{4,5},{5,4},{6,7},{7,6},{8,9},{9,8},{10,11... | collective-permute-start | bytes 1572872 | tf_op jit(solution)/shard_map/ppermute | solution.py:478
  82.5 15.7 %collective-permute-start.16 = (bf16[432,512]{1,0:T(8,128)(2,1)S(1)}, bf16[432,512]{1,0:T(8,128)(2,1)S(1)}, u32[]{:S(2)}, u32[]{:S(2)}) collective-permute-start(bf16[432,512]{1,0:T(8,128)(2,1)S(1)} %get-tuple-element.63.refs_16_.a_ref), channel_id=1, source_target_pairs={{0,2},{1,3},{2,0},{3,1},{4,6},{5,7},{6,4},{7,5},{8,10},{9,11},{10,... | collective-permute-start | bytes 1327112 | tf_op jit(solution)/shard_map/ppermute | solution.py:478
  84.3 14.0 %collective-permute-start.17 = (bf16[144,512]{1,0:T(8,128)(2,1)S(1)}, bf16[144,512]{1,0:T(8,128)(2,1)S(1)}, u32[]{:S(2)}, u32[]{:S(2)}) collective-permute-start(bf16[144,512]{1,0:T(8,128)(2,1)S(1)} %shard_map.108.refs_17_.b_ref), channel_id=1, source_target_pairs={{0,2},{1,3},{2,0},{3,1},{4,6},{5,7},{6,4},{7,5},{8,10},{9,11},{10,... | collective-permute-start | bytes 442376 | tf_op jit(solution)/shard_map/ppermute | solution.py:478
  84.6 0.9 copy-start.4
  101.2 16.4 %collective-permute-start.21 = (bf16[288,256]{1,0:T(8,128)(2,1)S(1)}, bf16[288,256]{1,0:T(8,128)(2,1)S(1)}, u32[]{:S(2)}, u32[]{:S(2)}) collective-permute-start(bf16[288,256]{1,0:T(8,128)(2,1)S(1)} %get-tuple-element.70), channel_id=1, source_target_pairs={{0,4},{1,5},{2,6},{3,7},{4,8},{5,9},{6,10},{7,11},{8,12},{9,13},{1... | collective-permute-start | bytes 442376 | tf_op jit(solution)/shard_map/ppermute | solution.py:478
  103.1 14.5 %collective-permute-start.22 = (bf16[288,256]{1,0:T(8,128)(2,1)S(1)}, bf16[288,256]{1,0:T(8,128)(2,1)S(1)}, u32[]{:S(2)}, u32[]{:S(2)}) collective-permute-start(bf16[288,256]{1,0:T(8,128)(2,1)S(1)} %get-tuple-element.71), channel_id=1, source_target_pairs={{0,1},{1,0},{2,3},{3,2},{4,5},{5,4},{6,7},{7,6},{8,9},{9,8},{10,11... | collective-permute-start | bytes 442376 | tf_op jit(solution)/shard_map/ppermute | solution.py:478
  103.1 14.5 %collective-permute-start.23 = (bf16[288,256]{1,0:T(8,128)(2,1)S(1)}, bf16[288,256]{1,0:T(8,128)(2,1)S(1)}, u32[]{:S(2)}, u32[]{:S(2)}) collective-permute-start(bf16[288,256]{1,0:T(8,128)(2,1)S(1)} %get-tuple-element.72), channel_id=1, source_target_pairs={{0,5},{1,4},{2,7},{3,6},{4,9},{5,8},{6,11},{7,10},{8,13},{9,12},{1... | collective-permute-start | bytes 442376 | tf_op jit(solution)/shard_map/ppermute | solution.py:478
  114.7 1.2 collective-permute-start.25
  115.9 5.7 %collective-permute-start.26 = (f32[8,256]{1,0:T(8,128)S(1)}, f32[8,256]{1,0:T(8,128)S(1)}, u32[]{:S(2)}, u32[]{:S(2)}) collective-permute-start(f32[8,256]{1,0:T(8,128)S(1)} %add.39), channel_id=1, source_target_pairs={{0,2},{1,3},{2,0},{3,1},{4,6},{5,7},{6,4},{7,5},{8,10},{9,11},{10,... | collective-permute-start | bytes 24584 | tf_op jit(solution)/shard_map/ppermute | solution.py:478
  121.5 2.1 %collective-permute-start.24 = (f32[6,256]{1,0:T(8,128)S(1)}, f32[6,256]{1,0:T(8,128)S(1)}, u32[]{:S(2)}, u32[]{:S(2)}) collective-permute-start(f32[6,256]{1,0:T(8,128)S(1)} %get-tuple-element.83), channel_id=1, source_target_pairs={{0,1},{1,0},{2,3},{3,2},{4,5},{5,4},{6,7},{7,6},{8,9},{9,8},{10,11... | collective-permute-start | bytes 18440 | tf_op jit(solution)/shard_map/ppermute | solution.py:478

commit v2 on v1

--- a/solution.py
+++ b/solution.py
@@ -478,6 +478,25 @@
     return lax.ppermute(block, ("lat", "tp"), route)
 
 
+def swap(block, other, flip):
+    count, tp = lax.axis_size("lat"), lax.axis_size("tp")
+    route = [(u * tp + t, (u ^ other) * tp + (t ^ flip)) for u in range(count) for t in range(tp)]
+    return lax.ppermute(block, ("lat", "tp"), route)
+
+
+def lat_sum(block, bit):
+    count = lax.axis_size("lat")
+    while bit < count:
+        if 4 * bit <= count:
+            a, b, c = swap(block, bit, 0), swap(block, 2 * bit, 0), swap(block, 3 * bit, 0)
+            block = (block + a) + (b + c)
+            bit *= 4
+        else:
+            block = block + swap(block, bit, 0)
+            bit *= 2
+    return block
+
+
 def after(block, *others):
     return lax.optimization_barrier((block, *others))[0]
 
@@ -494,6 +513,10 @@
     t_arr = jnp.reshape(t, (1,)).astype(jnp.int32)
     place = jnp.stack([offset, core]).astype(jnp.int32)
 
+    share = w_proj.shape[0] // 2
+    first = share * (sector % 2)
+    slab = send(lax.dynamic_slice_in_dim(w_proj, first, share, 0), 0, 2)
+
     m0, m1, p0, p1 = split(place, features)
     f02, f03 = send(m0, 0, 2), send(p0, 0, 3)
     f10, f11 = send(m1, -1, 0), send(p1, -1, 1)
@@ -517,14 +540,11 @@
     idq = jnp.concatenate([ids, ids], axis=2)
 
     g0, g1, q0, q1 = split(place, target)
+    more = swap(after(slab, f10, f11), 1, 0)
+    w1 = send(after(w_proj, f10, f11), 0, 1)
     g1, q1, q0 = lax.optimization_barrier((g1, q1, q0, f02, f03, f10, f11))[:3]
     t10, t11 = send(g1, -1, 0), send(q1, -1, 1)
     t01 = send(q0, 0, 1)
-    share = w_proj.shape[0] // count
-    slab = send(lax.dynamic_slice_in_dim(w_proj, sector * share, share, 0), 0, 2)
-    w2 = lax.all_gather(slab, "lat", axis=0, tiled=True)
-    w1 = send(after(w_proj, f10, f11), 0, 1)
-
     ya, yb, yc, yd = lax.optimization_barrier((g0, t01, t10, t11, f12, f13))[:4]
     t02, t03, t12, t13 = send(ya, 0, 2), send(yb, 0, 2), send(yc, 0, 2), send(yd, 0, 2)
     targets = [g0, t01, t02, t03, t10, t11, t12, t13]
@@ -535,7 +555,8 @@
     attn_b = last_window(after(qkv, t02, t03, t12, t13), idk, idq)
     other_b = send(attn_b, 0, 2)
     attn, attn_other = (attn_a, attn_b), (other_a, other_b)
-    w2 = after(w2, attn_b)
+    slab, more = lax.optimization_barrier((slab, more, attn_b))[:2]
+    w2 = lax.dynamic_slice_in_dim(jnp.concatenate([slab, more, slab], axis=0), first, 2 * share, 0)
     w_3 = send(w2, 0, 1)
     pc, pb = clip_proj([w_proj, w1, w2, w_3], proj_clip)
     normed_t, attn_t = turn(normed, attn)
@@ -546,14 +567,13 @@
     m11 = send(m11, 1, 1)
 
     grads, proj = backward(err, pc, attn_t, qkv, w_proj, w1, pb, idk, idq)
-    proj_peer = send(proj, 0, 1)
+    proj_1, proj_2, proj_3 = send(proj, 0, 1), send(proj, 0, 2), send(proj, 0, 3)
     grads = after(grads, m01, m10, m11)
     own, peer = qkv_sums(grads, normed_t, w3, w3_peer, b_own, b_peer)
-    proj = proj + proj_peer
-    proj_other = send(proj, 0, 2)
-    peer = send(peer, 0, 1)
-    sums = jnp.concatenate([own + peer, proj + proj_other], axis=0)
-    sums = jnp.sum(lax.all_gather(sums, "lat", axis=0), axis=0)
+    proj = (proj + proj_1) + (proj_2 + proj_3)
+    a, b, c = send(peer, 0, 1), swap(jnp.concatenate([own, proj], axis=0), 1, 0), swap(peer, 1, 1)
+    sums = jnp.concatenate([(own + a) + (b[:6] + c), proj + b[6:]], axis=0)
+    sums = lat_sum(sums, 2)
     mixed = join(place, [m00, m10, m01, m11], rows, lon, lev)
     qkv_sum = jnp.transpose(sums[:6].reshape(3, 2, width), (1, 0, 2))
     proj_sum = sums[6:].reshape(2, 4 * width)

time: 156 us -> 117 us (0.75)
  blocking collectives: 62.2 us -> 0 us
  waiting for transfers between devices: 15.5 us -> 29.5 us
  starting transfers between devices: 25.9 us -> 32.3 us
    all_gather x2 -> x0, blocking collectives: 62.2 us -> none  [the longest x1 31.6 us: local(): w2 = lax.all_gather(slab, 'lat', axis=0, tiled=True)]
    ppermute x27 -> x28, waiting for transfers between devices: 15.5 us -> 27.5 us  [send(): return lax.ppermute(block, ('lat', 'tp'), route)]
    ppermute x0 -> x6, starting transfers between devices: none -> 6.47 us  [swap(): return lax.ppermute(block, ('lat', 'tp'), route)]
    ppermute x0 -> x6, waiting for transfers between devices: none -> 2 us  [swap(): return lax.ppermute(block, ('lat', 'tp'), route)]
    unnamed x32 -> x30, local copies, waits for them, and re-layouts: 4.09 us -> 4.76 us
    ppermute x27 -> x28, starting transfers between devices: 25.9 us -> 25.8 us  [send(): return lax.ppermute(block, ('lat', 'tp'), route)]
  transfers between devices with their start and end apart: 27 -> 34, of which waited for: 4 -> 10; matrix products, arithmetic and copies ran while one was open for 4% -> 7% of each run, Pallas kernels for 23% -> 17%
where the time goes in v2:
time: 117 us; the launch traced here: 116 us
  Pallas kernels  38.1 us (33%)
  starting transfers between devices  32.3 us (28%)
  waiting for transfers between devices  29.5 us (25%)
  local copies, waits for them, and re-layouts  11.9 us (10%)
  other arithmetic  2.63 us (2%)
  between operations  1.65 us (1%)
    ppermute x28, waiting for transfers between devices, send(): return lax.ppermute(block, ('lat', 'tp'), route)  27.5 us
    ppermute x28, starting transfers between devices, send(): return lax.ppermute(block, ('lat', 'tp'), route)  25.8 us
    pallas_call x1, Pallas kernels, backward(): pl.pallas_call(backward_kernel, out_shape=(jax.ShapeDtypeStruct((6, n, wi...  11.3 us
    pallas_call x1, Pallas kernels, forward(): pl.pallas_call(forward_kernel, out_shape=(jax.ShapeDtypeStruct((2 * n, d)...  10.1 us
    ppermute x6, starting transfers between devices, swap(): return lax.ppermute(block, ('lat', 'tp'), route)  6.47 us
    unnamed x30, local copies, waits for them, and re-layouts  4.76 us
    pallas_call x1, Pallas kernels, qkv_sums(): pl.pallas_call(qkv_sums_kernel, out_shape=(jax.ShapeDtypeStruct((6, width...  3.83 us
    pallas_call x2, Pallas kernels, split(): pl.pallas_call(split_kernel, out_shape=(piece,) * 4, in_specs=[pl.BlockSp...  3.3 us
  transfers between devices with their start and end apart: 34, of which 10 were waited for; matrix products, arithmetic and copies ran while one was open for 7% of the time, Pallas kernels for 17%

profile of v2, /device:TPU:0, one launch (start us, length us, event | category | flops | bytes accessed | tf_op | source)
XLA Modules:
  0.0 116.1 jit_solution(12595336990176036141)
XLA Ops:
  0.6 0.5 collective-permute-start.14
  1.9 1.0 copy-done.2
  2.9 1.7 %shard_map.103 = (bf16[288,256]{1,0:T(8,128)(2,1)S(1)}, bf16[288,256]{1,0:T(8,128)(2,1)}, bf16[288,256]{1,0:T(8,128)(2,1)S(1)}, bf16[288,256]{1,0:T(8,128)(2,1)}) custom-call(s32[2]{0:T(128)S(1)} %pad_add_fusion.1.s_ref, bf16[42,12,2,256]{3,2,1,0:T(2,128)(2,1)S(1)} %bitcast.17), custom_call_target="tpu_custom_call" | custom-call | flops 1000000 | bytes 2000000 | tf_op jit(solution)/shard_map/pallas_call | solution.py:425
  4.6 0.7 copy-done.10
  5.3 2.7 %collective-permute-start.1 = (bf16[288,256]{1,0:T(8,128)(2,1)S(1)}, bf16[288,256]{1,0:T(8,128)(2,1)S(1)}, u32[]{:S(2)}, u32[]{:S(2)}) collective-permute-start(bf16[288,256]{1,0:T(8,128)(2,1)S(1)} %get-tuple-element.46.refs_0_), channel_id=1, source_target_pairs={{0,2},{1,3},{2,0},{3,1},{4,6},{5,7},{6,4},{7,5},{8,10},{9,11},{10,... | collective-permute-start | bytes 442376 | tf_op jit(solution)/shard_map/ppermute | solution.py:478
  7.9 4.5 %collective-permute-start.3 = (bf16[288,256]{1,0:T(8,128)(2,1)}, bf16[288,256]{1,0:T(8,128)(2,1)}, u32[]{:S(2)}, u32[]{:S(2)}) collective-permute-start(bf16[288,256]{1,0:T(8,128)(2,1)} %get-tuple-element.48), channel_id=1, source_target_pairs={{0,28},{1,29},{2,30},{3,31},{4,0},{5,1},{6,2},{7,3},{8,4},{9,5},{1... | collective-permute-start | bytes 442376 | tf_op jit(solution)/shard_map/ppermute | solution.py:478
  12.5 1.7 %constant_dynamic-slice_fusion = bf16[128,1024]{1,0:T(8,128)(2,1)} fusion(bf16[256,1024]{1,0:T(8,128)(2,1)} %po_ref.1, s32[]{:T(128)S(6)} %select_n.27), kind=kLoop, calls=%fused_computation.15 | loop fusion | bytes 524292 | tf_op jit(solution)/shard_map/dynamic_slice | solution.py:518
  14.1 0.5 collective-permute-start.19
  14.6 1.5 %collective-permute-start.2 = (bf16[288,256]{1,0:T(8,128)(2,1)}, bf16[288,256]{1,0:T(8,128)(2,1)}, u32[]{:S(2)}, u32[]{:S(2)}) collective-permute-start(bf16[288,256]{1,0:T(8,128)(2,1)} %copy-done.10), channel_id=1, source_target_pairs={{0,3},{1,2},{2,1},{3,0},{4,7},{5,6},{6,5},{7,4},{8,11},{9,10},{10,... | collective-permute-start | bytes 442376 | tf_op jit(solution)/shard_map/ppermute | solution.py:478
  16.1 0.9 collective-permute-done.3.refs_4_
  17.0 0.5 collective-permute-start.5
  17.5 1.8 %collective-permute-done.4.refs_5_ = bf16[288,256]{1,0:T(8,128)(2,1)} collective-permute-done((bf16[288,256]{1,0:T(8,128)(2,1)}, bf16[288,256]{1,0:T(8,128)(2,1)}, u32[]{:S(2)}, u32[]{:S(2)}) %collective-permute-start.4) | collective-permute-done | bytes 147488 | tf_op jit(solution)/shard_map/ppermute | solution.py:478
  19.3 0.5 collective-permute-start.6
  19.8 1.0 copy-done.3
  20.8 1.6 %shard_map.104 = (bf16[288,256]{1,0:T(8,128)(2,1)S(1)}, bf16[288,256]{1,0:T(8,128)(2,1)S(1)}, bf16[288,256]{1,0:T(8,128)(2,1)}, bf16[288,256]{1,0:T(8,128)(2,1)S(1)}) custom-call(s32[2]{0:T(128)S(1)} %pad_add_fusion.1.s_ref, bf16[42,12,2,256]{3,2,1,0:T(2,128)(2,1)S(1)} %bitcast.18), custom_call_target="tpu_custom_call" | custom-call | flops 1000000 | bytes 2000000 | tf_op jit(solution)/shard_map/pallas_call | solution.py:425
  22.5 0.7 copy-done.11
  23.1 0.7 copy-done.13
  23.8 0.7 copy-done.14
  24.5 1.7 %collective-permute-done.2.refs_3_ = bf16[288,256]{1,0:T(8,128)(2,1)} collective-permute-done((bf16[288,256]{1,0:T(8,128)(2,1)}, bf16[288,256]{1,0:T(8,128)(2,1)}, u32[]{:S(2)}, u32[]{:S(2)}) %collective-permute-start.2) | collective-permute-done | bytes 147488 | tf_op jit(solution)/shard_map/ppermute | solution.py:478
  26.1 0.5 collective-permute-start.7
  26.6 1.0 dynamic-slice_add_fusion
  27.7 0.1 collective-permute-start
  27.8 2.2 %collective-permute-done.5.refs_6_ = bf16[288,256]{1,0:T(8,128)(2,1)} collective-permute-done((bf16[288,256]{1,0:T(8,128)(2,1)}, bf16[288,256]{1,0:T(8,128)(2,1)}, u32[]{:S(2)}, u32[]{:S(2)}) %collective-permute-start.5) | collective-permute-done | bytes 147488 | tf_op jit(solution)/shard_map/ppermute | solution.py:478
  29.9 1.3 %collective-permute-start.8 = (bf16[288,256]{1,0:T(8,128)(2,1)}, bf16[288,256]{1,0:T(8,128)(2,1)}, u32[]{:S(2)}, u32[]{:S(2)}) collective-permute-start(bf16[288,256]{1,0:T(8,128)(2,1)} %copy-done.14), channel_id=1, source_target_pairs={{0,28},{1,29},{2,30},{3,31},{4,0},{5,1},{6,2},{7,3},{8,4},{9,5},{1... | collective-permute-start | bytes 442376 | tf_op jit(solution)/shard_map/ppermute | solution.py:478
  31.3 1.5 %collective-permute-done.6.refs_7_ = bf16[288,256]{1,0:T(8,128)(2,1)} collective-permute-done((bf16[288,256]{1,0:T(8,128)(2,1)}, bf16[288,256]{1,0:T(8,128)(2,1)}, u32[]{:S(2)}, u32[]{:S(2)}) %collective-permute-start.6) | collective-permute-done | bytes 147488 | tf_op jit(solution)/shard_map/ppermute | solution.py:478
  32.8 0.8 collective-permute-start.9
  33.9 0.9 copy.13
  34.7 1.0 copy.14
  35.7 0.7 collective-permute-start.15
  36.5 1.2 %copy.12 = s32[4,2,6,6,2]{4,3,2,1,0:T(8,128)} copy(s32[4,2,6,6,2]{2,0,4,3,1:T(4,128)S(1)} %bitcast.23) | data formatting | bytes 4608 | tf_op jit(solution)/shard_map/transpose | solution.py:537
  37.7 1.0 reshape_reshape.4.refs_10_.idk_ref.refs_21_
  38.8 0.7 shard_map.105
  39.5 0.7 collective-permute-start.20
  40.2 0.5 collective-permute-start.10
  40.7 1.5 %collective-permute-start.11 = (bf16[288,256]{1,0:T(8,128)(2,1)}, bf16[288,256]{1,0:T(8,128)(2,1)S(1)}, u32[]{:S(2)}, u32[]{:S(2)}) collective-permute-start(bf16[288,256]{1,0:T(8,128)(2,1)} %collective-permute-done.7.refs_9_), channel_id=1, source_target_pairs={{0,2},{1,3},{2,0},{3,1},{4,6},{5,7},{6,4},{7,5},{8,10},{9,11},{10,... | collective-permute-start | bytes 442376 | tf_op jit(solution)/shard_map/ppermute | solution.py:478
  42.2 0.5 collective-permute-start.12
  42.8 0.7 shard_map.106
  43.5 1.6 %collective-permute-start.13 = (bf16[288,256]{1,0:T(8,128)(2,1)}, bf16[288,256]{1,0:T(8,128)(2,1)S(1)}, u32[]{:S(2)}, u32[]{:S(2)}) collective-permute-start(bf16[288,256]{1,0:T(8,128)(2,1)} %collective-permute-done.9.refs_13_), channel_id=1, source_target_pairs={{0,2},{1,3},{2,0},{3,1},{4,6},{5,7},{6,4},{7,5},{8,10},{9,11},{10,... | collective-permute-start | bytes 442376 | tf_op jit(solution)/shard_map/ppermute | solution.py:478
  45.0 10.1 %shard_map.107 = (bf16[576,1024]{1,0:T(8,128)(2,1)S(1)}, bf16[6,576,256]{2,1,0:T(8,128)(2,1)S(1)}, bf16[432,512]{1,0:T(8,128)(2,1)S(1)}) custom-call(s32[1]{0:T(128)} %bitcast.1.t_ref, bf16[288,256]{1,0:T(8,128)(2,1)S(1)} %copy-done.7, bf16[288,256]{1,0:T(8,128)(2,1)} %collective-permute-done.refs_1_, bf16[288,256]{1,0:T(8,128)(2,1)S(1)} %copy-done.9, ...), custom_call_target="tpu_custom_call" | custom-call | flops 8000000000 | bytes 10000000 | tf_op jit(solution)/shard_map/pallas_call | solution.py:207
  55.3 1.3 %shard_map.108.refs_17_.b_ref = bf16[144,512]{1,0:T(8,128)(2,1)S(1)} custom-call(bf16[6,576,256]{2,1,0:T(8,128)(2,1)S(1)} %get-tuple-element.67.qkv_ref, s32[576,1]{1,0:T(8,128)S(1)} %reshape_reshape.4.refs_10_.idk_ref.refs_21_, s32[4,1,288]{2,1,0:T(1,128)S(1)} %pad_add_fusion.refs_11_.idq_ref), custom_call_target="tpu_custom_call" | custom-call | flops 1000000000 | bytes 2000000 | tf_op jit(solution)/shard_map/pallas_call | solution.py:194
  56.6 1.4 %fusion.1.w2 = bf16[256,1024]{1,0:T(8,128)(2,1)S(1)} fusion(s32[]{:T(128)S(6)} %select_n.28, bf16[128,1024]{1,0:T(8,128)(2,1)} %collective-permute-done.19, bf16[128,1024]{1,0:T(8,128)(2,1)S(1)} %collective-permute-done.20), kind=kLoop, calls=%fused_computation.4 | loop fusion | flops 1572864 | bytes 1048580 | tf_op jit(solution)/shard_map/concatenate | solution.py:559
  58.1 0.5 collective-permute-start.21
  58.6 0.5 collective-permute-start.16
  59.1 1.5 %collective-permute-start.17 = (bf16[144,512]{1,0:T(8,128)(2,1)S(1)}, bf16[144,512]{1,0:T(8,128)(2,1)S(1)}, u32[]{:S(2)}, u32[]{:S(2)}) collective-permute-start(bf16[144,512]{1,0:T(8,128)(2,1)S(1)} %shard_map.108.refs_17_.b_ref), channel_id=1, source_target_pairs={{0,2},{1,3},{2,0},{3,1},{4,6},{5,7},{6,4},{7,5},{8,10},{9,11},{10,... | collective-permute-start | bytes 442376 | tf_op jit(solution)/shard_map/ppermute | solution.py:478
  60.6 0.8 shard_map.112
  61.5 0.9 shard_map.109
  62.4 11.5 %collective-permute-done.17.refs_19_ = bf16[144,512]{1,0:T(8,128)(2,1)S(1)} collective-permute-done((bf16[144,512]{1,0:T(8,128)(2,1)S(1)}, bf16[144,512]{1,0:T(8,128)(2,1)S(1)}, u32[]{:S(2)}, u32[]{:S(2)}) %collective-permute-start.17) | collective-permute-done | bytes 147488 | tf_op jit(solution)/shard_map/ppermute | solution.py:478
  73.9 3.1 %shard_map.110 = (bf16[288,256]{1,0:T(8,128)(2,1)S(1)}, bf16[288,256]{1,0:T(8,128)(2,1)S(1)}, bf16[288,256]{1,0:T(8,128)(2,1)S(1)}, bf16[288,256]{1,0:T(8,128)(2,1)S(1)}, bf16[576,1024]{1,0:T(8,128)(2,1)S(1)}) custom-call(s32[1]{0:T(128)} %bitcast.1.t_ref, bf16[288,256]{1,0:T(8,128)(2,1)S(1)} %copy-done.7, bf16[288,256]{1,0:T(8,128)(2,1)} %collective-permute-done.refs_1_, ...), custom_call_target="tpu_custom_call" | custom-call | flops 2000000000 | bytes 8000000 | tf_op jit(solution)/shard_map/pallas_call | solution.py:295
  77.0 11.3 %shard_map.113 = (bf16[6,576,256]{2,1,0:T(8,128)(2,1)S(1)}, f32[8,256]{1,0:T(8,128)S(1)}) custom-call(bf16[576,1024]{1,0:T(8,128)(2,1)S(1)} %get-tuple-element.77.err_ref, bf16[1024,1024]{1,0:T(8,128)(2,1)S(1)} %get-tuple-element.72.refs_20_.wc_ref, bf16[512,576]{1,0:T(8,128)(2,1)S(1)} %get-tuple-element.79.attn_t, ...), custom_call_target="tpu_custom_call" | custom-call | flops 8000000000 | bytes 10000000 | tf_op jit(solution)/shard_map/pallas_call | solution.py:360
  88.4 0.6 collective-permute-start.27
  89.0 1.6 %collective-permute-start.26 = (f32[8,256]{1,0:T(8,128)S(1)}, f32[8,256]{1,0:T(8,128)S(1)}, u32[]{:S(2)}, u32[]{:S(2)}) collective-permute-start(f32[8,256]{1,0:T(8,128)S(1)} %get-tuple-element.88), channel_id=1, source_target_pairs={{0,1},{1,0},{2,3},{3,2},{4,5},{5,4},{6,7},{7,6},{8,9},{9,8},{10,11... | collective-permute-start | bytes 24584 | tf_op jit(solution)/shard_map/ppermute | solution.py:478
  90.6 1.6 %collective-permute-start.22 = (bf16[288,256]{1,0:T(8,128)(2,1)S(1)}, bf16[288,256]{1,0:T(8,128)(2,1)S(1)}, u32[]{:S(2)}, u32[]{:S(2)}) collective-permute-start(bf16[288,256]{1,0:T(8,128)(2,1)S(1)} %get-tuple-element.74), channel_id=1, source_target_pairs={{0,4},{1,5},{2,6},{3,7},{4,8},{5,9},{6,10},{7,11},{8,12},{9,13},{1... | collective-permute-start | bytes 442376 | tf_op jit(solution)/shard_map/ppermute | solution.py:478
  92.2 1.1 collective-permute-start.24
  93.3 6.7 %collective-permute-done.22.a1 = bf16[288,256]{1,0:T(8,128)(2,1)S(1)} collective-permute-done((bf16[288,256]{1,0:T(8,128)(2,1)S(1)}, bf16[288,256]{1,0:T(8,128)(2,1)S(1)}, u32[]{:S(2)}, u32[]{:S(2)}) %collective-permute-start.22) | collective-permute-done | bytes 147488 | tf_op jit(solution)/shard_map/ppermute | solution.py:478
  100.0 1.2 %collective-permute-done.24.b1 = bf16[288,256]{1,0:T(8,128)(2,1)S(1)} collective-permute-done((bf16[288,256]{1,0:T(8,128)(2,1)S(1)}, bf16[288,256]{1,0:T(8,128)(2,1)S(1)}, u32[]{:S(2)}, u32[]{:S(2)}) %collective-permute-start.24) | collective-permute-done | bytes 147488 | tf_op jit(solution)/shard_map/ppermute | solution.py:478
  101.2 3.8 %shard_map.114 = (f32[6,256]{1,0:T(8,128)S(1)}, f32[6,256]{1,0:T(8,128)S(1)}) custom-call(bf16[6,576,256]{2,1,0:T(8,128)(2,1)S(1)} %get-tuple-element.82.g_ref, bf16[1024,576]{1,0:T(8,128)(2,1)S(1)} %get-tuple-element.83.normed_t, bf16[3,1024,256]{2,1,0:T(8,128)(2,1)S(1)} %bitcast.16, bf16[3,1024,256]{2,1,0:T(8,128)(2,1)S(1)} %collective-permute-done.14.w_ref.wp_ref, ...), custom_call_target="tpu_custom_call" | custom-call | flops 4000000000 | bytes 8000000 | tf_op jit(solution)/shard_map/pallas_call | solution.py:387
  105.1 2.1 %collective-permute-start.30 = (f32[6,256]{1,0:T(8,128)S(1)}, f32[6,256]{1,0:T(8,128)S(1)}, u32[]{:S(2)}, u32[]{:S(2)}) collective-permute-start(f32[6,256]{1,0:T(8,128)S(1)} %get-tuple-element.87), channel_id=1, source_target_pairs={{0,5},{1,4},{2,7},{3,6},{4,1},{5,0},{6,3},{7,2},{8,13},{9,12},{10,... | collective-permute-start | bytes 18440 | tf_op jit(solution)/shard_map/ppermute | solution.py:484
  107.3 1.7 %collective-permute-done.29 = f32[14,256]{1,0:T(8,128)S(1)} collective-permute-done((f32[14,256]{1,0:T(8,128)S(1)}, f32[14,256]{1,0:T(8,128)S(1)}, u32[]{:S(2)}, u32[]{:S(2)}) %collective-permute-start.29) | collective-permute-done | bytes 14368 | tf_op jit(solution)/shard_map/ppermute | solution.py:484
  109.1 1.8 %collective-permute-start.33 = (f32[14,256]{1,0:T(8,128)S(1)}, f32[14,256]{1,0:T(8,128)S(1)}, u32[]{:S(2)}, u32[]{:S(2)}) collective-permute-start(f32[14,256]{1,0:T(8,128)S(1)} %pad_maximum_fusion.1), channel_id=1, source_target_pairs={{0,24},{1,25},{2,26},{3,27},{4,28},{5,29},{6,30},{7,31},{8,16},{9,... | collective-permute-start | bytes 43016 | tf_op jit(solution)/shard_map/ppermute | solution.py:484
  110.9 1.6 %collective-permute-start.31 = (f32[14,256]{1,0:T(8,128)S(1)}, f32[14,256]{1,0:T(8,128)S(1)}, u32[]{:S(2)}, u32[]{:S(2)}) collective-permute-start(f32[14,256]{1,0:T(8,128)S(1)} %pad_maximum_fusion.1), channel_id=1, source_target_pairs={{0,8},{1,9},{2,10},{3,11},{4,12},{5,13},{6,14},{7,15},{8,0},{9,1},... | collective-permute-start | bytes 43016 | tf_op jit(solution)/shard_map/ppermute | solution.py:484
  112.6 2.0 %shard_map.111 = bf16[42,12,2,256]{3,2,1,0:T(2,128)(2,1)} custom-call(s32[2]{0:T(128)S(1)} %pad_add_fusion.1.s_ref, bf16[288,256]{1,0:T(8,128)(2,1)S(1)} %get-tuple-element.73.a0, bf16[288,256]{1,0:T(8,128)(2,1)S(1)} %collective-permute-done.22.a1, bf16[288,256]{1,0:T(8,128)(2,1)S(1)} %collective-permute-done.23.b0, ...), custom_call_target="tpu_custom_call" | custom-call | flops 1000000 | bytes 2000000 | tf_op jit(solution)/shard_map/pallas_call | solution.py:461
  114.5 0.3 collective-permute-done.33
  114.9 0.6 reshape.26
  115.5 0.6 reshape.27
  (68 shorter events, 0.9 us)
Async XLA Ops:
  0.6 38.1 %copy-start = (bf16[1024,3,256]{2,0,1:T(8,128)(2,1)S(1)}, bf16[1024,3,256]{2,0,1:T(8,128)(2,1)}, u32[]{:S(2)}) copy-start(bf16[1024,3,256]{2,0,1:T(8,128)(2,1)} %param.10) | copy-start | bytes 4718596
  0.6 41.6 %collective-permute-start.14 = (bf16[3,1024,256]{2,1,0:T(8,128)(2,1)}, bf16[3,1024,256]{2,1,0:T(8,128)(2,1)S(1)}, u32[]{:S(2)}, u32[]{:S(2)}) collective-permute-start(bf16[3,1024,256]{2,1,0:T(8,128)(2,1)} %bitcast.14), channel_id=1, source_target_pairs={{0,1},{1,0},{2,3},{3,2},{4,5},{5,4},{6,7},{7,6},{8,9},{9,8},{10,11... | collective-permute-start | bytes 4718600 | tf_op jit(solution)/shard_map/ppermute | solution.py:478
  1.9 1.0 copy-start.2
  4.6 0.7 copy-start.10
  5.3 31.2 %copy-start.6 = (bf16[288,256]{1,0:T(8,128)(2,1)}, bf16[288,256]{1,0:T(8,128)(2,1)S(1)}, u32[]{:S(2)}) copy-start(bf16[288,256]{1,0:T(8,128)(2,1)S(1)} %get-tuple-element.46.refs_0_) | copy-start | bytes 442372
  5.3 9.4 %collective-permute-start.1 = (bf16[288,256]{1,0:T(8,128)(2,1)S(1)}, bf16[288,256]{1,0:T(8,128)(2,1)S(1)}, u32[]{:S(2)}, u32[]{:S(2)}) collective-permute-start(bf16[288,256]{1,0:T(8,128)(2,1)S(1)} %get-tuple-element.46.refs_0_), channel_id=1, source_target_pairs={{0,2},{1,3},{2,0},{3,1},{4,6},{5,7},{6,4},{7,5},{8,10},{9,11},{10,... | collective-permute-start | bytes 442376 | tf_op jit(solution)/shard_map/ppermute | solution.py:478
  7.9 9.1 %collective-permute-start.3 = (bf16[288,256]{1,0:T(8,128)(2,1)}, bf16[288,256]{1,0:T(8,128)(2,1)}, u32[]{:S(2)}, u32[]{:S(2)}) collective-permute-start(bf16[288,256]{1,0:T(8,128)(2,1)} %get-tuple-element.48), channel_id=1, source_target_pairs={{0,28},{1,29},{2,30},{3,31},{4,0},{5,1},{6,2},{7,3},{8,4},{9,5},{1... | collective-permute-start | bytes 442376 | tf_op jit(solution)/shard_map/ppermute | solution.py:478
  12.5 6.8 %collective-permute-start.4 = (bf16[288,256]{1,0:T(8,128)(2,1)}, bf16[288,256]{1,0:T(8,128)(2,1)}, u32[]{:S(2)}, u32[]{:S(2)}) collective-permute-start(bf16[288,256]{1,0:T(8,128)(2,1)} %get-tuple-element.49), channel_id=1, source_target_pairs={{0,29},{1,28},{2,31},{3,30},{4,1},{5,0},{6,3},{7,2},{8,5},{9,4},{1... | collective-permute-start | bytes 442376 | tf_op jit(solution)/shard_map/ppermute | solution.py:478
  14.1 13.5 %collective-permute-start.19 = (bf16[128,1024]{1,0:T(8,128)(2,1)}, bf16[128,1024]{1,0:T(8,128)(2,1)}, u32[]{:S(2)}, u32[]{:S(2)}) collective-permute-start(bf16[128,1024]{1,0:T(8,128)(2,1)} %constant_dynamic-slice_fusion), channel_id=1, source_target_pairs={{0,2},{1,3},{2,0},{3,1},{4,6},{5,7},{6,4},{7,5},{8,10},{9,11},{10,... | collective-permute-start | bytes 786440 | tf_op jit(solution)/shard_map/ppermute | solution.py:478
  14.6 21.8 %copy-start.8 = (bf16[288,256]{1,0:T(8,128)(2,1)}, bf16[288,256]{1,0:T(8,128)(2,1)S(1)}, u32[]{:S(2)}) copy-start(bf16[288,256]{1,0:T(8,128)(2,1)S(1)} %collective-permute-done.1.refs_2_) | copy-start | bytes 442372
  14.6 11.5 %collective-permute-start.2 = (bf16[288,256]{1,0:T(8,128)(2,1)}, bf16[288,256]{1,0:T(8,128)(2,1)}, u32[]{:S(2)}, u32[]{:S(2)}) collective-permute-start(bf16[288,256]{1,0:T(8,128)(2,1)} %copy-done.10), channel_id=1, source_target_pairs={{0,3},{1,2},{2,1},{3,0},{4,7},{5,6},{6,5},{7,4},{8,11},{9,10},{10,... | collective-permute-start | bytes 442376 | tf_op jit(solution)/shard_map/ppermute | solution.py:478
  17.0 12.9 %collective-permute-start.5 = (bf16[288,256]{1,0:T(8,128)(2,1)}, bf16[288,256]{1,0:T(8,128)(2,1)}, u32[]{:S(2)}, u32[]{:S(2)}) collective-permute-start(bf16[288,256]{1,0:T(8,128)(2,1)} %collective-permute-done.3.refs_4_), channel_id=1, source_target_pairs={{0,2},{1,3},{2,0},{3,1},{4,6},{5,7},{6,4},{7,5},{8,10},{9,11},{10,... | collective-permute-start | bytes 442376 | tf_op jit(solution)/shard_map/ppermute | solution.py:478
  19.3 13.5 %collective-permute-start.6 = (bf16[288,256]{1,0:T(8,128)(2,1)}, bf16[288,256]{1,0:T(8,128)(2,1)}, u32[]{:S(2)}, u32[]{:S(2)}) collective-permute-start(bf16[288,256]{1,0:T(8,128)(2,1)} %collective-permute-done.4.refs_5_), channel_id=1, source_target_pairs={{0,2},{1,3},{2,0},{3,1},{4,6},{5,7},{6,4},{7,5},{8,10},{9,11},{10,... | collective-permute-start | bytes 442376 | tf_op jit(solution)/shard_map/ppermute | solution.py:478
  19.8 1.0 copy-start.3
  20.8 17.9 %copy-start.5 = (f32[2,3,256]{2,0,1:T(2,128)S(1)}, f32[2,3,256]{2,0,1:T(2,128)}, u32[]{:S(2)}) copy-start(f32[2,3,256]{2,0,1:T(2,128)} %param.12) | copy-start | bytes 18436
  22.5 0.7 copy-start.11
  23.1 0.7 copy-start.13
  23.8 0.7 copy-start.14
  26.1 9.6 %collective-permute-start.7 = (bf16[288,256]{1,0:T(8,128)(2,1)}, bf16[288,256]{1,0:T(8,128)(2,1)}, u32[]{:S(2)}, u32[]{:S(2)}) collective-permute-start(bf16[288,256]{1,0:T(8,128)(2,1)} %get-tuple-element.53), channel_id=1, source_target_pairs={{0,1},{1,0},{2,3},{3,2},{4,5},{5,4},{6,7},{7,6},{8,9},{9,8},{10,11... | collective-permute-start | bytes 442376 | tf_op jit(solution)/shard_map/ppermute | solution.py:478
  27.7 15.8 %collective-permute-start = (bf16[288,256]{1,0:T(8,128)(2,1)}, bf16[288,256]{1,0:T(8,128)(2,1)}, u32[]{:S(2)}, u32[]{:S(2)}) collective-permute-start(bf16[288,256]{1,0:T(8,128)(2,1)} %copy-done.10), channel_id=1, source_target_pairs={{0,1},{1,0},{2,3},{3,2},{4,5},{5,4},{6,7},{7,6},{8,9},{9,8},{10,11... | collective-permute-start | bytes 442376 | tf_op jit(solution)/shard_map/ppermute | solution.py:478
  29.9 9.5 %collective-permute-start.8 = (bf16[288,256]{1,0:T(8,128)(2,1)}, bf16[288,256]{1,0:T(8,128)(2,1)}, u32[]{:S(2)}, u32[]{:S(2)}) collective-permute-start(bf16[288,256]{1,0:T(8,128)(2,1)} %copy-done.14), channel_id=1, source_target_pairs={{0,28},{1,29},{2,30},{3,31},{4,0},{5,1},{6,2},{7,3},{8,4},{9,5},{1... | collective-permute-start | bytes 442376 | tf_op jit(solution)/shard_map/ppermute | solution.py:478
  32.8 7.4 %collective-permute-start.9 = (bf16[288,256]{1,0:T(8,128)(2,1)}, bf16[288,256]{1,0:T(8,128)(2,1)}, u32[]{:S(2)}, u32[]{:S(2)}) collective-permute-start(bf16[288,256]{1,0:T(8,128)(2,1)} %copy-done.13), channel_id=1, source_target_pairs={{0,29},{1,28},{2,31},{3,30},{4,1},{5,0},{6,3},{7,2},{8,5},{9,4},{1... | collective-permute-start | bytes 442376 | tf_op jit(solution)/shard_map/ppermute | solution.py:478
  35.7 5.0 %collective-permute-start.15 = (f32[3,2,256]{2,1,0:T(2,128)}, f32[3,2,256]{2,1,0:T(2,128)S(1)}, u32[]{:S(2)}, u32[]{:S(2)}) collective-permute-start(f32[3,2,256]{2,1,0:T(2,128)} %bitcast.19), channel_id=1, source_target_pairs={{0,1},{1,0},{2,3},{3,2},{4,5},{5,4},{6,7},{7,6},{8,9},{9,8},{10,11... | collective-permute-start | bytes 18440 | tf_op jit(solution)/shard_map/ppermute | solution.py:478
  38.8 1.5 %copy-start.12 = (bf16[288,256]{1,0:T(8,128)(2,1)S(1)}, bf16[288,256]{1,0:T(8,128)(2,1)}, u32[]{:S(2)}) copy-start(bf16[288,256]{1,0:T(8,128)(2,1)} %copy-done.11) | copy-start | bytes 442372
  38.8 6.3 %copy-start.7 = (bf16[288,256]{1,0:T(8,128)(2,1)S(1)}, bf16[288,256]{1,0:T(8,128)(2,1)}, u32[]{:S(2)}) copy-start(bf16[288,256]{1,0:T(8,128)(2,1)} %copy-done.6) | copy-start | bytes 442372
  38.8 6.3 %copy-start.9 = (bf16[288,256]{1,0:T(8,128)(2,1)S(1)}, bf16[288,256]{1,0:T(8,128)(2,1)}, u32[]{:S(2)}) copy-start(bf16[288,256]{1,0:T(8,128)(2,1)} %copy-done.8) | copy-start | bytes 442372
  39.5 17.1 %collective-permute-start.20 = (bf16[128,1024]{1,0:T(8,128)(2,1)}, bf16[128,1024]{1,0:T(8,128)(2,1)S(1)}, u32[]{:S(2)}, u32[]{:S(2)}) collective-permute-start(bf16[128,1024]{1,0:T(8,128)(2,1)} %collective-permute-done.19), channel_id=1, source_target_pairs={{0,4},{1,5},{2,6},{3,7},{4,0},{5,1},{6,2},{7,3},{8,12},{9,13},{10,... | collective-permute-start | bytes 786440 | tf_op jit(solution)/shard_map/ppermute | solution.py:484
  40.2 15.0 %collective-permute-start.10 = (bf16[288,256]{1,0:T(8,128)(2,1)S(1)}, bf16[288,256]{1,0:T(8,128)(2,1)S(1)}, u32[]{:S(2)}, u32[]{:S(2)}) collective-permute-start(bf16[288,256]{1,0:T(8,128)(2,1)S(1)} %copy-done.12), channel_id=1, source_target_pairs={{0,2},{1,3},{2,0},{3,1},{4,6},{5,7},{6,4},{7,5},{8,10},{9,11},{10,... | collective-permute-start | bytes 442376 | tf_op jit(solution)/shard_map/ppermute | solution.py:478
  40.7 14.5 %collective-permute-start.11 = (bf16[288,256]{1,0:T(8,128)(2,1)}, bf16[288,256]{1,0:T(8,128)(2,1)S(1)}, u32[]{:S(2)}, u32[]{:S(2)}) collective-permute-start(bf16[288,256]{1,0:T(8,128)(2,1)} %collective-permute-done.7.refs_9_), channel_id=1, source_target_pairs={{0,2},{1,3},{2,0},{3,1},{4,6},{5,7},{6,4},{7,5},{8,10},{9,11},{10,... | collective-permute-start | bytes 442376 | tf_op jit(solution)/shard_map/ppermute | solution.py:478
  42.2 13.0 %collective-permute-start.12 = (bf16[288,256]{1,0:T(8,128)(2,1)}, bf16[288,256]{1,0:T(8,128)(2,1)S(1)}, u32[]{:S(2)}, u32[]{:S(2)}) collective-permute-start(bf16[288,256]{1,0:T(8,128)(2,1)} %collective-permute-done.8.refs_12_), channel_id=1, source_target_pairs={{0,2},{1,3},{2,0},{3,1},{4,6},{5,7},{6,4},{7,5},{8,10},{9,11},{10,... | collective-permute-start | bytes 442376 | tf_op jit(solution)/shard_map/ppermute | solution.py:478
  43.5 11.8 %collective-permute-start.13 = (bf16[288,256]{1,0:T(8,128)(2,1)}, bf16[288,256]{1,0:T(8,128)(2,1)S(1)}, u32[]{:S(2)}, u32[]{:S(2)}) collective-permute-start(bf16[288,256]{1,0:T(8,128)(2,1)} %collective-permute-done.9.refs_13_), channel_id=1, source_target_pairs={{0,2},{1,3},{2,0},{3,1},{4,6},{5,7},{6,4},{7,5},{8,10},{9,11},{10,... | collective-permute-start | bytes 442376 | tf_op jit(solution)/shard_map/ppermute | solution.py:478
  45.0 10.1 %copy-start.1 = (bf16[256,1024]{1,0:T(8,128)(2,1)S(1)}, bf16[256,1024]{1,0:T(8,128)(2,1)}, u32[]{:S(2)}) copy-start(bf16[256,1024]{1,0:T(8,128)(2,1)} %po_ref.1) | copy-start | bytes 1572868
  55.2 6.3 %collective-permute-start.18 = (bf16[256,1024]{1,0:T(8,128)(2,1)S(1)}, bf16[256,1024]{1,0:T(8,128)(2,1)S(1)}, u32[]{:S(2)}, u32[]{:S(2)}) collective-permute-start(bf16[256,1024]{1,0:T(8,128)(2,1)S(1)} %copy-done.1), channel_id=1, source_target_pairs={{0,1},{1,0},{2,3},{3,2},{4,5},{5,4},{6,7},{7,6},{8,9},{9,8},{10,11... | collective-permute-start | bytes 1572872 | tf_op jit(solution)/shard_map/ppermute | solution.py:478
  58.1 3.4 %collective-permute-start.21 = (bf16[256,1024]{1,0:T(8,128)(2,1)S(1)}, bf16[256,1024]{1,0:T(8,128)(2,1)S(1)}, u32[]{:S(2)}, u32[]{:S(2)}) collective-permute-start(bf16[256,1024]{1,0:T(8,128)(2,1)S(1)} %fusion.1.w2), channel_id=1, source_target_pairs={{0,1},{1,0},{2,3},{3,2},{4,5},{5,4},{6,7},{7,6},{8,9},{9,8},{10,11... | collective-permute-start | bytes 1572872 | tf_op jit(solution)/shard_map/ppermute | solution.py:478
  58.6 15.3 %collective-permute-start.16 = (bf16[432,512]{1,0:T(8,128)(2,1)S(1)}, bf16[432,512]{1,0:T(8,128)(2,1)S(1)}, u32[]{:S(2)}, u32[]{:S(2)}) collective-permute-start(bf16[432,512]{1,0:T(8,128)(2,1)S(1)} %get-tuple-element.65.refs_16_.a_ref), channel_id=1, source_target_pairs={{0,2},{1,3},{2,0},{3,1},{4,6},{5,7},{6,4},{7,5},{8,10},{9,11},{10,... | collective-permute-start | bytes 1327112 | tf_op jit(solution)/shard_map/ppermute | solution.py:478
  59.1 14.8 %collective-permute-start.17 = (bf16[144,512]{1,0:T(8,128)(2,1)S(1)}, bf16[144,512]{1,0:T(8,128)(2,1)S(1)}, u32[]{:S(2)}, u32[]{:S(2)}) collective-permute-start(bf16[144,512]{1,0:T(8,128)(2,1)S(1)} %shard_map.108.refs_17_.b_ref), channel_id=1, source_target_pairs={{0,2},{1,3},{2,0},{3,1},{4,6},{5,7},{6,4},{7,5},{8,10},{9,11},{10,... | collective-permute-start | bytes 442376 | tf_op jit(solution)/shard_map/ppermute | solution.py:478
  60.6 0.9 copy-start.4
  88.4 3.8 %collective-permute-start.27 = (f32[8,256]{1,0:T(8,128)S(1)}, f32[8,256]{1,0:T(8,128)S(1)}, u32[]{:S(2)}, u32[]{:S(2)}) collective-permute-start(f32[8,256]{1,0:T(8,128)S(1)} %get-tuple-element.88), channel_id=1, source_target_pairs={{0,2},{1,3},{2,0},{3,1},{4,6},{5,7},{6,4},{7,5},{8,10},{9,11},{10,... | collective-permute-start | bytes 24584 | tf_op jit(solution)/shard_map/ppermute | solution.py:478
  88.9 4.4 %collective-permute-start.28 = (f32[8,256]{1,0:T(8,128)S(1)}, f32[8,256]{1,0:T(8,128)S(1)}, u32[]{:S(2)}, u32[]{:S(2)}) collective-permute-start(f32[8,256]{1,0:T(8,128)S(1)} %get-tuple-element.88), channel_id=1, source_target_pairs={{0,3},{1,2},{2,1},{3,0},{4,7},{5,6},{6,5},{7,4},{8,11},{9,10},{10,... | collective-permute-start | bytes 24584 | tf_op jit(solution)/shard_map/ppermute | solution.py:478
  89.0 4.3 %collective-permute-start.26 = (f32[8,256]{1,0:T(8,128)S(1)}, f32[8,256]{1,0:T(8,128)S(1)}, u32[]{:S(2)}, u32[]{:S(2)}) collective-permute-start(f32[8,256]{1,0:T(8,128)S(1)} %get-tuple-element.88), channel_id=1, source_target_pairs={{0,1},{1,0},{2,3},{3,2},{4,5},{5,4},{6,7},{7,6},{8,9},{9,8},{10,11... | collective-permute-start | bytes 24584 | tf_op jit(solution)/shard_map/ppermute | solution.py:478
  90.6 9.4 %collective-permute-start.22 = (bf16[288,256]{1,0:T(8,128)(2,1)S(1)}, bf16[288,256]{1,0:T(8,128)(2,1)S(1)}, u32[]{:S(2)}, u32[]{:S(2)}) collective-permute-start(bf16[288,256]{1,0:T(8,128)(2,1)S(1)} %get-tuple-element.74), channel_id=1, source_target_pairs={{0,4},{1,5},{2,6},{3,7},{4,8},{5,9},{6,10},{7,11},{8,12},{9,13},{1... | collective-permute-start | bytes 442376 | tf_op jit(solution)/shard_map/ppermute | solution.py:478
  92.2 7.8 %collective-permute-start.23 = (bf16[288,256]{1,0:T(8,128)(2,1)S(1)}, bf16[288,256]{1,0:T(8,128)(2,1)S(1)}, u32[]{:S(2)}, u32[]{:S(2)}) collective-permute-start(bf16[288,256]{1,0:T(8,128)(2,1)S(1)} %get-tuple-element.75), channel_id=1, source_target_pairs={{0,1},{1,0},{2,3},{3,2},{4,5},{5,4},{6,7},{7,6},{8,9},{9,8},{10,11... | collective-permute-start | bytes 442376 | tf_op jit(solution)/shard_map/ppermute | solution.py:478
  92.2 9.0 %collective-permute-start.24 = (bf16[288,256]{1,0:T(8,128)(2,1)S(1)}, bf16[288,256]{1,0:T(8,128)(2,1)S(1)}, u32[]{:S(2)}, u32[]{:S(2)}) collective-permute-start(bf16[288,256]{1,0:T(8,128)(2,1)S(1)} %get-tuple-element.76), channel_id=1, source_target_pairs={{0,5},{1,4},{2,7},{3,6},{4,9},{5,8},{6,11},{7,10},{8,13},{9,12},{1... | collective-permute-start | bytes 442376 | tf_op jit(solution)/shard_map/ppermute | solution.py:478
  105.1 3.9 %collective-permute-start.29 = (f32[14,256]{1,0:T(8,128)S(1)}, f32[14,256]{1,0:T(8,128)S(1)}, u32[]{:S(2)}, u32[]{:S(2)}) collective-permute-start(f32[14,256]{1,0:T(8,128)S(1)} %pad_maximum_fusion), channel_id=1, source_target_pairs={{0,4},{1,5},{2,6},{3,7},{4,0},{5,1},{6,2},{7,3},{8,12},{9,13},{10,... | collective-permute-start | bytes 43016 | tf_op jit(solution)/shard_map/ppermute | solution.py:484
  105.1 3.8 %collective-permute-start.30 = (f32[6,256]{1,0:T(8,128)S(1)}, f32[6,256]{1,0:T(8,128)S(1)}, u32[]{:S(2)}, u32[]{:S(2)}) collective-permute-start(f32[6,256]{1,0:T(8,128)S(1)} %get-tuple-element.87), channel_id=1, source_target_pairs={{0,5},{1,4},{2,7},{3,6},{4,1},{5,0},{6,3},{7,2},{8,13},{9,12},{10,... | collective-permute-start | bytes 18440 | tf_op jit(solution)/shard_map/ppermute | solution.py:484
  107.3 1.7 %collective-permute-start.25 = (f32[6,256]{1,0:T(8,128)S(1)}, f32[6,256]{1,0:T(8,128)S(1)}, u32[]{:S(2)}, u32[]{:S(2)}) collective-permute-start(f32[6,256]{1,0:T(8,128)S(1)} %get-tuple-element.87), channel_id=1, source_target_pairs={{0,1},{1,0},{2,3},{3,2},{4,5},{5,4},{6,7},{7,6},{8,9},{9,8},{10,11... | collective-permute-start | bytes 18440 | tf_op jit(solution)/shard_map/ppermute | solution.py:478
  109.0 5.5 %collective-permute-start.32 = (f32[14,256]{1,0:T(8,128)S(1)}, f32[14,256]{1,0:T(8,128)S(1)}, u32[]{:S(2)}, u32[]{:S(2)}) collective-permute-start(f32[14,256]{1,0:T(8,128)S(1)} %pad_maximum_fusion.1), channel_id=1, source_target_pairs={{0,16},{1,17},{2,18},{3,19},{4,20},{5,21},{6,22},{7,23},{8,24},{9,... | collective-permute-start | bytes 43016 | tf_op jit(solution)/shard_map/ppermute | solution.py:484
  109.1 5.7 %collective-permute-start.33 = (f32[14,256]{1,0:T(8,128)S(1)}, f32[14,256]{1,0:T(8,128)S(1)}, u32[]{:S(2)}, u32[]{:S(2)}) collective-permute-start(f32[14,256]{1,0:T(8,128)S(1)} %pad_maximum_fusion.1), channel_id=1, source_target_pairs={{0,24},{1,25},{2,26},{3,27},{4,28},{5,29},{6,30},{7,31},{8,16},{9,... | collective-permute-start | bytes 43016 | tf_op jit(solution)/shard_map/ppermute | solution.py:484
  110.9 3.9 %collective-permute-start.31 = (f32[14,256]{1,0:T(8,128)S(1)}, f32[14,256]{1,0:T(8,128)S(1)}, u32[]{:S(2)}, u32[]{:S(2)}) collective-permute-start(f32[14,256]{1,0:T(8,128)S(1)} %pad_maximum_fusion.1), channel_id=1, source_target_pairs={{0,8},{1,9},{2,10},{3,11},{4,12},{5,13},{6,14},{7,15},{8,0},{9,1},... | collective-permute-start | bytes 43016 | tf_op jit(solution)/shard_map/ppermute | solution.py:484

commit v3 on v1

--- a/solution.py
+++ b/solution.py
@@ -127,31 +127,25 @@
 
 
 def forward_kernel(t_ref, *refs):
-    pieces = refs[:8]
-    wo_ref, wp_ref, idk_ref, idq_ref, normed_ref, qkv_ref, attn_ref, xs = refs[8:]
+    pieces = refs[:4]
+    wo_ref, wp_ref, idk_ref, idq_ref, normed_ref, qkv_ref, attn_ref = refs[4:]
     t = t_ref[0]
-    half = pieces[0].shape[0] // 4
-    cells = 2 * half
-    width = pieces[0].shape[1]
-    for k in range(4):
-        cols = pl.ds(pl.multiple_of((t ^ k) * width, width), width)
-        for s in range(2):
-            for p in range(2):
-                block = pieces[4 * s + k][cells * p : cells * (p + 1), :].astype(F32)
-                for i in range(2):
-                    first = cells * (2 * p + i) + half * s
-                    xs[first : first + half, cols] = block[half * i : half * (i + 1)]
+    n, width = pieces[0].shape
+    d = 4 * width
 
     def norm(w, carry):
         rows = pl.ds(pl.multiple_of(w * 48, 16), 48)
-        x = xs[rows, :]
-        mean = jnp.mean(x, axis=-1, keepdims=True)
-        x = x - mean
-        var = jnp.mean(x * x, axis=-1, keepdims=True)
-        normed_ref[rows, :] = (x * lax.rsqrt(var + EPS)).astype(BF)
-        return carry
-
-    lax.fori_loop(0, 12, norm, 0)
+        x = [r[rows, :].astype(F32) for r in pieces]
+        mean = sum(jnp.sum(b, axis=-1, keepdims=True) for b in x) / d
+        x = [b - mean for b in x]
+        var = sum(jnp.sum(b * b, axis=-1, keepdims=True) for b in x) / d
+        scale = lax.rsqrt(var + EPS)
+        for k in range(4):
+            cols = pl.ds(pl.multiple_of((t ^ k) * width, width), width)
+            normed_ref[rows, cols] = (x[k] * scale).astype(BF)
+        return carry
+
+    lax.fori_loop(0, n // 48, norm, 0)
 
     def project(i, carry):
         for g, w_ref in enumerate((wo_ref, wp_ref)):
@@ -207,14 +201,13 @@
     return pl.pallas_call(
         forward_kernel,
         out_shape=(
-            jax.ShapeDtypeStruct((2 * n, d), BF),
-            jax.ShapeDtypeStruct((6, 2 * n, width), BF),
-            jax.ShapeDtypeStruct((2 * n // 4 * 3, 2 * width), BF),
+            jax.ShapeDtypeStruct((n, d), BF),
+            jax.ShapeDtypeStruct((6, n, width), BF),
+            jax.ShapeDtypeStruct((n // 4 * 3, 2 * width), BF),
         ),
-        in_specs=[pl.BlockSpec(memory_space=pltpu.SMEM)] + spec(12),
+        in_specs=[pl.BlockSpec(memory_space=pltpu.SMEM)] + spec(8),
         out_specs=tuple(spec(3)),
-        scratch_shapes=[pltpu.VMEM((2 * n, d), F32)],
-        compiler_params=params(24),
+        compiler_params=params(20),
         cost_estimate=pl.CostEstimate(flops=8 * 10**9, bytes_accessed=10 * 10**6, transcendentals=10**6),
     )(t, *pieces, wo, wp, idk, idq)
 
@@ -246,59 +239,53 @@
         in_specs=spec(3),
         out_specs=tuple(spec(2)),
         compiler_params=params(16),
-        cost_estimate=pl.CostEstimate(flops=10**9, bytes_accessed=4 * n * (d + e), transcendentals=0),
+        cost_estimate=pl.CostEstimate(flops=1, bytes_accessed=1, transcendentals=0),
     )(normed, *attn)
 
 
 def output_kernel(t_ref, *refs):
-    pieces, targets = refs[:8], refs[8:16]
-    attns, wc_ref, idk_ref = refs[16:20], refs[20], refs[21]
-    mixed, err_ref, y_ref = refs[22:26], refs[26], refs[27]
+    pieces, targets = refs[:4], refs[4:8]
+    a0, a1, b0, b1, wc_ref, idk_ref = refs[8:14]
+    mixed, err_ref, y_ref = refs[14:18], refs[18], refs[19]
     t = t_ref[0]
-    half = pieces[0].shape[0] // 4
-    cells = 2 * half
-    width = pieces[0].shape[1]
-    e = attns[0].shape[1]
+    n, width = pieces[0].shape
+    cells = n // 4
+    half = cells // 2
+    e = a0.shape[1]
+    valid = idk_ref[...] >= 0
     for k in range(4):
+        x_ref, want_ref = pieces[k], targets[k]
         cols = pl.ds(pl.multiple_of((t ^ k) * width, width), width)
-        own = jnp.concatenate([attns[0][...], attns[1][...]], axis=0)
-        other = jnp.concatenate([attns[2][...], attns[3][...]], axis=0)
+        own = jnp.concatenate([a0[...], a1[...]], axis=0)
+        other = jnp.concatenate([b0[...], b1[...]], axis=0)
         y_ref[...] = jnp.dot(own, wc_ref[:e, cols], preferred_element_type=F32) + jnp.dot(
             other, wc_ref[e:, cols], preferred_element_type=F32
         )
         for p in range(2):
-            errs = [[None, None], [None, None]]
-            for s in range(2):
-                block = pieces[4 * s + k][cells * p : cells * (p + 1), :].astype(F32)
-                wanted = targets[4 * s + k][cells * p : cells * (p + 1), :].astype(F32)
-                ys = []
-                for i in range(2):
-                    first = cells * (2 * p + i) + half * s
-                    part = slice(half * i, half * (i + 1))
-                    y = block[part] + y_ref[first : first + half, :]
-                    ys.append(y)
-                    valid = idk_ref[first : first + half, :] >= 0
-                    errs[i][s] = jnp.where(valid, y - wanted[part], 0.0)
-                if k < 2:
-                    mixed[2 * s + k][cells * p : cells * (p + 1), :] = jnp.concatenate(
-                        ys, axis=0
-                    ).astype(BF)
+            ys = []
             for i in range(2):
-                first = cells * (2 * p + i)
-                err_ref[first : first + cells, cols] = jnp.concatenate(errs[i], axis=0).astype(BF)
+                rows = slice(cells * (2 * p + i), cells * (2 * p + i + 1))
+                y = x_ref[rows, :].astype(F32) + y_ref[rows, :]
+                ys.append(y)
+                err = y - want_ref[rows, :].astype(F32)
+                err_ref[rows, cols] = jnp.where(valid[rows], err, 0.0).astype(BF)
+            if k < 2:
+                at = slice(cells * p, cells * (p + 1))
+                for s in range(2):
+                    part = slice(half * s, half * (s + 1))
+                    mixed[2 * s + k][at, :] = jnp.concatenate([y[part] for y in ys], axis=0).astype(BF)
 
 
 def output(t, pieces, targets, own, other, wc, idk):
     n, width = pieces[0].shape
-    d = 4 * width
-    piece = jax.ShapeDtypeStruct((n, width), BF)
+    piece = jax.ShapeDtypeStruct((n // 2, width), BF)
     return pl.pallas_call(
         output_kernel,
-        out_shape=(piece, piece, piece, piece, jax.ShapeDtypeStruct((2 * n, d), BF)),
-        in_specs=[pl.BlockSpec(memory_space=pltpu.SMEM)] + spec(22),
+        out_shape=(piece, piece, piece, piece, jax.ShapeDtypeStruct((n, 4 * width), BF)),
+        in_specs=[pl.BlockSpec(memory_space=pltpu.SMEM)] + spec(14),
         out_specs=tuple(spec(5)),
-        scratch_shapes=[pltpu.VMEM((2 * n, width), F32)],
-        compiler_params=params(24),
+        scratch_shapes=[pltpu.VMEM((n, width), F32)],
+        compiler_params=params(20),
         cost_estimate=pl.CostEstimate(flops=2 * 10**9, bytes_accessed=8 * 10**6, transcendentals=0),
     )(t, *pieces, *targets, *own, *other, wc, idk)
 
@@ -309,10 +296,34 @@
     return g_hi, g_lo
 
 
-def backward_kernel(
-    err_ref, wc_ref, attn_t, qkv_ref, po_ref, pp_ref, pb_ref, idk_ref, idq_ref, g_ref, proj_ref, d_ref
-):
-    e = attn_t.shape[0]
+def proj_sums_kernel(err_ref, attn_t, po_ref, pp_ref, pb_ref, proj_ref):
+    def proj_part(i, carry):
+        cols = pl.ds(pl.multiple_of(i * 256, 256), 256)
+        grad = jnp.dot(attn_t[...], err_ref[:, cols], preferred_element_type=F32)
+        n = po_ref.shape[0]
+        b = pb_ref[:, cols]
+        h0, l0 = masked_sums(grad[:n], po_ref[:, cols].astype(F32), b)
+        h1, l1 = masked_sums(grad[n:], pp_ref[:, cols].astype(F32), b)
+        proj_ref[pl.ds(i, 1), :] = h0 + h1
+        proj_ref[pl.ds(4 + i, 1), :] = l0 + l1
+        return carry
+
+    lax.fori_loop(0, 4, proj_part, 0)
+
+
+def proj_sums(err, attn_t, po, pp, pb):
+    return pl.pallas_call(
+        proj_sums_kernel,
+        out_shape=jax.ShapeDtypeStruct((8, 256), F32),
+        in_specs=spec(5),
+        out_specs=spec(1)[0],
+        compiler_params=params(16),
+        cost_estimate=pl.CostEstimate(flops=10**9, bytes_accessed=3 * 10**6, transcendentals=0),
+    )(err, attn_t, po, pp, pb)
+
+
+def backward_kernel(err_ref, wc_ref, qkv_ref, idk_ref, idq_ref, g_ref, d_ref):
+    e = d_ref.shape[1]
     cells = idk_ref.shape[0] // 4
     d_ref[...] = lax.dot_general(err_ref[...], wc_ref[:e], NT, preferred_element_type=F32).astype(BF)
     mask_a, mask_b = head_masks()
@@ -341,31 +352,18 @@
 
     lax.fori_loop(0, 4, window, 0)
 
-    def proj_part(i, carry):
-        cols = pl.ds(pl.multiple_of(i * 256, 256), 256)
-        grad = jnp.dot(attn_t[...], err_ref[:, cols], preferred_element_type=F32)
-        n = po_ref.shape[0]
-        b = pb_ref[:, cols]
-        h0, l0 = masked_sums(grad[:n], po_ref[:, cols].astype(F32), b)
-        h1, l1 = masked_sums(grad[n:], pp_ref[:, cols].astype(F32), b)
-        proj_ref[pl.ds(i, 1), :] = h0 + h1
-        proj_ref[pl.ds(4 + i, 1), :] = l0 + l1
-        return carry
-
-    lax.fori_loop(0, err_ref.shape[1] // 256, proj_part, 0)
-
-
-def backward(err, wc, attn_t, qkv, po, pp, pb, idk, idq):
+
+def backward(err, wc, qkv, idk, idq):
     n, width = qkv.shape[1:]
     return pl.pallas_call(
         backward_kernel,
-        out_shape=(jax.ShapeDtypeStruct((6, n, width), BF), jax.ShapeDtypeStruct((8, width), F32)),
-        in_specs=spec(9),
-        out_specs=tuple(spec(2)),
-        scratch_shapes=[pltpu.VMEM((n, attn_t.shape[0]), BF)],
+        out_shape=jax.ShapeDtypeStruct((6, n, width), BF),
+        in_specs=spec(5),
+        out_specs=spec(1)[0],
+        scratch_shapes=[pltpu.VMEM((n, 2 * width), BF)],
         compiler_params=params(20),
         cost_estimate=pl.CostEstimate(flops=8 * 10**9, bytes_accessed=10 * 10**6, transcendentals=10**6),
-    )(err, wc, attn_t, qkv, po, pp, pb, idk, idq)
+    )(err, wc, qkv, idk, idq)
 
 
 def qkv_sums_kernel(g_ref, normed_t, wo_ref, wp_ref, bo_ref, bp_ref, own_ref, peer_ref):
@@ -394,42 +392,98 @@
     )(g, normed_t, wo, wp, bo, bp)
 
 
-def split_kernel(s_ref, x_ref, m0, m1, p0, p1):
+def split_kernel(s_ref, up_ref, low_ref, mine_ref, peer_ref):
     offset, core = s_ref[0], s_ref[1]
-    rows, lon, lev, width = x_ref.shape
+    rows, lon, lev, width = up_ref.shape
     many = (rows + WLAT) // 2
-    half = lon * lev // 2
-    for rel, outs in ((0, (m0, m1)), (1, (p0, p1))):
+    half = lon * lev
+    cells = 2 * WLAT * half
+    for rel, out_ref in ((0, mine_ref), (1, peer_ref)):
         base = many * (core ^ rel) - offset
 
-        def body(i, carry):
-            parts = [[], []]
-            for j in range(4):
-                r = base + 4 * i + j
-                v = x_ref[jnp.clip(r, 0, rows - 1)].astype(F32).reshape(lon * lev, width)
-                v = jnp.where((r >= 0) & (r < rows), v, 0.0)
-                parts[0].append(v[half:])
-                parts[1].append(v[:half])
-            at = pl.ds(pl.multiple_of(4 * half * i, 16), 4 * half)
-            for s in range(2):
-                outs[s][at, :] = jnp.concatenate(parts[s], axis=0).astype(BF)
+        def body(w, carry):
+            parts = []
+            for ref in (up_ref, low_ref):
+                for j in range(WLAT):
+                    r = base + WLAT * w + j
+                    v = ref[jnp.clip(r, 0, rows - 1)].astype(F32).reshape(half, width)
+                    parts.append(jnp.where((r >= 0) & (r < rows), v, 0.0))
+            at = pl.ds(pl.multiple_of(w * cells, 16), cells)
+            out_ref[at, :] = jnp.concatenate(parts, axis=0).astype(BF)
             return carry
 
-        lax.fori_loop(0, many // 4, body, 0)
-
-
-def split(place, block):
-    rows, lev, lon, width = block.shape
-    block = jnp.transpose(block, (0, 2, 1, 3))
-    piece = jax.ShapeDtypeStruct(((rows + WLAT) // 2 * lon * lev // 2, width), BF)
+        lax.fori_loop(0, many // WLAT, body, 0)
+
+
+def split(place, upper, lower):
+    rows, lon, lev, width = upper.shape
+    piece = jax.ShapeDtypeStruct(((rows + WLAT) * lon * lev, width), BF)
     return pl.pallas_call(
         split_kernel,
-        out_shape=(piece,) * 4,
-        in_specs=[pl.BlockSpec(memory_space=pltpu.SMEM)] + spec(1),
-        out_specs=tuple(spec(4)),
+        out_shape=(piece, piece),
+        in_specs=[pl.BlockSpec(memory_space=pltpu.SMEM)] + spec(2),
+        out_specs=tuple(spec(2)),
         compiler_params=params(16),
         cost_estimate=pl.CostEstimate(flops=10**6, bytes_accessed=2 * 10**6, transcendentals=0),
-    )(place, block)
+    )(place, upper, lower)
+
+
+def cell_at(c, window):
+    cells = 2 * WLAT * window
+    w = sum((c >= i * cells).astype(jnp.int32) for i in range(1, 4))
+    c = c - w * cells
+    s = (c >= WLAT * window).astype(jnp.int32)
+    c = c - s * WLAT * window
+    r = sum((c >= i * window).astype(jnp.int32) for i in range(1, WLAT))
+    c = c - r * window
+    return w * WLAT + r, s * (window // 2) + (c >> 1), c & 1
+
+
+def ids_kernel(s_ref, ids_ref, idk_ref, idq_ref):
+    offset, core, sector = s_ref[0], s_ref[1], s_ref[2]
+    rows, lev, total = ids_ref.shape
+    n = idk_ref.shape[0]
+    cells = n // 4
+    window = cells // (2 * WLAT)
+    many = (rows + WLAT) // 2
+    ids = ids_ref[...].astype(F32).reshape(rows * lev, total)
+
+    def find(c):
+        r, lon, level = cell_at(c, window)
+        r = r + many * core - offset
+        lon = lon + sector * window + window // 2
+        lon = jnp.where(lon >= total, lon - total, lon)
+        valid = (r >= 0) & (r < rows)
+        return jnp.where(valid, 2 * r + level, -1), lon, valid
+
+    spot, lon, valid = find(lax.broadcasted_iota(jnp.int32, (n, 1), 0))
+    at = lax.broadcasted_iota(jnp.int32, (n, rows * lev), 1) == spot
+    found = jnp.dot(jnp.where(at, 1.0, 0.0), ids, preferred_element_type=F32)
+    there = lax.broadcasted_iota(jnp.int32, (n, total), 1) == lon
+    found = jnp.sum(jnp.where(there, found, 0.0), axis=1, keepdims=True)
+    idk_ref[...] = jnp.where(valid, found, -1.0).astype(jnp.int32)
+    for w in range(4):
+        lane = lax.broadcasted_iota(jnp.int32, (1, 2 * cells), 1)
+        spot, lon, valid = find(w * cells + jnp.where(lane >= cells, lane - cells, lane))
+        there = lax.broadcasted_iota(jnp.int32, (total, 2 * cells), 0) == lon
+        found = jnp.dot(ids, jnp.where(there, 1.0, 0.0), preferred_element_type=F32)
+        at = lax.broadcasted_iota(jnp.int32, (rows * lev, 2 * cells), 0) == spot
+        found = jnp.sum(jnp.where(at, found, 0.0), axis=0, keepdims=True)
+        idq_ref[w] = jnp.where(valid, found, -1.0).astype(jnp.int32)
+
+
+def window_ids(place, ids, cells):
+    return pl.pallas_call(
+        ids_kernel,
+        out_shape=(
+            jax.ShapeDtypeStruct((4 * cells, 1), jnp.int32),
+            jax.ShapeDtypeStruct((4, 1, 2 * cells), jnp.int32),
+        ),
+        in_specs=[pl.BlockSpec(memory_space=pltpu.SMEM)] + spec(1),
+        out_specs=tuple(spec(2)),
+        compiler_params=params(16),
+        cost_estimate=pl.CostEstimate(flops=10**6, bytes_accessed=10**6, transcendentals=0),
+    )(place, ids)
 
 
 def join_kernel(s_ref, a0, a1, b0, b1, out_ref, grid_ref):
@@ -478,6 +532,51 @@
     return lax.ppermute(block, ("lat", "tp"), route)
 
 
+def swap(block, other, flip):
+    count, tp = lax.axis_size("lat"), lax.axis_size("tp")
+    route = [(u * tp + t, (u ^ other) * tp + (t ^ flip)) for u in range(count) for t in range(tp)]
+    return lax.ppermute(block, ("lat", "tp"), route)
+
+
+def lat_terms(block, bit):
+    count = lax.axis_size("lat")
+    terms = [block]
+    while bit < count:
+        block = added(terms)
+        terms = [block, swap(block, bit, 0)]
+        if 4 * bit <= count:
+            terms += [swap(block, 2 * bit, 0), swap(block, 3 * bit, 0)]
+        bit *= len(terms)
+    return terms
+
+
+def added(terms):
+    while len(terms) > 1:
+        terms = [a + b for a, b in zip(terms[::2], terms[1::2])]
+    return terms[0]
+
+
+def last_sum_kernel(*refs):
+    qkv_ref, proj_ref = refs[-2:]
+    total = added([r[...] for r in refs[:-2]])
+    width = total.shape[1]
+    for i in range(3):
+        qkv_ref[i] = total[2 * i : 2 * i + 2]
+    for i in range(4):
+        for j in range(2):
+            proj_ref[j : j + 1, width * i : width * (i + 1)] = total[6 + 4 * j + i : 7 + 4 * j + i]
+
+
+def last_sum(terms):
+    width = terms[0].shape[1]
+    return pl.pallas_call(
+        last_sum_kernel,
+        out_shape=(jax.ShapeDtypeStruct((3, 2, width), F32), jax.ShapeDtypeStruct((2, 4 * width), F32)),
+        in_specs=spec(len(terms)),
+        out_specs=tuple(spec(2)),
+    )(*terms)
+
+
 def after(block, *others):
     return lax.optimization_barrier((block, *others))[0]
 
@@ -485,79 +584,64 @@
 def local(features, target, w_qkv, w_proj, qkv_clip, proj_clip, shift_offset, region_ids):
     rows, lev, lon, width = features.shape
     half = lon // 2
-    many = (rows + WLAT) // 2
     sector = lax.axis_index("lat")
-    count = lax.axis_size("lat")
     t = lax.axis_index("tp")
-    core = t % 2
-    offset = shift_offset[0]
     t_arr = jnp.reshape(t, (1,)).astype(jnp.int32)
-    place = jnp.stack([offset, core]).astype(jnp.int32)
-
-    m0, m1, p0, p1 = split(place, features)
-    f02, f03 = send(m0, 0, 2), send(p0, 0, 3)
-    f10, f11 = send(m1, -1, 0), send(p1, -1, 1)
-    f01 = send(p0, 0, 1)
-    f12, f13 = send(f10, 0, 2), send(f11, 0, 2)
+    place = jnp.stack([shift_offset[0], t % 2, sector]).astype(jnp.int32)
+
+    def halves(block):
+        block = jnp.transpose(block, (0, 2, 1, 3))
+        return block[:, half:], block[:, :half]
 
     w3 = jnp.transpose(w_qkv, (1, 0, 2))
     c3 = jnp.transpose(qkv_clip, (1, 0, 2))
     w3_peer = send(w3, 0, 1)
     c3_peer = send(c3, 0, 1)
+    w1, w2 = send(w_proj, 0, 1), send(w_proj, 0, 2)
     wc_own, b_own = clip_qkv(w3, c3)
     wc_peer, b_peer = clip_qkv(w3_peer, c3_peer)
-
-    doubled = jnp.concatenate([region_ids, region_ids[:, :, :lon]], 2)
-    ids = lax.dynamic_slice_in_dim(doubled, sector * lon + half, lon, 2)
-    ids = jnp.pad(ids, ((WLAT, WLAT), (0, 0), (0, 0)), constant_values=-1)
-    ids = lax.dynamic_slice_in_dim(ids, WLAT - offset + many * core, many, 0)
-    ids = ids.reshape(many // WLAT, WLAT, lev, 2, half).transpose(0, 3, 1, 4, 2)
-    ids = ids.reshape(many // WLAT, 1, WLAT * lev * lon)
-    idk = ids.reshape(many * lev * lon, 1)
-    idq = jnp.concatenate([ids, ids], axis=2)
-
-    g0, g1, q0, q1 = split(place, target)
-    g1, q1, q0 = lax.optimization_barrier((g1, q1, q0, f02, f03, f10, f11))[:3]
-    t10, t11 = send(g1, -1, 0), send(q1, -1, 1)
-    t01 = send(q0, 0, 1)
-    share = w_proj.shape[0] // count
-    slab = send(lax.dynamic_slice_in_dim(w_proj, sector * share, share, 0), 0, 2)
-    w2 = lax.all_gather(slab, "lat", axis=0, tiled=True)
-    w1 = send(after(w_proj, f10, f11), 0, 1)
-
-    ya, yb, yc, yd = lax.optimization_barrier((g0, t01, t10, t11, f12, f13))[:4]
-    t02, t03, t12, t13 = send(ya, 0, 2), send(yb, 0, 2), send(yc, 0, 2), send(yd, 0, 2)
-    targets = [g0, t01, t02, t03, t10, t11, t12, t13]
-    f12, f13 = lax.optimization_barrier((f12, f13, t01, t10, t11))[:2]
-    pieces = [m0, f01, f02, f03, f10, f11, f12, f13]
+    idk, idq = window_ids(place, region_ids, WLAT * lev * lon)
+
+    f_up, f_low = halves(features)
+    t_up, t_low = halves(target)
+    f_low = send(f_low, -1, 0)
+    f_low, t_up, t_low, wc_own, wc_peer, idk, idq = lax.optimization_barrier(
+        (f_low, t_up, t_low, wc_own, wc_peer, idk, idq)
+    )
+    t_low = send(t_low, -1, 0)
+    mine, away = split(place, f_up, f_low)
+    pieces = [mine, send(away, 0, 1), send(mine, 0, 2), send(away, 0, 3)]
+
+    t_mine, t_away = split(place, t_up, t_low)
+    w_3 = send(after(w2, t_mine), 0, 1)
+    pc, pb = clip_proj([w_proj, w1, w2, w_3], proj_clip)
+    t_mine, t_away, *pieces = lax.optimization_barrier((t_mine, t_away, *pieces, pc))[:-1]
+    targets = [t_mine, send(t_away, 0, 1), send(t_mine, 0, 2), send(t_away, 0, 3)]
+
     normed, qkv, attn_a = forward(t_arr, pieces, wc_own, wc_peer, idk, idq)
     other_a = send(attn_a, 0, 2)
-    attn_b = last_window(after(qkv, t02, t03, t12, t13), idk, idq)
+    attn_b = last_window(after(qkv, *targets), idk, idq)
     other_b = send(attn_b, 0, 2)
-    attn, attn_other = (attn_a, attn_b), (other_a, other_b)
-    w2 = after(w2, attn_b)
-    w_3 = send(w2, 0, 1)
-    pc, pb = clip_proj([w_proj, w1, w2, w_3], proj_clip)
-    normed_t, attn_t = turn(normed, attn)
-
-    m00, m01, m10, m11, err = output(t_arr, pieces, targets, attn, attn_other, pc, idk)
+    normed_t, attn_t = turn(normed, (attn_a, attn_b))
+
+    m00, m01, m10, m11, err = output(
+        t_arr, pieces, targets, (attn_a, attn_b), (other_a, other_b), pc, idk
+    )
     m01 = send(m01, 0, 1)
     m10 = send(m10, 1, 0)
     m11 = send(m11, 1, 1)
 
-    grads, proj = backward(err, pc, attn_t, qkv, w_proj, w1, pb, idk, idq)
-    proj_peer = send(proj, 0, 1)
-    grads = after(grads, m01, m10, m11)
+    proj = proj_sums(err, attn_t, w_proj, w1, pb)
+    proj_y = send(proj, 0, 2)
+    grads = backward(err, pc, qkv, idk, idq)
+    grads = after(grads, m01, m10, m11, proj_y)
     own, peer = qkv_sums(grads, normed_t, w3, w3_peer, b_own, b_peer)
-    proj = proj + proj_peer
-    proj_other = send(proj, 0, 2)
-    peer = send(peer, 0, 1)
-    sums = jnp.concatenate([own + peer, proj + proj_other], axis=0)
-    sums = jnp.sum(lax.all_gather(sums, "lat", axis=0), axis=0)
+    proj = proj + proj_y
+    own, peer = jnp.concatenate([own, proj], axis=0), jnp.concatenate([peer, proj], axis=0)
+    sums = added([own, send(peer, 0, 1), swap(own, 1, 0), swap(peer, 1, 1)])
+    qkv_sum, proj_sum = last_sum(lat_terms(sums, 2))
     mixed = join(place, [m00, m10, m01, m11], rows, lon, lev)
-    qkv_sum = jnp.transpose(sums[:6].reshape(3, 2, width), (1, 0, 2))
-    proj_sum = sums[6:].reshape(2, 4 * width)
-    return (mixed, qkv_sum, proj_sum)
+    return (mixed, jnp.transpose(qkv_sum, (1, 0, 2)), proj_sum)
 
 
 def solution(mesh):

time: 156 us -> 107 us (0.69)
  blocking collectives: 62.2 us -> 0 us
  waiting for transfers between devices: 15.5 us -> 31.6 us
  local copies, waits for them, and re-layouts: 11.1 us -> 4.22 us
  starting transfers between devices: 25.9 us -> 31.6 us
    all_gather x2 -> x0, blocking collectives: 62.2 us -> none  [the longest x1 31.6 us: local(): w2 = lax.all_gather(slab, 'lat', axis=0, tiled=True)]
    ppermute x27 -> x20, waiting for transfers between devices: 15.5 us -> 27.9 us  [send(): return lax.ppermute(block, ('lat', 'tp'), route)]
    ppermute x0 -> x5, starting transfers between devices: none -> 8.25 us  [swap(): return lax.ppermute(block, ('lat', 'tp'), route)]
    ppermute x0 -> x5, waiting for transfers between devices: none -> 3.68 us  [swap(): return lax.ppermute(block, ('lat', 'tp'), route)]
    slice x2, local copies, waits for them, and re-layouts: 0.01 us -> 3.56 us  [halves(): return (block[:, half:], block[:, :half])]
    unnamed x32 -> x18, local copies, waits for them, and re-layouts: 4.09 us -> 0.66 us
    ppermute x27 -> x20, starting transfers between devices: 25.9 us -> 23.4 us  [send(): return lax.ppermute(block, ('lat', 'tp'), route)]
    reshape x4 -> x0, local copies, waits for them, and re-layouts: 2.26 us -> none  [the longest x1 0.96 us: local(): ids = ids.reshape(many // WLAT, 1, WLAT * lev * lon)]
  transfers between devices with their start and end apart: 27 -> 25, of which waited for: 4 -> 9; matrix products, arithmetic and copies ran while one was open for 4% -> 3% of each run, Pallas kernels for 23% -> 29%
where the time goes in v3:
time: 107 us
  Pallas kernels  38 us (36%)
  starting transfers between devices  31.6 us (30%)
  waiting for transfers between devices  31.6 us (30%)
  local copies, waits for them, and re-layouts  4.22 us (4%)
  between operations  1.58 us (1%)
    ppermute x20, waiting for transfers between devices, send(): return lax.ppermute(block, ('lat', 'tp'), route)  27.9 us
    ppermute x20, starting transfers between devices, send(): return lax.ppermute(block, ('lat', 'tp'), route)  23.4 us
    pallas_call x1, Pallas kernels, backward(): pl.pallas_call(backward_kernel, out_shape=jax.ShapeDtypeStruct((6, n, wid...  9.76 us
    pallas_call x1, Pallas kernels, forward(): pl.pallas_call(forward_kernel, out_shape=(jax.ShapeDtypeStruct((n, d), BF...  8.94 us
    ppermute x5, starting transfers between devices, swap(): return lax.ppermute(block, ('lat', 'tp'), route)  8.25 us
    pallas_call x1, Pallas kernels, qkv_sums(): pl.pallas_call(qkv_sums_kernel, out_shape=(jax.ShapeDtypeStruct((6, width...  3.85 us
    ppermute x5, waiting for transfers between devices, swap(): return lax.ppermute(block, ('lat', 'tp'), route)  3.68 us
    slice x2, local copies, waits for them, and re-layouts, halves(): return (block[:, half:], block[:, :half])  3.56 us
  transfers between devices with their start and end apart: 25, of which 9 were waited for; matrix products, arithmetic and copies ran while one was open for 3% of the time, Pallas kernels for 29%

profile of v3, /device:TPU:0, one launch (start us, length us, event | category | flops | bytes accessed | tf_op | source)
XLA Modules:
  0.0 107.1 jit_solution(1699800568439283406)
XLA Ops:
  0.7 0.5 collective-permute-start.1
  1.2 0.1 collective-permute-start.2
  1.3 2.1 %fusion = (bf16[42,6,2,256]{3,2,1,0:T(2,128)(2,1)S(1)}, bf16[42,6,2,256]{3,2,1,0:T(2,128)(2,1)}) fusion(bf16[42,12,2,256]{3,2,1,0:T(2,128)(2,1)} %bitcast.14), kind=kLoop, calls=%fused_computation.4 | loop fusion | bytes 1032192 | tf_op jit(solution)/shard_map/slice | solution.py:594
  3.4 6.0 %collective-permute-start = (bf16[42,6,2,256]{3,2,1,0:T(2,128)(2,1)}, bf16[42,6,2,256]{3,2,1,0:T(2,128)(2,1)}, u32[]{:S(2)}, u32[]{:S(2)}) collective-permute-start(bf16[42,6,2,256]{3,2,1,0:T(2,128)(2,1)} %get-tuple-element.88), channel_id=1, source_target_pairs={{0,28},{1,29},{2,30},{3,31},{4,0},{5,1},{6,2},{7,3},{8,4},{9,5},{1... | collective-permute-start | bytes 774152 | tf_op jit(solution)/shard_map/ppermute | solution.py:532
  9.3 1.5 %collective-permute-start.8 = (bf16[256,1024]{1,0:T(8,128)(2,1)}, bf16[256,1024]{1,0:T(8,128)(2,1)}, u32[]{:S(2)}, u32[]{:S(2)}) collective-permute-start(bf16[256,1024]{1,0:T(8,128)(2,1)} %po_ref.1), channel_id=1, source_target_pairs={{0,2},{1,3},{2,0},{3,1},{4,6},{5,7},{6,4},{7,5},{8,10},{9,11},{10,... | collective-permute-start | bytes 1572872 | tf_op jit(solution)/shard_map/ppermute | solution.py:532
  11.5 1.4 %fusion.1 = (bf16[42,6,2,256]{3,2,1,0:T(2,128)(2,1)S(1)}, bf16[42,6,2,256]{3,2,1,0:T(2,128)(2,1)S(1)}) fusion(bf16[42,12,2,256]{3,2,1,0:T(2,128)(2,1)} %bitcast.15), kind=kLoop, calls=%fused_computation.5 | loop fusion | bytes 1032192 | tf_op jit(solution)/shard_map/slice | solution.py:594
  13.0 0.1 pad_add_fusion.s_ref
  13.0 1.0 shard_map.105
  14.1 0.0 copy-start.1
  14.1 0.7 shard_map.103
  14.8 0.0 copy-start.3
  14.8 0.0 collective-permute-done.2.c_ref
  14.8 0.0 collective-permute-done.1.w_ref.wp_ref
  14.8 0.7 shard_map.104
  15.5 0.0 collective-permute-done.low_ref
  15.5 5.0 %collective-permute-start.3 = (bf16[42,6,2,256]{3,2,1,0:T(2,128)(2,1)S(1)}, bf16[42,6,2,256]{3,2,1,0:T(2,128)(2,1)S(1)}, u32[]{:S(2)}, u32[]{:S(2)}) collective-permute-start(bf16[42,6,2,256]{3,2,1,0:T(2,128)(2,1)S(1)} %get-tuple-element.50), channel_id=1, source_target_pairs={{0,28},{1,29},{2,30},{3,31},{4,0},{5,1},{6,2},{7,3},{8,4},{9,5},{1... | collective-permute-start | bytes 774152 | tf_op jit(solution)/shard_map/ppermute | solution.py:532
  20.6 0.0 collective-permute-start.7
  20.6 4.9 %collective-permute-done.3.low_ref = bf16[42,6,2,256]{3,2,1,0:T(2,128)(2,1)S(1)} collective-permute-done((bf16[42,6,2,256]{3,2,1,0:T(2,128)(2,1)S(1)}, bf16[42,6,2,256]{3,2,1,0:T(2,128)(2,1)S(1)}, u32[]{:S(2)}, u32[]{:S(2)}) %collective-permute-start.3) | collective-permute-done | bytes 258080 | tf_op jit(solution)/shard_map/ppermute | solution.py:532
  25.4 0.9 shard_map.106
  26.4 0.1 collective-permute-start.9
  26.5 1.4 %shard_map.107 = (bf16[576,256]{1,0:T(8,128)(2,1)S(1)}, bf16[576,256]{1,0:T(8,128)(2,1)S(1)}) custom-call(s32[3]{0:T(128)S(1)} %pad_add_fusion.s_ref, bf16[42,6,2,256]{3,2,1,0:T(2,128)(2,1)S(1)} %get-tuple-element.87.up_ref, bf16[42,6,2,256]{3,2,1,0:T(2,128)(2,1)} %collective-permute-done.low_ref), custom_call_target="tpu_custom_call" | custom-call | flops 1000000 | bytes 2000000 | tf_op jit(solution)/shard_map/pallas_call | solution.py:421
  27.9 1.6 %collective-permute-start.5 = (bf16[576,256]{1,0:T(8,128)(2,1)S(1)}, bf16[576,256]{1,0:T(8,128)(2,1)S(1)}, u32[]{:S(2)}, u32[]{:S(2)}) collective-permute-start(bf16[576,256]{1,0:T(8,128)(2,1)S(1)} %get-tuple-element.58.refs_0_), channel_id=1, source_target_pairs={{0,2},{1,3},{2,0},{3,1},{4,6},{5,7},{6,4},{7,5},{8,10},{9,11},{10,... | collective-permute-start | bytes 884744 | tf_op jit(solution)/shard_map/ppermute | solution.py:532
  29.5 0.3 collective-permute-start.6
  29.8 0.3 collective-permute-start.4
  30.1 2.0 %shard_map.108 = (bf16[1024,1024]{1,0:T(8,128)(2,1)S(1)}, f32[8,1024]{1,0:T(8,128)S(1)}) custom-call(bf16[256,1024]{1,0:T(8,128)(2,1)S(1)} %copy-done.1, bf16[256,1024]{1,0:T(8,128)(2,1)S(1)} %collective-permute-done.7.w1.pp_ref, bf16[256,1024]{1,0:T(8,128)(2,1)} %collective-permute-done.8.w2, bf16[256,1024]{1,0:T(8,128)(2,1)S(1)} %collective-permute-done.9.w3, ...), custom_call_target="tpu_custom_call" | custom-call | flops 10485760 | bytes 4194304 | tf_op jit(solution)/shard_map/pallas_call | solution.py:85
  32.1 5.7 %collective-permute-done.5.refs_2_ = bf16[576,256]{1,0:T(8,128)(2,1)S(1)} collective-permute-done((bf16[576,256]{1,0:T(8,128)(2,1)S(1)}, bf16[576,256]{1,0:T(8,128)(2,1)S(1)}, u32[]{:S(2)}, u32[]{:S(2)}) %collective-permute-start.5) | collective-permute-done | bytes 294944 | tf_op jit(solution)/shard_map/ppermute | solution.py:532
  37.7 5.5 %collective-permute-done.6.refs_3_ = bf16[576,256]{1,0:T(8,128)(2,1)S(1)} collective-permute-done((bf16[576,256]{1,0:T(8,128)(2,1)S(1)}, bf16[576,256]{1,0:T(8,128)(2,1)S(1)}, u32[]{:S(2)}, u32[]{:S(2)}) %collective-permute-start.6) | collective-permute-done | bytes 294944 | tf_op jit(solution)/shard_map/ppermute | solution.py:532
  43.3 0.0 collective-permute-done.4.refs_1_
  43.3 1.3 %collective-permute-start.12 = (bf16[576,256]{1,0:T(8,128)(2,1)S(1)}, bf16[576,256]{1,0:T(8,128)(2,1)S(1)}, u32[]{:S(2)}, u32[]{:S(2)}) collective-permute-start(bf16[576,256]{1,0:T(8,128)(2,1)S(1)} %get-tuple-element.63), channel_id=1, source_target_pairs={{0,3},{1,2},{2,1},{3,0},{4,7},{5,6},{6,5},{7,4},{8,11},{9,10},{10,... | collective-permute-start | bytes 884744 | tf_op jit(solution)/shard_map/ppermute | solution.py:532
  44.6 0.3 collective-permute-start.10
  44.9 0.5 collective-permute-start.11
  45.4 8.9 %shard_map.109 = (bf16[576,1024]{1,0:T(8,128)(2,1)S(1)}, bf16[6,576,256]{2,1,0:T(8,128)(2,1)S(1)}, bf16[432,512]{1,0:T(8,128)(2,1)S(1)}) custom-call(s32[1]{0:T(128)} %bitcast.2.t_ref, bf16[576,256]{1,0:T(8,128)(2,1)S(1)} %get-tuple-element.58.refs_0_, bf16[576,256]{1,0:T(8,128)(2,1)S(1)} %collective-permute-done.4.refs_1_, ...), custom_call_target="tpu_custom_call" | custom-call | flops 8000000000 | bytes 10000000 | tf_op jit(solution)/shard_map/pallas_call | solution.py:201
  54.4 1.6 %collective-permute-start.13 = (bf16[432,512]{1,0:T(8,128)(2,1)S(1)}, bf16[432,512]{1,0:T(8,128)(2,1)S(1)}, u32[]{:S(2)}, u32[]{:S(2)}) collective-permute-start(bf16[432,512]{1,0:T(8,128)(2,1)S(1)} %get-tuple-element.68.refs_8_.a_ref), channel_id=1, source_target_pairs={{0,2},{1,3},{2,0},{3,1},{4,6},{5,7},{6,4},{7,5},{8,10},{9,11},{10,... | collective-permute-start | bytes 1327112 | tf_op jit(solution)/shard_map/ppermute | solution.py:532
  55.9 3.3 %collective-permute-done.11.refs_6_ = bf16[576,256]{1,0:T(8,128)(2,1)S(1)} collective-permute-done((bf16[576,256]{1,0:T(8,128)(2,1)S(1)}, bf16[576,256]{1,0:T(8,128)(2,1)S(1)}, u32[]{:S(2)}, u32[]{:S(2)}) %collective-permute-start.11) | collective-permute-done | bytes 294944 | tf_op jit(solution)/shard_map/ppermute | solution.py:532
  59.2 1.3 %shard_map.110.refs_9_.b_ref = bf16[144,512]{1,0:T(8,128)(2,1)S(1)} custom-call(bf16[6,576,256]{2,1,0:T(8,128)(2,1)S(1)} %get-tuple-element.70.qkv_ref, s32[576,1]{1,0:T(8,128)S(1)} %get-tuple-element.66.refs_6_.idk_ref.refs_13_, s32[4,1,288]{2,1,0:T(1,128)S(1)} %get-tuple-element.67.refs_7_.idq_ref), custom_call_target="tpu_custom_call" | custom-call | flops 1000000000 | bytes 2000000 | tf_op jit(solution)/shard_map/pallas_call | solution.py:188
  60.5 1.6 %collective-permute-start.14 = (bf16[144,512]{1,0:T(8,128)(2,1)S(1)}, bf16[144,512]{1,0:T(8,128)(2,1)S(1)}, u32[]{:S(2)}, u32[]{:S(2)}) collective-permute-start(bf16[144,512]{1,0:T(8,128)(2,1)S(1)} %shard_map.110.refs_9_.b_ref), channel_id=1, source_target_pairs={{0,2},{1,3},{2,0},{3,1},{4,6},{5,7},{6,4},{7,5},{8,10},{9,11},{10,... | collective-permute-start | bytes 442376 | tf_op jit(solution)/shard_map/ppermute | solution.py:532
  62.1 0.8 shard_map.114
  63.0 8.6 %collective-permute-done.14.refs_11_ = bf16[144,512]{1,0:T(8,128)(2,1)S(1)} collective-permute-done((bf16[144,512]{1,0:T(8,128)(2,1)S(1)}, bf16[144,512]{1,0:T(8,128)(2,1)S(1)}, u32[]{:S(2)}, u32[]{:S(2)}) %collective-permute-start.14) | collective-permute-done | bytes 147488 | tf_op jit(solution)/shard_map/ppermute | solution.py:532
  71.5 0.0 collective-permute-done.13.refs_10_
  71.5 1.6 %shard_map.111 = (bf16[288,256]{1,0:T(8,128)(2,1)S(1)}, bf16[288,256]{1,0:T(8,128)(2,1)S(1)}, bf16[288,256]{1,0:T(8,128)(2,1)S(1)}, bf16[288,256]{1,0:T(8,128)(2,1)S(1)}, bf16[576,1024]{1,0:T(8,128)(2,1)S(1)}) custom-call(s32[1]{0:T(128)} %bitcast.2.t_ref, bf16[576,256]{1,0:T(8,128)(2,1)S(1)} %get-tuple-element.58.refs_0_, ...), custom_call_target="tpu_custom_call" | custom-call | flops 2000000000 | bytes 8000000 | tf_op jit(solution)/shard_map/pallas_call | solution.py:282
  73.2 0.1 collective-permute-start.15
  73.2 0.1 collective-permute-start.16
  73.3 0.2 collective-permute-start.17
  73.6 1.6 %shard_map.115 = f32[8,256]{1,0:T(8,128)S(1)} custom-call(bf16[576,1024]{1,0:T(8,128)(2,1)S(1)} %get-tuple-element.75.err_ref, bf16[512,576]{1,0:T(8,128)(2,1)S(1)} %get-tuple-element.77.attn_t, bf16[256,1024]{1,0:T(8,128)(2,1)S(1)} %copy-done.1, bf16[256,1024]{1,0:T(8,128)(2,1)S(1)} %collective-permute-done.7.w1.pp_ref, f32[8,1024]{1,0:T(8,128)S(1)} %get-tuple-element.78.pb_ref), custom_call_target="tpu_custom_call" | custom-call | flops 1000000000 | bytes 3000000 | tf_op jit(solution)/shard_map/pallas_call | solution.py:315
  75.1 1.6 %collective-permute-start.18 = (f32[8,256]{1,0:T(8,128)S(1)}, f32[8,256]{1,0:T(8,128)S(1)}, u32[]{:S(2)}, u32[]{:S(2)}) collective-permute-start(f32[8,256]{1,0:T(8,128)S(1)} %shard_map.115), channel_id=1, source_target_pairs={{0,2},{1,3},{2,0},{3,1},{4,6},{5,7},{6,4},{7,5},{8,10},{9,11},{10,... | collective-permute-start | bytes 24584 | tf_op jit(solution)/shard_map/ppermute | solution.py:532
  76.7 9.8 %shard_map.113.g_ref = bf16[6,576,256]{2,1,0:T(8,128)(2,1)S(1)} custom-call(bf16[576,1024]{1,0:T(8,128)(2,1)S(1)} %get-tuple-element.75.err_ref, bf16[1024,1024]{1,0:T(8,128)(2,1)S(1)} %get-tuple-element.57.refs_12_.wc_ref, bf16[6,576,256]{2,1,0:T(8,128)(2,1)S(1)} %get-tuple-element.70.qkv_ref, s32[576,1]{1,0:T(8,128)S(1)} %get-tuple-element.66.refs_6_.idk_ref.refs_13_, ...), custom_call_target="tpu_custom_call" | custom-call | flops 8000000000 | bytes 10000000 | tf_op jit(solution)/shard_map/pallas_call | solution.py:358
  86.5 0.0 collective-permute-done.15.a1
  86.6 3.8 %shard_map.116 = (f32[6,256]{1,0:T(8,128)S(1)}, f32[6,256]{1,0:T(8,128)S(1)}) custom-call(bf16[6,576,256]{2,1,0:T(8,128)(2,1)S(1)} %shard_map.113.g_ref, bf16[1024,576]{1,0:T(8,128)(2,1)S(1)} %get-tuple-element.80.normed_t, bf16[3,1024,256]{2,1,0:T(8,128)(2,1)S(1)} %bitcast.11, bf16[3,1024,256]{2,1,0:T(8,128)(2,1)S(1)} %collective-permute-done.1.w_ref.wp_ref, ...), custom_call_target="tpu_custom_call" | custom-call | flops 4000000000 | bytes 8000000 | tf_op jit(solution)/shard_map/pallas_call | solution.py:385
  90.4 1.4 %collective-permute-start.20 = (f32[14,256]{1,0:T(8,128)S(1)}, f32[14,256]{1,0:T(8,128)S(1)}, u32[]{:S(2)}, u32[]{:S(2)}) collective-permute-start(f32[14,256]{1,0:T(8,128)S(1)} %get-tuple-element.92), channel_id=1, source_target_pairs={{0,4},{1,5},{2,6},{3,7},{4,0},{5,1},{6,2},{7,3},{8,12},{9,13},{10,... | collective-permute-start | bytes 43016 | tf_op jit(solution)/shard_map/ppermute | solution.py:538
  91.9 0.0 collective-permute-start.21
  91.9 0.8 collective-permute-start.19
  92.6 1.6 %collective-permute-done.20 = f32[14,256]{1,0:T(8,128)S(1)} collective-permute-done((f32[14,256]{1,0:T(8,128)S(1)}, f32[14,256]{1,0:T(8,128)S(1)}, u32[]{:S(2)}, u32[]{:S(2)}) %collective-permute-start.20) | collective-permute-done | bytes 14368 | tf_op jit(solution)/shard_map/ppermute | solution.py:538
  94.2 0.8 collective-permute-done.21
  95.0 0.0 collective-permute-done.19
  95.1 4.9 %collective-permute-start.24 = (f32[14,256]{1,0:T(8,128)S(1)}, f32[14,256]{1,0:T(8,128)S(1)}, u32[]{:S(2)}, u32[]{:S(2)}) collective-permute-start(f32[14,256]{1,0:T(8,128)S(1)} %add_add_fusion.refs_0_), channel_id=1, source_target_pairs={{0,24},{1,25},{2,26},{3,27},{4,28},{5,29},{6,30},{7,31},{8,16},{9,... | collective-permute-start | bytes 43016 | tf_op jit(solution)/shard_map/ppermute | solution.py:538
  99.9 1.5 %collective-permute-start.23 = (f32[14,256]{1,0:T(8,128)S(1)}, f32[14,256]{1,0:T(8,128)S(1)}, u32[]{:S(2)}, u32[]{:S(2)}) collective-permute-start(f32[14,256]{1,0:T(8,128)S(1)} %add_add_fusion.refs_0_), channel_id=1, source_target_pairs={{0,16},{1,17},{2,18},{3,19},{4,20},{5,21},{6,22},{7,23},{8,24},{9,... | collective-permute-start | bytes 43016 | tf_op jit(solution)/shard_map/ppermute | solution.py:538
  101.4 0.5 collective-permute-start.22
  101.9 2.0 %shard_map.112 = bf16[42,12,2,256]{3,2,1,0:T(2,128)(2,1)} custom-call(s32[3]{0:T(128)S(1)} %pad_add_fusion.s_ref, bf16[288,256]{1,0:T(8,128)(2,1)S(1)} %get-tuple-element.71.a0, bf16[288,256]{1,0:T(8,128)(2,1)S(1)} %collective-permute-done.15.a1, bf16[288,256]{1,0:T(8,128)(2,1)S(1)} %collective-permute-done.16.b0, ...), custom_call_target="tpu_custom_call" | custom-call | flops 1000000 | bytes 2000000 | tf_op jit(solution)/shard_map/pallas_call | solution.py:515
  103.8 0.0 collective-permute-done.24.refs_3_
  103.8 0.7 collective-permute-done.23.refs_2_
  104.6 0.6 collective-permute-done.22.refs_1_
  105.1 0.0 copy-done.7
  105.2 0.6 copy-done.8
  105.8 1.4 %shard_map.117 = (f32[3,2,256]{2,1,0:T(2,128)}, f32[2,1024]{1,0:T(2,128)}) custom-call(f32[14,256]{1,0:T(8,128)} %copy-done.5, f32[14,256]{1,0:T(8,128)} %copy-done.8, f32[14,256]{1,0:T(8,128)} %copy-done.7, f32[14,256]{1,0:T(8,128)} %copy-done.6), custom_call_target="tpu_custom_call" | custom-call | tf_op jit(solution)/shard_map/pallas_call | solution.py:572
  (25 shorter events, 0.1 us)
Async XLA Ops:
  0.6 13.4 %copy-start = (bf16[1024,3,256]{2,0,1:T(8,128)(2,1)S(1)}, bf16[1024,3,256]{2,0,1:T(8,128)(2,1)}, u32[]{:S(2)}) copy-start(bf16[1024,3,256]{2,0,1:T(8,128)(2,1)} %param.10) | copy-start | bytes 4718596
  0.6 13.4 %copy-start.4 = (f32[2,3,256]{2,0,1:T(2,128)S(1)}, f32[2,3,256]{2,0,1:T(2,128)}, u32[]{:S(2)}) copy-start(f32[2,3,256]{2,0,1:T(2,128)} %param.12) | copy-start | bytes 18436
  0.7 12.4 %copy-start.2 = (s32[42,2,96]{2,1,0:T(2,128)S(1)}, s32[42,2,96]{2,1,0:T(2,128)}, u32[]{:S(2)}) copy-start(s32[42,2,96]{2,1,0:T(2,128)} %ids_ref.1) | copy-start | bytes 96772
  0.7 14.2 %collective-permute-start.1 = (bf16[3,1024,256]{2,1,0:T(8,128)(2,1)}, bf16[3,1024,256]{2,1,0:T(8,128)(2,1)S(1)}, u32[]{:S(2)}, u32[]{:S(2)}) collective-permute-start(bf16[3,1024,256]{2,1,0:T(8,128)(2,1)} %bitcast.9), channel_id=1, source_target_pairs={{0,1},{1,0},{2,3},{3,2},{4,5},{5,4},{6,7},{7,6},{8,9},{9,8},{10,11... | collective-permute-start | bytes 4718600 | tf_op jit(solution)/shard_map/ppermute | solution.py:532
  1.2 13.6 %collective-permute-start.2 = (f32[3,2,256]{2,1,0:T(2,128)}, f32[3,2,256]{2,1,0:T(2,128)S(1)}, u32[]{:S(2)}, u32[]{:S(2)}) collective-permute-start(f32[3,2,256]{2,1,0:T(2,128)} %bitcast.12), channel_id=1, source_target_pairs={{0,1},{1,0},{2,3},{3,2},{4,5},{5,4},{6,7},{7,6},{8,9},{9,8},{10,11... | collective-permute-start | bytes 18440 | tf_op jit(solution)/shard_map/ppermute | solution.py:532
  3.4 12.1 %collective-permute-start = (bf16[42,6,2,256]{3,2,1,0:T(2,128)(2,1)}, bf16[42,6,2,256]{3,2,1,0:T(2,128)(2,1)}, u32[]{:S(2)}, u32[]{:S(2)}) collective-permute-start(bf16[42,6,2,256]{3,2,1,0:T(2,128)(2,1)} %get-tuple-element.88), channel_id=1, source_target_pairs={{0,28},{1,29},{2,30},{3,31},{4,0},{5,1},{6,2},{7,3},{8,4},{9,5},{1... | collective-permute-start | bytes 774152 | tf_op jit(solution)/shard_map/ppermute | solution.py:532
  9.3 17.0 %collective-permute-start.8 = (bf16[256,1024]{1,0:T(8,128)(2,1)}, bf16[256,1024]{1,0:T(8,128)(2,1)}, u32[]{:S(2)}, u32[]{:S(2)}) collective-permute-start(bf16[256,1024]{1,0:T(8,128)(2,1)} %po_ref.1), channel_id=1, source_target_pairs={{0,2},{1,3},{2,0},{3,1},{4,6},{5,7},{6,4},{7,5},{8,10},{9,11},{10,... | collective-permute-start | bytes 1572872 | tf_op jit(solution)/shard_map/ppermute | solution.py:532
  14.1 6.5 %copy-start.1 = (bf16[256,1024]{1,0:T(8,128)(2,1)S(1)}, bf16[256,1024]{1,0:T(8,128)(2,1)}, u32[]{:S(2)}) copy-start(bf16[256,1024]{1,0:T(8,128)(2,1)} %po_ref.1) | copy-start | bytes 1572868
  14.8 15.3 %copy-start.3 = (f32[2,1024]{1,0:T(2,128)S(1)}, f32[2,1024]{1,0:T(2,128)}, u32[]{:S(2)}) copy-start(f32[2,1024]{1,0:T(2,128)} %c_ref.1) | copy-start | bytes 24580
  15.5 9.9 %collective-permute-start.3 = (bf16[42,6,2,256]{3,2,1,0:T(2,128)(2,1)S(1)}, bf16[42,6,2,256]{3,2,1,0:T(2,128)(2,1)S(1)}, u32[]{:S(2)}, u32[]{:S(2)}) collective-permute-start(bf16[42,6,2,256]{3,2,1,0:T(2,128)(2,1)S(1)} %get-tuple-element.50), channel_id=1, source_target_pairs={{0,28},{1,29},{2,30},{3,31},{4,0},{5,1},{6,2},{7,3},{8,4},{9,5},{1... | collective-permute-start | bytes 774152 | tf_op jit(solution)/shard_map/ppermute | solution.py:532
  20.6 9.5 %collective-permute-start.7 = (bf16[256,1024]{1,0:T(8,128)(2,1)S(1)}, bf16[256,1024]{1,0:T(8,128)(2,1)S(1)}, u32[]{:S(2)}, u32[]{:S(2)}) collective-permute-start(bf16[256,1024]{1,0:T(8,128)(2,1)S(1)} %copy-done.1), channel_id=1, source_target_pairs={{0,1},{1,0},{2,3},{3,2},{4,5},{5,4},{6,7},{7,6},{8,9},{9,8},{10,11... | collective-permute-start | bytes 1572872 | tf_op jit(solution)/shard_map/ppermute | solution.py:532
  26.4 3.7 %collective-permute-start.9 = (bf16[256,1024]{1,0:T(8,128)(2,1)}, bf16[256,1024]{1,0:T(8,128)(2,1)S(1)}, u32[]{:S(2)}, u32[]{:S(2)}) collective-permute-start(bf16[256,1024]{1,0:T(8,128)(2,1)} %collective-permute-done.8.w2), channel_id=1, source_target_pairs={{0,1},{1,0},{2,3},{3,2},{4,5},{5,4},{6,7},{7,6},{8,9},{9,8},{10,11... | collective-permute-start | bytes 1572872 | tf_op jit(solution)/shard_map/ppermute | solution.py:532
  27.9 9.9 %collective-permute-start.5 = (bf16[576,256]{1,0:T(8,128)(2,1)S(1)}, bf16[576,256]{1,0:T(8,128)(2,1)S(1)}, u32[]{:S(2)}, u32[]{:S(2)}) collective-permute-start(bf16[576,256]{1,0:T(8,128)(2,1)S(1)} %get-tuple-element.58.refs_0_), channel_id=1, source_target_pairs={{0,2},{1,3},{2,0},{3,1},{4,6},{5,7},{6,4},{7,5},{8,10},{9,11},{10,... | collective-permute-start | bytes 884744 | tf_op jit(solution)/shard_map/ppermute | solution.py:532
  29.5 13.8 %collective-permute-start.6 = (bf16[576,256]{1,0:T(8,128)(2,1)S(1)}, bf16[576,256]{1,0:T(8,128)(2,1)S(1)}, u32[]{:S(2)}, u32[]{:S(2)}) collective-permute-start(bf16[576,256]{1,0:T(8,128)(2,1)S(1)} %get-tuple-element.55), channel_id=1, source_target_pairs={{0,3},{1,2},{2,1},{3,0},{4,7},{5,6},{6,5},{7,4},{8,11},{9,10},{10,... | collective-permute-start | bytes 884744 | tf_op jit(solution)/shard_map/ppermute | solution.py:532
  29.8 13.5 %collective-permute-start.4 = (bf16[576,256]{1,0:T(8,128)(2,1)S(1)}, bf16[576,256]{1,0:T(8,128)(2,1)S(1)}, u32[]{:S(2)}, u32[]{:S(2)}) collective-permute-start(bf16[576,256]{1,0:T(8,128)(2,1)S(1)} %get-tuple-element.55), channel_id=1, source_target_pairs={{0,1},{1,0},{2,3},{3,2},{4,5},{5,4},{6,7},{7,6},{8,9},{9,8},{10,11... | collective-permute-start | bytes 884744 | tf_op jit(solution)/shard_map/ppermute | solution.py:532
  43.3 12.7 %collective-permute-start.12 = (bf16[576,256]{1,0:T(8,128)(2,1)S(1)}, bf16[576,256]{1,0:T(8,128)(2,1)S(1)}, u32[]{:S(2)}, u32[]{:S(2)}) collective-permute-start(bf16[576,256]{1,0:T(8,128)(2,1)S(1)} %get-tuple-element.63), channel_id=1, source_target_pairs={{0,3},{1,2},{2,1},{3,0},{4,7},{5,6},{6,5},{7,4},{8,11},{9,10},{10,... | collective-permute-start | bytes 884744 | tf_op jit(solution)/shard_map/ppermute | solution.py:532
  44.6 11.3 %collective-permute-start.10 = (bf16[576,256]{1,0:T(8,128)(2,1)S(1)}, bf16[576,256]{1,0:T(8,128)(2,1)S(1)}, u32[]{:S(2)}, u32[]{:S(2)}) collective-permute-start(bf16[576,256]{1,0:T(8,128)(2,1)S(1)} %get-tuple-element.63), channel_id=1, source_target_pairs={{0,1},{1,0},{2,3},{3,2},{4,5},{5,4},{6,7},{7,6},{8,9},{9,8},{10,11... | collective-permute-start | bytes 884744 | tf_op jit(solution)/shard_map/ppermute | solution.py:532
  44.9 14.3 %collective-permute-start.11 = (bf16[576,256]{1,0:T(8,128)(2,1)S(1)}, bf16[576,256]{1,0:T(8,128)(2,1)S(1)}, u32[]{:S(2)}, u32[]{:S(2)}) collective-permute-start(bf16[576,256]{1,0:T(8,128)(2,1)S(1)} %get-tuple-element.62.refs_4_), channel_id=1, source_target_pairs={{0,2},{1,3},{2,0},{3,1},{4,6},{5,7},{6,4},{7,5},{8,10},{9,11},{10,... | collective-permute-start | bytes 884744 | tf_op jit(solution)/shard_map/ppermute | solution.py:532
  54.4 17.2 %collective-permute-start.13 = (bf16[432,512]{1,0:T(8,128)(2,1)S(1)}, bf16[432,512]{1,0:T(8,128)(2,1)S(1)}, u32[]{:S(2)}, u32[]{:S(2)}) collective-permute-start(bf16[432,512]{1,0:T(8,128)(2,1)S(1)} %get-tuple-element.68.refs_8_.a_ref), channel_id=1, source_target_pairs={{0,2},{1,3},{2,0},{3,1},{4,6},{5,7},{6,4},{7,5},{8,10},{9,11},{10,... | collective-permute-start | bytes 1327112 | tf_op jit(solution)/shard_map/ppermute | solution.py:532
  60.5 11.0 %collective-permute-start.14 = (bf16[144,512]{1,0:T(8,128)(2,1)S(1)}, bf16[144,512]{1,0:T(8,128)(2,1)S(1)}, u32[]{:S(2)}, u32[]{:S(2)}) collective-permute-start(bf16[144,512]{1,0:T(8,128)(2,1)S(1)} %shard_map.110.refs_9_.b_ref), channel_id=1, source_target_pairs={{0,2},{1,3},{2,0},{3,1},{4,6},{5,7},{6,4},{7,5},{8,10},{9,11},{10,... | collective-permute-start | bytes 442376 | tf_op jit(solution)/shard_map/ppermute | solution.py:532
  73.2 13.4 %collective-permute-start.15 = (bf16[288,256]{1,0:T(8,128)(2,1)S(1)}, bf16[288,256]{1,0:T(8,128)(2,1)S(1)}, u32[]{:S(2)}, u32[]{:S(2)}) collective-permute-start(bf16[288,256]{1,0:T(8,128)(2,1)S(1)} %get-tuple-element.72), channel_id=1, source_target_pairs={{0,4},{1,5},{2,6},{3,7},{4,8},{5,9},{6,10},{7,11},{8,12},{9,13},{1... | collective-permute-start | bytes 442376 | tf_op jit(solution)/shard_map/ppermute | solution.py:532
  73.2 13.3 %collective-permute-start.16 = (bf16[288,256]{1,0:T(8,128)(2,1)S(1)}, bf16[288,256]{1,0:T(8,128)(2,1)S(1)}, u32[]{:S(2)}, u32[]{:S(2)}) collective-permute-start(bf16[288,256]{1,0:T(8,128)(2,1)S(1)} %get-tuple-element.73), channel_id=1, source_target_pairs={{0,1},{1,0},{2,3},{3,2},{4,5},{5,4},{6,7},{7,6},{8,9},{9,8},{10,11... | collective-permute-start | bytes 442376 | tf_op jit(solution)/shard_map/ppermute | solution.py:532
  73.3 13.2 %collective-permute-start.17 = (bf16[288,256]{1,0:T(8,128)(2,1)S(1)}, bf16[288,256]{1,0:T(8,128)(2,1)S(1)}, u32[]{:S(2)}, u32[]{:S(2)}) collective-permute-start(bf16[288,256]{1,0:T(8,128)(2,1)S(1)} %get-tuple-element.74), channel_id=1, source_target_pairs={{0,5},{1,4},{2,7},{3,6},{4,9},{5,8},{6,11},{7,10},{8,13},{9,12},{1... | collective-permute-start | bytes 442376 | tf_op jit(solution)/shard_map/ppermute | solution.py:532
  75.1 11.4 %collective-permute-start.18 = (f32[8,256]{1,0:T(8,128)S(1)}, f32[8,256]{1,0:T(8,128)S(1)}, u32[]{:S(2)}, u32[]{:S(2)}) collective-permute-start(f32[8,256]{1,0:T(8,128)S(1)} %shard_map.115), channel_id=1, source_target_pairs={{0,2},{1,3},{2,0},{3,1},{4,6},{5,7},{6,4},{7,5},{8,10},{9,11},{10,... | collective-permute-start | bytes 24584 | tf_op jit(solution)/shard_map/ppermute | solution.py:532
  90.4 3.8 %collective-permute-start.20 = (f32[14,256]{1,0:T(8,128)S(1)}, f32[14,256]{1,0:T(8,128)S(1)}, u32[]{:S(2)}, u32[]{:S(2)}) collective-permute-start(f32[14,256]{1,0:T(8,128)S(1)} %get-tuple-element.92), channel_id=1, source_target_pairs={{0,4},{1,5},{2,6},{3,7},{4,0},{5,1},{6,2},{7,3},{8,12},{9,13},{10,... | collective-permute-start | bytes 43016 | tf_op jit(solution)/shard_map/ppermute | solution.py:538
  91.9 3.2 %collective-permute-start.21 = (f32[14,256]{1,0:T(8,128)S(1)}, f32[14,256]{1,0:T(8,128)S(1)}, u32[]{:S(2)}, u32[]{:S(2)}) collective-permute-start(f32[14,256]{1,0:T(8,128)S(1)} %get-tuple-element.91), channel_id=1, source_target_pairs={{0,5},{1,4},{2,7},{3,6},{4,1},{5,0},{6,3},{7,2},{8,13},{9,12},{10,... | collective-permute-start | bytes 43016 | tf_op jit(solution)/shard_map/ppermute | solution.py:538
  91.9 3.2 %collective-permute-start.19 = (f32[14,256]{1,0:T(8,128)S(1)}, f32[14,256]{1,0:T(8,128)S(1)}, u32[]{:S(2)}, u32[]{:S(2)}) collective-permute-start(f32[14,256]{1,0:T(8,128)S(1)} %get-tuple-element.91), channel_id=1, source_target_pairs={{0,1},{1,0},{2,3},{3,2},{4,5},{5,4},{6,7},{7,6},{8,9},{9,8},{10,11... | collective-permute-start | bytes 43016 | tf_op jit(solution)/shard_map/ppermute | solution.py:532
  95.0 10.1 %copy-start.5 = (f32[14,256]{1,0:T(8,128)}, f32[14,256]{1,0:T(8,128)S(1)}, u32[]{:S(2)}) copy-start(f32[14,256]{1,0:T(8,128)S(1)} %add_add_fusion.refs_0_) | copy-start | bytes 43012
  95.1 8.8 %collective-permute-start.24 = (f32[14,256]{1,0:T(8,128)S(1)}, f32[14,256]{1,0:T(8,128)S(1)}, u32[]{:S(2)}, u32[]{:S(2)}) collective-permute-start(f32[14,256]{1,0:T(8,128)S(1)} %add_add_fusion.refs_0_), channel_id=1, source_target_pairs={{0,24},{1,25},{2,26},{3,27},{4,28},{5,29},{6,30},{7,31},{8,16},{9,... | collective-permute-start | bytes 43016 | tf_op jit(solution)/shard_map/ppermute | solution.py:538
  99.9 4.6 %collective-permute-start.23 = (f32[14,256]{1,0:T(8,128)S(1)}, f32[14,256]{1,0:T(8,128)S(1)}, u32[]{:S(2)}, u32[]{:S(2)}) collective-permute-start(f32[14,256]{1,0:T(8,128)S(1)} %add_add_fusion.refs_0_), channel_id=1, source_target_pairs={{0,16},{1,17},{2,18},{3,19},{4,20},{5,21},{6,22},{7,23},{8,24},{9,... | collective-permute-start | bytes 43016 | tf_op jit(solution)/shard_map/ppermute | solution.py:538
  101.4 3.7 %collective-permute-start.22 = (f32[14,256]{1,0:T(8,128)S(1)}, f32[14,256]{1,0:T(8,128)S(1)}, u32[]{:S(2)}, u32[]{:S(2)}) collective-permute-start(f32[14,256]{1,0:T(8,128)S(1)} %add_add_fusion.refs_0_), channel_id=1, source_target_pairs={{0,8},{1,9},{2,10},{3,11},{4,12},{5,13},{6,14},{7,15},{8,0},{9,1},... | collective-permute-start | bytes 43016 | tf_op jit(solution)/shard_map/ppermute | solution.py:538
  103.8 1.3 %copy-start.6 = (f32[14,256]{1,0:T(8,128)}, f32[14,256]{1,0:T(8,128)S(1)}, u32[]{:S(2)}) copy-start(f32[14,256]{1,0:T(8,128)S(1)} %collective-permute-done.24.refs_3_) | copy-start | bytes 43012
  104.6 0.6 copy-start.7
  105.2 0.6 copy-start.8

commit v4 on v3

--- a/solution.py
+++ b/solution.py
@@ -1,3 +1,5 @@
+import functools
+
 import jax
 import jax.numpy as jnp
 from jax import lax
@@ -14,6 +16,7 @@
 SCALE = HD ** (-0.5)
 NT = (((1,), (1,)), ((), ()))
 TN = (((0,), (0,)), ((), ()))
+SMALL = pl.CostEstimate(flops=1, bytes_accessed=1, transcendentals=0)
 
 
 def spec(n):
@@ -57,7 +60,7 @@
         in_specs=spec(2),
         out_specs=tuple(spec(2)),
         compiler_params=params(24),
-        cost_estimate=pl.CostEstimate(flops=10 * n * d * e, bytes_accessed=4 * n * d * e, transcendentals=0),
+        cost_estimate=SMALL,
     )(w, clips)
 
 
@@ -91,7 +94,7 @@
         in_specs=spec(5),
         out_specs=tuple(spec(2)),
         compiler_params=params(24),
-        cost_estimate=pl.CostEstimate(flops=40 * e * d, bytes_accessed=16 * e * d, transcendentals=0),
+        cost_estimate=SMALL,
     )(*shards, clips)
 
 
@@ -155,7 +158,7 @@
         return carry
 
     lax.fori_loop(0, 3, project, 0)
-    attend(qkv_ref, idk_ref, idq_ref, attn_ref, 0, 3)
+    attend(qkv_ref, idk_ref, idq_ref, attn_ref, 0, 2)
 
 
 def attend(qkv_ref, idk_ref, idq_ref, attn_ref, first, last):
@@ -180,14 +183,14 @@
 
 
 def last_kernel(qkv_ref, idk_ref, idq_ref, attn_ref):
-    attend(qkv_ref, idk_ref, idq_ref, attn_ref, 3, 4)
-
-
-def last_window(qkv, idk, idq):
+    attend(qkv_ref, idk_ref, idq_ref, attn_ref, 2, 4)
+
+
+def last_windows(qkv, idk, idq):
     n, width = qkv.shape[1:]
     return pl.pallas_call(
         last_kernel,
-        out_shape=jax.ShapeDtypeStruct((n // 4, 2 * width), BF),
+        out_shape=jax.ShapeDtypeStruct((n // 2, 2 * width), BF),
         in_specs=spec(3),
         out_specs=spec(1)[0],
         compiler_params=params(16),
@@ -203,7 +206,7 @@
         out_shape=(
             jax.ShapeDtypeStruct((n, d), BF),
             jax.ShapeDtypeStruct((6, n, width), BF),
-            jax.ShapeDtypeStruct((n // 4 * 3, 2 * width), BF),
+            jax.ShapeDtypeStruct((n // 2, 2 * width), BF),
         ),
         in_specs=[pl.BlockSpec(memory_space=pltpu.SMEM)] + spec(8),
         out_specs=tuple(spec(3)),
@@ -239,55 +242,86 @@
         in_specs=spec(3),
         out_specs=tuple(spec(2)),
         compiler_params=params(16),
-        cost_estimate=pl.CostEstimate(flops=1, bytes_accessed=1, transcendentals=0),
+        cost_estimate=SMALL,
     )(normed, *attn)
 
 
-def output_kernel(t_ref, *refs):
-    pieces, targets = refs[:4], refs[4:8]
-    a0, a1, b0, b1, wc_ref, idk_ref = refs[8:14]
-    mixed, err_ref, y_ref = refs[14:18], refs[18], refs[19]
+def output_kernel(group, t_ref, *refs):
+    pieces, targets = refs[:4], (refs[4], refs[6].at[0], refs[5], refs[6].at[1])
+    own_ref, other_ref, wc_ref, idk_ref = refs[7:11]
+    before, refs = refs[11 : 11 + 4 * group], refs[11 + 4 * group :]
+    mixed, err_ref, y_ref = refs[:4], refs[4], refs[5]
     t = t_ref[0]
     n, width = pieces[0].shape
     cells = n // 4
     half = cells // 2
-    e = a0.shape[1]
-    valid = idk_ref[...] >= 0
+    e = own_ref.shape[1]
+    for old, new in zip(before, mixed):
+        new[: group * cells, :] = old[...]
     for k in range(4):
         x_ref, want_ref = pieces[k], targets[k]
         cols = pl.ds(pl.multiple_of((t ^ k) * width, width), width)
-        own = jnp.concatenate([a0[...], a1[...]], axis=0)
-        other = jnp.concatenate([b0[...], b1[...]], axis=0)
-        y_ref[...] = jnp.dot(own, wc_ref[:e, cols], preferred_element_type=F32) + jnp.dot(
-            other, wc_ref[e:, cols], preferred_element_type=F32
+        y_ref[...] = jnp.dot(own_ref[...], wc_ref[:e, cols], preferred_element_type=F32) + jnp.dot(
+            other_ref[...], wc_ref[e:, cols], preferred_element_type=F32
         )
-        for p in range(2):
-            ys = []
-            for i in range(2):
-                rows = slice(cells * (2 * p + i), cells * (2 * p + i + 1))
-                y = x_ref[rows, :].astype(F32) + y_ref[rows, :]
-                ys.append(y)
-                err = y - want_ref[rows, :].astype(F32)
-                err_ref[rows, cols] = jnp.where(valid[rows], err, 0.0).astype(BF)
-            if k < 2:
-                at = slice(cells * p, cells * (p + 1))
-                for s in range(2):
-                    part = slice(half * s, half * (s + 1))
-                    mixed[2 * s + k][at, :] = jnp.concatenate([y[part] for y in ys], axis=0).astype(BF)
-
-
-def output(t, pieces, targets, own, other, wc, idk):
+        ys = []
+        for i in range(2):
+            at = slice(cells * i, cells * (i + 1))
+            rows = slice(cells * (2 * group + i), cells * (2 * group + i + 1))
+            y = x_ref[rows, :].astype(F32) + y_ref[at, :]
+            ys.append(y)
+            err = y - want_ref[rows, :].astype(F32)
+            valid = idk_ref[rows, :] >= 0
+            err_ref[at, cols] = jnp.where(valid, err, 0.0).astype(BF)
+        if k < 2:
+            at = slice(cells * group, cells * (group + 1))
+            for s in range(2):
+                part = slice(half * s, half * (s + 1))
+                mixed[2 * s + k][at, :] = jnp.concatenate([y[part] for y in ys], axis=0).astype(BF)
+
+
+def output(t, pieces, targets, own, other, wc, idk, before=()):
     n, width = pieces[0].shape
-    piece = jax.ShapeDtypeStruct((n // 2, width), BF)
-    return pl.pallas_call(
-        output_kernel,
-        out_shape=(piece, piece, piece, piece, jax.ShapeDtypeStruct((n, 4 * width), BF)),
-        in_specs=[pl.BlockSpec(memory_space=pltpu.SMEM)] + spec(14),
+    group = 1 if before else 0
+    piece = jax.ShapeDtypeStruct((n // 4 * (1 + group), width), BF)
+    return pl.pallas_call(
+        functools.partial(output_kernel, group),
+        out_shape=(piece, piece, piece, piece, jax.ShapeDtypeStruct((n // 2, 4 * width), BF)),
+        in_specs=[pl.BlockSpec(memory_space=pltpu.SMEM)] + spec(11 + len(before)),
         out_specs=tuple(spec(5)),
-        scratch_shapes=[pltpu.VMEM((n, width), F32)],
+        scratch_shapes=[pltpu.VMEM((n // 2, width), F32)],
         compiler_params=params(20),
-        cost_estimate=pl.CostEstimate(flops=2 * 10**9, bytes_accessed=8 * 10**6, transcendentals=0),
-    )(t, *pieces, *targets, *own, *other, wc, idk)
+        cost_estimate=pl.CostEstimate(flops=10**9, bytes_accessed=4 * 10**6, transcendentals=0),
+    )(t, *pieces, *targets, own, other, wc, idk, *before)
+
+
+def probs_kernel(group, qkv_ref, idk_ref, idq_ref, p_ref):
+    cells = idk_ref.shape[0] // 4
+    mask_a, mask_b = head_masks()
+
+    def window(i, carry):
+        w = 2 * group + i
+        rows = pl.ds(pl.multiple_of(w * cells, 16), cells)
+        allowed = allowed_t(idk_ref, idq_ref, w, cells)
+        for hp in range(4):
+            g, lanes = hp // 2, slice(128 * (hp % 2), 128 * (hp % 2) + 128)
+            q2 = stacked(qkv_ref[3 * g, rows, lanes], mask_a, mask_b)
+            p_ref[4 * i + hp] = probs_t(qkv_ref[3 * g + 1, rows, lanes], q2, allowed)
+        return carry
+
+    lax.fori_loop(0, 2, window, 0)
+
+
+def probs_of(group, qkv, idk, idq):
+    n, width = qkv.shape[1:]
+    return pl.pallas_call(
+        functools.partial(probs_kernel, group),
+        out_shape=jax.ShapeDtypeStruct((8, n // 4, n // 2), F32),
+        in_specs=spec(3),
+        out_specs=spec(1)[0],
+        compiler_params=params(16),
+        cost_estimate=SMALL,
+    )(qkv, idk, idq)
 
 
 def masked_sums(grad, w, bounds):
@@ -296,10 +330,11 @@
     return g_hi, g_lo
 
 
-def proj_sums_kernel(err_ref, attn_t, po_ref, pp_ref, pb_ref, proj_ref):
+def proj_sums_kernel(e0_ref, e1_ref, attn_t, po_ref, pp_ref, pb_ref, proj_ref):
     def proj_part(i, carry):
         cols = pl.ds(pl.multiple_of(i * 256, 256), 256)
-        grad = jnp.dot(attn_t[...], err_ref[:, cols], preferred_element_type=F32)
+        err = jnp.concatenate([e0_ref[:, cols], e1_ref[:, cols]], axis=0)
+        grad = jnp.dot(attn_t[...], err, preferred_element_type=F32)
         n = po_ref.shape[0]
         b = pb_ref[:, cols]
         h0, l0 = masked_sums(grad[:n], po_ref[:, cols].astype(F32), b)
@@ -311,67 +346,68 @@
     lax.fori_loop(0, 4, proj_part, 0)
 
 
-def proj_sums(err, attn_t, po, pp, pb):
+def proj_sums(errs, attn_t, po, pp, pb):
     return pl.pallas_call(
         proj_sums_kernel,
         out_shape=jax.ShapeDtypeStruct((8, 256), F32),
-        in_specs=spec(5),
+        in_specs=spec(6),
         out_specs=spec(1)[0],
         compiler_params=params(16),
         cost_estimate=pl.CostEstimate(flops=10**9, bytes_accessed=3 * 10**6, transcendentals=0),
-    )(err, attn_t, po, pp, pb)
-
-
-def backward_kernel(err_ref, wc_ref, qkv_ref, idk_ref, idq_ref, g_ref, d_ref):
+    )(*errs, attn_t, po, pp, pb)
+
+
+def backward_kernel(group, err_ref, wc_ref, qkv_ref, p_ref, g_ref, d_ref):
     e = d_ref.shape[1]
-    cells = idk_ref.shape[0] // 4
+    cells = d_ref.shape[0] // 2
     d_ref[...] = lax.dot_general(err_ref[...], wc_ref[:e], NT, preferred_element_type=F32).astype(BF)
     mask_a, mask_b = head_masks()
 
-    def window(w, carry):
-        rows = pl.ds(pl.multiple_of(w * cells, 16), cells)
-        allowed = allowed_t(idk_ref, idq_ref, w, cells)
+    def window(i, carry):
+        rows = pl.ds(pl.multiple_of((2 * group + i) * cells, 16), cells)
+        at = pl.ds(pl.multiple_of(i * cells, 16), cells)
         for hp in range(4):
             g, lanes = hp // 2, slice(128 * (hp % 2), 128 * (hp % 2) + 128)
             q2 = stacked(qkv_ref[3 * g, rows, lanes], mask_a, mask_b)
             k = qkv_ref[3 * g + 1, rows, lanes]
             v = qkv_ref[3 * g + 2, rows, lanes]
-            pt = probs_t(k, q2, allowed)
-            d2 = stacked(d_ref[rows, 128 * hp : 128 * hp + 128], mask_a, mask_b)
-            g_ref[3 * g + 2, rows, lanes] = jnp.dot(
+            pt = p_ref[4 * i + hp]
+            d2 = stacked(d_ref[at, 128 * hp : 128 * hp + 128], mask_a, mask_b)
+            g_ref[3 * g + 2, at, lanes] = jnp.dot(
                 pt.astype(BF), d2, preferred_element_type=F32
             ).astype(BF)
             dpt = lax.dot_general(v, d2, NT, preferred_element_type=F32)
             gst = (pt * (dpt - jnp.sum(pt * dpt, axis=0, keepdims=True))).astype(BF)
-            g_ref[3 * g + 1, rows, lanes] = (
+            g_ref[3 * g + 1, at, lanes] = (
                 jnp.dot(gst, q2, preferred_element_type=F32) * SCALE
             ).astype(BF)
             gqt = lax.dot_general(k, gst, TN, preferred_element_type=F32) * SCALE
-            g_ref[3 * g, rows, lanes] = merge_heads(gqt).astype(BF)
-        return carry
-
-    lax.fori_loop(0, 4, window, 0)
-
-
-def backward(err, wc, qkv, idk, idq):
+            g_ref[3 * g, at, lanes] = merge_heads(gqt).astype(BF)
+        return carry
+
+    lax.fori_loop(0, 2, window, 0)
+
+
+def backward(group, err, wc, qkv, probs):
     n, width = qkv.shape[1:]
     return pl.pallas_call(
-        backward_kernel,
-        out_shape=jax.ShapeDtypeStruct((6, n, width), BF),
-        in_specs=spec(5),
+        functools.partial(backward_kernel, group),
+        out_shape=jax.ShapeDtypeStruct((6, n // 2, width), BF),
+        in_specs=spec(4),
         out_specs=spec(1)[0],
-        scratch_shapes=[pltpu.VMEM((n, 2 * width), BF)],
+        scratch_shapes=[pltpu.VMEM((n // 2, 2 * width), BF)],
         compiler_params=params(20),
-        cost_estimate=pl.CostEstimate(flops=8 * 10**9, bytes_accessed=10 * 10**6, transcendentals=10**6),
-    )(err, wc, qkv, idk, idq)
-
-
-def qkv_sums_kernel(g_ref, normed_t, wo_ref, wp_ref, bo_ref, bp_ref, own_ref, peer_ref):
+        cost_estimate=pl.CostEstimate(flops=4 * 10**9, bytes_accessed=5 * 10**6, transcendentals=10**6),
+    )(err, wc, qkv, probs)
+
+
+def qkv_sums_kernel(g0_ref, g1_ref, normed_t, wo_ref, wp_ref, bo_ref, bp_ref, own_ref, peer_ref):
     def qkv_part(i, carry):
         for g, (w_ref, b_ref, to_ref) in enumerate(
             ((wo_ref, bo_ref, own_ref), (wp_ref, bp_ref, peer_ref))
         ):
-            grad = jnp.dot(normed_t[...], g_ref[3 * g + i], preferred_element_type=F32)
+            cells = jnp.concatenate([g0_ref[3 * g + i], g1_ref[3 * g + i]], axis=0)
+            grad = jnp.dot(normed_t[...], cells, preferred_element_type=F32)
             hi, lo = masked_sums(grad, w_ref[i].astype(F32), b_ref[i])
             to_ref[pl.ds(2 * i, 1), :] = hi
             to_ref[pl.ds(2 * i + 1, 1), :] = lo
@@ -381,51 +417,60 @@
 
 
 def qkv_sums(g, normed_t, wo, wp, bo, bp):
-    width = g.shape[2]
+    width = g[0].shape[2]
     return pl.pallas_call(
         qkv_sums_kernel,
         out_shape=(jax.ShapeDtypeStruct((6, width), F32),) * 2,
-        in_specs=spec(6),
+        in_specs=spec(7),
         out_specs=tuple(spec(2)),
         compiler_params=params(20),
         cost_estimate=pl.CostEstimate(flops=4 * 10**9, bytes_accessed=8 * 10**6, transcendentals=0),
-    )(g, normed_t, wo, wp, bo, bp)
-
-
-def split_kernel(s_ref, up_ref, low_ref, mine_ref, peer_ref):
+    )(*g, normed_t, wo, wp, bo, bp)
+
+
+def split_kernel(s_ref, *refs):
     offset, core = s_ref[0], s_ref[1]
-    rows, lon, lev, width = up_ref.shape
+    pairs = (len(refs) - 1) // 3
+    rows, lon, lev, width = refs[1].shape
     many = (rows + WLAT) // 2
     half = lon * lev
     cells = 2 * WLAT * half
-    for rel, out_ref in ((0, mine_ref), (1, peer_ref)):
+    for rel in range(2):
         base = many * (core ^ rel) - offset
 
         def body(w, carry):
-            parts = []
-            for ref in (up_ref, low_ref):
-                for j in range(WLAT):
-                    r = base + WLAT * w + j
-                    v = ref[jnp.clip(r, 0, rows - 1)].astype(F32).reshape(half, width)
-                    parts.append(jnp.where((r >= 0) & (r < rows), v, 0.0))
             at = pl.ds(pl.multiple_of(w * cells, 16), cells)
-            out_ref[at, :] = jnp.concatenate(parts, axis=0).astype(BF)
+            for i in range(pairs):
+                up_ref, low_ref = refs[2 * i : 2 * i + 2]
+                parts = []
+                for ref, part in ((up_ref, slice(up_ref.shape[1] - lon, up_ref.shape[1])), (low_ref, slice(0, lon))):
+                    for j in range(WLAT):
+                        r = base + WLAT * w + j
+                        v = ref[jnp.clip(r, 0, rows - 1), part].astype(F32).reshape(half, width)
+                        parts.append(jnp.where((r >= 0) & (r < rows), v, 0.0))
+                block = jnp.concatenate(parts, axis=0).astype(BF)
+                if rel:
+                    refs[-1][i, at, :] = block
+                else:
+                    refs[2 * pairs + i][at, :] = block
             return carry
 
         lax.fori_loop(0, many // WLAT, body, 0)
 
 
-def split(place, upper, lower):
-    rows, lon, lev, width = upper.shape
-    piece = jax.ShapeDtypeStruct(((rows + WLAT) * lon * lev, width), BF)
+def split(place, *halves):
+    rows, lon, lev, width = halves[1].shape
+    pairs = len(halves) // 2
+    n = (rows + WLAT) * lon * lev
     return pl.pallas_call(
         split_kernel,
-        out_shape=(piece, piece),
-        in_specs=[pl.BlockSpec(memory_space=pltpu.SMEM)] + spec(2),
-        out_specs=tuple(spec(2)),
+        out_shape=(jax.ShapeDtypeStruct((n, width), BF),) * pairs
+        + (jax.ShapeDtypeStruct((pairs, n, width), BF),),
+        in_specs=[pl.BlockSpec(memory_space=pltpu.SMEM)] + spec(2 * pairs),
+        out_specs=tuple(spec(pairs + 1)),
         compiler_params=params(16),
-        cost_estimate=pl.CostEstimate(flops=10**6, bytes_accessed=2 * 10**6, transcendentals=0),
-    )(place, upper, lower)
+        cost_estimate=SMALL,
+    )(place, *halves)
 
 
 def cell_at(c, window):
@@ -482,7 +527,7 @@
         in_specs=[pl.BlockSpec(memory_space=pltpu.SMEM)] + spec(1),
         out_specs=tuple(spec(2)),
         compiler_params=params(16),
-        cost_estimate=pl.CostEstimate(flops=10**6, bytes_accessed=10**6, transcendentals=0),
+        cost_estimate=SMALL,
     )(place, ids)
 
 
@@ -519,7 +564,7 @@
         out_specs=spec(1)[0],
         scratch_shapes=[pltpu.VMEM((rows + WLAT, lon * lev, width), F32)],
         compiler_params=params(16),
-        cost_estimate=pl.CostEstimate(flops=10**6, bytes_accessed=2 * 10**6, transcendentals=0),
+        cost_estimate=SMALL,
     )(place, *parts)
     return jnp.transpose(out, (0, 2, 1, 3))
 
@@ -589,9 +634,8 @@
     t_arr = jnp.reshape(t, (1,)).astype(jnp.int32)
     place = jnp.stack([shift_offset[0], t % 2, sector]).astype(jnp.int32)
 
-    def halves(block):
-        block = jnp.transpose(block, (0, 2, 1, 3))
-        return block[:, half:], block[:, :half]
+    f_raw, t_raw = (jnp.transpose(block, (0, 2, 1, 3)) for block in (features, target))
+    f_low = send(f_raw[:, :half], -1, 0)
 
     w3 = jnp.transpose(w_qkv, (1, 0, 2))
     c3 = jnp.transpose(qkv_clip, (1, 0, 2))
@@ -602,39 +646,42 @@
     wc_peer, b_peer = clip_qkv(w3_peer, c3_peer)
     idk, idq = window_ids(place, region_ids, WLAT * lev * lon)
 
-    f_up, f_low = halves(features)
-    t_up, t_low = halves(target)
-    f_low = send(f_low, -1, 0)
-    f_low, t_up, t_low, wc_own, wc_peer, idk, idq = lax.optimization_barrier(
-        (f_low, t_up, t_low, wc_own, wc_peer, idk, idq)
+    f_low, w1, wc_own, wc_peer, idk, idq = lax.optimization_barrier(
+        (f_low, w1, wc_own, wc_peer, idk, idq)
     )
-    t_low = send(t_low, -1, 0)
-    mine, away = split(place, f_up, f_low)
+    mine, away = split(place, f_raw, f_low)
+    away = away.reshape(mine.shape)
     pieces = [mine, send(away, 0, 1), send(mine, 0, 2), send(away, 0, 3)]
-
-    t_mine, t_away = split(place, t_up, t_low)
-    w_3 = send(after(w2, t_mine), 0, 1)
+    w_3 = send(after(w2, mine), 0, 1)
     pc, pb = clip_proj([w_proj, w1, w2, w_3], proj_clip)
-    t_mine, t_away, *pieces = lax.optimization_barrier((t_mine, t_away, *pieces, pc))[:-1]
-    targets = [t_mine, send(t_away, 0, 1), send(t_mine, 0, 2), send(t_away, 0, 3)]
-
-    normed, qkv, attn_a = forward(t_arr, pieces, wc_own, wc_peer, idk, idq)
-    other_a = send(attn_a, 0, 2)
-    attn_b = last_window(after(qkv, *targets), idk, idq)
-    other_b = send(attn_b, 0, 2)
-    normed_t, attn_t = turn(normed, (attn_a, attn_b))
-
-    m00, m01, m10, m11, err = output(
-        t_arr, pieces, targets, (attn_a, attn_b), (other_a, other_b), pc, idk
-    )
+
+    t_low = send(after(t_raw, f_low)[:, :half], -1, 0)
+    t_up, t_low, *pieces = lax.optimization_barrier((t_raw[:, half:], t_low, *pieces, pc))[:-1]
+    t_up_y, t_low_y = send(t_up, 0, 2), send(t_low, 0, 2)
+
+    normed, qkv, attn_0 = forward(t_arr, pieces, wc_own, wc_peer, idk, idq)
+    other_0 = send(attn_0, 0, 2)
+    probs_0 = probs_of(0, qkv, idk, idq)
+    t_up_y, t_low_y = lax.optimization_barrier((t_up_y, t_low_y, probs_0))[:2]
+    t_0, t_2, t_away = split(place, t_raw, t_low, t_up_y, t_low_y)
+    targets = (t_0, t_2, send(t_away, 0, 1))
+    attn_1 = last_windows(after(qkv, probs_0, t_away), idk, idq)
+    other_1 = send(attn_1, 0, 2)
+    normed_t, attn_t = turn(normed, (attn_0, attn_1))
+    probs = (probs_0, probs_of(1, after(qkv, attn_1), idk, idq))
+
+    *mixed, err_0 = output(t_arr, pieces, targets, attn_0, other_0, pc, idk)
+    grads_0 = backward(0, err_0, pc, qkv, probs[0])
+    other_1 = after(other_1, grads_0)
+    m00, m01, m10, m11, err_1 = output(t_arr, pieces, targets, attn_1, other_1, pc, idk, mixed)
     m01 = send(m01, 0, 1)
     m10 = send(m10, 1, 0)
     m11 = send(m11, 1, 1)
-
-    proj = proj_sums(err, attn_t, w_proj, w1, pb)
+    proj = proj_sums((err_0, err_1), attn_t, w_proj, w1, pb)
     proj_y = send(proj, 0, 2)
-    grads = backward(err, pc, qkv, idk, idq)
-    grads = after(grads, m01, m10, m11, proj_y)
+    grads_1 = backward(1, err_1, pc, qkv, probs[1])
+    grads_1 = after(grads_1, m01, m10, m11, proj_y)
+    grads = (grads_0, grads_1)
     own, peer = qkv_sums(grads, normed_t, w3, w3_peer, b_own, b_peer)
     proj = proj + proj_y
     own, peer = jnp.concatenate([own, proj], axis=0), jnp.concatenate([peer, proj], axis=0)

time: 107 us -> 91.7 us (0.86)
  waiting for transfers between devices: 31.6 us -> 18.2 us
  Pallas kernels: 38 us -> 35.8 us
    ppermute x20, waiting for transfers between devices: 27.9 us -> 16.3 us  [send(): return lax.ppermute(block, ('lat', 'tp'), route)]
    unnamed x18 -> x24, local copies, waits for them, and re-layouts: 0.66 us -> 3.33 us
    slice x2 -> x3, local copies, waits for them, and re-layouts: 3.56 us -> 1.48 us  [the longest x1 1.13 us: local(): f_low = send(f_raw[:, :half], -1, 0)]
    ppermute x5, waiting for transfers between devices: 3.68 us -> 1.89 us  [swap(): return lax.ppermute(block, ('lat', 'tp'), route)]
    ppermute x5, starting transfers between devices: 8.25 us -> 6.84 us  [swap(): return lax.ppermute(block, ('lat', 'tp'), route)]
    pallas_call x1, Pallas kernels: 8.94 us -> 7.61 us  [forward(): pl.pallas_call(forward_kernel, out_shape=(jax.ShapeDtypeStruct((n, d), BF...]
    pallas_call x5 -> x9, Pallas kernels: 15.1 us -> 15.3 us  [the longest x2 6.4 us: backward(): pl.pallas_call(functools.partial(backward_kernel, group), out_shape=jax.S...]
  transfers between devices with their start and end apart: 25 -> 25, of which waited for: 9 -> 12; matrix products, arithmetic and copies ran while one was open for 3% -> 2% of each run, Pallas kernels for 29% -> 31%
where the time goes in v4:
time: 91.7 us; the launch traced here: 91.4 us
  Pallas kernels  35.8 us (39%)
  starting transfers between devices  31 us (34%)
  waiting for transfers between devices  18.2 us (20%)
  local copies, waits for them, and re-layouts  4.81 us (5%)
  between operations  1.59 us (2%)
    ppermute x20, starting transfers between devices, send(): return lax.ppermute(block, ('lat', 'tp'), route)  24.1 us
    ppermute x20, waiting for transfers between devices, send(): return lax.ppermute(block, ('lat', 'tp'), route)  16.3 us
    pallas_call x1, Pallas kernels, forward(): pl.pallas_call(forward_kernel, out_shape=(jax.ShapeDtypeStruct((n, d), BF...  7.61 us
    ppermute x5, starting transfers between devices, swap(): return lax.ppermute(block, ('lat', 'tp'), route)  6.84 us
    pallas_call x2, Pallas kernels, backward(): pl.pallas_call(functools.partial(backward_kernel, group), out_shape=jax.S...  6.4 us
    pallas_call x1, Pallas kernels, qkv_sums(): pl.pallas_call(qkv_sums_kernel, out_shape=(jax.ShapeDtypeStruct((6, width...  3.83 us
    unnamed x24, local copies, waits for them, and re-layouts  3.33 us
    pallas_call x1, Pallas kernels, last_windows(): pl.pallas_call(last_kernel, out_shape=jax.ShapeDtypeStruct((n // 2, 2 * w...  2.66 us
  transfers between devices with their start and end apart: 25, of which 12 were waited for; matrix products, arithmetic and copies ran while one was open for 2% of the time, Pallas kernels for 31%

profile of v4, /device:TPU:0, one launch (start us, length us, event | category | flops | bytes accessed | tf_op | source)
XLA Modules:
  0.0 91.4 jit_solution(17271458415245502416)
XLA Ops:
  0.6 0.5 collective-permute-start.2
  1.2 0.1 collective-permute-start.1
  1.2 2.9 %collective-permute-start.8 = (bf16[256,1024]{1,0:T(8,128)(2,1)}, bf16[256,1024]{1,0:T(8,128)(2,1)S(1)}, u32[]{:S(2)}, u32[]{:S(2)}) collective-permute-start(bf16[256,1024]{1,0:T(8,128)(2,1)} %po_ref.1), channel_id=1, source_target_pairs={{0,2},{1,3},{2,0},{3,1},{4,6},{5,7},{6,4},{7,5},{8,10},{9,11},{10,... | collective-permute-start | bytes 1572872 | tf_op jit(solution)/shard_map/ppermute | solution.py:577
  4.2 1.1 %slice.13 = bf16[42,6,2,256]{3,2,1,0:T(2,128)(2,1)S(1)} slice(bf16[42,12,2,256]{3,2,1,0:T(2,128)(2,1)} %bitcast.16), slice={[0:42], [0:6], [0:2], [0:256]} | slice | bytes 516096 | tf_op jit(solution)/shard_map/slice | solution.py:638
  5.3 4.6 %collective-permute-start = (bf16[42,6,2,256]{3,2,1,0:T(2,128)(2,1)S(1)}, bf16[42,6,2,256]{3,2,1,0:T(2,128)(2,1)S(1)}, u32[]{:S(2)}, u32[]{:S(2)}) collective-permute-start(bf16[42,6,2,256]{3,2,1,0:T(2,128)(2,1)S(1)} %slice.13), channel_id=1, source_target_pairs={{0,28},{1,29},{2,30},{3,31},{4,0},{5,1},{6,2},{7,3},{8,4},{9,5},{1... | collective-permute-start | bytes 774152 | tf_op jit(solution)/shard_map/ppermute | solution.py:577
  10.6 0.1 pad_add_fusion.s_ref
  10.6 1.4 %copy-done.1 = bf16[1024,3,256]{2,0,1:T(8,128)(2,1)S(1)} copy-done((bf16[1024,3,256]{2,0,1:T(8,128)(2,1)S(1)}, bf16[1024,3,256]{2,0,1:T(8,128)(2,1)}, u32[]{:S(2)}) %copy-start.1) | copy-done | bytes 1572888
  12.0 0.7 copy-done.7
  12.7 0.7 shard_map.103
  13.4 0.0 copy-start
  13.5 1.0 %shard_map.105 = (s32[576,1]{1,0:T(8,128)S(1)}, s32[4,1,288]{2,1,0:T(1,128)S(1)}) custom-call(s32[3]{0:T(128)S(1)} %pad_add_fusion.s_ref, s32[42,2,96]{2,1,0:T(2,128)S(1)} %copy-done.5), custom_call_target="tpu_custom_call" | custom-call | flops 1 | bytes 1 | tf_op jit(solution)/shard_map/pallas_call | solution.py:521
  14.5 0.0 copy-start.4
  14.5 0.7 shard_map.104
  15.2 0.1 collective-permute-done.refs_1_
  15.3 1.0 %shard_map.106 = (bf16[576,256]{1,0:T(8,128)(2,1)S(1)}, bf16[1,576,256]{2,1,0:T(8,128)(2,1)S(1)}) custom-call(s32[3]{0:T(128)S(1)} %pad_add_fusion.s_ref, bf16[42,12,2,256]{3,2,1,0:T(2,128)(2,1)S(1)} %bitcast.17, bf16[42,6,2,256]{3,2,1,0:T(2,128)(2,1)S(1)} %collective-permute-done.refs_1_), custom_call_target="tpu_custom_call" | custom-call | flops 1 | bytes 1 | tf_op jit(solution)/shard_map/pallas_call | solution.py:465
  16.3 0.2 collective-permute-done.8.w2
  16.6 0.3 collective-permute-start.9
  16.8 1.6 %collective-permute-start.7 = (bf16[576,256]{1,0:T(8,128)(2,1)S(1)}, bf16[576,256]{1,0:T(8,128)(2,1)S(1)}, u32[]{:S(2)}, u32[]{:S(2)}) collective-permute-start(bf16[576,256]{1,0:T(8,128)(2,1)S(1)} %bitcast.20), channel_id=1, source_target_pairs={{0,3},{1,2},{2,1},{3,0},{4,7},{5,6},{6,5},{7,4},{8,11},{9,10},{10,... | collective-permute-start | bytes 884744 | tf_op jit(solution)/shard_map/ppermute | solution.py:577
  18.4 0.5 collective-permute-start.6
  19.0 0.2 slice.11
  19.1 4.9 %collective-permute-start.4 = (bf16[42,6,2,256]{3,2,1,0:T(2,128)(2,1)S(1)}, bf16[42,6,2,256]{3,2,1,0:T(2,128)(2,1)S(1)}, u32[]{:S(2)}, u32[]{:S(2)}) collective-permute-start(bf16[42,6,2,256]{3,2,1,0:T(2,128)(2,1)S(1)} %slice.11), channel_id=1, source_target_pairs={{0,28},{1,29},{2,30},{3,31},{4,0},{5,1},{6,2},{7,3},{8,4},{9,5},{1... | collective-permute-start | bytes 774152 | tf_op jit(solution)/shard_map/ppermute | solution.py:577
  24.0 0.2 slice.12
  24.2 0.9 %shard_map.107 = (bf16[1024,1024]{1,0:T(8,128)(2,1)S(1)}, f32[8,1024]{1,0:T(8,128)S(1)}) custom-call(bf16[256,1024]{1,0:T(8,128)(2,1)S(1)} %copy-done.4, bf16[256,1024]{1,0:T(8,128)(2,1)S(1)} %collective-permute-done.1.w1.pp_ref, bf16[256,1024]{1,0:T(8,128)(2,1)S(1)} %collective-permute-done.8.w2, bf16[256,1024]{1,0:T(8,128)(2,1)S(1)} %collective-permute-done.9.w3, ...), custom_call_target="tpu_custom_call" | custom-call | flops 1 | bytes 1 | tf_op jit(solution)/shard_map/pallas_call | solution.py:88
  25.2 4.7 %collective-permute-done.4.refs_1_ = bf16[42,6,2,256]{3,2,1,0:T(2,128)(2,1)S(1)} collective-permute-done((bf16[42,6,2,256]{3,2,1,0:T(2,128)(2,1)S(1)}, bf16[42,6,2,256]{3,2,1,0:T(2,128)(2,1)S(1)}, u32[]{:S(2)}, u32[]{:S(2)}) %collective-permute-start.4) | collective-permute-done | bytes 258080 | tf_op jit(solution)/shard_map/ppermute | solution.py:577
  29.8 2.6 %collective-permute-done.6.refs_2_ = bf16[576,256]{1,0:T(8,128)(2,1)S(1)} collective-permute-done((bf16[576,256]{1,0:T(8,128)(2,1)S(1)}, bf16[576,256]{1,0:T(8,128)(2,1)S(1)}, u32[]{:S(2)}, u32[]{:S(2)}) %collective-permute-start.6) | collective-permute-done | bytes 294944 | tf_op jit(solution)/shard_map/ppermute | solution.py:577
  32.4 1.5 %collective-permute-start.10 = (bf16[42,6,2,256]{3,2,1,0:T(2,128)(2,1)S(1)}, bf16[42,6,2,256]{3,2,1,0:T(2,128)(2,1)S(1)}, u32[]{:S(2)}, u32[]{:S(2)}) collective-permute-start(bf16[42,6,2,256]{3,2,1,0:T(2,128)(2,1)S(1)} %slice.12), channel_id=1, source_target_pairs={{0,2},{1,3},{2,0},{3,1},{4,6},{5,7},{6,4},{7,5},{8,10},{9,11},{10,... | collective-permute-start | bytes 774152 | tf_op jit(solution)/shard_map/ppermute | solution.py:577
  33.9 0.5 collective-permute-start.11
  34.5 7.6 %shard_map.108 = (bf16[576,1024]{1,0:T(8,128)(2,1)S(1)}, bf16[6,576,256]{2,1,0:T(8,128)(2,1)S(1)}, bf16[288,512]{1,0:T(8,128)(2,1)S(1)}) custom-call(s32[1]{0:T(128)} %bitcast.2.t_ref, bf16[576,256]{1,0:T(8,128)(2,1)S(1)} %get-tuple-element.66.refs_0_, bf16[576,256]{1,0:T(8,128)(2,1)S(1)} %collective-permute-done.5.refs_1_, ...), custom_call_target="tpu_custom_call" | custom-call | flops 8000000000 | bytes 10000000 | tf_op jit(solution)/shard_map/pallas_call | solution.py:204
  42.1 1.0 %shard_map.109.p_ref = f32[8,144,288]{2,1,0:T(8,128)S(1)} custom-call(bf16[6,576,256]{2,1,0:T(8,128)(2,1)S(1)} %get-tuple-element.95.qkv_ref, s32[576,1]{1,0:T(8,128)S(1)} %get-tuple-element.74.refs_6_.idk_ref.refs_10_, s32[4,1,288]{2,1,0:T(1,128)S(1)} %get-tuple-element.75.refs_7_.idq_ref), custom_call_target="tpu_custom_call" | custom-call | flops 1 | bytes 1 | tf_op jit(solution)/shard_map/pallas_call | solution.py:317
  43.1 2.7 %collective-permute-done.11.refs_3_ = bf16[42,6,2,256]{3,2,1,0:T(2,128)(2,1)S(1)} collective-permute-done((bf16[42,6,2,256]{3,2,1,0:T(2,128)(2,1)S(1)}, bf16[42,6,2,256]{3,2,1,0:T(2,128)(2,1)S(1)}, u32[]{:S(2)}, u32[]{:S(2)}) %collective-permute-start.11) | collective-permute-done | bytes 258080 | tf_op jit(solution)/shard_map/ppermute | solution.py:577
  45.9 1.3 %shard_map.110 = (bf16[576,256]{1,0:T(8,128)(2,1)S(1)}, bf16[576,256]{1,0:T(8,128)(2,1)S(1)}, bf16[2,576,256]{2,1,0:T(8,128)(2,1)S(1)}) custom-call(s32[3]{0:T(128)S(1)} %pad_add_fusion.s_ref, bf16[42,12,2,256]{3,2,1,0:T(2,128)(2,1)S(1)} %bitcast.12, bf16[42,6,2,256]{3,2,1,0:T(2,128)(2,1)S(1)} %collective-permute-done.4.refs_1_, ...), custom_call_target="tpu_custom_call" | custom-call | flops 1 | bytes 1 | tf_op jit(solution)/shard_map/pallas_call | solution.py:465
  47.1 0.1 collective-permute-start.12
  47.2 1.3 %collective-permute-start.14 = (bf16[288,512]{1,0:T(8,128)(2,1)S(1)}, bf16[288,512]{1,0:T(8,128)(2,1)S(1)}, u32[]{:S(2)}, u32[]{:S(2)}) collective-permute-start(bf16[288,512]{1,0:T(8,128)(2,1)S(1)} %get-tuple-element.83.refs_7_.a_ref), channel_id=1, source_target_pairs={{0,2},{1,3},{2,0},{3,1},{4,6},{5,7},{6,4},{7,5},{8,10},{9,11},{10,... | collective-permute-start | bytes 884744 | tf_op jit(solution)/shard_map/ppermute | solution.py:577
  48.5 2.7 %shard_map.111.refs_7_.b_ref = bf16[288,512]{1,0:T(8,128)(2,1)S(1)} custom-call(bf16[6,576,256]{2,1,0:T(8,128)(2,1)S(1)} %get-tuple-element.95.qkv_ref, s32[576,1]{1,0:T(8,128)S(1)} %get-tuple-element.74.refs_6_.idk_ref.refs_10_, s32[4,1,288]{2,1,0:T(1,128)S(1)} %get-tuple-element.75.refs_7_.idq_ref), custom_call_target="tpu_custom_call" | custom-call | flops 1000000000 | bytes 2000000 | tf_op jit(solution)/shard_map/pallas_call | solution.py:191
  51.1 0.9 collective-permute-start.13
  52.0 0.8 shard_map.118
  52.9 1.0 %shard_map.116.p_ref = f32[8,144,288]{2,1,0:T(8,128)S(1)} custom-call(bf16[6,576,256]{2,1,0:T(8,128)(2,1)S(1)} %get-tuple-element.95.qkv_ref, s32[576,1]{1,0:T(8,128)S(1)} %get-tuple-element.74.refs_6_.idk_ref.refs_10_, s32[4,1,288]{2,1,0:T(1,128)S(1)} %get-tuple-element.75.refs_7_.idq_ref), custom_call_target="tpu_custom_call" | custom-call | flops 1 | bytes 1 | tf_op jit(solution)/shard_map/pallas_call | solution.py:317
  53.9 3.2 %collective-permute-done.14.refs_8_ = bf16[288,512]{1,0:T(8,128)(2,1)S(1)} collective-permute-done((bf16[288,512]{1,0:T(8,128)(2,1)S(1)}, bf16[288,512]{1,0:T(8,128)(2,1)S(1)}, u32[]{:S(2)}, u32[]{:S(2)}) %collective-permute-start.14) | collective-permute-done | bytes 294944 | tf_op jit(solution)/shard_map/ppermute | solution.py:577
  57.1 1.0 %shard_map.112 = (bf16[144,256]{1,0:T(8,128)(2,1)S(1)}, bf16[144,256]{1,0:T(8,128)(2,1)S(1)}, bf16[144,256]{1,0:T(8,128)(2,1)S(1)}, bf16[144,256]{1,0:T(8,128)(2,1)S(1)}, bf16[288,1024]{1,0:T(8,128)(2,1)S(1)}) custom-call(s32[1]{0:T(128)} %bitcast.2.t_ref, bf16[576,256]{1,0:T(8,128)(2,1)S(1)} %get-tuple-element.66.refs_0_, ...), custom_call_target="tpu_custom_call" | custom-call | flops 1000000000 | bytes 4000000 | tf_op jit(solution)/shard_map/pallas_call | solution.py:287
  58.1 3.2 %shard_map.113.g0_ref = bf16[6,288,256]{2,1,0:T(8,128)(2,1)S(1)} custom-call(bf16[288,1024]{1,0:T(8,128)(2,1)S(1)} %get-tuple-element.84.err_ref.e0_ref, bf16[1024,1024]{1,0:T(8,128)(2,1)S(1)} %get-tuple-element.65.refs_9_.wc_ref, bf16[6,576,256]{2,1,0:T(8,128)(2,1)S(1)} %get-tuple-element.95.qkv_ref, f32[8,144,288]{2,1,0:T(8,128)S(1)} %shard_map.109.p_ref), custom_call_target="tpu_custom_call" | custom-call | flops 4000000000 | bytes 5000000 | tf_op jit(solution)/shard_map/pallas_call | solution.py:393
  61.3 1.7 %collective-permute-done.13.refs_8_ = bf16[288,512]{1,0:T(8,128)(2,1)S(1)} collective-permute-done((bf16[288,512]{1,0:T(8,128)(2,1)S(1)}, bf16[288,512]{1,0:T(8,128)(2,1)S(1)}, u32[]{:S(2)}, u32[]{:S(2)}) %collective-permute-start.13) | collective-permute-done | bytes 294944 | tf_op jit(solution)/shard_map/ppermute | solution.py:577
  63.0 1.0 %shard_map.114 = (bf16[288,256]{1,0:T(8,128)(2,1)S(1)}, bf16[288,256]{1,0:T(8,128)(2,1)S(1)}, bf16[288,256]{1,0:T(8,128)(2,1)S(1)}, bf16[288,256]{1,0:T(8,128)(2,1)S(1)}, bf16[288,1024]{1,0:T(8,128)(2,1)S(1)}) custom-call(s32[1]{0:T(128)} %bitcast.2.t_ref, bf16[576,256]{1,0:T(8,128)(2,1)S(1)} %get-tuple-element.66.refs_0_, ...), custom_call_target="tpu_custom_call" | custom-call | flops 1000000000 | bytes 4000000 | tf_op jit(solution)/shard_map/pallas_call | solution.py:287
  63.9 1.2 %collective-permute-start.15 = (bf16[288,256]{1,0:T(8,128)(2,1)S(1)}, bf16[288,256]{1,0:T(8,128)(2,1)S(1)}, u32[]{:S(2)}, u32[]{:S(2)}) collective-permute-start(bf16[288,256]{1,0:T(8,128)(2,1)S(1)} %get-tuple-element.91), channel_id=1, source_target_pairs={{0,4},{1,5},{2,6},{3,7},{4,8},{5,9},{6,10},{7,11},{8,12},{9,13},{1... | collective-permute-start | bytes 442376 | tf_op jit(solution)/shard_map/ppermute | solution.py:577
  65.1 1.7 %collective-permute-start.17 = (bf16[288,256]{1,0:T(8,128)(2,1)S(1)}, bf16[288,256]{1,0:T(8,128)(2,1)S(1)}, u32[]{:S(2)}, u32[]{:S(2)}) collective-permute-start(bf16[288,256]{1,0:T(8,128)(2,1)S(1)} %get-tuple-element.93), channel_id=1, source_target_pairs={{0,5},{1,4},{2,7},{3,6},{4,9},{5,8},{6,11},{7,10},{8,13},{9,12},{1... | collective-permute-start | bytes 442376 | tf_op jit(solution)/shard_map/ppermute | solution.py:577
  66.8 1.6 %shard_map.119 = f32[8,256]{1,0:T(8,128)S(1)} custom-call(bf16[288,1024]{1,0:T(8,128)(2,1)S(1)} %get-tuple-element.84.err_ref.e0_ref, bf16[288,1024]{1,0:T(8,128)(2,1)S(1)} %get-tuple-element.94.err_ref.e1_ref, bf16[512,576]{1,0:T(8,128)(2,1)S(1)} %get-tuple-element.97.attn_t, bf16[256,1024]{1,0:T(8,128)(2,1)S(1)} %copy-done.4, ...), custom_call_target="tpu_custom_call" | custom-call | flops 1000000000 | bytes 3000000 | tf_op jit(solution)/shard_map/pallas_call | solution.py:350
  68.4 0.0 copy-start.2
  68.4 1.6 %collective-permute-start.18 = (f32[8,256]{1,0:T(8,128)S(1)}, f32[8,256]{1,0:T(8,128)S(1)}, u32[]{:S(2)}, u32[]{:S(2)}) collective-permute-start(f32[8,256]{1,0:T(8,128)S(1)} %shard_map.119), channel_id=1, source_target_pairs={{0,2},{1,3},{2,0},{3,1},{4,6},{5,7},{6,4},{7,5},{8,10},{9,11},{10,... | collective-permute-start | bytes 24584 | tf_op jit(solution)/shard_map/ppermute | solution.py:577
  70.0 3.2 %shard_map.117.g1_ref = bf16[6,288,256]{2,1,0:T(8,128)(2,1)S(1)} custom-call(bf16[288,1024]{1,0:T(8,128)(2,1)S(1)} %get-tuple-element.94.err_ref.e1_ref, bf16[1024,1024]{1,0:T(8,128)(2,1)S(1)} %get-tuple-element.65.refs_9_.wc_ref, bf16[6,576,256]{2,1,0:T(8,128)(2,1)S(1)} %get-tuple-element.95.qkv_ref, f32[8,144,288]{2,1,0:T(8,128)S(1)} %shard_map.116.p_ref), custom_call_target="tpu_custom_call" | custom-call | flops 4000000000 | bytes 5000000 | tf_op jit(solution)/shard_map/pallas_call | solution.py:393
  73.2 0.2 collective-permute-done.15.a1
  73.4 0.9 collective-permute-done.17.b1
  74.3 3.8 %shard_map.120 = (f32[6,256]{1,0:T(8,128)S(1)}, f32[6,256]{1,0:T(8,128)S(1)}) custom-call(bf16[6,288,256]{2,1,0:T(8,128)(2,1)S(1)} %shard_map.113.g0_ref, bf16[6,288,256]{2,1,0:T(8,128)(2,1)S(1)} %shard_map.117.g1_ref, bf16[1024,576]{1,0:T(8,128)(2,1)S(1)} %get-tuple-element.100.normed_t, bf16[3,1024,256]{2,1,0:T(8,128)(2,1)S(1)} %bitcast.15, ...), custom_call_target="tpu_custom_call" | custom-call | flops 4000000000 | bytes 8000000 | tf_op jit(solution)/shard_map/pallas_call | solution.py:421
  78.1 0.5 collective-permute-start.20
  78.7 1.9 %collective-permute-start.21 = (f32[14,256]{1,0:T(8,128)S(1)}, f32[14,256]{1,0:T(8,128)S(1)}, u32[]{:S(2)}, u32[]{:S(2)}) collective-permute-start(f32[14,256]{1,0:T(8,128)S(1)} %get-tuple-element.107), channel_id=1, source_target_pairs={{0,5},{1,4},{2,7},{3,6},{4,1},{5,0},{6,3},{7,2},{8,13},{9,12},{10,... | collective-permute-start | bytes 43016 | tf_op jit(solution)/shard_map/ppermute | solution.py:583
  80.5 1.6 %collective-permute-done.20 = f32[14,256]{1,0:T(8,128)S(1)} collective-permute-done((f32[14,256]{1,0:T(8,128)S(1)}, f32[14,256]{1,0:T(8,128)S(1)}, u32[]{:S(2)}, u32[]{:S(2)}) %collective-permute-start.20) | collective-permute-done | bytes 14368 | tf_op jit(solution)/shard_map/ppermute | solution.py:583
  82.1 0.2 collective-permute-done.21
  82.3 1.9 %collective-permute-start.24 = (f32[14,256]{1,0:T(8,128)S(1)}, f32[14,256]{1,0:T(8,128)S(1)}, u32[]{:S(2)}, u32[]{:S(2)}) collective-permute-start(f32[14,256]{1,0:T(8,128)S(1)} %add_add_fusion.refs_0_), channel_id=1, source_target_pairs={{0,24},{1,25},{2,26},{3,27},{4,28},{5,29},{6,30},{7,31},{8,16},{9,... | collective-permute-start | bytes 43016 | tf_op jit(solution)/shard_map/ppermute | solution.py:583
  84.2 0.8 collective-permute-start.23
  84.9 1.8 %collective-permute-start.22 = (f32[14,256]{1,0:T(8,128)S(1)}, f32[14,256]{1,0:T(8,128)S(1)}, u32[]{:S(2)}, u32[]{:S(2)}) collective-permute-start(f32[14,256]{1,0:T(8,128)S(1)} %add_add_fusion.refs_0_), channel_id=1, source_target_pairs={{0,8},{1,9},{2,10},{3,11},{4,12},{5,13},{6,14},{7,15},{8,0},{9,1},... | collective-permute-start | bytes 43016 | tf_op jit(solution)/shard_map/ppermute | solution.py:583
  86.8 2.0 %shard_map.115 = bf16[42,12,2,256]{3,2,1,0:T(2,128)(2,1)} custom-call(s32[3]{0:T(128)S(1)} %pad_add_fusion.s_ref, bf16[288,256]{1,0:T(8,128)(2,1)S(1)} %get-tuple-element.90.a0, bf16[288,256]{1,0:T(8,128)(2,1)S(1)} %collective-permute-done.15.a1, bf16[288,256]{1,0:T(8,128)(2,1)S(1)} %collective-permute-done.16.b0, ...), custom_call_target="tpu_custom_call" | custom-call | flops 1 | bytes 1 | tf_op jit(solution)/shard_map/pallas_call | solution.py:560
  88.7 0.1 collective-permute-done.23.refs_2_
  88.9 0.5 copy-done.9
  89.3 0.1 copy-done.10
  89.5 0.6 copy-done.11
  90.1 1.4 %shard_map.121 = (f32[3,2,256]{2,1,0:T(2,128)}, f32[2,1024]{1,0:T(2,128)}) custom-call(f32[14,256]{1,0:T(8,128)} %copy-done.8, f32[14,256]{1,0:T(8,128)} %copy-done.11, f32[14,256]{1,0:T(8,128)} %copy-done.10, f32[14,256]{1,0:T(8,128)} %copy-done.9), custom_call_target="tpu_custom_call" | custom-call | tf_op jit(solution)/shard_map/pallas_call | solution.py:617
  (36 shorter events, 0.1 us)
Async XLA Ops:
  0.6 12.8 %copy-start.5 = (s32[42,2,96]{2,1,0:T(2,128)S(1)}, s32[42,2,96]{2,1,0:T(2,128)}, u32[]{:S(2)}) copy-start(s32[42,2,96]{2,1,0:T(2,128)} %ids_ref.1) | copy-start | bytes 96772
  0.6 13.9 %collective-permute-start.2 = (bf16[3,1024,256]{2,1,0:T(8,128)(2,1)}, bf16[3,1024,256]{2,1,0:T(8,128)(2,1)S(1)}, u32[]{:S(2)}, u32[]{:S(2)}) collective-permute-start(bf16[3,1024,256]{2,1,0:T(8,128)(2,1)} %bitcast.13), channel_id=1, source_target_pairs={{0,1},{1,0},{2,3},{3,2},{4,5},{5,4},{6,7},{7,6},{8,9},{9,8},{10,11... | collective-permute-start | bytes 4718600 | tf_op jit(solution)/shard_map/ppermute | solution.py:577
  1.2 14.2 %collective-permute-start.1 = (bf16[256,1024]{1,0:T(8,128)(2,1)}, bf16[256,1024]{1,0:T(8,128)(2,1)S(1)}, u32[]{:S(2)}, u32[]{:S(2)}) collective-permute-start(bf16[256,1024]{1,0:T(8,128)(2,1)} %po_ref.1), channel_id=1, source_target_pairs={{0,1},{1,0},{2,3},{3,2},{4,5},{5,4},{6,7},{7,6},{8,9},{9,8},{10,11... | collective-permute-start | bytes 1572872 | tf_op jit(solution)/shard_map/ppermute | solution.py:577
  1.2 15.3 %collective-permute-start.8 = (bf16[256,1024]{1,0:T(8,128)(2,1)}, bf16[256,1024]{1,0:T(8,128)(2,1)S(1)}, u32[]{:S(2)}, u32[]{:S(2)}) collective-permute-start(bf16[256,1024]{1,0:T(8,128)(2,1)} %po_ref.1), channel_id=1, source_target_pairs={{0,2},{1,3},{2,0},{3,1},{4,6},{5,7},{6,4},{7,5},{8,10},{9,11},{10,... | collective-permute-start | bytes 1572872 | tf_op jit(solution)/shard_map/ppermute | solution.py:577
  5.3 10.0 %collective-permute-start = (bf16[42,6,2,256]{3,2,1,0:T(2,128)(2,1)S(1)}, bf16[42,6,2,256]{3,2,1,0:T(2,128)(2,1)S(1)}, u32[]{:S(2)}, u32[]{:S(2)}) collective-permute-start(bf16[42,6,2,256]{3,2,1,0:T(2,128)(2,1)S(1)} %slice.13), channel_id=1, source_target_pairs={{0,28},{1,29},{2,30},{3,31},{4,0},{5,1},{6,2},{7,3},{8,4},{9,5},{1... | collective-permute-start | bytes 774152 | tf_op jit(solution)/shard_map/ppermute | solution.py:577
  9.9 4.6 %collective-permute-start.3 = (f32[3,2,256]{2,1,0:T(2,128)}, f32[3,2,256]{2,1,0:T(2,128)S(1)}, u32[]{:S(2)}, u32[]{:S(2)}) collective-permute-start(f32[3,2,256]{2,1,0:T(2,128)} %bitcast.18), channel_id=1, source_target_pairs={{0,1},{1,0},{2,3},{3,2},{4,5},{5,4},{6,7},{7,6},{8,9},{9,8},{10,11... | collective-permute-start | bytes 18440 | tf_op jit(solution)/shard_map/ppermute | solution.py:577
  10.6 1.4 %copy-start.1 = (bf16[1024,3,256]{2,0,1:T(8,128)(2,1)S(1)}, bf16[1024,3,256]{2,0,1:T(8,128)(2,1)}, u32[]{:S(2)}) copy-start(bf16[1024,3,256]{2,0,1:T(8,128)(2,1)} %param.10) | copy-start | bytes 4718596
  12.0 0.7 copy-start.7
  12.7 2.6 %copy-start.3 = (bf16[42,2,12,256]{3,1,2,0:T(2,128)(2,1)S(1)}, bf16[42,2,12,256]{3,1,2,0:T(2,128)(2,1)}, u32[]{:S(2)}) copy-start(bf16[42,2,12,256]{3,1,2,0:T(2,128)(2,1)} %param.8) | copy-start | bytes 1548292
  13.4 5.5 %copy-start = (bf16[42,2,12,256]{3,1,2,0:T(2,128)(2,1)S(1)}, bf16[42,2,12,256]{3,1,2,0:T(2,128)(2,1)}, u32[]{:S(2)}) copy-start(bf16[42,2,12,256]{3,1,2,0:T(2,128)(2,1)} %param.9) | copy-start | bytes 1548292
  14.5 9.7 %copy-start.4 = (bf16[256,1024]{1,0:T(8,128)(2,1)S(1)}, bf16[256,1024]{1,0:T(8,128)(2,1)}, u32[]{:S(2)}) copy-start(bf16[256,1024]{1,0:T(8,128)(2,1)} %po_ref.1) | copy-start | bytes 1572868
  14.5 9.7 %copy-start.6 = (f32[2,1024]{1,0:T(2,128)S(1)}, f32[2,1024]{1,0:T(2,128)}, u32[]{:S(2)}) copy-start(f32[2,1024]{1,0:T(2,128)} %c_ref.1) | copy-start | bytes 24580
  16.6 7.7 %collective-permute-start.9 = (bf16[256,1024]{1,0:T(8,128)(2,1)S(1)}, bf16[256,1024]{1,0:T(8,128)(2,1)S(1)}, u32[]{:S(2)}, u32[]{:S(2)}) collective-permute-start(bf16[256,1024]{1,0:T(8,128)(2,1)S(1)} %collective-permute-done.8.w2), channel_id=1, source_target_pairs={{0,1},{1,0},{2,3},{3,2},{4,5},{5,4},{6,7},{7,6},{8,9},{9,8},{10,11... | collective-permute-start | bytes 1572872 | tf_op jit(solution)/shard_map/ppermute | solution.py:577
  16.8 13.0 %collective-permute-start.7 = (bf16[576,256]{1,0:T(8,128)(2,1)S(1)}, bf16[576,256]{1,0:T(8,128)(2,1)S(1)}, u32[]{:S(2)}, u32[]{:S(2)}) collective-permute-start(bf16[576,256]{1,0:T(8,128)(2,1)S(1)} %bitcast.20), channel_id=1, source_target_pairs={{0,3},{1,2},{2,1},{3,0},{4,7},{5,6},{6,5},{7,4},{8,11},{9,10},{10,... | collective-permute-start | bytes 884744 | tf_op jit(solution)/shard_map/ppermute | solution.py:577
  18.4 11.4 %collective-permute-start.5 = (bf16[576,256]{1,0:T(8,128)(2,1)S(1)}, bf16[576,256]{1,0:T(8,128)(2,1)S(1)}, u32[]{:S(2)}, u32[]{:S(2)}) collective-permute-start(bf16[576,256]{1,0:T(8,128)(2,1)S(1)} %bitcast.21), channel_id=1, source_target_pairs={{0,1},{1,0},{2,3},{3,2},{4,5},{5,4},{6,7},{7,6},{8,9},{9,8},{10,11... | collective-permute-start | bytes 884744 | tf_op jit(solution)/shard_map/ppermute | solution.py:577
  18.4 14.0 %collective-permute-start.6 = (bf16[576,256]{1,0:T(8,128)(2,1)S(1)}, bf16[576,256]{1,0:T(8,128)(2,1)S(1)}, u32[]{:S(2)}, u32[]{:S(2)}) collective-permute-start(bf16[576,256]{1,0:T(8,128)(2,1)S(1)} %get-tuple-element.66.refs_0_), channel_id=1, source_target_pairs={{0,2},{1,3},{2,0},{3,1},{4,6},{5,7},{6,4},{7,5},{8,10},{9,11},{10,... | collective-permute-start | bytes 884744 | tf_op jit(solution)/shard_map/ppermute | solution.py:577
  19.1 10.7 %collective-permute-start.4 = (bf16[42,6,2,256]{3,2,1,0:T(2,128)(2,1)S(1)}, bf16[42,6,2,256]{3,2,1,0:T(2,128)(2,1)S(1)}, u32[]{:S(2)}, u32[]{:S(2)}) collective-permute-start(bf16[42,6,2,256]{3,2,1,0:T(2,128)(2,1)S(1)} %slice.11), channel_id=1, source_target_pairs={{0,28},{1,29},{2,30},{3,31},{4,0},{5,1},{6,2},{7,3},{8,4},{9,5},{1... | collective-permute-start | bytes 774152 | tf_op jit(solution)/shard_map/ppermute | solution.py:577
  32.4 10.7 %collective-permute-start.10 = (bf16[42,6,2,256]{3,2,1,0:T(2,128)(2,1)S(1)}, bf16[42,6,2,256]{3,2,1,0:T(2,128)(2,1)S(1)}, u32[]{:S(2)}, u32[]{:S(2)}) collective-permute-start(bf16[42,6,2,256]{3,2,1,0:T(2,128)(2,1)S(1)} %slice.12), channel_id=1, source_target_pairs={{0,2},{1,3},{2,0},{3,1},{4,6},{5,7},{6,4},{7,5},{8,10},{9,11},{10,... | collective-permute-start | bytes 774152 | tf_op jit(solution)/shard_map/ppermute | solution.py:577
  33.9 11.9 %collective-permute-start.11 = (bf16[42,6,2,256]{3,2,1,0:T(2,128)(2,1)S(1)}, bf16[42,6,2,256]{3,2,1,0:T(2,128)(2,1)S(1)}, u32[]{:S(2)}, u32[]{:S(2)}) collective-permute-start(bf16[42,6,2,256]{3,2,1,0:T(2,128)(2,1)S(1)} %collective-permute-done.4.refs_1_), channel_id=1, source_target_pairs={{0,2},{1,3},{2,0},{3,1},{4,6},{5,7},{6,4},{7,5},{8,10},{9,11},{10,... | collective-permute-start | bytes 774152 | tf_op jit(solution)/shard_map/ppermute | solution.py:577
  47.1 10.0 %collective-permute-start.12 = (bf16[2,576,256]{2,1,0:T(8,128)(2,1)S(1)}, bf16[2,576,256]{2,1,0:T(8,128)(2,1)S(1)}, u32[]{:S(2)}, u32[]{:S(2)}) collective-permute-start(bf16[2,576,256]{2,1,0:T(8,128)(2,1)S(1)} %get-tuple-element.81), channel_id=1, source_target_pairs={{0,1},{1,0},{2,3},{3,2},{4,5},{5,4},{6,7},{7,6},{8,9},{9,8},{10,11... | collective-permute-start | bytes 1769480 | tf_op jit(solution)/shard_map/ppermute | solution.py:577
  47.2 9.9 %collective-permute-start.14 = (bf16[288,512]{1,0:T(8,128)(2,1)S(1)}, bf16[288,512]{1,0:T(8,128)(2,1)S(1)}, u32[]{:S(2)}, u32[]{:S(2)}) collective-permute-start(bf16[288,512]{1,0:T(8,128)(2,1)S(1)} %get-tuple-element.83.refs_7_.a_ref), channel_id=1, source_target_pairs={{0,2},{1,3},{2,0},{3,1},{4,6},{5,7},{6,4},{7,5},{8,10},{9,11},{10,... | collective-permute-start | bytes 884744 | tf_op jit(solution)/shard_map/ppermute | solution.py:577
  51.1 11.8 %collective-permute-start.13 = (bf16[288,512]{1,0:T(8,128)(2,1)S(1)}, bf16[288,512]{1,0:T(8,128)(2,1)S(1)}, u32[]{:S(2)}, u32[]{:S(2)}) collective-permute-start(bf16[288,512]{1,0:T(8,128)(2,1)S(1)} %shard_map.111.refs_7_.b_ref), channel_id=1, source_target_pairs={{0,2},{1,3},{2,0},{3,1},{4,6},{5,7},{6,4},{7,5},{8,10},{9,11},{10,... | collective-permute-start | bytes 884744 | tf_op jit(solution)/shard_map/ppermute | solution.py:577
  63.9 9.5 %collective-permute-start.15 = (bf16[288,256]{1,0:T(8,128)(2,1)S(1)}, bf16[288,256]{1,0:T(8,128)(2,1)S(1)}, u32[]{:S(2)}, u32[]{:S(2)}) collective-permute-start(bf16[288,256]{1,0:T(8,128)(2,1)S(1)} %get-tuple-element.91), channel_id=1, source_target_pairs={{0,4},{1,5},{2,6},{3,7},{4,8},{5,9},{6,10},{7,11},{8,12},{9,13},{1... | collective-permute-start | bytes 442376 | tf_op jit(solution)/shard_map/ppermute | solution.py:577
  65.1 8.3 %collective-permute-start.16 = (bf16[288,256]{1,0:T(8,128)(2,1)S(1)}, bf16[288,256]{1,0:T(8,128)(2,1)S(1)}, u32[]{:S(2)}, u32[]{:S(2)}) collective-permute-start(bf16[288,256]{1,0:T(8,128)(2,1)S(1)} %get-tuple-element.92), channel_id=1, source_target_pairs={{0,1},{1,0},{2,3},{3,2},{4,5},{5,4},{6,7},{7,6},{8,9},{9,8},{10,11... | collective-permute-start | bytes 442376 | tf_op jit(solution)/shard_map/ppermute | solution.py:577
  65.1 9.1 %collective-permute-start.17 = (bf16[288,256]{1,0:T(8,128)(2,1)S(1)}, bf16[288,256]{1,0:T(8,128)(2,1)S(1)}, u32[]{:S(2)}, u32[]{:S(2)}) collective-permute-start(bf16[288,256]{1,0:T(8,128)(2,1)S(1)} %get-tuple-element.93), channel_id=1, source_target_pairs={{0,5},{1,4},{2,7},{3,6},{4,9},{5,8},{6,11},{7,10},{8,13},{9,12},{1... | collective-permute-start | bytes 442376 | tf_op jit(solution)/shard_map/ppermute | solution.py:577
  68.4 5.9 %copy-start.2 = (bf16[1024,3,256]{2,0,1:T(8,128)(2,1)S(1)}, bf16[1024,3,256]{2,0,1:T(8,128)(2,1)}, u32[]{:S(2)}) copy-start(bf16[1024,3,256]{2,0,1:T(8,128)(2,1)} %param.10) | copy-start | bytes 4718596
  68.4 4.8 %collective-permute-start.18 = (f32[8,256]{1,0:T(8,128)S(1)}, f32[8,256]{1,0:T(8,128)S(1)}, u32[]{:S(2)}, u32[]{:S(2)}) collective-permute-start(f32[8,256]{1,0:T(8,128)S(1)} %shard_map.119), channel_id=1, source_target_pairs={{0,2},{1,3},{2,0},{3,1},{4,6},{5,7},{6,4},{7,5},{8,10},{9,11},{10,... | collective-permute-start | bytes 24584 | tf_op jit(solution)/shard_map/ppermute | solution.py:577
  78.1 4.0 %collective-permute-start.20 = (f32[14,256]{1,0:T(8,128)S(1)}, f32[14,256]{1,0:T(8,128)S(1)}, u32[]{:S(2)}, u32[]{:S(2)}) collective-permute-start(f32[14,256]{1,0:T(8,128)S(1)} %get-tuple-element.108), channel_id=1, source_target_pairs={{0,4},{1,5},{2,6},{3,7},{4,0},{5,1},{6,2},{7,3},{8,12},{9,13},{10,... | collective-permute-start | bytes 43016 | tf_op jit(solution)/shard_map/ppermute | solution.py:583
  78.7 3.6 %collective-permute-start.21 = (f32[14,256]{1,0:T(8,128)S(1)}, f32[14,256]{1,0:T(8,128)S(1)}, u32[]{:S(2)}, u32[]{:S(2)}) collective-permute-start(f32[14,256]{1,0:T(8,128)S(1)} %get-tuple-element.107), channel_id=1, source_target_pairs={{0,5},{1,4},{2,7},{3,6},{4,1},{5,0},{6,3},{7,2},{8,13},{9,12},{10,... | collective-permute-start | bytes 43016 | tf_op jit(solution)/shard_map/ppermute | solution.py:583
  80.5 1.8 %collective-permute-start.19 = (f32[14,256]{1,0:T(8,128)S(1)}, f32[14,256]{1,0:T(8,128)S(1)}, u32[]{:S(2)}, u32[]{:S(2)}) collective-permute-start(f32[14,256]{1,0:T(8,128)S(1)} %get-tuple-element.107), channel_id=1, source_target_pairs={{0,1},{1,0},{2,3},{3,2},{4,5},{5,4},{6,7},{7,6},{8,9},{9,8},{10,11... | collective-permute-start | bytes 43016 | tf_op jit(solution)/shard_map/ppermute | solution.py:577
  82.3 6.6 %copy-start.8 = (f32[14,256]{1,0:T(8,128)}, f32[14,256]{1,0:T(8,128)S(1)}, u32[]{:S(2)}) copy-start(f32[14,256]{1,0:T(8,128)S(1)} %add_add_fusion.refs_0_) | copy-start | bytes 43012
  82.3 6.4 %collective-permute-start.24 = (f32[14,256]{1,0:T(8,128)S(1)}, f32[14,256]{1,0:T(8,128)S(1)}, u32[]{:S(2)}, u32[]{:S(2)}) collective-permute-start(f32[14,256]{1,0:T(8,128)S(1)} %add_add_fusion.refs_0_), channel_id=1, source_target_pairs={{0,24},{1,25},{2,26},{3,27},{4,28},{5,29},{6,30},{7,31},{8,16},{9,... | collective-permute-start | bytes 43016 | tf_op jit(solution)/shard_map/ppermute | solution.py:583
  84.2 4.7 %collective-permute-start.23 = (f32[14,256]{1,0:T(8,128)S(1)}, f32[14,256]{1,0:T(8,128)S(1)}, u32[]{:S(2)}, u32[]{:S(2)}) collective-permute-start(f32[14,256]{1,0:T(8,128)S(1)} %add_add_fusion.refs_0_), channel_id=1, source_target_pairs={{0,16},{1,17},{2,18},{3,19},{4,20},{5,21},{6,22},{7,23},{8,24},{9,... | collective-permute-start | bytes 43016 | tf_op jit(solution)/shard_map/ppermute | solution.py:583
  84.9 3.9 %collective-permute-start.22 = (f32[14,256]{1,0:T(8,128)S(1)}, f32[14,256]{1,0:T(8,128)S(1)}, u32[]{:S(2)}, u32[]{:S(2)}) collective-permute-start(f32[14,256]{1,0:T(8,128)S(1)} %add_add_fusion.refs_0_), channel_id=1, source_target_pairs={{0,8},{1,9},{2,10},{3,11},{4,12},{5,13},{6,14},{7,15},{8,0},{9,1},... | collective-permute-start | bytes 43016 | tf_op jit(solution)/shard_map/ppermute | solution.py:583
  88.7 0.6 copy-start.9
  88.9 0.6 copy-start.10
  89.5 0.6 copy-start.11

commit v5 on v4

--- a/solution.py
+++ b/solution.py
@@ -16,6 +16,7 @@
 SCALE = HD ** (-0.5)
 NT = (((1,), (1,)), ((), ()))
 TN = (((0,), (0,)), ((), ()))
+LARGE = pl.CostEstimate(flops=8 * 10**9, bytes_accessed=10**7, transcendentals=10**6)
 SMALL = pl.CostEstimate(flops=1, bytes_accessed=1, transcendentals=0)
 
 
@@ -64,13 +65,16 @@
     )(w, clips)
 
 
-def clip_proj_kernel(w0, w1, w2, w3, c_ref, wc_ref, b_ref):
-    shards = (w0, w1, w2, w3)
-    size = w0.shape[0]
+def clip_proj_kernel(s_ref, w0, w1, a2, b2, a3, b3, c_ref, wc_ref, b_ref):
+    second = s_ref[2] % 2 == 1
 
     def body(i, carry):
         cols = pl.ds(pl.multiple_of(i * 256, 256), 256)
-        w = jnp.concatenate([s[:, cols].astype(F32) for s in shards], axis=0)
+        parts = [w0[:, cols].astype(F32), w1[:, cols].astype(F32)]
+        for first_ref, other_ref in ((a2, b2), (a3, b3)):
+            a, b = first_ref[:, cols].astype(F32), other_ref[:, cols].astype(F32)
+            parts += [jnp.where(second, b, a), jnp.where(second, a, b)]
+        w = jnp.concatenate(parts, axis=0)
         up, lw, fh, fl = bounds_of(w, c_ref[0:1, cols], c_ref[1:2, cols])
         wc = jnp.minimum(jnp.maximum(w, lw), up).astype(BF)
         wc_ref[:, cols] = wc
@@ -83,7 +87,7 @@
     lax.fori_loop(0, w0.shape[1] // 256, body, 0)
 
 
-def clip_proj(shards, clips):
+def clip_proj(place, shards, clips):
     e, d = shards[0].shape
     return pl.pallas_call(
         clip_proj_kernel,
@@ -91,11 +95,11 @@
             jax.ShapeDtypeStruct((4 * e, d), BF),
             jax.ShapeDtypeStruct((8, d), F32),
         ),
-        in_specs=spec(5),
+        in_specs=[pl.BlockSpec(memory_space=pltpu.SMEM)] + spec(7),
         out_specs=tuple(spec(2)),
         compiler_params=params(24),
         cost_estimate=SMALL,
-    )(*shards, clips)
+    )(place, *shards, clips)
 
 
 def stacked(block, mask_a, mask_b):
@@ -129,9 +133,14 @@
     return (idk == idq_ref[w]) & (idk >= 0)
 
 
+def blocks(refs):
+    own, other, away = refs
+    return own, away.at[0], other, away.at[1]
+
+
 def forward_kernel(t_ref, *refs):
-    pieces = refs[:4]
-    wo_ref, wp_ref, idk_ref, idq_ref, normed_ref, qkv_ref, attn_ref = refs[4:]
+    pieces = blocks(refs[:3])
+    wo_ref, wp_ref, idk_ref, idq_ref, normed_ref, qkv_ref, attn_ref = refs[3:]
     t = t_ref[0]
     n, width = pieces[0].shape
     d = 4 * width
@@ -194,7 +203,7 @@
         in_specs=spec(3),
         out_specs=spec(1)[0],
         compiler_params=params(16),
-        cost_estimate=pl.CostEstimate(flops=10**9, bytes_accessed=2 * 10**6, transcendentals=10**6),
+        cost_estimate=pl.CostEstimate(flops=8 * 10**9, bytes_accessed=2 * 10**6, transcendentals=10**6),
     )(qkv, idk, idq)
 
 
@@ -208,7 +217,7 @@
             jax.ShapeDtypeStruct((6, n, width), BF),
             jax.ShapeDtypeStruct((n // 2, 2 * width), BF),
         ),
-        in_specs=[pl.BlockSpec(memory_space=pltpu.SMEM)] + spec(8),
+        in_specs=[pl.BlockSpec(memory_space=pltpu.SMEM)] + spec(7),
         out_specs=tuple(spec(3)),
         compiler_params=params(20),
         cost_estimate=pl.CostEstimate(flops=8 * 10**9, bytes_accessed=10 * 10**6, transcendentals=10**6),
@@ -247,9 +256,9 @@
 
 
 def output_kernel(group, t_ref, *refs):
-    pieces, targets = refs[:4], (refs[4], refs[6].at[0], refs[5], refs[6].at[1])
-    own_ref, other_ref, wc_ref, idk_ref = refs[7:11]
-    before, refs = refs[11 : 11 + 4 * group], refs[11 + 4 * group :]
+    pieces, targets = blocks(refs[:3]), blocks(refs[3:6])
+    own_ref, other_ref, wc_ref, idk_ref = refs[6:10]
+    before, refs = refs[10 : 10 + 4 * group], refs[10 + 4 * group :]
     mixed, err_ref, y_ref = refs[:4], refs[4], refs[5]
     t = t_ref[0]
     n, width = pieces[0].shape
@@ -287,11 +296,11 @@
     return pl.pallas_call(
         functools.partial(output_kernel, group),
         out_shape=(piece, piece, piece, piece, jax.ShapeDtypeStruct((n // 2, 4 * width), BF)),
-        in_specs=[pl.BlockSpec(memory_space=pltpu.SMEM)] + spec(11 + len(before)),
+        in_specs=[pl.BlockSpec(memory_space=pltpu.SMEM)] + spec(10 + len(before)),
         out_specs=tuple(spec(5)),
         scratch_shapes=[pltpu.VMEM((n // 2, width), F32)],
         compiler_params=params(20),
-        cost_estimate=pl.CostEstimate(flops=10**9, bytes_accessed=4 * 10**6, transcendentals=0),
+        cost_estimate=SMALL,
     )(t, *pieces, *targets, own, other, wc, idk, *before)
 
 
@@ -339,8 +348,8 @@
         b = pb_ref[:, cols]
         h0, l0 = masked_sums(grad[:n], po_ref[:, cols].astype(F32), b)
         h1, l1 = masked_sums(grad[n:], pp_ref[:, cols].astype(F32), b)
-        proj_ref[pl.ds(i, 1), :] = h0 + h1
-        proj_ref[pl.ds(4 + i, 1), :] = l0 + l1
+        proj_ref[0:1, cols] = h0 + h1
+        proj_ref[1:2, cols] = l0 + l1
         return carry
 
     lax.fori_loop(0, 4, proj_part, 0)
@@ -349,7 +358,7 @@
 def proj_sums(errs, attn_t, po, pp, pb):
     return pl.pallas_call(
         proj_sums_kernel,
-        out_shape=jax.ShapeDtypeStruct((8, 256), F32),
+        out_shape=jax.ShapeDtypeStruct((2, errs[0].shape[1]), F32),
         in_specs=spec(6),
         out_specs=spec(1)[0],
         compiler_params=params(16),
@@ -397,11 +406,13 @@
         out_specs=spec(1)[0],
         scratch_shapes=[pltpu.VMEM((n // 2, 2 * width), BF)],
         compiler_params=params(20),
-        cost_estimate=pl.CostEstimate(flops=4 * 10**9, bytes_accessed=5 * 10**6, transcendentals=10**6),
+        cost_estimate=LARGE if group else SMALL,
     )(err, wc, qkv, probs)
 
 
 def qkv_sums_kernel(g0_ref, g1_ref, normed_t, wo_ref, wp_ref, bo_ref, bp_ref, own_ref, peer_ref):
+    width = g0_ref.shape[2]
+
     def qkv_part(i, carry):
         for g, (w_ref, b_ref, to_ref) in enumerate(
             ((wo_ref, bo_ref, own_ref), (wp_ref, bp_ref, peer_ref))
@@ -409,8 +420,8 @@
             cells = jnp.concatenate([g0_ref[3 * g + i], g1_ref[3 * g + i]], axis=0)
             grad = jnp.dot(normed_t[...], cells, preferred_element_type=F32)
             hi, lo = masked_sums(grad, w_ref[i].astype(F32), b_ref[i])
-            to_ref[pl.ds(2 * i, 1), :] = hi
-            to_ref[pl.ds(2 * i + 1, 1), :] = lo
+            to_ref[0:1, pl.ds(pl.multiple_of(i * width, width), width)] = hi
+            to_ref[1:2, pl.ds(pl.multiple_of(i * width, width), width)] = lo
         return carry
 
     lax.fori_loop(0, 3, qkv_part, 0)
@@ -420,7 +431,7 @@
     width = g[0].shape[2]
     return pl.pallas_call(
         qkv_sums_kernel,
-        out_shape=(jax.ShapeDtypeStruct((6, width), F32),) * 2,
+        out_shape=(jax.ShapeDtypeStruct((2, 3 * width), F32),) * 2,
         in_specs=spec(7),
         out_specs=tuple(spec(2)),
         compiler_params=params(20),
@@ -601,27 +612,6 @@
     return terms[0]
 
 
-def last_sum_kernel(*refs):
-    qkv_ref, proj_ref = refs[-2:]
-    total = added([r[...] for r in refs[:-2]])
-    width = total.shape[1]
-    for i in range(3):
-        qkv_ref[i] = total[2 * i : 2 * i + 2]
-    for i in range(4):
-        for j in range(2):
-            proj_ref[j : j + 1, width * i : width * (i + 1)] = total[6 + 4 * j + i : 7 + 4 * j + i]
-
-
-def last_sum(terms):
-    width = terms[0].shape[1]
-    return pl.pallas_call(
-        last_sum_kernel,
-        out_shape=(jax.ShapeDtypeStruct((3, 2, width), F32), jax.ShapeDtypeStruct((2, 4 * width), F32)),
-        in_specs=spec(len(terms)),
-        out_specs=tuple(spec(2)),
-    )(*terms)
-
-
 def after(block, *others):
     return lax.optimization_barrier((block, *others))[0]
 
@@ -635,37 +625,42 @@
     place = jnp.stack([shift_offset[0], t % 2, sector]).astype(jnp.int32)
 
     f_raw, t_raw = (jnp.transpose(block, (0, 2, 1, 3)) for block in (features, target))
-    f_low = send(f_raw[:, :half], -1, 0)
+    f_low, f_up, w_qkv, w_proj = lax.optimization_barrier((f_raw[:, :half], f_raw[:, half:], w_qkv, w_proj))
+    f_low = send(f_low, -1, 0)
+    f_up_y = send(f_up, 0, 2)
 
     w3 = jnp.transpose(w_qkv, (1, 0, 2))
     c3 = jnp.transpose(qkv_clip, (1, 0, 2))
     w3_peer = send(w3, 0, 1)
     c3_peer = send(c3, 0, 1)
-    w1, w2 = send(w_proj, 0, 1), send(w_proj, 0, 2)
+    share = w_proj.shape[0] // 2
+    slab = send(lax.dynamic_slice_in_dim(w_proj, share * (sector % 2), share, 0), 0, 2)
+    w1 = send(w_proj, 0, 1)
     wc_own, b_own = clip_qkv(w3, c3)
     wc_peer, b_peer = clip_qkv(w3_peer, c3_peer)
     idk, idq = window_ids(place, region_ids, WLAT * lev * lon)
-
-    f_low, w1, wc_own, wc_peer, idk, idq = lax.optimization_barrier(
-        (f_low, w1, wc_own, wc_peer, idk, idq)
+    f_low, f_up_y, w1, wc_own, wc_peer, idk, idq = lax.optimization_barrier(
+        (f_low, f_up_y, w1, wc_own, wc_peer, idk, idq)
     )
-    mine, away = split(place, f_raw, f_low)
-    away = away.reshape(mine.shape)
-    pieces = [mine, send(away, 0, 1), send(mine, 0, 2), send(away, 0, 3)]
-    w_3 = send(after(w2, mine), 0, 1)
-    pc, pb = clip_proj([w_proj, w1, w2, w_3], proj_clip)
-
+    f_low_y = send(f_low, 0, 2)
     t_low = send(after(t_raw, f_low)[:, :half], -1, 0)
-    t_up, t_low, *pieces = lax.optimization_barrier((t_raw[:, half:], t_low, *pieces, pc))[:-1]
+    f_low_y, t_low, slab = lax.optimization_barrier((f_low_y, t_low, slab))
+    x_0, x_2, x_away = split(place, f_raw, f_low, f_up_y, f_low_y)
+    pieces = (x_0, x_2, send(x_away, 0, 1))
+
+    t_up = after(t_raw, f_low_y)[:, half:]
     t_up_y, t_low_y = send(t_up, 0, 2), send(t_low, 0, 2)
+    more = swap(slab, 1, 0)
 
     normed, qkv, attn_0 = forward(t_arr, pieces, wc_own, wc_peer, idk, idq)
     other_0 = send(attn_0, 0, 2)
     probs_0 = probs_of(0, qkv, idk, idq)
-    t_up_y, t_low_y = lax.optimization_barrier((t_up_y, t_low_y, probs_0))[:2]
+    attn_1 = last_windows(after(qkv, probs_0, t_up_y, t_low_y, more), idk, idq)
+    slab_3, more_3 = send(after(slab, attn_1), 0, 1), send(after(more, attn_1), 0, 1)
+    pc, pb = clip_proj(place, [w_proj, w1, slab, more, slab_3, more_3], proj_clip)
+    t_up_y, t_low_y = lax.optimization_barrier((t_up_y, t_low_y, other_0, attn_1))[:2]
     t_0, t_2, t_away = split(place, t_raw, t_low, t_up_y, t_low_y)
     targets = (t_0, t_2, send(t_away, 0, 1))
-    attn_1 = last_windows(after(qkv, probs_0, t_away), idk, idq)
     other_1 = send(attn_1, 0, 2)
     normed_t, attn_t = turn(normed, (attn_0, attn_1))
     probs = (probs_0, probs_of(1, after(qkv, attn_1), idk, idq))
@@ -684,11 +679,11 @@
     grads = (grads_0, grads_1)
     own, peer = qkv_sums(grads, normed_t, w3, w3_peer, b_own, b_peer)
     proj = proj + proj_y
-    own, peer = jnp.concatenate([own, proj], axis=0), jnp.concatenate([peer, proj], axis=0)
+    own, peer = jnp.concatenate([own, proj], axis=1), jnp.concatenate([peer, proj], axis=1)
     sums = added([own, send(peer, 0, 1), swap(own, 1, 0), swap(peer, 1, 1)])
-    qkv_sum, proj_sum = last_sum(lat_terms(sums, 2))
+    sums = added(lat_terms(sums, 2))
     mixed = join(place, [m00, m10, m01, m11], rows, lon, lev)
-    return (mixed, jnp.transpose(qkv_sum, (1, 0, 2)), proj_sum)
+    return (mixed, sums[:, : 3 * width].reshape(2, 3, width), sums[:, 3 * width :])
 
 
 def solution(mesh):

time: 91.7 us -> 90.7 us (0.989)
  starting transfers between devices: 31 us -> 24.9 us
  waiting for transfers between devices: 18.2 us -> 20.6 us
  Pallas kernels: 35.8 us -> 37.3 us
  local copies, waits for them, and re-layouts: 4.81 us -> 5.79 us
    ppermute x20 -> x21, starting transfers between devices: 24.1 us -> 19.4 us  [send(): return lax.ppermute(block, ('lat', 'tp'), route)]
    unnamed x24 -> x14, local copies, waits for them, and re-layouts: 3.33 us -> 0.19 us
    slice x2 -> x4, local copies, waits for them, and re-layouts: 1.31 us -> 3.75 us  [the longest x1 2.38 us: local(): f_raw[:, half:]]
    ppermute x20 -> x21, waiting for transfers between devices: 16.3 us -> 18.2 us  [send(): return lax.ppermute(block, ('lat', 'tp'), route)]
    dynamic_slice x0 -> x1, local copies, waits for them, and re-layouts: none -> 1.67 us  [local(): lax.dynamic_slice_in_dim(w_proj, share * (sector % 2), share, 0)]
    ppermute x5 -> x6, starting transfers between devices: 6.84 us -> 5.54 us  [swap(): return lax.ppermute(block, ('lat', 'tp'), route)]
    pallas_call x1, Pallas kernels: 0.93 us -> 2.07 us  [clip_proj(): pl.pallas_call(clip_proj_kernel, out_shape=(jax.ShapeDtypeStruct((4 * e,...]
    ppermute x5 -> x6, waiting for transfers between devices: 1.89 us -> 2.45 us  [swap(): return lax.ppermute(block, ('lat', 'tp'), route)]
  transfers between devices with their start and end apart: 25 -> 27, of which waited for: 12 -> 9; matrix products, arithmetic and copies ran while one was open for 2% -> 2% of each run, Pallas kernels for 31% -> 33%
where the time goes in v5:
time: 90.7 us; the launch traced here: 90.4 us
  Pallas kernels  37.3 us (41%)
  starting transfers between devices  24.9 us (27%)
  waiting for transfers between devices  20.6 us (23%)
  local copies, waits for them, and re-layouts  5.79 us (6%)
  between operations  1.63 us (2%)
    ppermute x21, starting transfers between devices, send(): return lax.ppermute(block, ('lat', 'tp'), route)  19.4 us
    ppermute x21, waiting for transfers between devices, send(): return lax.ppermute(block, ('lat', 'tp'), route)  18.2 us
    pallas_call x1, Pallas kernels, forward(): pl.pallas_call(forward_kernel, out_shape=(jax.ShapeDtypeStruct((n, d), BF...  7.63 us
    pallas_call x2, Pallas kernels, backward(): pl.pallas_call(functools.partial(backward_kernel, group), out_shape=jax.S...  6.39 us
    ppermute x6, starting transfers between devices, swap(): return lax.ppermute(block, ('lat', 'tp'), route)  5.54 us
    pallas_call x1, Pallas kernels, qkv_sums(): pl.pallas_call(qkv_sums_kernel, out_shape=(jax.ShapeDtypeStruct((2, 3 * w...  3.85 us
    pallas_call x2, Pallas kernels, split(): pl.pallas_call(split_kernel, out_shape=(jax.ShapeDtypeStruct((n, width),...  2.95 us
    pallas_call x1, Pallas kernels, last_windows(): pl.pallas_call(last_kernel, out_shape=jax.ShapeDtypeStruct((n // 2, 2 * w...  2.66 us
  transfers between devices with their start and end apart: 27, of which 9 were waited for; matrix products, arithmetic and copies ran while one was open for 2% of the time, Pallas kernels for 33%

profile of v5, /device:TPU:0, one launch (start us, length us, event | category | flops | bytes accessed | tf_op | source)
XLA Modules:
  0.0 90.4 jit_solution(8715208508785597457)
XLA Ops:
  0.6 0.0 copy-start.2
  0.6 0.0 copy-start.6
  0.7 2.4 %fusion = (bf16[42,6,2,256]{3,2,1,0:T(2,128)(2,1)}, bf16[42,6,2,256]{3,2,1,0:T(2,128)(2,1)}) fusion(bf16[42,12,2,256]{3,2,1,0:T(2,128)(2,1)} %bitcast.9), kind=kLoop, calls=%fused_computation.6 | loop fusion | bytes 1032192 | tf_op jit(solution)/shard_map/slice | solution.py:628
  3.0 0.5 collective-permute-start.3
  3.5 0.1 collective-permute-start.2
  3.6 6.0 %collective-permute-start = (bf16[42,6,2,256]{3,2,1,0:T(2,128)(2,1)}, bf16[42,6,2,256]{3,2,1,0:T(2,128)(2,1)S(1)}, u32[]{:S(2)}, u32[]{:S(2)}) collective-permute-start(bf16[42,6,2,256]{3,2,1,0:T(2,128)(2,1)} %get-tuple-element.58), channel_id=1, source_target_pairs={{0,28},{1,29},{2,30},{3,31},{4,0},{5,1},{6,2},{7,3},{8,4},{9,5},{1... | collective-permute-start | bytes 774152 | tf_op jit(solution)/shard_map/ppermute | solution.py:588
  9.5 1.5 %collective-permute-start.1 = (bf16[42,6,2,256]{3,2,1,0:T(2,128)(2,1)}, bf16[42,6,2,256]{3,2,1,0:T(2,128)(2,1)}, u32[]{:S(2)}, u32[]{:S(2)}) collective-permute-start(bf16[42,6,2,256]{3,2,1,0:T(2,128)(2,1)} %get-tuple-element.59), channel_id=1, source_target_pairs={{0,2},{1,3},{2,0},{3,1},{4,6},{5,7},{6,4},{7,5},{8,10},{9,11},{10,... | collective-permute-start | bytes 774152 | tf_op jit(solution)/shard_map/ppermute | solution.py:588
  11.1 1.7 %constant_dynamic-slice_fusion = bf16[128,1024]{1,0:T(8,128)(2,1)} fusion(bf16[256,1024]{1,0:T(8,128)(2,1)} %po_ref, s32[]{:T(128)S(6)} %select_n.16), kind=kLoop, calls=%fused_computation.5 | loop fusion | bytes 524292 | tf_op jit(solution)/shard_map/dynamic_slice | solution.py:637
  13.4 0.6 collective-permute-start.7
  14.0 0.1 pad_add_fusion.s_ref
  14.1 0.7 shard_map.103
  14.8 1.0 %shard_map.105 = (s32[576,1]{1,0:T(8,128)S(1)}, s32[4,1,288]{2,1,0:T(1,128)S(1)}) custom-call(s32[3]{0:T(128)S(1)} %pad_add_fusion.s_ref, s32[42,2,96]{2,1,0:T(2,128)S(1)} %copy-done.4), custom_call_target="tpu_custom_call" | custom-call | flops 1 | bytes 1 | tf_op jit(solution)/shard_map/pallas_call | solution.py:532
  15.8 0.7 shard_map.104
  16.5 1.9 %collective-permute-done.1.refs_2_ = bf16[42,6,2,256]{3,2,1,0:T(2,128)(2,1)} collective-permute-done((bf16[42,6,2,256]{3,2,1,0:T(2,128)(2,1)}, bf16[42,6,2,256]{3,2,1,0:T(2,128)(2,1)}, u32[]{:S(2)}, u32[]{:S(2)}) %collective-permute-start.1) | collective-permute-done | bytes 258080 | tf_op jit(solution)/shard_map/ppermute | solution.py:588
  18.4 2.0 %collective-permute-start.5 = (bf16[42,6,2,256]{3,2,1,0:T(2,128)(2,1)S(1)}, bf16[42,6,2,256]{3,2,1,0:T(2,128)(2,1)S(1)}, u32[]{:S(2)}, u32[]{:S(2)}) collective-permute-start(bf16[42,6,2,256]{3,2,1,0:T(2,128)(2,1)S(1)} %collective-permute-done.refs_1_), channel_id=1, source_target_pairs={{0,2},{1,3},{2,0},{3,1},{4,6},{5,7},{6,4},{7,5},{8,10},{9,11},{10,... | collective-permute-start | bytes 774152 | tf_op jit(solution)/shard_map/ppermute | solution.py:588
  20.5 0.2 slice.20
  20.7 1.6 %collective-permute-start.6 = (bf16[42,6,2,256]{3,2,1,0:T(2,128)(2,1)S(1)}, bf16[42,6,2,256]{3,2,1,0:T(2,128)(2,1)S(1)}, u32[]{:S(2)}, u32[]{:S(2)}) collective-permute-start(bf16[42,6,2,256]{3,2,1,0:T(2,128)(2,1)S(1)} %slice.20), channel_id=1, source_target_pairs={{0,28},{1,29},{2,30},{3,31},{4,0},{5,1},{6,2},{7,3},{8,4},{9,5},{1... | collective-permute-start | bytes 774152 | tf_op jit(solution)/shard_map/ppermute | solution.py:588
  22.3 1.6 %collective-permute-done.7.a2 = bf16[128,1024]{1,0:T(8,128)(2,1)S(1)} collective-permute-done((bf16[128,1024]{1,0:T(8,128)(2,1)}, bf16[128,1024]{1,0:T(8,128)(2,1)S(1)}, u32[]{:S(2)}, u32[]{:S(2)}) %collective-permute-start.7) | collective-permute-done | bytes 262176 | tf_op jit(solution)/shard_map/ppermute | solution.py:588
  24.0 4.8 %collective-permute-done.5.refs_3_ = bf16[42,6,2,256]{3,2,1,0:T(2,128)(2,1)S(1)} collective-permute-done((bf16[42,6,2,256]{3,2,1,0:T(2,128)(2,1)S(1)}, bf16[42,6,2,256]{3,2,1,0:T(2,128)(2,1)S(1)}, u32[]{:S(2)}, u32[]{:S(2)}) %collective-permute-start.5) | collective-permute-done | bytes 258080 | tf_op jit(solution)/shard_map/ppermute | solution.py:588
  28.7 1.7 %shard_map.106 = (bf16[576,256]{1,0:T(8,128)(2,1)S(1)}, bf16[576,256]{1,0:T(8,128)(2,1)S(1)}, bf16[2,576,256]{2,1,0:T(8,128)(2,1)S(1)}) custom-call(s32[3]{0:T(128)S(1)} %pad_add_fusion.s_ref, bf16[42,12,2,256]{3,2,1,0:T(2,128)(2,1)S(1)} %bitcast.10, bf16[42,6,2,256]{3,2,1,0:T(2,128)(2,1)S(1)} %collective-permute-done.refs_1_, ...), custom_call_target="tpu_custom_call" | custom-call | flops 1 | bytes 1 | tf_op jit(solution)/shard_map/pallas_call | solution.py:476
  30.4 0.1 collective-permute-start.8
  30.5 0.2 slice.21
  30.7 1.6 %collective-permute-start.9 = (bf16[42,6,2,256]{3,2,1,0:T(2,128)(2,1)S(1)}, bf16[42,6,2,256]{3,2,1,0:T(2,128)(2,1)S(1)}, u32[]{:S(2)}, u32[]{:S(2)}) collective-permute-start(bf16[42,6,2,256]{3,2,1,0:T(2,128)(2,1)S(1)} %slice.21), channel_id=1, source_target_pairs={{0,2},{1,3},{2,0},{3,1},{4,6},{5,7},{6,4},{7,5},{8,10},{9,11},{10,... | collective-permute-start | bytes 774152 | tf_op jit(solution)/shard_map/ppermute | solution.py:588
  32.3 0.5 collective-permute-start.10
  32.8 7.6 %shard_map.107 = (bf16[576,1024]{1,0:T(8,128)(2,1)S(1)}, bf16[6,576,256]{2,1,0:T(8,128)(2,1)S(1)}, bf16[288,512]{1,0:T(8,128)(2,1)S(1)}) custom-call(s32[1]{0:T(128)} %bitcast.2.t_ref, bf16[576,256]{1,0:T(8,128)(2,1)S(1)} %get-tuple-element.70.refs_0_, bf16[576,256]{1,0:T(8,128)(2,1)S(1)} %get-tuple-element.71.refs_1_, ...), custom_call_target="tpu_custom_call" | custom-call | flops 8000000000 | bytes 10000000 | tf_op jit(solution)/shard_map/pallas_call | solution.py:213
  40.4 1.6 %collective-permute-start.11 = (bf16[288,512]{1,0:T(8,128)(2,1)S(1)}, bf16[288,512]{1,0:T(8,128)(2,1)S(1)}, u32[]{:S(2)}, u32[]{:S(2)}) collective-permute-start(bf16[288,512]{1,0:T(8,128)(2,1)S(1)} %get-tuple-element.79.refs_6_.a_ref), channel_id=1, source_target_pairs={{0,2},{1,3},{2,0},{3,1},{4,6},{5,7},{6,4},{7,5},{8,10},{9,11},{10,... | collective-permute-start | bytes 884744 | tf_op jit(solution)/shard_map/ppermute | solution.py:588
  42.0 1.0 %shard_map.108.p_ref = f32[8,144,288]{2,1,0:T(8,128)S(1)} custom-call(bf16[6,576,256]{2,1,0:T(8,128)(2,1)S(1)} %get-tuple-element.103.qkv_ref, s32[576,1]{1,0:T(8,128)S(1)} %get-tuple-element.77.refs_5_.idk_ref.refs_9_, s32[4,1,288]{2,1,0:T(1,128)S(1)} %get-tuple-element.78.refs_6_.idq_ref), custom_call_target="tpu_custom_call" | custom-call | flops 1 | bytes 1 | tf_op jit(solution)/shard_map/pallas_call | solution.py:326
  43.1 2.2 %collective-permute-done.10.refs_3_ = bf16[42,6,2,256]{3,2,1,0:T(2,128)(2,1)S(1)} collective-permute-done((bf16[42,6,2,256]{3,2,1,0:T(2,128)(2,1)S(1)}, bf16[42,6,2,256]{3,2,1,0:T(2,128)(2,1)S(1)}, u32[]{:S(2)}, u32[]{:S(2)}) %collective-permute-start.10) | collective-permute-done | bytes 258080 | tf_op jit(solution)/shard_map/ppermute | solution.py:588
  45.3 2.7 %shard_map.109.refs_6_.b_ref = bf16[288,512]{1,0:T(8,128)(2,1)S(1)} custom-call(bf16[6,576,256]{2,1,0:T(8,128)(2,1)S(1)} %get-tuple-element.103.qkv_ref, s32[576,1]{1,0:T(8,128)S(1)} %get-tuple-element.77.refs_5_.idk_ref.refs_9_, s32[4,1,288]{2,1,0:T(1,128)S(1)} %get-tuple-element.78.refs_6_.idq_ref), custom_call_target="tpu_custom_call" | custom-call | flops 8000000000 | bytes 2000000 | tf_op jit(solution)/shard_map/pallas_call | solution.py:200
  48.0 3.2 %collective-permute-done.11.refs_7_ = bf16[288,512]{1,0:T(8,128)(2,1)S(1)} collective-permute-done((bf16[288,512]{1,0:T(8,128)(2,1)S(1)}, bf16[288,512]{1,0:T(8,128)(2,1)S(1)}, u32[]{:S(2)}, u32[]{:S(2)}) %collective-permute-start.11) | collective-permute-done | bytes 294944 | tf_op jit(solution)/shard_map/ppermute | solution.py:588
  51.2 1.3 %shard_map.110 = (bf16[576,256]{1,0:T(8,128)(2,1)S(1)}, bf16[576,256]{1,0:T(8,128)(2,1)S(1)}, bf16[2,576,256]{2,1,0:T(8,128)(2,1)S(1)}) custom-call(s32[3]{0:T(128)S(1)} %pad_add_fusion.s_ref, bf16[42,12,2,256]{3,2,1,0:T(2,128)(2,1)S(1)} %bitcast.13, bf16[42,6,2,256]{3,2,1,0:T(2,128)(2,1)S(1)} %collective-permute-done.6.refs_1_, ...), custom_call_target="tpu_custom_call" | custom-call | flops 1 | bytes 1 | tf_op jit(solution)/shard_map/pallas_call | solution.py:476
  52.5 0.1 collective-permute-start.13
  52.6 1.6 %collective-permute-start.14 = (bf16[288,512]{1,0:T(8,128)(2,1)S(1)}, bf16[288,512]{1,0:T(8,128)(2,1)S(1)}, u32[]{:S(2)}, u32[]{:S(2)}) collective-permute-start(bf16[288,512]{1,0:T(8,128)(2,1)S(1)} %shard_map.109.refs_6_.b_ref), channel_id=1, source_target_pairs={{0,2},{1,3},{2,0},{3,1},{4,6},{5,7},{6,4},{7,5},{8,10},{9,11},{10,... | collective-permute-start | bytes 884744 | tf_op jit(solution)/shard_map/ppermute | solution.py:588
  54.2 0.2 collective-permute-start.15
  54.3 0.3 collective-permute-start.16
  54.7 1.0 %shard_map.116.p_ref = f32[8,144,288]{2,1,0:T(8,128)S(1)} custom-call(bf16[6,576,256]{2,1,0:T(8,128)(2,1)S(1)} %get-tuple-element.103.qkv_ref, s32[576,1]{1,0:T(8,128)S(1)} %get-tuple-element.77.refs_5_.idk_ref.refs_9_, s32[4,1,288]{2,1,0:T(1,128)S(1)} %get-tuple-element.78.refs_6_.idq_ref), custom_call_target="tpu_custom_call" | custom-call | flops 1 | bytes 1 | tf_op jit(solution)/shard_map/pallas_call | solution.py:326
  55.7 0.0 copy-start.3
  55.7 0.0 copy-start.5
  55.7 0.8 shard_map.118
  56.6 0.1 copy-done.3
  56.8 2.1 %shard_map.111 = (bf16[1024,1024]{1,0:T(8,128)(2,1)S(1)}, f32[8,1024]{1,0:T(8,128)S(1)}) custom-call(s32[3]{0:T(128)S(1)} %pad_add_fusion.s_ref, bf16[256,1024]{1,0:T(8,128)(2,1)S(1)} %copy-done.3, bf16[256,1024]{1,0:T(8,128)(2,1)} %collective-permute-done.2.w1.pp_ref, bf16[128,1024]{1,0:T(8,128)(2,1)S(1)} %collective-permute-done.7.a2, ...), custom_call_target="tpu_custom_call" | custom-call | flops 1 | bytes 1 | tf_op jit(solution)/shard_map/pallas_call | solution.py:92
  58.8 0.9 %shard_map.112 = (bf16[144,256]{1,0:T(8,128)(2,1)S(1)}, bf16[144,256]{1,0:T(8,128)(2,1)S(1)}, bf16[144,256]{1,0:T(8,128)(2,1)S(1)}, bf16[144,256]{1,0:T(8,128)(2,1)S(1)}, bf16[288,1024]{1,0:T(8,128)(2,1)S(1)}) custom-call(s32[1]{0:T(128)} %bitcast.2.t_ref, bf16[576,256]{1,0:T(8,128)(2,1)S(1)} %get-tuple-element.70.refs_0_, ...), custom_call_target="tpu_custom_call" | custom-call | flops 1 | bytes 1 | tf_op jit(solution)/shard_map/pallas_call | solution.py:296
  59.8 3.2 %shard_map.113.g0_ref = bf16[6,288,256]{2,1,0:T(8,128)(2,1)S(1)} custom-call(bf16[288,1024]{1,0:T(8,128)(2,1)S(1)} %get-tuple-element.92.err_ref.e0_ref, bf16[1024,1024]{1,0:T(8,128)(2,1)S(1)} %get-tuple-element.91.refs_8_.wc_ref, bf16[6,576,256]{2,1,0:T(8,128)(2,1)S(1)} %get-tuple-element.103.qkv_ref, f32[8,144,288]{2,1,0:T(8,128)S(1)} %shard_map.108.p_ref), custom_call_target="tpu_custom_call" | custom-call | flops 1 | bytes 1 | tf_op jit(solution)/shard_map/pallas_call | solution.py:402
  63.0 1.0 %shard_map.114 = (bf16[288,256]{1,0:T(8,128)(2,1)S(1)}, bf16[288,256]{1,0:T(8,128)(2,1)S(1)}, bf16[288,256]{1,0:T(8,128)(2,1)S(1)}, bf16[288,256]{1,0:T(8,128)(2,1)S(1)}, bf16[288,1024]{1,0:T(8,128)(2,1)S(1)}) custom-call(s32[1]{0:T(128)} %bitcast.2.t_ref, bf16[576,256]{1,0:T(8,128)(2,1)S(1)} %get-tuple-element.70.refs_0_, ...), custom_call_target="tpu_custom_call" | custom-call | flops 1 | bytes 1 | tf_op jit(solution)/shard_map/pallas_call | solution.py:296
  64.0 0.1 collective-permute-start.17
  64.1 0.3 collective-permute-start.18
  64.3 0.1 collective-permute-start.19
  64.4 2.6 %shard_map.119 = f32[2,1024]{1,0:T(2,128)S(1)} custom-call(bf16[288,1024]{1,0:T(8,128)(2,1)S(1)} %get-tuple-element.92.err_ref.e0_ref, bf16[288,1024]{1,0:T(8,128)(2,1)S(1)} %get-tuple-element.102.err_ref.e1_ref, bf16[512,576]{1,0:T(8,128)(2,1)S(1)} %get-tuple-element.105.attn_t, bf16[256,1024]{1,0:T(8,128)(2,1)S(1)} %copy-done.3, ...), custom_call_target="tpu_custom_call" | custom-call | flops 1000000000 | bytes 3000000 | tf_op jit(solution)/shard_map/pallas_call | solution.py:359
  67.0 0.6 collective-permute-start.20
  67.6 3.2 %shard_map.117.g1_ref = bf16[6,288,256]{2,1,0:T(8,128)(2,1)S(1)} custom-call(bf16[288,1024]{1,0:T(8,128)(2,1)S(1)} %get-tuple-element.102.err_ref.e1_ref, bf16[1024,1024]{1,0:T(8,128)(2,1)S(1)} %get-tuple-element.91.refs_8_.wc_ref, bf16[6,576,256]{2,1,0:T(8,128)(2,1)S(1)} %get-tuple-element.103.qkv_ref, f32[8,144,288]{2,1,0:T(8,128)S(1)} %shard_map.116.p_ref), custom_call_target="tpu_custom_call" | custom-call | flops 8000000000 | bytes 10000000 | tf_op jit(solution)/shard_map/pallas_call | solution.py:402
  70.8 2.6 %collective-permute-done.17.a1 = bf16[288,256]{1,0:T(8,128)(2,1)S(1)} collective-permute-done((bf16[288,256]{1,0:T(8,128)(2,1)S(1)}, bf16[288,256]{1,0:T(8,128)(2,1)S(1)}, u32[]{:S(2)}, u32[]{:S(2)}) %collective-permute-start.17) | collective-permute-done | bytes 147488 | tf_op jit(solution)/shard_map/ppermute | solution.py:588
  73.4 1.7 %collective-permute-done.19.b1 = bf16[288,256]{1,0:T(8,128)(2,1)S(1)} collective-permute-done((bf16[288,256]{1,0:T(8,128)(2,1)S(1)}, bf16[288,256]{1,0:T(8,128)(2,1)S(1)}, u32[]{:S(2)}, u32[]{:S(2)}) %collective-permute-start.19) | collective-permute-done | bytes 147488 | tf_op jit(solution)/shard_map/ppermute | solution.py:588
  75.1 3.8 %shard_map.120 = (f32[2,768]{1,0:T(2,128)S(1)}, f32[2,768]{1,0:T(2,128)S(1)}) custom-call(bf16[6,288,256]{2,1,0:T(8,128)(2,1)S(1)} %shard_map.113.g0_ref, bf16[6,288,256]{2,1,0:T(8,128)(2,1)S(1)} %shard_map.117.g1_ref, bf16[1024,576]{1,0:T(8,128)(2,1)S(1)} %get-tuple-element.108.normed_t, bf16[3,1024,256]{2,1,0:T(8,128)(2,1)S(1)} %bitcast.16, ...), custom_call_target="tpu_custom_call" | custom-call | flops 4000000000 | bytes 8000000 | tf_op jit(solution)/shard_map/pallas_call | solution.py:432
  79.0 0.1 collective-permute-start.22
  79.1 1.9 %collective-permute-start.23 = (f32[2,1792]{1,0:T(2,128)S(1)}, f32[2,1792]{1,0:T(2,128)S(1)}, u32[]{:S(2)}, u32[]{:S(2)}) collective-permute-start(f32[2,1792]{1,0:T(2,128)S(1)} %get-tuple-element.121), channel_id=1, source_target_pairs={{0,5},{1,4},{2,7},{3,6},{4,1},{5,0},{6,3},{7,2},{8,13},{9,12},{10,... | collective-permute-start | bytes 43016 | tf_op jit(solution)/shard_map/ppermute | solution.py:594
  81.0 0.2 collective-permute-start.21
  81.2 1.6 %collective-permute-done.22 = f32[2,1792]{1,0:T(2,128)S(1)} collective-permute-done((f32[2,1792]{1,0:T(2,128)S(1)}, f32[2,1792]{1,0:T(2,128)S(1)}, u32[]{:S(2)}, u32[]{:S(2)}) %collective-permute-start.22) | collective-permute-done | bytes 14368 | tf_op jit(solution)/shard_map/ppermute | solution.py:594
  82.8 0.9 collective-permute-start.25
  83.7 0.1 collective-permute-start.26
  83.7 2.6 %collective-permute-start.24 = (f32[2,1792]{1,0:T(2,128)S(1)}, f32[2,1792]{1,0:T(2,128)S(1)}, u32[]{:S(2)}, u32[]{:S(2)}) collective-permute-start(f32[2,1792]{1,0:T(2,128)S(1)} %add_add_fusion.1), channel_id=1, source_target_pairs={{0,8},{1,9},{2,10},{3,11},{4,12},{5,13},{6,14},{7,15},{8,0},{9,1},... | collective-permute-start | bytes 43016 | tf_op jit(solution)/shard_map/ppermute | solution.py:594
  86.3 2.0 %shard_map.115 = bf16[42,12,2,256]{3,2,1,0:T(2,128)(2,1)} custom-call(s32[3]{0:T(128)S(1)} %pad_add_fusion.s_ref, bf16[288,256]{1,0:T(8,128)(2,1)S(1)} %get-tuple-element.98.a0, bf16[288,256]{1,0:T(8,128)(2,1)S(1)} %collective-permute-done.17.a1, bf16[288,256]{1,0:T(8,128)(2,1)S(1)} %collective-permute-done.18.b0, ...), custom_call_target="tpu_custom_call" | custom-call | flops 1 | bytes 1 | tf_op jit(solution)/shard_map/pallas_call | solution.py:571
  88.3 0.9 collective-permute-done.26
  89.2 0.6 slice.26
  89.8 0.6 slice.27
  (33 shorter events, 0.1 us)
Async XLA Ops:
  0.6 13.4 %copy-start.2 = (bf16[1024,3,256]{2,0,1:T(8,128)(2,1)S(1)}, bf16[1024,3,256]{2,0,1:T(8,128)(2,1)}, u32[]{:S(2)}) copy-start(bf16[1024,3,256]{2,0,1:T(8,128)(2,1)} %param.10) | copy-start | bytes 4718596
  0.6 13.4 %copy-start.6 = (f32[2,3,256]{2,0,1:T(2,128)S(1)}, f32[2,3,256]{2,0,1:T(2,128)}, u32[]{:S(2)}) copy-start(f32[2,3,256]{2,0,1:T(2,128)} %param.12) | copy-start | bytes 18436
  0.7 14.1 %copy-start.4 = (s32[42,2,96]{2,1,0:T(2,128)S(1)}, s32[42,2,96]{2,1,0:T(2,128)}, u32[]{:S(2)}) copy-start(s32[42,2,96]{2,1,0:T(2,128)} %ids_ref.1) | copy-start | bytes 96772
  3.0 12.8 %collective-permute-start.3 = (bf16[3,1024,256]{2,1,0:T(8,128)(2,1)}, bf16[3,1024,256]{2,1,0:T(8,128)(2,1)S(1)}, u32[]{:S(2)}, u32[]{:S(2)}) collective-permute-start(bf16[3,1024,256]{2,1,0:T(8,128)(2,1)} %bitcast.14), channel_id=1, source_target_pairs={{0,1},{1,0},{2,3},{3,2},{4,5},{5,4},{6,7},{7,6},{8,9},{9,8},{10,11... | collective-permute-start | bytes 4718600 | tf_op jit(solution)/shard_map/ppermute | solution.py:588
  3.5 15.0 %collective-permute-start.2 = (bf16[256,1024]{1,0:T(8,128)(2,1)}, bf16[256,1024]{1,0:T(8,128)(2,1)}, u32[]{:S(2)}, u32[]{:S(2)}) collective-permute-start(bf16[256,1024]{1,0:T(8,128)(2,1)} %po_ref), channel_id=1, source_target_pairs={{0,1},{1,0},{2,3},{3,2},{4,5},{5,4},{6,7},{7,6},{8,9},{9,8},{10,11... | collective-permute-start | bytes 1572872 | tf_op jit(solution)/shard_map/ppermute | solution.py:588
  3.6 13.0 %collective-permute-start = (bf16[42,6,2,256]{3,2,1,0:T(2,128)(2,1)}, bf16[42,6,2,256]{3,2,1,0:T(2,128)(2,1)S(1)}, u32[]{:S(2)}, u32[]{:S(2)}) collective-permute-start(bf16[42,6,2,256]{3,2,1,0:T(2,128)(2,1)} %get-tuple-element.58), channel_id=1, source_target_pairs={{0,28},{1,29},{2,30},{3,31},{4,0},{5,1},{6,2},{7,3},{8,4},{9,5},{1... | collective-permute-start | bytes 774152 | tf_op jit(solution)/shard_map/ppermute | solution.py:588
  9.5 8.9 %collective-permute-start.1 = (bf16[42,6,2,256]{3,2,1,0:T(2,128)(2,1)}, bf16[42,6,2,256]{3,2,1,0:T(2,128)(2,1)}, u32[]{:S(2)}, u32[]{:S(2)}) collective-permute-start(bf16[42,6,2,256]{3,2,1,0:T(2,128)(2,1)} %get-tuple-element.59), channel_id=1, source_target_pairs={{0,2},{1,3},{2,0},{3,1},{4,6},{5,7},{6,4},{7,5},{8,10},{9,11},{10,... | collective-permute-start | bytes 774152 | tf_op jit(solution)/shard_map/ppermute | solution.py:588
  11.1 2.3 %collective-permute-start.4 = (f32[3,2,256]{2,1,0:T(2,128)}, f32[3,2,256]{2,1,0:T(2,128)S(1)}, u32[]{:S(2)}, u32[]{:S(2)}) collective-permute-start(f32[3,2,256]{2,1,0:T(2,128)} %bitcast.17), channel_id=1, source_target_pairs={{0,1},{1,0},{2,3},{3,2},{4,5},{5,4},{6,7},{7,6},{8,9},{9,8},{10,11... | collective-permute-start | bytes 18440 | tf_op jit(solution)/shard_map/ppermute | solution.py:588
  13.4 10.6 %collective-permute-start.7 = (bf16[128,1024]{1,0:T(8,128)(2,1)}, bf16[128,1024]{1,0:T(8,128)(2,1)S(1)}, u32[]{:S(2)}, u32[]{:S(2)}) collective-permute-start(bf16[128,1024]{1,0:T(8,128)(2,1)} %constant_dynamic-slice_fusion), channel_id=1, source_target_pairs={{0,2},{1,3},{2,0},{3,1},{4,6},{5,7},{6,4},{7,5},{8,10},{9,11},{10,... | collective-permute-start | bytes 786440 | tf_op jit(solution)/shard_map/ppermute | solution.py:588
  14.0 6.5 %copy-start.1 = (bf16[42,2,12,256]{3,1,2,0:T(2,128)(2,1)S(1)}, bf16[42,2,12,256]{3,1,2,0:T(2,128)(2,1)}, u32[]{:S(2)}) copy-start(bf16[42,2,12,256]{3,1,2,0:T(2,128)(2,1)} %param.9) | copy-start | bytes 1548292
  14.0 14.7 %copy-start = (bf16[42,2,12,256]{3,1,2,0:T(2,128)(2,1)S(1)}, bf16[42,2,12,256]{3,1,2,0:T(2,128)(2,1)}, u32[]{:S(2)}) copy-start(bf16[42,2,12,256]{3,1,2,0:T(2,128)(2,1)} %param.8) | copy-start | bytes 1548292
  18.4 10.3 %collective-permute-start.5 = (bf16[42,6,2,256]{3,2,1,0:T(2,128)(2,1)S(1)}, bf16[42,6,2,256]{3,2,1,0:T(2,128)(2,1)S(1)}, u32[]{:S(2)}, u32[]{:S(2)}) collective-permute-start(bf16[42,6,2,256]{3,2,1,0:T(2,128)(2,1)S(1)} %collective-permute-done.refs_1_), channel_id=1, source_target_pairs={{0,2},{1,3},{2,0},{3,1},{4,6},{5,7},{6,4},{7,5},{8,10},{9,11},{10,... | collective-permute-start | bytes 774152 | tf_op jit(solution)/shard_map/ppermute | solution.py:588
  20.7 8.1 %collective-permute-start.6 = (bf16[42,6,2,256]{3,2,1,0:T(2,128)(2,1)S(1)}, bf16[42,6,2,256]{3,2,1,0:T(2,128)(2,1)S(1)}, u32[]{:S(2)}, u32[]{:S(2)}) collective-permute-start(bf16[42,6,2,256]{3,2,1,0:T(2,128)(2,1)S(1)} %slice.20), channel_id=1, source_target_pairs={{0,28},{1,29},{2,30},{3,31},{4,0},{5,1},{6,2},{7,3},{8,4},{9,5},{1... | collective-permute-start | bytes 774152 | tf_op jit(solution)/shard_map/ppermute | solution.py:588
  30.4 2.4 %collective-permute-start.8 = (bf16[2,576,256]{2,1,0:T(8,128)(2,1)S(1)}, bf16[2,576,256]{2,1,0:T(8,128)(2,1)S(1)}, u32[]{:S(2)}, u32[]{:S(2)}) collective-permute-start(bf16[2,576,256]{2,1,0:T(8,128)(2,1)S(1)} %get-tuple-element.72), channel_id=1, source_target_pairs={{0,1},{1,0},{2,3},{3,2},{4,5},{5,4},{6,7},{7,6},{8,9},{9,8},{10,11... | collective-permute-start | bytes 1769480 | tf_op jit(solution)/shard_map/ppermute | solution.py:588
  30.7 12.4 %collective-permute-start.9 = (bf16[42,6,2,256]{3,2,1,0:T(2,128)(2,1)S(1)}, bf16[42,6,2,256]{3,2,1,0:T(2,128)(2,1)S(1)}, u32[]{:S(2)}, u32[]{:S(2)}) collective-permute-start(bf16[42,6,2,256]{3,2,1,0:T(2,128)(2,1)S(1)} %slice.21), channel_id=1, source_target_pairs={{0,2},{1,3},{2,0},{3,1},{4,6},{5,7},{6,4},{7,5},{8,10},{9,11},{10,... | collective-permute-start | bytes 774152 | tf_op jit(solution)/shard_map/ppermute | solution.py:588
  32.3 13.0 %collective-permute-start.10 = (bf16[42,6,2,256]{3,2,1,0:T(2,128)(2,1)S(1)}, bf16[42,6,2,256]{3,2,1,0:T(2,128)(2,1)S(1)}, u32[]{:S(2)}, u32[]{:S(2)}) collective-permute-start(bf16[42,6,2,256]{3,2,1,0:T(2,128)(2,1)S(1)} %collective-permute-done.6.refs_1_), channel_id=1, source_target_pairs={{0,2},{1,3},{2,0},{3,1},{4,6},{5,7},{6,4},{7,5},{8,10},{9,11},{10,... | collective-permute-start | bytes 774152 | tf_op jit(solution)/shard_map/ppermute | solution.py:588
  32.8 12.5 %collective-permute-start.12 = (bf16[128,1024]{1,0:T(8,128)(2,1)S(1)}, bf16[128,1024]{1,0:T(8,128)(2,1)S(1)}, u32[]{:S(2)}, u32[]{:S(2)}) collective-permute-start(bf16[128,1024]{1,0:T(8,128)(2,1)S(1)} %collective-permute-done.7.a2), channel_id=1, source_target_pairs={{0,4},{1,5},{2,6},{3,7},{4,0},{5,1},{6,2},{7,3},{8,12},{9,13},{10,... | collective-permute-start | bytes 786440 | tf_op jit(solution)/shard_map/ppermute | solution.py:594
  40.4 10.8 %collective-permute-start.11 = (bf16[288,512]{1,0:T(8,128)(2,1)S(1)}, bf16[288,512]{1,0:T(8,128)(2,1)S(1)}, u32[]{:S(2)}, u32[]{:S(2)}) collective-permute-start(bf16[288,512]{1,0:T(8,128)(2,1)S(1)} %get-tuple-element.79.refs_6_.a_ref), channel_id=1, source_target_pairs={{0,2},{1,3},{2,0},{3,1},{4,6},{5,7},{6,4},{7,5},{8,10},{9,11},{10,... | collective-permute-start | bytes 884744 | tf_op jit(solution)/shard_map/ppermute | solution.py:588
  52.5 6.3 %collective-permute-start.13 = (bf16[2,576,256]{2,1,0:T(8,128)(2,1)S(1)}, bf16[2,576,256]{2,1,0:T(8,128)(2,1)S(1)}, u32[]{:S(2)}, u32[]{:S(2)}) collective-permute-start(bf16[2,576,256]{2,1,0:T(8,128)(2,1)S(1)} %get-tuple-element.87), channel_id=1, source_target_pairs={{0,1},{1,0},{2,3},{3,2},{4,5},{5,4},{6,7},{7,6},{8,9},{9,8},{10,11... | collective-permute-start | bytes 1769480 | tf_op jit(solution)/shard_map/ppermute | solution.py:588
  52.6 10.4 %collective-permute-start.14 = (bf16[288,512]{1,0:T(8,128)(2,1)S(1)}, bf16[288,512]{1,0:T(8,128)(2,1)S(1)}, u32[]{:S(2)}, u32[]{:S(2)}) collective-permute-start(bf16[288,512]{1,0:T(8,128)(2,1)S(1)} %shard_map.109.refs_6_.b_ref), channel_id=1, source_target_pairs={{0,2},{1,3},{2,0},{3,1},{4,6},{5,7},{6,4},{7,5},{8,10},{9,11},{10,... | collective-permute-start | bytes 884744 | tf_op jit(solution)/shard_map/ppermute | solution.py:588
  54.2 2.4 %collective-permute-start.15 = (bf16[128,1024]{1,0:T(8,128)(2,1)S(1)}, bf16[128,1024]{1,0:T(8,128)(2,1)S(1)}, u32[]{:S(2)}, u32[]{:S(2)}) collective-permute-start(bf16[128,1024]{1,0:T(8,128)(2,1)S(1)} %collective-permute-done.7.a2), channel_id=1, source_target_pairs={{0,1},{1,0},{2,3},{3,2},{4,5},{5,4},{6,7},{7,6},{8,9},{9,8},{10,11... | collective-permute-start | bytes 786440 | tf_op jit(solution)/shard_map/ppermute | solution.py:588
  54.3 2.3 %collective-permute-start.16 = (bf16[128,1024]{1,0:T(8,128)(2,1)S(1)}, bf16[128,1024]{1,0:T(8,128)(2,1)S(1)}, u32[]{:S(2)}, u32[]{:S(2)}) collective-permute-start(bf16[128,1024]{1,0:T(8,128)(2,1)S(1)} %collective-permute-done.12.b2), channel_id=1, source_target_pairs={{0,1},{1,0},{2,3},{3,2},{4,5},{5,4},{6,7},{7,6},{8,9},{9,8},{10,11... | collective-permute-start | bytes 786440 | tf_op jit(solution)/shard_map/ppermute | solution.py:588
  55.7 1.0 %copy-start.3 = (bf16[256,1024]{1,0:T(8,128)(2,1)S(1)}, bf16[256,1024]{1,0:T(8,128)(2,1)}, u32[]{:S(2)}) copy-start(bf16[256,1024]{1,0:T(8,128)(2,1)} %po_ref) | copy-start | bytes 1572868
  55.7 1.0 %copy-start.5 = (f32[2,1024]{1,0:T(2,128)S(1)}, f32[2,1024]{1,0:T(2,128)}, u32[]{:S(2)}) copy-start(f32[2,1024]{1,0:T(2,128)} %c_ref.1) | copy-start | bytes 24580
  64.0 9.4 %collective-permute-start.17 = (bf16[288,256]{1,0:T(8,128)(2,1)S(1)}, bf16[288,256]{1,0:T(8,128)(2,1)S(1)}, u32[]{:S(2)}, u32[]{:S(2)}) collective-permute-start(bf16[288,256]{1,0:T(8,128)(2,1)S(1)} %get-tuple-element.99), channel_id=1, source_target_pairs={{0,4},{1,5},{2,6},{3,7},{4,8},{5,9},{6,10},{7,11},{8,12},{9,13},{1... | collective-permute-start | bytes 442376 | tf_op jit(solution)/shard_map/ppermute | solution.py:588
  64.1 9.4 %collective-permute-start.18 = (bf16[288,256]{1,0:T(8,128)(2,1)S(1)}, bf16[288,256]{1,0:T(8,128)(2,1)S(1)}, u32[]{:S(2)}, u32[]{:S(2)}) collective-permute-start(bf16[288,256]{1,0:T(8,128)(2,1)S(1)} %get-tuple-element.100), channel_id=1, source_target_pairs={{0,1},{1,0},{2,3},{3,2},{4,5},{5,4},{6,7},{7,6},{8,9},{9,8},{10,11... | collective-permute-start | bytes 442376 | tf_op jit(solution)/shard_map/ppermute | solution.py:588
  64.3 10.8 %collective-permute-start.19 = (bf16[288,256]{1,0:T(8,128)(2,1)S(1)}, bf16[288,256]{1,0:T(8,128)(2,1)S(1)}, u32[]{:S(2)}, u32[]{:S(2)}) collective-permute-start(bf16[288,256]{1,0:T(8,128)(2,1)S(1)} %get-tuple-element.101), channel_id=1, source_target_pairs={{0,5},{1,4},{2,7},{3,6},{4,9},{5,8},{6,11},{7,10},{8,13},{9,12},{1... | collective-permute-start | bytes 442376 | tf_op jit(solution)/shard_map/ppermute | solution.py:588
  67.0 3.8 %collective-permute-start.20 = (f32[2,1024]{1,0:T(2,128)S(1)}, f32[2,1024]{1,0:T(2,128)S(1)}, u32[]{:S(2)}, u32[]{:S(2)}) collective-permute-start(f32[2,1024]{1,0:T(2,128)S(1)} %shard_map.119), channel_id=1, source_target_pairs={{0,2},{1,3},{2,0},{3,1},{4,6},{5,7},{6,4},{7,5},{8,10},{9,11},{10,... | collective-permute-start | bytes 24584 | tf_op jit(solution)/shard_map/ppermute | solution.py:588
  79.0 3.8 %collective-permute-start.22 = (f32[2,1792]{1,0:T(2,128)S(1)}, f32[2,1792]{1,0:T(2,128)S(1)}, u32[]{:S(2)}, u32[]{:S(2)}) collective-permute-start(f32[2,1792]{1,0:T(2,128)S(1)} %get-tuple-element.122), channel_id=1, source_target_pairs={{0,4},{1,5},{2,6},{3,7},{4,0},{5,1},{6,2},{7,3},{8,12},{9,13},{10,... | collective-permute-start | bytes 43016 | tf_op jit(solution)/shard_map/ppermute | solution.py:594
  79.1 3.7 %collective-permute-start.23 = (f32[2,1792]{1,0:T(2,128)S(1)}, f32[2,1792]{1,0:T(2,128)S(1)}, u32[]{:S(2)}, u32[]{:S(2)}) collective-permute-start(f32[2,1792]{1,0:T(2,128)S(1)} %get-tuple-element.121), channel_id=1, source_target_pairs={{0,5},{1,4},{2,7},{3,6},{4,1},{5,0},{6,3},{7,2},{8,13},{9,12},{10,... | collective-permute-start | bytes 43016 | tf_op jit(solution)/shard_map/ppermute | solution.py:594
  81.0 1.8 %collective-permute-start.21 = (f32[2,1792]{1,0:T(2,128)S(1)}, f32[2,1792]{1,0:T(2,128)S(1)}, u32[]{:S(2)}, u32[]{:S(2)}) collective-permute-start(f32[2,1792]{1,0:T(2,128)S(1)} %get-tuple-element.121), channel_id=1, source_target_pairs={{0,1},{1,0},{2,3},{3,2},{4,5},{5,4},{6,7},{7,6},{8,9},{9,8},{10,11... | collective-permute-start | bytes 43016 | tf_op jit(solution)/shard_map/ppermute | solution.py:588
  82.8 5.5 %collective-permute-start.25 = (f32[2,1792]{1,0:T(2,128)S(1)}, f32[2,1792]{1,0:T(2,128)S(1)}, u32[]{:S(2)}, u32[]{:S(2)}) collective-permute-start(f32[2,1792]{1,0:T(2,128)S(1)} %add_add_fusion.1), channel_id=1, source_target_pairs={{0,16},{1,17},{2,18},{3,19},{4,20},{5,21},{6,22},{7,23},{8,24},{9,... | collective-permute-start | bytes 43016 | tf_op jit(solution)/shard_map/ppermute | solution.py:594
  83.7 5.5 %collective-permute-start.26 = (f32[2,1792]{1,0:T(2,128)S(1)}, f32[2,1792]{1,0:T(2,128)S(1)}, u32[]{:S(2)}, u32[]{:S(2)}) collective-permute-start(f32[2,1792]{1,0:T(2,128)S(1)} %add_add_fusion.1), channel_id=1, source_target_pairs={{0,24},{1,25},{2,26},{3,27},{4,28},{5,29},{6,30},{7,31},{8,16},{9,... | collective-permute-start | bytes 43016 | tf_op jit(solution)/shard_map/ppermute | solution.py:594
  83.7 5.4 %collective-permute-start.24 = (f32[2,1792]{1,0:T(2,128)S(1)}, f32[2,1792]{1,0:T(2,128)S(1)}, u32[]{:S(2)}, u32[]{:S(2)}) collective-permute-start(f32[2,1792]{1,0:T(2,128)S(1)} %add_add_fusion.1), channel_id=1, source_target_pairs={{0,8},{1,9},{2,10},{3,11},{4,12},{5,13},{6,14},{7,15},{8,0},{9,1},... | collective-permute-start | bytes 43016 | tf_op jit(solution)/shard_map/ppermute | solution.py:594

commit v6 on v5

--- a/solution.py
+++ b/solution.py
@@ -256,9 +256,9 @@
 
 
 def output_kernel(group, t_ref, *refs):
-    pieces, targets = blocks(refs[:3]), blocks(refs[3:6])
-    own_ref, other_ref, wc_ref, idk_ref = refs[6:10]
-    before, refs = refs[10 : 10 + 4 * group], refs[10 + 4 * group :]
+    pieces, targets = blocks(refs[:3]), refs[3:7]
+    own_ref, other_ref, wc_ref, idk_ref = refs[7:11]
+    before, refs = refs[11 : 11 + 4 * group], refs[11 + 4 * group :]
     mixed, err_ref, y_ref = refs[:4], refs[4], refs[5]
     t = t_ref[0]
     n, width = pieces[0].shape
@@ -296,7 +296,7 @@
     return pl.pallas_call(
         functools.partial(output_kernel, group),
         out_shape=(piece, piece, piece, piece, jax.ShapeDtypeStruct((n // 2, 4 * width), BF)),
-        in_specs=[pl.BlockSpec(memory_space=pltpu.SMEM)] + spec(10 + len(before)),
+        in_specs=[pl.BlockSpec(memory_space=pltpu.SMEM)] + spec(11 + len(before)),
         out_specs=tuple(spec(5)),
         scratch_shapes=[pltpu.VMEM((n // 2, width), F32)],
         compiler_params=params(20),
@@ -410,33 +410,30 @@
     )(err, wc, qkv, probs)
 
 
-def qkv_sums_kernel(g0_ref, g1_ref, normed_t, wo_ref, wp_ref, bo_ref, bp_ref, own_ref, peer_ref):
+def qkv_sums_kernel(side, g0_ref, g1_ref, normed_t, w_ref, b_ref, to_ref):
     width = g0_ref.shape[2]
 
     def qkv_part(i, carry):
-        for g, (w_ref, b_ref, to_ref) in enumerate(
-            ((wo_ref, bo_ref, own_ref), (wp_ref, bp_ref, peer_ref))
-        ):
-            cells = jnp.concatenate([g0_ref[3 * g + i], g1_ref[3 * g + i]], axis=0)
-            grad = jnp.dot(normed_t[...], cells, preferred_element_type=F32)
-            hi, lo = masked_sums(grad, w_ref[i].astype(F32), b_ref[i])
-            to_ref[0:1, pl.ds(pl.multiple_of(i * width, width), width)] = hi
-            to_ref[1:2, pl.ds(pl.multiple_of(i * width, width), width)] = lo
+        cells = jnp.concatenate([g0_ref[3 * side + i], g1_ref[3 * side + i]], axis=0)
+        grad = jnp.dot(normed_t[...], cells, preferred_element_type=F32)
+        hi, lo = masked_sums(grad, w_ref[i].astype(F32), b_ref[i])
+        to_ref[0:1, pl.ds(pl.multiple_of(i * width, width), width)] = hi
+        to_ref[1:2, pl.ds(pl.multiple_of(i * width, width), width)] = lo
         return carry
 
     lax.fori_loop(0, 3, qkv_part, 0)
 
 
-def qkv_sums(g, normed_t, wo, wp, bo, bp):
+def qkv_sums(side, g, normed_t, w, b):
     width = g[0].shape[2]
     return pl.pallas_call(
-        qkv_sums_kernel,
-        out_shape=(jax.ShapeDtypeStruct((2, 3 * width), F32),) * 2,
-        in_specs=spec(7),
-        out_specs=tuple(spec(2)),
+        functools.partial(qkv_sums_kernel, side),
+        out_shape=jax.ShapeDtypeStruct((2, 3 * width), F32),
+        in_specs=spec(5),
+        out_specs=spec(1)[0],
         compiler_params=params(20),
-        cost_estimate=pl.CostEstimate(flops=4 * 10**9, bytes_accessed=8 * 10**6, transcendentals=0),
-    )(*g, normed_t, wo, wp, bo, bp)
+        cost_estimate=LARGE,
+    )(*g, normed_t, w, b)
 
 
 def split_kernel(s_ref, *refs):
@@ -625,16 +622,17 @@
     place = jnp.stack([shift_offset[0], t % 2, sector]).astype(jnp.int32)
 
     f_raw, t_raw = (jnp.transpose(block, (0, 2, 1, 3)) for block in (features, target))
-    f_low, f_up, w_qkv, w_proj = lax.optimization_barrier((f_raw[:, :half], f_raw[:, half:], w_qkv, w_proj))
+    f_low, w_qkv, w_proj = lax.optimization_barrier((f_raw[:, :half], w_qkv, w_proj))
+    f_up_y = send(after(f_raw, f_low)[:, half:], 0, 2)
     f_low = send(f_low, -1, 0)
-    f_up_y = send(f_up, 0, 2)
 
     w3 = jnp.transpose(w_qkv, (1, 0, 2))
     c3 = jnp.transpose(qkv_clip, (1, 0, 2))
     w3_peer = send(w3, 0, 1)
     c3_peer = send(c3, 0, 1)
     share = w_proj.shape[0] // 2
-    slab = send(lax.dynamic_slice_in_dim(w_proj, share * (sector % 2), share, 0), 0, 2)
+    slab = after(w_proj, c3_peer)
+    slab = send(lax.dynamic_slice_in_dim(slab, share * (sector % 2), share, 0), 0, 2)
     w1 = send(w_proj, 0, 1)
     wc_own, b_own = clip_qkv(w3, c3)
     wc_peer, b_peer = clip_qkv(w3_peer, c3_peer)
@@ -644,23 +642,22 @@
     )
     f_low_y = send(f_low, 0, 2)
     t_low = send(after(t_raw, f_low)[:, :half], -1, 0)
-    f_low_y, t_low, slab = lax.optimization_barrier((f_low_y, t_low, slab))
+    t_own, t_away = split(place, t_raw, t_low)
+    t_away = t_away.reshape(t_own.shape)
+    t_1 = send(t_away, 0, 1)
+    f_low_y, t_own, t_away, slab = lax.optimization_barrier((f_low_y, t_own, t_away, slab))
     x_0, x_2, x_away = split(place, f_raw, f_low, f_up_y, f_low_y)
     pieces = (x_0, x_2, send(x_away, 0, 1))
 
-    t_up = after(t_raw, f_low_y)[:, half:]
-    t_up_y, t_low_y = send(t_up, 0, 2), send(t_low, 0, 2)
+    targets = (t_own, t_1, send(t_own, 0, 2), send(t_away, 0, 3))
     more = swap(slab, 1, 0)
 
     normed, qkv, attn_0 = forward(t_arr, pieces, wc_own, wc_peer, idk, idq)
     other_0 = send(attn_0, 0, 2)
     probs_0 = probs_of(0, qkv, idk, idq)
-    attn_1 = last_windows(after(qkv, probs_0, t_up_y, t_low_y, more), idk, idq)
+    attn_1 = last_windows(after(qkv, probs_0, *targets, more), idk, idq)
     slab_3, more_3 = send(after(slab, attn_1), 0, 1), send(after(more, attn_1), 0, 1)
     pc, pb = clip_proj(place, [w_proj, w1, slab, more, slab_3, more_3], proj_clip)
-    t_up_y, t_low_y = lax.optimization_barrier((t_up_y, t_low_y, other_0, attn_1))[:2]
-    t_0, t_2, t_away = split(place, t_raw, t_low, t_up_y, t_low_y)
-    targets = (t_0, t_2, send(t_away, 0, 1))
     other_1 = send(attn_1, 0, 2)
     normed_t, attn_t = turn(normed, (attn_0, attn_1))
     probs = (probs_0, probs_of(1, after(qkv, attn_1), idk, idq))
@@ -674,13 +671,15 @@
     m11 = send(m11, 1, 1)
     proj = proj_sums((err_0, err_1), attn_t, w_proj, w1, pb)
     proj_y = send(proj, 0, 2)
-    grads_1 = backward(1, err_1, pc, qkv, probs[1])
-    grads_1 = after(grads_1, m01, m10, m11, proj_y)
-    grads = (grads_0, grads_1)
-    own, peer = qkv_sums(grads, normed_t, w3, w3_peer, b_own, b_peer)
+    grads = (grads_0, backward(1, err_1, pc, qkv, probs[1]))
+    peer = qkv_sums(1, grads, normed_t, w3_peer, b_peer)
     proj = proj + proj_y
-    own, peer = jnp.concatenate([own, proj], axis=1), jnp.concatenate([peer, proj], axis=1)
-    sums = added([own, send(peer, 0, 1), swap(own, 1, 0), swap(peer, 1, 1)])
+    peer = jnp.concatenate([peer, proj], axis=1)
+    terms = [send(peer, 0, 1), swap(peer, 1, 1)]
+    grads = lax.optimization_barrier((*grads, m01, m10, m11, peer))[:2]
+    own = qkv_sums(0, grads, normed_t, w3, b_own)
+    own = jnp.concatenate([own, proj], axis=1)
+    sums = added([own, terms[0], swap(own, 1, 0), terms[1]])
     sums = added(lat_terms(sums, 2))
     mixed = join(place, [m00, m10, m01, m11], rows, lon, lev)
     return (mixed, sums[:, : 3 * width].reshape(2, 3, width), sums[:, 3 * width :])

time: 90.7 us -> 90.3 us (level)
    ppermute x21, waiting for transfers between devices: 18.2 us -> 16.4 us  [send(): return lax.ppermute(block, ('lat', 'tp'), route)]
    ppermute x6, starting transfers between devices: 5.54 us -> 7.25 us  [swap(): return lax.ppermute(block, ('lat', 'tp'), route)]
    ppermute x21, starting transfers between devices: 19.4 us -> 17.7 us  [send(): return lax.ppermute(block, ('lat', 'tp'), route)]
    slice x2, local copies, waits for them, and re-layouts: 2.56 us -> 3.77 us  [the longest x1 1.94 us: local(): f_raw[:, :half]]
    ppermute x6, waiting for transfers between devices: 2.45 us -> 3.66 us  [swap(): return lax.ppermute(block, ('lat', 'tp'), route)]
    pallas_call x1 -> x2, Pallas kernels: 3.85 us -> 3.61 us  [qkv_sums(): pl.pallas_call(functools.partial(qkv_sums_kernel, side), out_shape=jax.Sh...]
  transfers between devices with their start and end apart: 27 -> 27, of which waited for: 9 -> 11; matrix products, arithmetic and copies ran while one was open for 2% -> 3% of each run, Pallas kernels for 33% -> 38%
where the time goes in v6:
time: 90.3 us; the launch traced here: 89.9 us
  Pallas kernels  36.8 us (41%)
  starting transfers between devices  25 us (28%)
  waiting for transfers between devices  20.1 us (22%)
  local copies, waits for them, and re-layouts  6.3 us (7%)
  between operations  1.62 us (2%)
    ppermute x21, starting transfers between devices, send(): return lax.ppermute(block, ('lat', 'tp'), route)  17.7 us
    ppermute x21, waiting for transfers between devices, send(): return lax.ppermute(block, ('lat', 'tp'), route)  16.4 us
    pallas_call x1, Pallas kernels, forward(): pl.pallas_call(forward_kernel, out_shape=(jax.ShapeDtypeStruct((n, d), BF...  7.62 us
    ppermute x6, starting transfers between devices, swap(): return lax.ppermute(block, ('lat', 'tp'), route)  7.25 us
    pallas_call x2, Pallas kernels, backward(): pl.pallas_call(functools.partial(backward_kernel, group), out_shape=jax.S...  6.44 us
    ppermute x6, waiting for transfers between devices, swap(): return lax.ppermute(block, ('lat', 'tp'), route)  3.66 us
    pallas_call x2, Pallas kernels, qkv_sums(): pl.pallas_call(functools.partial(qkv_sums_kernel, side), out_shape=jax.Sh...  3.61 us
    pallas_call x1, Pallas kernels, last_windows(): pl.pallas_call(last_kernel, out_shape=jax.ShapeDtypeStruct((n // 2, 2 * w...  2.66 us
  transfers between devices with their start and end apart: 27, of which 11 were waited for; matrix products, arithmetic and copies ran while one was open for 3% of the time, Pallas kernels for 38%

profile of v6, /device:TPU:0, one launch (start us, length us, event | category | flops | bytes accessed | tf_op | source)
XLA Modules:
  0.0 89.9 jit_solution(15603555124201031063)
XLA Ops:
  0.6 0.0 copy-start.1
  0.7 1.9 %slice.20 = bf16[42,6,2,256]{3,2,1,0:T(2,128)(2,1)} slice(bf16[42,12,2,256]{3,2,1,0:T(2,128)(2,1)} %bitcast.10), slice={[0:42], [0:6], [0:2], [0:256]} | slice | bytes 516096 | tf_op jit(solution)/shard_map/slice | solution.py:625
  2.6 0.5 collective-permute-start.3
  3.1 0.1 collective-permute-start.2
  3.1 6.0 %collective-permute-start = (bf16[42,6,2,256]{3,2,1,0:T(2,128)(2,1)}, bf16[42,6,2,256]{3,2,1,0:T(2,128)(2,1)S(1)}, u32[]{:S(2)}, u32[]{:S(2)}) collective-permute-start(bf16[42,6,2,256]{3,2,1,0:T(2,128)(2,1)} %slice.20), channel_id=1, source_target_pairs={{0,28},{1,29},{2,30},{3,31},{4,0},{5,1},{6,2},{7,3},{8,4},{9,5},{1... | collective-permute-start | bytes 774152 | tf_op jit(solution)/shard_map/ppermute | solution.py:585
  9.1 1.8 %slice.16 = bf16[42,6,2,256]{3,2,1,0:T(2,128)(2,1)} slice(bf16[42,12,2,256]{3,2,1,0:T(2,128)(2,1)} %bitcast.11), slice={[0:42], [6:12], [0:2], [0:256]} | slice | bytes 516096 | tf_op jit(solution)/shard_map/slice | solution.py:626
  10.9 1.5 %collective-permute-start.1 = (bf16[42,6,2,256]{3,2,1,0:T(2,128)(2,1)}, bf16[42,6,2,256]{3,2,1,0:T(2,128)(2,1)}, u32[]{:S(2)}, u32[]{:S(2)}) collective-permute-start(bf16[42,6,2,256]{3,2,1,0:T(2,128)(2,1)} %slice.16), channel_id=1, source_target_pairs={{0,2},{1,3},{2,0},{3,1},{4,6},{5,7},{6,4},{7,5},{8,10},{9,11},{10,... | collective-permute-start | bytes 774152 | tf_op jit(solution)/shard_map/ppermute | solution.py:585
  13.1 0.7 collective-permute-done.4.c_ref
  13.8 1.0 %constant_dynamic-slice_fusion = bf16[128,1024]{1,0:T(8,128)(2,1)S(1)} fusion(bf16[256,1024]{1,0:T(8,128)(2,1)} %po_ref, s32[]{:T(128)S(6)} %select_n.16), kind=kLoop, calls=%fused_computation.5 | loop fusion | bytes 524292 | tf_op jit(solution)/shard_map/dynamic_slice | solution.py:635
  14.8 0.6 collective-permute-start.7
  15.4 0.1 pad_add_fusion.s_ref
  15.5 0.7 shard_map.103
  16.2 0.0 copy-start
  16.2 1.0 %shard_map.105 = (s32[576,1]{1,0:T(8,128)S(1)}, s32[4,1,288]{2,1,0:T(1,128)S(1)}) custom-call(s32[3]{0:T(128)S(1)} %pad_add_fusion.s_ref, s32[42,2,96]{2,1,0:T(2,128)S(1)} %copy-done.4), custom_call_target="tpu_custom_call" | custom-call | flops 1 | bytes 1 | tf_op jit(solution)/shard_map/pallas_call | solution.py:529
  17.2 0.7 shard_map.104
  17.9 2.4 %collective-permute-done.1.refs_2_ = bf16[42,6,2,256]{3,2,1,0:T(2,128)(2,1)} collective-permute-done((bf16[42,6,2,256]{3,2,1,0:T(2,128)(2,1)}, bf16[42,6,2,256]{3,2,1,0:T(2,128)(2,1)}, u32[]{:S(2)}, u32[]{:S(2)}) %collective-permute-start.1) | collective-permute-done | bytes 258080 | tf_op jit(solution)/shard_map/ppermute | solution.py:585
  20.4 0.2 slice.17
  20.6 0.6 collective-permute-start.6
  21.1 1.5 %collective-permute-start.5 = (bf16[42,6,2,256]{3,2,1,0:T(2,128)(2,1)S(1)}, bf16[42,6,2,256]{3,2,1,0:T(2,128)(2,1)S(1)}, u32[]{:S(2)}, u32[]{:S(2)}) collective-permute-start(bf16[42,6,2,256]{3,2,1,0:T(2,128)(2,1)S(1)} %collective-permute-done.refs_1_), channel_id=1, source_target_pairs={{0,2},{1,3},{2,0},{3,1},{4,6},{5,7},{6,4},{7,5},{8,10},{9,11},{10,... | collective-permute-start | bytes 774152 | tf_op jit(solution)/shard_map/ppermute | solution.py:585
  22.7 4.3 %collective-permute-done.6.refs_1_ = bf16[42,6,2,256]{3,2,1,0:T(2,128)(2,1)S(1)} collective-permute-done((bf16[42,6,2,256]{3,2,1,0:T(2,128)(2,1)S(1)}, bf16[42,6,2,256]{3,2,1,0:T(2,128)(2,1)S(1)}, u32[]{:S(2)}, u32[]{:S(2)}) %collective-permute-start.6) | collective-permute-done | bytes 258080 | tf_op jit(solution)/shard_map/ppermute | solution.py:585
  26.9 1.0 %shard_map.106 = (bf16[576,256]{1,0:T(8,128)(2,1)S(1)}, bf16[1,576,256]{2,1,0:T(8,128)(2,1)S(1)}) custom-call(s32[3]{0:T(128)S(1)} %pad_add_fusion.s_ref, bf16[42,12,2,256]{3,2,1,0:T(2,128)(2,1)S(1)} %bitcast.17, bf16[42,6,2,256]{3,2,1,0:T(2,128)(2,1)S(1)} %collective-permute-done.6.refs_1_), custom_call_target="tpu_custom_call" | custom-call | flops 1 | bytes 1 | tf_op jit(solution)/shard_map/pallas_call | solution.py:473
  27.9 2.2 %collective-permute-done.5.refs_3_ = bf16[42,6,2,256]{3,2,1,0:T(2,128)(2,1)S(1)} collective-permute-done((bf16[42,6,2,256]{3,2,1,0:T(2,128)(2,1)S(1)}, bf16[42,6,2,256]{3,2,1,0:T(2,128)(2,1)S(1)}, u32[]{:S(2)}, u32[]{:S(2)}) %collective-permute-start.5) | collective-permute-done | bytes 258080 | tf_op jit(solution)/shard_map/ppermute | solution.py:585
  30.1 1.7 %shard_map.107 = (bf16[576,256]{1,0:T(8,128)(2,1)S(1)}, bf16[576,256]{1,0:T(8,128)(2,1)S(1)}, bf16[2,576,256]{2,1,0:T(8,128)(2,1)S(1)}) custom-call(s32[3]{0:T(128)S(1)} %pad_add_fusion.s_ref, bf16[42,12,2,256]{3,2,1,0:T(2,128)(2,1)S(1)} %bitcast.12, bf16[42,6,2,256]{3,2,1,0:T(2,128)(2,1)S(1)} %collective-permute-done.refs_1_, ...), custom_call_target="tpu_custom_call" | custom-call | flops 1 | bytes 1 | tf_op jit(solution)/shard_map/pallas_call | solution.py:473
  31.8 0.1 collective-permute-start.8
  31.9 0.5 collective-permute-start.9
  32.4 1.5 %collective-permute-start.10 = (bf16[576,256]{1,0:T(8,128)(2,1)S(1)}, bf16[576,256]{1,0:T(8,128)(2,1)S(1)}, u32[]{:S(2)}, u32[]{:S(2)}) collective-permute-start(bf16[576,256]{1,0:T(8,128)(2,1)S(1)} %get-tuple-element.73.refs_3_), channel_id=1, source_target_pairs={{0,2},{1,3},{2,0},{3,1},{4,6},{5,7},{6,4},{7,5},{8,10},{9,11},{10,... | collective-permute-start | bytes 884744 | tf_op jit(solution)/shard_map/ppermute | solution.py:585
  33.9 7.6 %shard_map.108 = (bf16[576,1024]{1,0:T(8,128)(2,1)S(1)}, bf16[6,576,256]{2,1,0:T(8,128)(2,1)S(1)}, bf16[288,512]{1,0:T(8,128)(2,1)S(1)}) custom-call(s32[1]{0:T(128)} %bitcast.2.t_ref, bf16[576,256]{1,0:T(8,128)(2,1)S(1)} %get-tuple-element.70.refs_0_, bf16[576,256]{1,0:T(8,128)(2,1)S(1)} %get-tuple-element.71.refs_1_, ...), custom_call_target="tpu_custom_call" | custom-call | flops 8000000000 | bytes 10000000 | tf_op jit(solution)/shard_map/pallas_call | solution.py:213
  41.6 1.0 %shard_map.109.p_ref = f32[8,144,288]{2,1,0:T(8,128)S(1)} custom-call(bf16[6,576,256]{2,1,0:T(8,128)(2,1)S(1)} %get-tuple-element.98.qkv_ref, s32[576,1]{1,0:T(8,128)S(1)} %get-tuple-element.77.refs_5_.idk_ref.refs_10_, s32[4,1,288]{2,1,0:T(1,128)S(1)} %get-tuple-element.78.refs_6_.idq_ref), custom_call_target="tpu_custom_call" | custom-call | flops 1 | bytes 1 | tf_op jit(solution)/shard_map/pallas_call | solution.py:326
  42.6 0.2 collective-permute-done.12.b2
  42.8 4.1 %collective-permute-done.11.refs_6_ = bf16[576,256]{1,0:T(8,128)(2,1)S(1)} collective-permute-done((bf16[576,256]{1,0:T(8,128)(2,1)S(1)}, bf16[576,256]{1,0:T(8,128)(2,1)S(1)}, u32[]{:S(2)}, u32[]{:S(2)}) %collective-permute-start.11) | collective-permute-done | bytes 294944 | tf_op jit(solution)/shard_map/ppermute | solution.py:585
  46.8 1.5 %collective-permute-start.14 = (bf16[288,512]{1,0:T(8,128)(2,1)S(1)}, bf16[288,512]{1,0:T(8,128)(2,1)S(1)}, u32[]{:S(2)}, u32[]{:S(2)}) collective-permute-start(bf16[288,512]{1,0:T(8,128)(2,1)S(1)} %get-tuple-element.82.refs_7_.a_ref), channel_id=1, source_target_pairs={{0,2},{1,3},{2,0},{3,1},{4,6},{5,7},{6,4},{7,5},{8,10},{9,11},{10,... | collective-permute-start | bytes 884744 | tf_op jit(solution)/shard_map/ppermute | solution.py:585
  48.4 2.7 %shard_map.110.refs_7_.b_ref = bf16[288,512]{1,0:T(8,128)(2,1)S(1)} custom-call(bf16[6,576,256]{2,1,0:T(8,128)(2,1)S(1)} %get-tuple-element.98.qkv_ref, s32[576,1]{1,0:T(8,128)S(1)} %get-tuple-element.77.refs_5_.idk_ref.refs_10_, s32[4,1,288]{2,1,0:T(1,128)S(1)} %get-tuple-element.78.refs_6_.idq_ref), custom_call_target="tpu_custom_call" | custom-call | flops 8000000000 | bytes 2000000 | tf_op jit(solution)/shard_map/pallas_call | solution.py:200
  51.0 0.6 collective-permute-start.13
  51.6 0.2 collective-permute-start.15
  51.7 0.4 collective-permute-start.16
  52.1 1.0 %shard_map.116.p_ref = f32[8,144,288]{2,1,0:T(8,128)S(1)} custom-call(bf16[6,576,256]{2,1,0:T(8,128)(2,1)S(1)} %get-tuple-element.98.qkv_ref, s32[576,1]{1,0:T(8,128)S(1)} %get-tuple-element.77.refs_5_.idk_ref.refs_10_, s32[4,1,288]{2,1,0:T(1,128)S(1)} %get-tuple-element.78.refs_6_.idq_ref), custom_call_target="tpu_custom_call" | custom-call | flops 1 | bytes 1 | tf_op jit(solution)/shard_map/pallas_call | solution.py:326
  53.2 0.8 shard_map.118
  54.0 0.1 copy-done.2
  54.2 2.1 %shard_map.111 = (bf16[1024,1024]{1,0:T(8,128)(2,1)S(1)}, f32[8,1024]{1,0:T(8,128)S(1)}) custom-call(s32[3]{0:T(128)S(1)} %pad_add_fusion.s_ref, bf16[256,1024]{1,0:T(8,128)(2,1)S(1)} %copy-done.2, bf16[256,1024]{1,0:T(8,128)(2,1)} %collective-permute-done.2.w1.pp_ref, bf16[128,1024]{1,0:T(8,128)(2,1)S(1)} %collective-permute-done.7.a2, ...), custom_call_target="tpu_custom_call" | custom-call | flops 1 | bytes 1 | tf_op jit(solution)/shard_map/pallas_call | solution.py:92
  56.2 0.5 collective-permute-done.14.refs_8_
  56.7 0.9 %shard_map.112 = (bf16[144,256]{1,0:T(8,128)(2,1)S(1)}, bf16[144,256]{1,0:T(8,128)(2,1)S(1)}, bf16[144,256]{1,0:T(8,128)(2,1)S(1)}, bf16[144,256]{1,0:T(8,128)(2,1)S(1)}, bf16[288,1024]{1,0:T(8,128)(2,1)S(1)}) custom-call(s32[1]{0:T(128)} %bitcast.2.t_ref, bf16[576,256]{1,0:T(8,128)(2,1)S(1)} %get-tuple-element.70.refs_0_, ...), custom_call_target="tpu_custom_call" | custom-call | flops 1 | bytes 1 | tf_op jit(solution)/shard_map/pallas_call | solution.py:296
  57.7 3.2 %shard_map.113.g0_ref = bf16[6,288,256]{2,1,0:T(8,128)(2,1)S(1)} custom-call(bf16[288,1024]{1,0:T(8,128)(2,1)S(1)} %get-tuple-element.87.err_ref.e0_ref, bf16[1024,1024]{1,0:T(8,128)(2,1)S(1)} %get-tuple-element.86.refs_9_.wc_ref, bf16[6,576,256]{2,1,0:T(8,128)(2,1)S(1)} %get-tuple-element.98.qkv_ref, f32[8,144,288]{2,1,0:T(8,128)S(1)} %shard_map.109.p_ref), custom_call_target="tpu_custom_call" | custom-call | flops 1 | bytes 1 | tf_op jit(solution)/shard_map/pallas_call | solution.py:402
  60.9 1.9 %collective-permute-done.13.refs_8_ = bf16[288,512]{1,0:T(8,128)(2,1)S(1)} collective-permute-done((bf16[288,512]{1,0:T(8,128)(2,1)S(1)}, bf16[288,512]{1,0:T(8,128)(2,1)S(1)}, u32[]{:S(2)}, u32[]{:S(2)}) %collective-permute-start.13) | collective-permute-done | bytes 294944 | tf_op jit(solution)/shard_map/ppermute | solution.py:585
  62.8 1.0 %shard_map.114 = (bf16[288,256]{1,0:T(8,128)(2,1)S(1)}, bf16[288,256]{1,0:T(8,128)(2,1)S(1)}, bf16[288,256]{1,0:T(8,128)(2,1)S(1)}, bf16[288,256]{1,0:T(8,128)(2,1)S(1)}, bf16[288,1024]{1,0:T(8,128)(2,1)S(1)}) custom-call(s32[1]{0:T(128)} %bitcast.2.t_ref, bf16[576,256]{1,0:T(8,128)(2,1)S(1)} %get-tuple-element.70.refs_0_, ...), custom_call_target="tpu_custom_call" | custom-call | flops 1 | bytes 1 | tf_op jit(solution)/shard_map/pallas_call | solution.py:296
  63.7 0.1 collective-permute-start.17
  63.8 0.1 collective-permute-start.18
  63.9 0.2 collective-permute-start.19
  64.1 3.2 %shard_map.117.g1_ref = bf16[6,288,256]{2,1,0:T(8,128)(2,1)S(1)} custom-call(bf16[288,1024]{1,0:T(8,128)(2,1)S(1)} %get-tuple-element.97.err_ref.e1_ref, bf16[1024,1024]{1,0:T(8,128)(2,1)S(1)} %get-tuple-element.86.refs_9_.wc_ref, bf16[6,576,256]{2,1,0:T(8,128)(2,1)S(1)} %get-tuple-element.98.qkv_ref, f32[8,144,288]{2,1,0:T(8,128)S(1)} %shard_map.116.p_ref), custom_call_target="tpu_custom_call" | custom-call | flops 8000000000 | bytes 10000000 | tf_op jit(solution)/shard_map/pallas_call | solution.py:402
  67.3 2.6 %shard_map.120 = f32[2,1024]{1,0:T(2,128)S(1)} custom-call(bf16[288,1024]{1,0:T(8,128)(2,1)S(1)} %get-tuple-element.87.err_ref.e0_ref, bf16[288,1024]{1,0:T(8,128)(2,1)S(1)} %get-tuple-element.97.err_ref.e1_ref, bf16[512,576]{1,0:T(8,128)(2,1)S(1)} %get-tuple-element.102.attn_t, bf16[256,1024]{1,0:T(8,128)(2,1)S(1)} %copy-done.2, ...), custom_call_target="tpu_custom_call" | custom-call | flops 1000000000 | bytes 3000000 | tf_op jit(solution)/shard_map/pallas_call | solution.py:359
  70.0 1.6 %collective-permute-start.20 = (f32[2,1024]{1,0:T(2,128)S(1)}, f32[2,1024]{1,0:T(2,128)S(1)}, u32[]{:S(2)}, u32[]{:S(2)}) collective-permute-start(f32[2,1024]{1,0:T(2,128)S(1)} %shard_map.120), channel_id=1, source_target_pairs={{0,2},{1,3},{2,0},{3,1},{4,6},{5,7},{6,4},{7,5},{8,10},{9,11},{10,... | collective-permute-start | bytes 24584 | tf_op jit(solution)/shard_map/ppermute | solution.py:585
  71.5 1.8 %shard_map.119 = f32[2,768]{1,0:T(2,128)S(1)} custom-call(bf16[6,288,256]{2,1,0:T(8,128)(2,1)S(1)} %shard_map.113.g0_ref, bf16[6,288,256]{2,1,0:T(8,128)(2,1)S(1)} %shard_map.117.g1_ref, bf16[1024,576]{1,0:T(8,128)(2,1)S(1)} %get-tuple-element.100.normed_t, bf16[3,1024,256]{2,1,0:T(8,128)(2,1)S(1)} %collective-permute-done.3.w_ref, ...), custom_call_target="tpu_custom_call" | custom-call | flops 8000000000 | bytes 10000000 | tf_op jit(solution)/shard_map/pallas_call | solution.py:429
  73.4 0.3 collective-permute-done.20
  73.7 0.1 collective-permute-start.23
  73.8 0.4 collective-permute-start.21
  74.2 1.8 %shard_map.121 = f32[2,768]{1,0:T(2,128)S(1)} custom-call(bf16[6,288,256]{2,1,0:T(8,128)(2,1)S(1)} %shard_map.113.g0_ref, bf16[6,288,256]{2,1,0:T(8,128)(2,1)S(1)} %shard_map.117.g1_ref, bf16[1024,576]{1,0:T(8,128)(2,1)S(1)} %get-tuple-element.100.normed_t, bf16[3,1024,256]{2,1,0:T(8,128)(2,1)S(1)} %bitcast.15, f32[3,8,256]{2,1,0:T(8,128)S(1)} %get-tuple-element.106.b_ref), custom_call_target="tpu_custom_call" | custom-call | flops 8000000000 | bytes 10000000 | tf_op jit(solution)/shard_map/pallas_call | solution.py:429
  76.0 1.8 %collective-permute-start.22 = (f32[2,1792]{1,0:T(2,128)S(1)}, f32[2,1792]{1,0:T(2,128)S(1)}, u32[]{:S(2)}, u32[]{:S(2)}) collective-permute-start(f32[2,1792]{1,0:T(2,128)S(1)} %pad_maximum_fusion.1), channel_id=1, source_target_pairs={{0,4},{1,5},{2,6},{3,7},{4,0},{5,1},{6,2},{7,3},{8,12},{9,13},{10,... | collective-permute-start | bytes 43016 | tf_op jit(solution)/shard_map/ppermute | solution.py:591
  77.8 2.1 %collective-permute-done.22 = f32[2,1792]{1,0:T(2,128)S(1)} collective-permute-done((f32[2,1792]{1,0:T(2,128)S(1)}, f32[2,1792]{1,0:T(2,128)S(1)}, u32[]{:S(2)}, u32[]{:S(2)}) %collective-permute-start.22) | collective-permute-done | bytes 14368 | tf_op jit(solution)/shard_map/ppermute | solution.py:591
  79.9 3.3 %collective-permute-start.25 = (f32[2,1792]{1,0:T(2,128)S(1)}, f32[2,1792]{1,0:T(2,128)S(1)}, u32[]{:S(2)}, u32[]{:S(2)}) collective-permute-start(f32[2,1792]{1,0:T(2,128)S(1)} %add_add_fusion.1), channel_id=1, source_target_pairs={{0,16},{1,17},{2,18},{3,19},{4,20},{5,21},{6,22},{7,23},{8,24},{9,... | collective-permute-start | bytes 43016 | tf_op jit(solution)/shard_map/ppermute | solution.py:591
  83.2 1.6 %collective-permute-start.26 = (f32[2,1792]{1,0:T(2,128)S(1)}, f32[2,1792]{1,0:T(2,128)S(1)}, u32[]{:S(2)}, u32[]{:S(2)}) collective-permute-start(f32[2,1792]{1,0:T(2,128)S(1)} %add_add_fusion.1), channel_id=1, source_target_pairs={{0,24},{1,25},{2,26},{3,27},{4,28},{5,29},{6,30},{7,31},{8,16},{9,... | collective-permute-start | bytes 43016 | tf_op jit(solution)/shard_map/ppermute | solution.py:591
  84.8 0.5 collective-permute-start.24
  85.3 2.0 %shard_map.115 = bf16[42,12,2,256]{3,2,1,0:T(2,128)(2,1)} custom-call(s32[3]{0:T(128)S(1)} %pad_add_fusion.s_ref, bf16[288,256]{1,0:T(8,128)(2,1)S(1)} %get-tuple-element.93.a0, bf16[288,256]{1,0:T(8,128)(2,1)S(1)} %collective-permute-done.17.a1, bf16[288,256]{1,0:T(8,128)(2,1)S(1)} %collective-permute-done.18.b0, ...), custom_call_target="tpu_custom_call" | custom-call | flops 1 | bytes 1 | tf_op jit(solution)/shard_map/pallas_call | solution.py:568
  87.3 1.4 %collective-permute-done.26 = f32[2,1792]{1,0:T(2,128)S(1)} collective-permute-done((f32[2,1792]{1,0:T(2,128)S(1)}, f32[2,1792]{1,0:T(2,128)S(1)}, u32[]{:S(2)}, u32[]{:S(2)}) %collective-permute-start.26) | collective-permute-done | bytes 14368 | tf_op jit(solution)/shard_map/ppermute | solution.py:591
  88.7 0.6 slice.21
  89.3 0.6 slice.22
  (35 shorter events, 0.1 us)
Async XLA Ops:
  0.6 14.8 %copy-start.1 = (bf16[1024,3,256]{2,0,1:T(8,128)(2,1)S(1)}, bf16[1024,3,256]{2,0,1:T(8,128)(2,1)}, u32[]{:S(2)}) copy-start(bf16[1024,3,256]{2,0,1:T(8,128)(2,1)} %param.10) | copy-start | bytes 4718596
  0.6 14.8 %copy-start.6 = (f32[2,3,256]{2,0,1:T(2,128)S(1)}, f32[2,3,256]{2,0,1:T(2,128)}, u32[]{:S(2)}) copy-start(f32[2,3,256]{2,0,1:T(2,128)} %param.12) | copy-start | bytes 18436
  0.7 15.5 %copy-start.4 = (s32[42,2,96]{2,1,0:T(2,128)S(1)}, s32[42,2,96]{2,1,0:T(2,128)}, u32[]{:S(2)}) copy-start(s32[42,2,96]{2,1,0:T(2,128)} %ids_ref.1) | copy-start | bytes 96772
  2.6 14.6 %collective-permute-start.3 = (bf16[3,1024,256]{2,1,0:T(8,128)(2,1)}, bf16[3,1024,256]{2,1,0:T(8,128)(2,1)S(1)}, u32[]{:S(2)}, u32[]{:S(2)}) collective-permute-start(bf16[3,1024,256]{2,1,0:T(8,128)(2,1)} %bitcast.13), channel_id=1, source_target_pairs={{0,1},{1,0},{2,3},{3,2},{4,5},{5,4},{6,7},{7,6},{8,9},{9,8},{10,11... | collective-permute-start | bytes 4718600 | tf_op jit(solution)/shard_map/ppermute | solution.py:585
  3.1 17.3 %collective-permute-start.2 = (bf16[256,1024]{1,0:T(8,128)(2,1)}, bf16[256,1024]{1,0:T(8,128)(2,1)}, u32[]{:S(2)}, u32[]{:S(2)}) collective-permute-start(bf16[256,1024]{1,0:T(8,128)(2,1)} %po_ref), channel_id=1, source_target_pairs={{0,1},{1,0},{2,3},{3,2},{4,5},{5,4},{6,7},{7,6},{8,9},{9,8},{10,11... | collective-permute-start | bytes 1572872 | tf_op jit(solution)/shard_map/ppermute | solution.py:585
  3.1 14.8 %collective-permute-start = (bf16[42,6,2,256]{3,2,1,0:T(2,128)(2,1)}, bf16[42,6,2,256]{3,2,1,0:T(2,128)(2,1)S(1)}, u32[]{:S(2)}, u32[]{:S(2)}) collective-permute-start(bf16[42,6,2,256]{3,2,1,0:T(2,128)(2,1)} %slice.20), channel_id=1, source_target_pairs={{0,28},{1,29},{2,30},{3,31},{4,0},{5,1},{6,2},{7,3},{8,4},{9,5},{1... | collective-permute-start | bytes 774152 | tf_op jit(solution)/shard_map/ppermute | solution.py:585
  10.9 9.4 %collective-permute-start.1 = (bf16[42,6,2,256]{3,2,1,0:T(2,128)(2,1)}, bf16[42,6,2,256]{3,2,1,0:T(2,128)(2,1)}, u32[]{:S(2)}, u32[]{:S(2)}) collective-permute-start(bf16[42,6,2,256]{3,2,1,0:T(2,128)(2,1)} %slice.16), channel_id=1, source_target_pairs={{0,2},{1,3},{2,0},{3,1},{4,6},{5,7},{6,4},{7,5},{8,10},{9,11},{10,... | collective-permute-start | bytes 774152 | tf_op jit(solution)/shard_map/ppermute | solution.py:585
  12.4 1.4 %collective-permute-start.4 = (f32[3,2,256]{2,1,0:T(2,128)}, f32[3,2,256]{2,1,0:T(2,128)S(1)}, u32[]{:S(2)}, u32[]{:S(2)}) collective-permute-start(f32[3,2,256]{2,1,0:T(2,128)} %bitcast.18), channel_id=1, source_target_pairs={{0,1},{1,0},{2,3},{3,2},{4,5},{5,4},{6,7},{7,6},{8,9},{9,8},{10,11... | collective-permute-start | bytes 18440 | tf_op jit(solution)/shard_map/ppermute | solution.py:585
  14.8 13.1 %collective-permute-start.7 = (bf16[128,1024]{1,0:T(8,128)(2,1)S(1)}, bf16[128,1024]{1,0:T(8,128)(2,1)S(1)}, u32[]{:S(2)}, u32[]{:S(2)}) collective-permute-start(bf16[128,1024]{1,0:T(8,128)(2,1)S(1)} %constant_dynamic-slice_fusion), channel_id=1, source_target_pairs={{0,2},{1,3},{2,0},{3,1},{4,6},{5,7},{6,4},{7,5},{8,10},{9,11},{10,... | collective-permute-start | bytes 786440 | tf_op jit(solution)/shard_map/ppermute | solution.py:585
  15.4 4.9 %copy-start.3 = (bf16[42,2,12,256]{3,1,2,0:T(2,128)(2,1)S(1)}, bf16[42,2,12,256]{3,1,2,0:T(2,128)(2,1)}, u32[]{:S(2)}) copy-start(bf16[42,2,12,256]{3,1,2,0:T(2,128)(2,1)} %param.9) | copy-start | bytes 1548292
  16.2 14.0 %copy-start = (bf16[42,2,12,256]{3,1,2,0:T(2,128)(2,1)S(1)}, bf16[42,2,12,256]{3,1,2,0:T(2,128)(2,1)}, u32[]{:S(2)}) copy-start(bf16[42,2,12,256]{3,1,2,0:T(2,128)(2,1)} %param.8) | copy-start | bytes 1548292
  20.6 6.4 %collective-permute-start.6 = (bf16[42,6,2,256]{3,2,1,0:T(2,128)(2,1)S(1)}, bf16[42,6,2,256]{3,2,1,0:T(2,128)(2,1)S(1)}, u32[]{:S(2)}, u32[]{:S(2)}) collective-permute-start(bf16[42,6,2,256]{3,2,1,0:T(2,128)(2,1)S(1)} %slice.17), channel_id=1, source_target_pairs={{0,28},{1,29},{2,30},{3,31},{4,0},{5,1},{6,2},{7,3},{8,4},{9,5},{1... | collective-permute-start | bytes 774152 | tf_op jit(solution)/shard_map/ppermute | solution.py:585
  21.1 9.0 %collective-permute-start.5 = (bf16[42,6,2,256]{3,2,1,0:T(2,128)(2,1)S(1)}, bf16[42,6,2,256]{3,2,1,0:T(2,128)(2,1)S(1)}, u32[]{:S(2)}, u32[]{:S(2)}) collective-permute-start(bf16[42,6,2,256]{3,2,1,0:T(2,128)(2,1)S(1)} %collective-permute-done.refs_1_), channel_id=1, source_target_pairs={{0,2},{1,3},{2,0},{3,1},{4,6},{5,7},{6,4},{7,5},{8,10},{9,11},{10,... | collective-permute-start | bytes 774152 | tf_op jit(solution)/shard_map/ppermute | solution.py:585
  31.8 2.1 %collective-permute-start.8 = (bf16[2,576,256]{2,1,0:T(8,128)(2,1)S(1)}, bf16[2,576,256]{2,1,0:T(8,128)(2,1)S(1)}, u32[]{:S(2)}, u32[]{:S(2)}) collective-permute-start(bf16[2,576,256]{2,1,0:T(8,128)(2,1)S(1)} %get-tuple-element.72), channel_id=1, source_target_pairs={{0,1},{1,0},{2,3},{3,2},{4,5},{5,4},{6,7},{7,6},{8,9},{9,8},{10,11... | collective-permute-start | bytes 1769480 | tf_op jit(solution)/shard_map/ppermute | solution.py:585
  31.9 10.9 %collective-permute-start.9 = (bf16[576,256]{1,0:T(8,128)(2,1)S(1)}, bf16[576,256]{1,0:T(8,128)(2,1)S(1)}, u32[]{:S(2)}, u32[]{:S(2)}) collective-permute-start(bf16[576,256]{1,0:T(8,128)(2,1)S(1)} %bitcast.20), channel_id=1, source_target_pairs={{0,1},{1,0},{2,3},{3,2},{4,5},{5,4},{6,7},{7,6},{8,9},{9,8},{10,11... | collective-permute-start | bytes 884744 | tf_op jit(solution)/shard_map/ppermute | solution.py:585
  32.4 10.4 %collective-permute-start.10 = (bf16[576,256]{1,0:T(8,128)(2,1)S(1)}, bf16[576,256]{1,0:T(8,128)(2,1)S(1)}, u32[]{:S(2)}, u32[]{:S(2)}) collective-permute-start(bf16[576,256]{1,0:T(8,128)(2,1)S(1)} %get-tuple-element.73.refs_3_), channel_id=1, source_target_pairs={{0,2},{1,3},{2,0},{3,1},{4,6},{5,7},{6,4},{7,5},{8,10},{9,11},{10,... | collective-permute-start | bytes 884744 | tf_op jit(solution)/shard_map/ppermute | solution.py:585
  33.9 12.9 %collective-permute-start.11 = (bf16[576,256]{1,0:T(8,128)(2,1)S(1)}, bf16[576,256]{1,0:T(8,128)(2,1)S(1)}, u32[]{:S(2)}, u32[]{:S(2)}) collective-permute-start(bf16[576,256]{1,0:T(8,128)(2,1)S(1)} %bitcast.21), channel_id=1, source_target_pairs={{0,3},{1,2},{2,1},{3,0},{4,7},{5,6},{6,5},{7,4},{8,11},{9,10},{10,... | collective-permute-start | bytes 884744 | tf_op jit(solution)/shard_map/ppermute | solution.py:585
  33.9 8.8 %collective-permute-start.12 = (bf16[128,1024]{1,0:T(8,128)(2,1)S(1)}, bf16[128,1024]{1,0:T(8,128)(2,1)S(1)}, u32[]{:S(2)}, u32[]{:S(2)}) collective-permute-start(bf16[128,1024]{1,0:T(8,128)(2,1)S(1)} %collective-permute-done.7.a2), channel_id=1, source_target_pairs={{0,4},{1,5},{2,6},{3,7},{4,0},{5,1},{6,2},{7,3},{8,12},{9,13},{10,... | collective-permute-start | bytes 786440 | tf_op jit(solution)/shard_map/ppermute | solution.py:591
  46.8 9.9 %collective-permute-start.14 = (bf16[288,512]{1,0:T(8,128)(2,1)S(1)}, bf16[288,512]{1,0:T(8,128)(2,1)S(1)}, u32[]{:S(2)}, u32[]{:S(2)}) collective-permute-start(bf16[288,512]{1,0:T(8,128)(2,1)S(1)} %get-tuple-element.82.refs_7_.a_ref), channel_id=1, source_target_pairs={{0,2},{1,3},{2,0},{3,1},{4,6},{5,7},{6,4},{7,5},{8,10},{9,11},{10,... | collective-permute-start | bytes 884744 | tf_op jit(solution)/shard_map/ppermute | solution.py:585
  51.0 11.7 %collective-permute-start.13 = (bf16[288,512]{1,0:T(8,128)(2,1)S(1)}, bf16[288,512]{1,0:T(8,128)(2,1)S(1)}, u32[]{:S(2)}, u32[]{:S(2)}) collective-permute-start(bf16[288,512]{1,0:T(8,128)(2,1)S(1)} %shard_map.110.refs_7_.b_ref), channel_id=1, source_target_pairs={{0,2},{1,3},{2,0},{3,1},{4,6},{5,7},{6,4},{7,5},{8,10},{9,11},{10,... | collective-permute-start | bytes 884744 | tf_op jit(solution)/shard_map/ppermute | solution.py:585
  51.6 2.4 %collective-permute-start.15 = (bf16[128,1024]{1,0:T(8,128)(2,1)S(1)}, bf16[128,1024]{1,0:T(8,128)(2,1)S(1)}, u32[]{:S(2)}, u32[]{:S(2)}) collective-permute-start(bf16[128,1024]{1,0:T(8,128)(2,1)S(1)} %collective-permute-done.7.a2), channel_id=1, source_target_pairs={{0,1},{1,0},{2,3},{3,2},{4,5},{5,4},{6,7},{7,6},{8,9},{9,8},{10,11... | collective-permute-start | bytes 786440 | tf_op jit(solution)/shard_map/ppermute | solution.py:585
  51.7 2.3 %collective-permute-start.16 = (bf16[128,1024]{1,0:T(8,128)(2,1)S(1)}, bf16[128,1024]{1,0:T(8,128)(2,1)S(1)}, u32[]{:S(2)}, u32[]{:S(2)}) collective-permute-start(bf16[128,1024]{1,0:T(8,128)(2,1)S(1)} %collective-permute-done.12.b2), channel_id=1, source_target_pairs={{0,1},{1,0},{2,3},{3,2},{4,5},{5,4},{6,7},{7,6},{8,9},{9,8},{10,11... | collective-permute-start | bytes 786440 | tf_op jit(solution)/shard_map/ppermute | solution.py:585
  53.1 1.0 %copy-start.2 = (bf16[256,1024]{1,0:T(8,128)(2,1)S(1)}, bf16[256,1024]{1,0:T(8,128)(2,1)}, u32[]{:S(2)}) copy-start(bf16[256,1024]{1,0:T(8,128)(2,1)} %po_ref) | copy-start | bytes 1572868
  53.1 1.0 %copy-start.5 = (f32[2,1024]{1,0:T(2,128)S(1)}, f32[2,1024]{1,0:T(2,128)}, u32[]{:S(2)}) copy-start(f32[2,1024]{1,0:T(2,128)} %c_ref.1) | copy-start | bytes 24580
  63.7 10.5 %collective-permute-start.17 = (bf16[288,256]{1,0:T(8,128)(2,1)S(1)}, bf16[288,256]{1,0:T(8,128)(2,1)S(1)}, u32[]{:S(2)}, u32[]{:S(2)}) collective-permute-start(bf16[288,256]{1,0:T(8,128)(2,1)S(1)} %get-tuple-element.94), channel_id=1, source_target_pairs={{0,4},{1,5},{2,6},{3,7},{4,8},{5,9},{6,10},{7,11},{8,12},{9,13},{1... | collective-permute-start | bytes 442376 | tf_op jit(solution)/shard_map/ppermute | solution.py:585
  63.8 10.4 %collective-permute-start.18 = (bf16[288,256]{1,0:T(8,128)(2,1)S(1)}, bf16[288,256]{1,0:T(8,128)(2,1)S(1)}, u32[]{:S(2)}, u32[]{:S(2)}) collective-permute-start(bf16[288,256]{1,0:T(8,128)(2,1)S(1)} %get-tuple-element.95), channel_id=1, source_target_pairs={{0,1},{1,0},{2,3},{3,2},{4,5},{5,4},{6,7},{7,6},{8,9},{9,8},{10,11... | collective-permute-start | bytes 442376 | tf_op jit(solution)/shard_map/ppermute | solution.py:585
  63.9 10.3 %collective-permute-start.19 = (bf16[288,256]{1,0:T(8,128)(2,1)S(1)}, bf16[288,256]{1,0:T(8,128)(2,1)S(1)}, u32[]{:S(2)}, u32[]{:S(2)}) collective-permute-start(bf16[288,256]{1,0:T(8,128)(2,1)S(1)} %get-tuple-element.96), channel_id=1, source_target_pairs={{0,5},{1,4},{2,7},{3,6},{4,9},{5,8},{6,11},{7,10},{8,13},{9,12},{1... | collective-permute-start | bytes 442376 | tf_op jit(solution)/shard_map/ppermute | solution.py:585
  70.0 3.7 %collective-permute-start.20 = (f32[2,1024]{1,0:T(2,128)S(1)}, f32[2,1024]{1,0:T(2,128)S(1)}, u32[]{:S(2)}, u32[]{:S(2)}) collective-permute-start(f32[2,1024]{1,0:T(2,128)S(1)} %shard_map.120), channel_id=1, source_target_pairs={{0,2},{1,3},{2,0},{3,1},{4,6},{5,7},{6,4},{7,5},{8,10},{9,11},{10,... | collective-permute-start | bytes 24584 | tf_op jit(solution)/shard_map/ppermute | solution.py:585
  73.7 4.1 %collective-permute-start.23 = (f32[2,1792]{1,0:T(2,128)S(1)}, f32[2,1792]{1,0:T(2,128)S(1)}, u32[]{:S(2)}, u32[]{:S(2)}) collective-permute-start(f32[2,1792]{1,0:T(2,128)S(1)} %pad_maximum_fusion), channel_id=1, source_target_pairs={{0,5},{1,4},{2,7},{3,6},{4,1},{5,0},{6,3},{7,2},{8,13},{9,12},{10,... | collective-permute-start | bytes 43016 | tf_op jit(solution)/shard_map/ppermute | solution.py:591
  73.8 4.0 %collective-permute-start.21 = (f32[2,1792]{1,0:T(2,128)S(1)}, f32[2,1792]{1,0:T(2,128)S(1)}, u32[]{:S(2)}, u32[]{:S(2)}) collective-permute-start(f32[2,1792]{1,0:T(2,128)S(1)} %pad_maximum_fusion), channel_id=1, source_target_pairs={{0,1},{1,0},{2,3},{3,2},{4,5},{5,4},{6,7},{7,6},{8,9},{9,8},{10,11... | collective-permute-start | bytes 43016 | tf_op jit(solution)/shard_map/ppermute | solution.py:585
  76.0 3.8 %collective-permute-start.22 = (f32[2,1792]{1,0:T(2,128)S(1)}, f32[2,1792]{1,0:T(2,128)S(1)}, u32[]{:S(2)}, u32[]{:S(2)}) collective-permute-start(f32[2,1792]{1,0:T(2,128)S(1)} %pad_maximum_fusion.1), channel_id=1, source_target_pairs={{0,4},{1,5},{2,6},{3,7},{4,0},{5,1},{6,2},{7,3},{8,12},{9,13},{10,... | collective-permute-start | bytes 43016 | tf_op jit(solution)/shard_map/ppermute | solution.py:591
  79.9 7.4 %collective-permute-start.25 = (f32[2,1792]{1,0:T(2,128)S(1)}, f32[2,1792]{1,0:T(2,128)S(1)}, u32[]{:S(2)}, u32[]{:S(2)}) collective-permute-start(f32[2,1792]{1,0:T(2,128)S(1)} %add_add_fusion.1), channel_id=1, source_target_pairs={{0,16},{1,17},{2,18},{3,19},{4,20},{5,21},{6,22},{7,23},{8,24},{9,... | collective-permute-start | bytes 43016 | tf_op jit(solution)/shard_map/ppermute | solution.py:591
  83.2 5.5 %collective-permute-start.26 = (f32[2,1792]{1,0:T(2,128)S(1)}, f32[2,1792]{1,0:T(2,128)S(1)}, u32[]{:S(2)}, u32[]{:S(2)}) collective-permute-start(f32[2,1792]{1,0:T(2,128)S(1)} %add_add_fusion.1), channel_id=1, source_target_pairs={{0,24},{1,25},{2,26},{3,27},{4,28},{5,29},{6,30},{7,31},{8,16},{9,... | collective-permute-start | bytes 43016 | tf_op jit(solution)/shard_map/ppermute | solution.py:591
  84.8 3.9 %collective-permute-start.24 = (f32[2,1792]{1,0:T(2,128)S(1)}, f32[2,1792]{1,0:T(2,128)S(1)}, u32[]{:S(2)}, u32[]{:S(2)}) collective-permute-start(f32[2,1792]{1,0:T(2,128)S(1)} %add_add_fusion.1), channel_id=1, source_target_pairs={{0,8},{1,9},{2,10},{3,11},{4,12},{5,13},{6,14},{7,15},{8,0},{9,1},... | collective-permute-start | bytes 43016 | tf_op jit(solution)/shard_map/ppermute | solution.py:591

commit v7 on v6

--- a/solution.py
+++ b/solution.py
@@ -203,7 +203,7 @@
         in_specs=spec(3),
         out_specs=spec(1)[0],
         compiler_params=params(16),
-        cost_estimate=pl.CostEstimate(flops=8 * 10**9, bytes_accessed=2 * 10**6, transcendentals=10**6),
+        cost_estimate=pl.CostEstimate(flops=1, bytes_accessed=1, transcendentals=0),
     )(qkv, idk, idq)
 
 
@@ -436,6 +436,30 @@
     )(*g, normed_t, w, b)
 
 
+def halves_kernel(x_ref, low_ref, up_ref, sems):
+    half = low_ref.shape[1]
+    low = pltpu.make_async_copy(x_ref.at[:, :half], low_ref, sems.at[0])
+    up = pltpu.make_async_copy(x_ref.at[:, half:], up_ref, sems.at[1])
+    low.start()
+    up.start()
+    low.wait()
+    up.wait()
+
+
+def halves_of(block):
+    rows, lon, lev, width = block.shape
+    half = jax.ShapeDtypeStruct((rows, lon // 2, lev, width), BF)
+    return pl.pallas_call(
+        halves_kernel,
+        out_shape=(half, half),
+        in_specs=[pl.BlockSpec(memory_space=pltpu.HBM)],
+        out_specs=tuple(spec(2)),
+        scratch_shapes=[pltpu.SemaphoreType.DMA((2,))],
+        compiler_params=params(16),
+        cost_estimate=SMALL,
+    )(block)
+
+
 def split_kernel(s_ref, *refs):
     offset, core = s_ref[0], s_ref[1]
     pairs = (len(refs) - 1) // 3
@@ -622,9 +646,9 @@
     place = jnp.stack([shift_offset[0], t % 2, sector]).astype(jnp.int32)
 
     f_raw, t_raw = (jnp.transpose(block, (0, 2, 1, 3)) for block in (features, target))
-    f_low, w_qkv, w_proj = lax.optimization_barrier((f_raw[:, :half], w_qkv, w_proj))
-    f_up_y = send(after(f_raw, f_low)[:, half:], 0, 2)
-    f_low = send(f_low, -1, 0)
+    f_low, f_up = halves_of(f_raw)
+    f_low, f_up, w_qkv, w_proj = lax.optimization_barrier((f_low, f_up, w_qkv, w_proj))
+    f_low, f_up_y = send(f_low, -1, 0), send(f_up, 0, 2)
 
     w3 = jnp.transpose(w_qkv, (1, 0, 2))
     c3 = jnp.transpose(qkv_clip, (1, 0, 2))
@@ -637,15 +661,15 @@
     wc_own, b_own = clip_qkv(w3, c3)
     wc_peer, b_peer = clip_qkv(w3_peer, c3_peer)
     idk, idq = window_ids(place, region_ids, WLAT * lev * lon)
-    f_low, f_up_y, w1, wc_own, wc_peer, idk, idq = lax.optimization_barrier(
-        (f_low, f_up_y, w1, wc_own, wc_peer, idk, idq)
-    )
+    f_low, f_up_y, w1 = lax.optimization_barrier((f_low, f_up_y, w1))
     f_low_y = send(f_low, 0, 2)
     t_low = send(after(t_raw, f_low)[:, :half], -1, 0)
     t_own, t_away = split(place, t_raw, t_low)
     t_away = t_away.reshape(t_own.shape)
     t_1 = send(t_away, 0, 1)
-    f_low_y, t_own, t_away, slab = lax.optimization_barrier((f_low_y, t_own, t_away, slab))
+    f_low_y, t_own, t_away, slab, wc_own, wc_peer, idk, idq = lax.optimization_barrier(
+        (f_low_y, t_own, t_away, slab, wc_own, wc_peer, idk, idq)
+    )
     x_0, x_2, x_away = split(place, f_raw, f_low, f_up_y, f_low_y)
     pieces = (x_0, x_2, send(x_away, 0, 1))
 

time: 90.3 us -> 92.9 us (1.029)
  waiting for transfers between devices: 20.1 us -> 16.4 us
  Pallas kernels: 36.8 us -> 39.5 us
  starting transfers between devices: 25 us -> 27 us
  local copies, waits for them, and re-layouts: 6.3 us -> 7.84 us
    ppermute x21, waiting for transfers between devices: 16.4 us -> 9.76 us  [send(): return lax.ppermute(block, ('lat', 'tp'), route)]
    slice x2 -> x0, local copies, waits for them, and re-layouts: 3.77 us -> none  [the longest x1 1.94 us: local(): f_raw[:, :half]]
    ppermute x6, waiting for transfers between devices: 3.66 us -> 6.6 us  [swap(): return lax.ppermute(block, ('lat', 'tp'), route)]
    unnamed x14 -> x24, local copies, waits for them, and re-layouts: 0.19 us -> 3.06 us
    ppermute x21, starting transfers between devices: 17.7 us -> 20 us  [send(): return lax.ppermute(block, ('lat', 'tp'), route)]
    slice x1, local copies, waits for them, and re-layouts: 0.18 us -> 1.92 us  [local(): t_low = send(after(t_raw, f_low)[:, :half], -1, 0)]
    pallas_call x2, Pallas kernels: 1.39 us -> 2.91 us  [clip_qkv(): pl.pallas_call(clip_qkv_kernel, out_shape=(jax.ShapeDtypeStruct((n, d, e)...]
    pallas_call x2, Pallas kernels: 3.61 us -> 5.02 us  [qkv_sums(): pl.pallas_call(functools.partial(qkv_sums_kernel, side), out_shape=jax.Sh...]
  transfers between devices with their start and end apart: 27 -> 27, of which waited for: 11 -> 9; matrix products, arithmetic and copies ran while one was open for 3% -> 4% of each run, Pallas kernels for 38% -> 39%
where the time goes in v7:
time: 92.9 us; the launch traced here: 92.6 us
  Pallas kernels  39.5 us (43%)
  starting transfers between devices  27 us (29%)
  waiting for transfers between devices  16.4 us (18%)
  local copies, waits for them, and re-layouts  7.84 us (8%)
  between operations  1.72 us (2%)
    ppermute x21, starting transfers between devices, send(): return lax.ppermute(block, ('lat', 'tp'), route)  20 us
    ppermute x21, waiting for transfers between devices, send(): return lax.ppermute(block, ('lat', 'tp'), route)  9.76 us
    pallas_call x1, Pallas kernels, forward(): pl.pallas_call(forward_kernel, out_shape=(jax.ShapeDtypeStruct((n, d), BF...  7.61 us
    ppermute x6, starting transfers between devices, swap(): return lax.ppermute(block, ('lat', 'tp'), route)  6.94 us
    ppermute x6, waiting for transfers between devices, swap(): return lax.ppermute(block, ('lat', 'tp'), route)  6.6 us
    pallas_call x2, Pallas kernels, backward(): pl.pallas_call(functools.partial(backward_kernel, group), out_shape=jax.S...  6.43 us
    pallas_call x2, Pallas kernels, qkv_sums(): pl.pallas_call(functools.partial(qkv_sums_kernel, side), out_shape=jax.Sh...  5.02 us
    pallas_call x2, Pallas kernels, split(): pl.pallas_call(split_kernel, out_shape=(jax.ShapeDtypeStruct((n, width),...  3.2 us
  transfers between devices with their start and end apart: 27, of which 9 were waited for; matrix products, arithmetic and copies ran while one was open for 4% of the time, Pallas kernels for 39%

profile of v7, /device:TPU:0, one launch (start us, length us, event | category | flops | bytes accessed | tf_op | source)
XLA Modules:
  0.0 92.6 jit_solution(17208165851421206749)
XLA Ops:
  0.6 0.0 copy-start
  0.6 1.0 %copy-done = bf16[42,2,12,256]{3,1,2,0:T(2,128)(2,1)S(1)} copy-done((bf16[42,2,12,256]{3,1,2,0:T(2,128)(2,1)S(1)}, bf16[42,2,12,256]{3,1,2,0:T(2,128)(2,1)}, u32[]{:S(2)}) %copy-start) | copy-done | bytes 516120
  1.7 0.8 shard_map.103
  2.5 0.5 collective-permute-start.7
  3.0 0.1 collective-permute-start.2
  3.1 6.0 %collective-permute-start = (bf16[42,6,2,256]{3,2,1,0:T(2,128)(2,1)}, bf16[42,6,2,256]{3,2,1,0:T(2,128)(2,1)}, u32[]{:S(2)}, u32[]{:S(2)}) collective-permute-start(bf16[42,6,2,256]{3,2,1,0:T(2,128)(2,1)} %get-tuple-element.59), channel_id=1, source_target_pairs={{0,28},{1,29},{2,30},{3,31},{4,0},{5,1},{6,2},{7,3},{8,4},{9,5},{1... | collective-permute-start | bytes 774152 | tf_op jit(solution)/shard_map/ppermute | solution.py:609
  9.0 1.5 %collective-permute-start.1 = (bf16[42,6,2,256]{3,2,1,0:T(2,128)(2,1)S(1)}, bf16[42,6,2,256]{3,2,1,0:T(2,128)(2,1)S(1)}, u32[]{:S(2)}, u32[]{:S(2)}) collective-permute-start(bf16[42,6,2,256]{3,2,1,0:T(2,128)(2,1)S(1)} %get-tuple-element.60), channel_id=1, source_target_pairs={{0,2},{1,3},{2,0},{3,1},{4,6},{5,7},{6,4},{7,5},{8,10},{9,11},{10,... | collective-permute-start | bytes 774152 | tf_op jit(solution)/shard_map/ppermute | solution.py:609
  10.5 1.4 %collective-permute-done.5.c_ref = f32[3,2,256]{2,1,0:T(2,128)S(1)} collective-permute-done((f32[3,2,256]{2,1,0:T(2,128)}, f32[3,2,256]{2,1,0:T(2,128)S(1)}, u32[]{:S(2)}, u32[]{:S(2)}) %collective-permute-start.5) | collective-permute-done | bytes 6176 | tf_op jit(solution)/shard_map/ppermute | solution.py:609
  11.9 1.7 %constant_dynamic-slice_fusion = bf16[128,1024]{1,0:T(8,128)(2,1)} fusion(bf16[256,1024]{1,0:T(8,128)(2,1)} %po_ref, s32[]{:T(128)S(6)} %select_n.16), kind=kLoop, calls=%fused_computation.5 | loop fusion | bytes 524292 | tf_op jit(solution)/shard_map/dynamic_slice | solution.py:659
  13.6 0.5 collective-permute-start.6
  14.1 1.0 %collective-permute-done.refs_1_ = bf16[42,6,2,256]{3,2,1,0:T(2,128)(2,1)} collective-permute-done((bf16[42,6,2,256]{3,2,1,0:T(2,128)(2,1)}, bf16[42,6,2,256]{3,2,1,0:T(2,128)(2,1)}, u32[]{:S(2)}, u32[]{:S(2)}) %collective-permute-start) | collective-permute-done | bytes 258080 | tf_op jit(solution)/shard_map/ppermute | solution.py:609
  15.1 2.2 %collective-permute-done.1.refs_2_ = bf16[42,6,2,256]{3,2,1,0:T(2,128)(2,1)S(1)} collective-permute-done((bf16[42,6,2,256]{3,2,1,0:T(2,128)(2,1)S(1)}, bf16[42,6,2,256]{3,2,1,0:T(2,128)(2,1)S(1)}, u32[]{:S(2)}, u32[]{:S(2)}) %collective-permute-start.1) | collective-permute-done | bytes 258080 | tf_op jit(solution)/shard_map/ppermute | solution.py:609
  17.3 1.9 %slice.9 = bf16[42,6,2,256]{3,2,1,0:T(2,128)(2,1)} slice(bf16[42,12,2,256]{3,2,1,0:T(2,128)(2,1)} %bitcast.15), slice={[0:42], [0:6], [0:2], [0:256]} | slice | bytes 516096 | tf_op jit(solution)/shard_map/slice | solution.py:666
  19.2 3.0 %collective-permute-start.4 = (bf16[42,6,2,256]{3,2,1,0:T(2,128)(2,1)}, bf16[42,6,2,256]{3,2,1,0:T(2,128)(2,1)}, u32[]{:S(2)}, u32[]{:S(2)}) collective-permute-start(bf16[42,6,2,256]{3,2,1,0:T(2,128)(2,1)} %slice.9), channel_id=1, source_target_pairs={{0,28},{1,29},{2,30},{3,31},{4,0},{5,1},{6,2},{7,3},{8,4},{9,5},{1... | collective-permute-start | bytes 774152 | tf_op jit(solution)/shard_map/ppermute | solution.py:609
  22.2 1.5 %collective-permute-start.3 = (bf16[42,6,2,256]{3,2,1,0:T(2,128)(2,1)}, bf16[42,6,2,256]{3,2,1,0:T(2,128)(2,1)}, u32[]{:S(2)}, u32[]{:S(2)}) collective-permute-start(bf16[42,6,2,256]{3,2,1,0:T(2,128)(2,1)} %collective-permute-done.refs_1_), channel_id=1, source_target_pairs={{0,2},{1,3},{2,0},{3,1},{4,6},{5,7},{6,4},{7,5},{8,10},{9,11},{10,... | collective-permute-start | bytes 774152 | tf_op jit(solution)/shard_map/ppermute | solution.py:609
  23.7 0.7 copy-done.9
  24.4 0.7 shard_map.105
  25.1 1.1 %copy-done.10 = bf16[3,1024,256]{2,1,0:T(8,128)(2,1)} copy-done((bf16[3,1024,256]{2,1,0:T(8,128)(2,1)}, bf16[3,1024,256]{2,1,0:T(8,128)(2,1)S(1)}, u32[]{:S(2)}) %copy-start.10) | copy-done | bytes 1572888
  27.0 0.1 pad_add_fusion.s_ref
  27.0 1.0 %shard_map.107 = (s32[576,1]{1,0:T(8,128)S(1)}, s32[4,1,288]{2,1,0:T(1,128)S(1)}) custom-call(s32[3]{0:T(128)S(1)} %pad_add_fusion.s_ref, s32[42,2,96]{2,1,0:T(2,128)S(1)} %copy-done.7), custom_call_target="tpu_custom_call" | custom-call | flops 1 | bytes 1 | tf_op jit(solution)/shard_map/pallas_call | solution.py:553
  28.1 1.4 %shard_map.104 = (bf16[576,256]{1,0:T(8,128)(2,1)S(1)}, bf16[1,576,256]{2,1,0:T(8,128)(2,1)S(1)}) custom-call(s32[3]{0:T(128)S(1)} %pad_add_fusion.s_ref, bf16[42,12,2,256]{3,2,1,0:T(2,128)(2,1)S(1)} %bitcast.16, bf16[42,6,2,256]{3,2,1,0:T(2,128)(2,1)} %collective-permute-done.4.refs_1_), custom_call_target="tpu_custom_call" | custom-call | flops 1 | bytes 1 | tf_op jit(solution)/shard_map/pallas_call | solution.py:497
  29.5 2.2 %shard_map.106 = (bf16[3,1024,256]{2,1,0:T(8,128)(2,1)S(1)}, f32[3,8,256]{2,1,0:T(8,128)S(1)}) custom-call(bf16[3,1024,256]{2,1,0:T(8,128)(2,1)} %collective-permute-done.7.w_ref, f32[3,2,256]{2,1,0:T(2,128)S(1)} %collective-permute-done.5.c_ref), custom_call_target="tpu_custom_call" | custom-call | flops 1 | bytes 1 | tf_op jit(solution)/shard_map/pallas_call | solution.py:55
  31.8 1.8 %shard_map.108 = (bf16[576,256]{1,0:T(8,128)(2,1)S(1)}, bf16[576,256]{1,0:T(8,128)(2,1)S(1)}, bf16[2,576,256]{2,1,0:T(8,128)(2,1)S(1)}) custom-call(s32[3]{0:T(128)S(1)} %pad_add_fusion.s_ref, bf16[42,12,2,256]{3,2,1,0:T(2,128)(2,1)S(1)} %bitcast.11, bf16[42,6,2,256]{3,2,1,0:T(2,128)(2,1)} %collective-permute-done.refs_1_, ...), custom_call_target="tpu_custom_call" | custom-call | flops 1 | bytes 1 | tf_op jit(solution)/shard_map/pallas_call | solution.py:497
  33.6 0.1 collective-permute-start.8
  33.7 0.5 collective-permute-start.9
  34.2 0.8 collective-permute-start.10
  35.0 0.6 collective-permute-start.11
  35.6 0.1 collective-permute-done.8.refs_2_
  35.7 7.6 %shard_map.109 = (bf16[576,1024]{1,0:T(8,128)(2,1)S(1)}, bf16[6,576,256]{2,1,0:T(8,128)(2,1)S(1)}, bf16[288,512]{1,0:T(8,128)(2,1)S(1)}) custom-call(s32[1]{0:T(128)} %bitcast.2.t_ref, bf16[576,256]{1,0:T(8,128)(2,1)S(1)} %get-tuple-element.74.refs_0_, bf16[576,256]{1,0:T(8,128)(2,1)S(1)} %get-tuple-element.75.refs_1_, ...), custom_call_target="tpu_custom_call" | custom-call | flops 8000000000 | bytes 10000000 | tf_op jit(solution)/shard_map/pallas_call | solution.py:213
  43.3 1.0 %shard_map.110.p_ref = f32[8,144,288]{2,1,0:T(8,128)S(1)} custom-call(bf16[6,576,256]{2,1,0:T(8,128)(2,1)S(1)} %get-tuple-element.102.qkv_ref, s32[576,1]{1,0:T(8,128)S(1)} %get-tuple-element.81.refs_5_.idk_ref.refs_10_, s32[4,1,288]{2,1,0:T(1,128)S(1)} %get-tuple-element.82.refs_6_.idq_ref), custom_call_target="tpu_custom_call" | custom-call | flops 1 | bytes 1 | tf_op jit(solution)/shard_map/pallas_call | solution.py:326
  44.3 0.9 collective-permute-start.14
  45.2 3.5 %collective-permute-done.11.refs_6_ = bf16[576,256]{1,0:T(8,128)(2,1)S(1)} collective-permute-done((bf16[576,256]{1,0:T(8,128)(2,1)S(1)}, bf16[576,256]{1,0:T(8,128)(2,1)S(1)}, u32[]{:S(2)}, u32[]{:S(2)}) %collective-permute-start.11) | collective-permute-done | bytes 294944 | tf_op jit(solution)/shard_map/ppermute | solution.py:609
  48.7 2.7 %shard_map.111.refs_7_.b_ref = bf16[288,512]{1,0:T(8,128)(2,1)S(1)} custom-call(bf16[6,576,256]{2,1,0:T(8,128)(2,1)S(1)} %get-tuple-element.102.qkv_ref, s32[576,1]{1,0:T(8,128)S(1)} %get-tuple-element.81.refs_5_.idk_ref.refs_10_, s32[4,1,288]{2,1,0:T(1,128)S(1)} %get-tuple-element.82.refs_6_.idq_ref), custom_call_target="tpu_custom_call" | custom-call | flops 1 | bytes 1 | tf_op jit(solution)/shard_map/pallas_call | solution.py:200
  51.3 1.3 %collective-permute-start.13 = (bf16[288,512]{1,0:T(8,128)(2,1)S(1)}, bf16[288,512]{1,0:T(8,128)(2,1)S(1)}, u32[]{:S(2)}, u32[]{:S(2)}) collective-permute-start(bf16[288,512]{1,0:T(8,128)(2,1)S(1)} %shard_map.111.refs_7_.b_ref), channel_id=1, source_target_pairs={{0,2},{1,3},{2,0},{3,1},{4,6},{5,7},{6,4},{7,5},{8,10},{9,11},{10,... | collective-permute-start | bytes 884744 | tf_op jit(solution)/shard_map/ppermute | solution.py:609
  52.6 0.8 collective-permute-start.15
  53.4 1.0 %shard_map.117.p_ref = f32[8,144,288]{2,1,0:T(8,128)S(1)} custom-call(bf16[6,576,256]{2,1,0:T(8,128)(2,1)S(1)} %get-tuple-element.102.qkv_ref, s32[576,1]{1,0:T(8,128)S(1)} %get-tuple-element.81.refs_5_.idk_ref.refs_10_, s32[4,1,288]{2,1,0:T(1,128)S(1)} %get-tuple-element.82.refs_6_.idq_ref), custom_call_target="tpu_custom_call" | custom-call | flops 1 | bytes 1 | tf_op jit(solution)/shard_map/pallas_call | solution.py:326
  54.5 0.0 copy-start.3
  54.5 0.0 copy-start.8
  54.5 0.8 shard_map.119
  55.4 0.1 copy-done.3
  55.5 1.6 %shard_map.112 = (bf16[1024,1024]{1,0:T(8,128)(2,1)S(1)}, f32[8,1024]{1,0:T(8,128)S(1)}) custom-call(s32[3]{0:T(128)S(1)} %pad_add_fusion.s_ref, bf16[256,1024]{1,0:T(8,128)(2,1)S(1)} %copy-done.3, bf16[256,1024]{1,0:T(8,128)(2,1)S(1)} %collective-permute-done.2.w1.pp_ref, bf16[128,1024]{1,0:T(8,128)(2,1)S(1)} %collective-permute-done.6.a2, ...), custom_call_target="tpu_custom_call" | custom-call | flops 1 | bytes 1 | tf_op jit(solution)/shard_map/pallas_call | solution.py:92
  57.1 1.0 %shard_map.113 = (bf16[144,256]{1,0:T(8,128)(2,1)S(1)}, bf16[144,256]{1,0:T(8,128)(2,1)S(1)}, bf16[144,256]{1,0:T(8,128)(2,1)S(1)}, bf16[144,256]{1,0:T(8,128)(2,1)S(1)}, bf16[288,1024]{1,0:T(8,128)(2,1)S(1)}) custom-call(s32[1]{0:T(128)} %bitcast.2.t_ref, bf16[576,256]{1,0:T(8,128)(2,1)S(1)} %get-tuple-element.74.refs_0_, ...), custom_call_target="tpu_custom_call" | custom-call | flops 1 | bytes 1 | tf_op jit(solution)/shard_map/pallas_call | solution.py:296
  58.1 3.2 %shard_map.114.g0_ref = bf16[6,288,256]{2,1,0:T(8,128)(2,1)S(1)} custom-call(bf16[288,1024]{1,0:T(8,128)(2,1)S(1)} %get-tuple-element.91.err_ref.e0_ref, bf16[1024,1024]{1,0:T(8,128)(2,1)S(1)} %get-tuple-element.90.refs_9_.wc_ref, bf16[6,576,256]{2,1,0:T(8,128)(2,1)S(1)} %get-tuple-element.102.qkv_ref, f32[8,144,288]{2,1,0:T(8,128)S(1)} %shard_map.110.p_ref), custom_call_target="tpu_custom_call" | custom-call | flops 1 | bytes 1 | tf_op jit(solution)/shard_map/pallas_call | solution.py:402
  61.3 0.8 collective-permute-done.13.refs_8_
  62.1 0.9 %shard_map.115 = (bf16[288,256]{1,0:T(8,128)(2,1)S(1)}, bf16[288,256]{1,0:T(8,128)(2,1)S(1)}, bf16[288,256]{1,0:T(8,128)(2,1)S(1)}, bf16[288,256]{1,0:T(8,128)(2,1)S(1)}, bf16[288,1024]{1,0:T(8,128)(2,1)S(1)}) custom-call(s32[1]{0:T(128)} %bitcast.2.t_ref, bf16[576,256]{1,0:T(8,128)(2,1)S(1)} %get-tuple-element.74.refs_0_, ...), custom_call_target="tpu_custom_call" | custom-call | flops 1 | bytes 1 | tf_op jit(solution)/shard_map/pallas_call | solution.py:296
  63.1 0.1 collective-permute-start.17
  63.1 0.1 collective-permute-start.18
  63.2 0.2 collective-permute-start.19
  63.5 3.2 %shard_map.118.g1_ref = bf16[6,288,256]{2,1,0:T(8,128)(2,1)S(1)} custom-call(bf16[288,1024]{1,0:T(8,128)(2,1)S(1)} %get-tuple-element.101.err_ref.e1_ref, bf16[1024,1024]{1,0:T(8,128)(2,1)S(1)} %get-tuple-element.90.refs_9_.wc_ref, bf16[6,576,256]{2,1,0:T(8,128)(2,1)S(1)} %get-tuple-element.102.qkv_ref, f32[8,144,288]{2,1,0:T(8,128)S(1)} %shard_map.117.p_ref), custom_call_target="tpu_custom_call" | custom-call | flops 8000000000 | bytes 10000000 | tf_op jit(solution)/shard_map/pallas_call | solution.py:402
  66.7 1.6 %shard_map.121 = f32[2,1024]{1,0:T(2,128)S(1)} custom-call(bf16[288,1024]{1,0:T(8,128)(2,1)S(1)} %get-tuple-element.91.err_ref.e0_ref, bf16[288,1024]{1,0:T(8,128)(2,1)S(1)} %get-tuple-element.101.err_ref.e1_ref, bf16[512,576]{1,0:T(8,128)(2,1)S(1)} %get-tuple-element.106.attn_t, bf16[256,1024]{1,0:T(8,128)(2,1)S(1)} %copy-done.3, ...), custom_call_target="tpu_custom_call" | custom-call | flops 1000000000 | bytes 3000000 | tf_op jit(solution)/shard_map/pallas_call | solution.py:359
  68.3 0.9 collective-permute-start.20
  69.1 3.2 %shard_map.120 = f32[2,768]{1,0:T(2,128)S(1)} custom-call(bf16[6,288,256]{2,1,0:T(8,128)(2,1)S(1)} %shard_map.114.g0_ref, bf16[6,288,256]{2,1,0:T(8,128)(2,1)S(1)} %shard_map.118.g1_ref, bf16[1024,576]{1,0:T(8,128)(2,1)S(1)} %get-tuple-element.104.normed_t, bf16[3,1024,256]{2,1,0:T(8,128)(2,1)} %collective-permute-done.7.w_ref, ...), custom_call_target="tpu_custom_call" | custom-call | flops 8000000000 | bytes 10000000 | tf_op jit(solution)/shard_map/pallas_call | solution.py:429
  72.4 0.8 collective-permute-start.23
  73.1 0.8 collective-permute-start.21
  73.9 0.8 collective-permute-done.19.b1
  74.7 1.8 %shard_map.122 = f32[2,768]{1,0:T(2,128)S(1)} custom-call(bf16[6,288,256]{2,1,0:T(8,128)(2,1)S(1)} %shard_map.114.g0_ref, bf16[6,288,256]{2,1,0:T(8,128)(2,1)S(1)} %shard_map.118.g1_ref, bf16[1024,576]{1,0:T(8,128)(2,1)S(1)} %get-tuple-element.104.normed_t, bf16[3,1024,256]{2,1,0:T(8,128)(2,1)S(1)} %bitcast.14, f32[3,8,256]{2,1,0:T(8,128)S(1)} %get-tuple-element.110.b_ref), custom_call_target="tpu_custom_call" | custom-call | flops 8000000000 | bytes 10000000 | tf_op jit(solution)/shard_map/pallas_call | solution.py:429
  76.6 0.1 collective-permute-start.22
  76.7 3.7 %collective-permute-done.22 = f32[2,1792]{1,0:T(2,128)S(1)} collective-permute-done((f32[2,1792]{1,0:T(2,128)S(1)}, f32[2,1792]{1,0:T(2,128)S(1)}, u32[]{:S(2)}, u32[]{:S(2)}) %collective-permute-start.22) | collective-permute-done | bytes 14368 | tf_op jit(solution)/shard_map/ppermute | solution.py:615
  80.4 5.5 %collective-permute-start.25 = (f32[2,1792]{1,0:T(2,128)S(1)}, f32[2,1792]{1,0:T(2,128)S(1)}, u32[]{:S(2)}, u32[]{:S(2)}) collective-permute-start(f32[2,1792]{1,0:T(2,128)S(1)} %add_add_fusion.1), channel_id=1, source_target_pairs={{0,16},{1,17},{2,18},{3,19},{4,20},{5,21},{6,22},{7,23},{8,24},{9,... | collective-permute-start | bytes 43016 | tf_op jit(solution)/shard_map/ppermute | solution.py:615
  85.8 0.6 collective-permute-start.24
  86.5 2.0 %shard_map.116 = bf16[42,12,2,256]{3,2,1,0:T(2,128)(2,1)} custom-call(s32[3]{0:T(128)S(1)} %pad_add_fusion.s_ref, bf16[288,256]{1,0:T(8,128)(2,1)S(1)} %get-tuple-element.97.a0, bf16[288,256]{1,0:T(8,128)(2,1)S(1)} %collective-permute-done.17.a1, bf16[288,256]{1,0:T(8,128)(2,1)S(1)} %collective-permute-done.18.b0, ...), custom_call_target="tpu_custom_call" | custom-call | flops 1 | bytes 1 | tf_op jit(solution)/shard_map/pallas_call | solution.py:592
  88.4 2.9 %collective-permute-done.26 = f32[2,1792]{1,0:T(2,128)S(1)} collective-permute-done((f32[2,1792]{1,0:T(2,128)S(1)}, f32[2,1792]{1,0:T(2,128)S(1)}, u32[]{:S(2)}, u32[]{:S(2)}) %collective-permute-start.26) | collective-permute-done | bytes 14368 | tf_op jit(solution)/shard_map/ppermute | solution.py:615
  91.4 0.6 slice.12
  92.0 0.6 slice.13
  (44 shorter events, 0.2 us)
Async XLA Ops:
  0.6 1.0 %copy-start = (bf16[42,2,12,256]{3,1,2,0:T(2,128)(2,1)S(1)}, bf16[42,2,12,256]{3,1,2,0:T(2,128)(2,1)}, u32[]{:S(2)}) copy-start(bf16[42,2,12,256]{3,1,2,0:T(2,128)(2,1)} %param.8) | copy-start | bytes 1548292
  1.7 22.0 %copy-start.2 = (bf16[1024,3,256]{2,0,1:T(8,128)(2,1)S(1)}, bf16[1024,3,256]{2,0,1:T(8,128)(2,1)}, u32[]{:S(2)}) copy-start(bf16[1024,3,256]{2,0,1:T(8,128)(2,1)} %param.10) | copy-start | bytes 4718596
  1.7 25.4 %copy-start.7 = (s32[42,2,96]{2,1,0:T(2,128)S(1)}, s32[42,2,96]{2,1,0:T(2,128)}, u32[]{:S(2)}) copy-start(s32[42,2,96]{2,1,0:T(2,128)} %ids_ref.1) | copy-start | bytes 96772
  1.7 26.4 %copy-start.4 = (bf16[42,2,12,256]{3,1,2,0:T(2,128)(2,1)S(1)}, bf16[42,2,12,256]{3,1,2,0:T(2,128)(2,1)}, u32[]{:S(2)}) copy-start(bf16[42,2,12,256]{3,1,2,0:T(2,128)(2,1)} %param.9) | copy-start | bytes 1548292
  2.5 27.0 %collective-permute-start.7 = (bf16[3,1024,256]{2,1,0:T(8,128)(2,1)}, bf16[3,1024,256]{2,1,0:T(8,128)(2,1)}, u32[]{:S(2)}, u32[]{:S(2)}) collective-permute-start(bf16[3,1024,256]{2,1,0:T(8,128)(2,1)} %bitcast.12), channel_id=1, source_target_pairs={{0,1},{1,0},{2,3},{3,2},{4,5},{5,4},{6,7},{7,6},{8,9},{9,8},{10,11... | collective-permute-start | bytes 4718600 | tf_op jit(solution)/shard_map/ppermute | solution.py:609
  3.0 14.3 %collective-permute-start.2 = (bf16[256,1024]{1,0:T(8,128)(2,1)}, bf16[256,1024]{1,0:T(8,128)(2,1)S(1)}, u32[]{:S(2)}, u32[]{:S(2)}) collective-permute-start(bf16[256,1024]{1,0:T(8,128)(2,1)} %po_ref), channel_id=1, source_target_pairs={{0,1},{1,0},{2,3},{3,2},{4,5},{5,4},{6,7},{7,6},{8,9},{9,8},{10,11... | collective-permute-start | bytes 1572872 | tf_op jit(solution)/shard_map/ppermute | solution.py:609
  3.1 12.0 %collective-permute-start = (bf16[42,6,2,256]{3,2,1,0:T(2,128)(2,1)}, bf16[42,6,2,256]{3,2,1,0:T(2,128)(2,1)}, u32[]{:S(2)}, u32[]{:S(2)}) collective-permute-start(bf16[42,6,2,256]{3,2,1,0:T(2,128)(2,1)} %get-tuple-element.59), channel_id=1, source_target_pairs={{0,28},{1,29},{2,30},{3,31},{4,0},{5,1},{6,2},{7,3},{8,4},{9,5},{1... | collective-permute-start | bytes 774152 | tf_op jit(solution)/shard_map/ppermute | solution.py:609
  9.0 8.2 %collective-permute-start.1 = (bf16[42,6,2,256]{3,2,1,0:T(2,128)(2,1)S(1)}, bf16[42,6,2,256]{3,2,1,0:T(2,128)(2,1)S(1)}, u32[]{:S(2)}, u32[]{:S(2)}) collective-permute-start(bf16[42,6,2,256]{3,2,1,0:T(2,128)(2,1)S(1)} %get-tuple-element.60), channel_id=1, source_target_pairs={{0,2},{1,3},{2,0},{3,1},{4,6},{5,7},{6,4},{7,5},{8,10},{9,11},{10,... | collective-permute-start | bytes 774152 | tf_op jit(solution)/shard_map/ppermute | solution.py:609
  10.5 1.4 %collective-permute-start.5 = (f32[3,2,256]{2,1,0:T(2,128)}, f32[3,2,256]{2,1,0:T(2,128)S(1)}, u32[]{:S(2)}, u32[]{:S(2)}) collective-permute-start(f32[3,2,256]{2,1,0:T(2,128)} %bitcast.17), channel_id=1, source_target_pairs={{0,1},{1,0},{2,3},{3,2},{4,5},{5,4},{6,7},{7,6},{8,9},{9,8},{10,11... | collective-permute-start | bytes 18440 | tf_op jit(solution)/shard_map/ppermute | solution.py:609
  13.6 18.1 %collective-permute-start.6 = (bf16[128,1024]{1,0:T(8,128)(2,1)}, bf16[128,1024]{1,0:T(8,128)(2,1)S(1)}, u32[]{:S(2)}, u32[]{:S(2)}) collective-permute-start(bf16[128,1024]{1,0:T(8,128)(2,1)} %constant_dynamic-slice_fusion), channel_id=1, source_target_pairs={{0,2},{1,3},{2,0},{3,1},{4,6},{5,7},{6,4},{7,5},{8,10},{9,11},{10,... | collective-permute-start | bytes 786440 | tf_op jit(solution)/shard_map/ppermute | solution.py:609
  17.3 6.4 %copy-start.5 = (bf16[42,6,2,256]{3,2,1,0:T(2,128)(2,1)}, bf16[42,6,2,256]{3,2,1,0:T(2,128)(2,1)S(1)}, u32[]{:S(2)}) copy-start(bf16[42,6,2,256]{3,2,1,0:T(2,128)(2,1)S(1)} %collective-permute-done.1.refs_2_) | copy-start | bytes 774148
  19.2 8.9 %collective-permute-start.4 = (bf16[42,6,2,256]{3,2,1,0:T(2,128)(2,1)}, bf16[42,6,2,256]{3,2,1,0:T(2,128)(2,1)}, u32[]{:S(2)}, u32[]{:S(2)}) collective-permute-start(bf16[42,6,2,256]{3,2,1,0:T(2,128)(2,1)} %slice.9), channel_id=1, source_target_pairs={{0,28},{1,29},{2,30},{3,31},{4,0},{5,1},{6,2},{7,3},{8,4},{9,5},{1... | collective-permute-start | bytes 774152 | tf_op jit(solution)/shard_map/ppermute | solution.py:609
  22.2 9.6 %collective-permute-start.3 = (bf16[42,6,2,256]{3,2,1,0:T(2,128)(2,1)}, bf16[42,6,2,256]{3,2,1,0:T(2,128)(2,1)}, u32[]{:S(2)}, u32[]{:S(2)}) collective-permute-start(bf16[42,6,2,256]{3,2,1,0:T(2,128)(2,1)} %collective-permute-done.refs_1_), channel_id=1, source_target_pairs={{0,2},{1,3},{2,0},{3,1},{4,6},{5,7},{6,4},{7,5},{8,10},{9,11},{10,... | collective-permute-start | bytes 774152 | tf_op jit(solution)/shard_map/ppermute | solution.py:609
  23.7 0.7 copy-start.9
  25.1 1.2 %copy-start.10 = (bf16[3,1024,256]{2,1,0:T(8,128)(2,1)}, bf16[3,1024,256]{2,1,0:T(8,128)(2,1)S(1)}, u32[]{:S(2)}) copy-start(bf16[3,1024,256]{2,1,0:T(8,128)(2,1)S(1)} %get-tuple-element.79.refs_3_) | copy-start | bytes 4718596
  26.2 5.5 %copy-start.1 = (bf16[42,2,12,256]{3,1,2,0:T(2,128)(2,1)S(1)}, bf16[42,2,12,256]{3,1,2,0:T(2,128)(2,1)}, u32[]{:S(2)}) copy-start(bf16[42,2,12,256]{3,1,2,0:T(2,128)(2,1)} %param.8) | copy-start | bytes 1548292
  27.0 4.8 %copy-start.6 = (bf16[42,6,2,256]{3,2,1,0:T(2,128)(2,1)S(1)}, bf16[42,6,2,256]{3,2,1,0:T(2,128)(2,1)}, u32[]{:S(2)}) copy-start(bf16[42,6,2,256]{3,2,1,0:T(2,128)(2,1)} %copy-done.5) | copy-start | bytes 774148
  29.5 6.2 %copy-start.11 = (bf16[3,1024,256]{2,1,0:T(8,128)(2,1)S(1)}, bf16[3,1024,256]{2,1,0:T(8,128)(2,1)}, u32[]{:S(2)}) copy-start(bf16[3,1024,256]{2,1,0:T(8,128)(2,1)} %copy-done.10) | copy-start | bytes 4718596
  33.6 2.1 %collective-permute-start.8 = (bf16[2,576,256]{2,1,0:T(8,128)(2,1)S(1)}, bf16[2,576,256]{2,1,0:T(8,128)(2,1)S(1)}, u32[]{:S(2)}, u32[]{:S(2)}) collective-permute-start(bf16[2,576,256]{2,1,0:T(8,128)(2,1)S(1)} %get-tuple-element.76), channel_id=1, source_target_pairs={{0,1},{1,0},{2,3},{3,2},{4,5},{5,4},{6,7},{7,6},{8,9},{9,8},{10,11... | collective-permute-start | bytes 1769480 | tf_op jit(solution)/shard_map/ppermute | solution.py:609
  33.7 11.5 %collective-permute-start.9 = (bf16[576,256]{1,0:T(8,128)(2,1)S(1)}, bf16[576,256]{1,0:T(8,128)(2,1)S(1)}, u32[]{:S(2)}, u32[]{:S(2)}) collective-permute-start(bf16[576,256]{1,0:T(8,128)(2,1)S(1)} %bitcast.19), channel_id=1, source_target_pairs={{0,1},{1,0},{2,3},{3,2},{4,5},{5,4},{6,7},{7,6},{8,9},{9,8},{10,11... | collective-permute-start | bytes 884744 | tf_op jit(solution)/shard_map/ppermute | solution.py:609
  34.2 11.0 %collective-permute-start.10 = (bf16[576,256]{1,0:T(8,128)(2,1)S(1)}, bf16[576,256]{1,0:T(8,128)(2,1)S(1)}, u32[]{:S(2)}, u32[]{:S(2)}) collective-permute-start(bf16[576,256]{1,0:T(8,128)(2,1)S(1)} %get-tuple-element.77.refs_3_), channel_id=1, source_target_pairs={{0,2},{1,3},{2,0},{3,1},{4,6},{5,7},{6,4},{7,5},{8,10},{9,11},{10,... | collective-permute-start | bytes 884744 | tf_op jit(solution)/shard_map/ppermute | solution.py:609
  35.0 13.7 %collective-permute-start.11 = (bf16[576,256]{1,0:T(8,128)(2,1)S(1)}, bf16[576,256]{1,0:T(8,128)(2,1)S(1)}, u32[]{:S(2)}, u32[]{:S(2)}) collective-permute-start(bf16[576,256]{1,0:T(8,128)(2,1)S(1)} %bitcast.20), channel_id=1, source_target_pairs={{0,3},{1,2},{2,1},{3,0},{4,7},{5,6},{6,5},{7,4},{8,11},{9,10},{10,... | collective-permute-start | bytes 884744 | tf_op jit(solution)/shard_map/ppermute | solution.py:609
  35.6 9.6 %collective-permute-start.12 = (bf16[128,1024]{1,0:T(8,128)(2,1)S(1)}, bf16[128,1024]{1,0:T(8,128)(2,1)S(1)}, u32[]{:S(2)}, u32[]{:S(2)}) collective-permute-start(bf16[128,1024]{1,0:T(8,128)(2,1)S(1)} %collective-permute-done.6.a2), channel_id=1, source_target_pairs={{0,4},{1,5},{2,6},{3,7},{4,0},{5,1},{6,2},{7,3},{8,12},{9,13},{10,... | collective-permute-start | bytes 786440 | tf_op jit(solution)/shard_map/ppermute | solution.py:615
  44.3 12.8 %collective-permute-start.14 = (bf16[288,512]{1,0:T(8,128)(2,1)S(1)}, bf16[288,512]{1,0:T(8,128)(2,1)S(1)}, u32[]{:S(2)}, u32[]{:S(2)}) collective-permute-start(bf16[288,512]{1,0:T(8,128)(2,1)S(1)} %get-tuple-element.86.refs_7_.a_ref), channel_id=1, source_target_pairs={{0,2},{1,3},{2,0},{3,1},{4,6},{5,7},{6,4},{7,5},{8,10},{9,11},{10,... | collective-permute-start | bytes 884744 | tf_op jit(solution)/shard_map/ppermute | solution.py:609
  51.3 10.8 %collective-permute-start.13 = (bf16[288,512]{1,0:T(8,128)(2,1)S(1)}, bf16[288,512]{1,0:T(8,128)(2,1)S(1)}, u32[]{:S(2)}, u32[]{:S(2)}) collective-permute-start(bf16[288,512]{1,0:T(8,128)(2,1)S(1)} %shard_map.111.refs_7_.b_ref), channel_id=1, source_target_pairs={{0,2},{1,3},{2,0},{3,1},{4,6},{5,7},{6,4},{7,5},{8,10},{9,11},{10,... | collective-permute-start | bytes 884744 | tf_op jit(solution)/shard_map/ppermute | solution.py:609
  52.6 2.7 %collective-permute-start.15 = (bf16[128,1024]{1,0:T(8,128)(2,1)S(1)}, bf16[128,1024]{1,0:T(8,128)(2,1)S(1)}, u32[]{:S(2)}, u32[]{:S(2)}) collective-permute-start(bf16[128,1024]{1,0:T(8,128)(2,1)S(1)} %collective-permute-done.6.a2), channel_id=1, source_target_pairs={{0,1},{1,0},{2,3},{3,2},{4,5},{5,4},{6,7},{7,6},{8,9},{9,8},{10,11... | collective-permute-start | bytes 786440 | tf_op jit(solution)/shard_map/ppermute | solution.py:609
  53.4 1.9 %collective-permute-start.16 = (bf16[128,1024]{1,0:T(8,128)(2,1)S(1)}, bf16[128,1024]{1,0:T(8,128)(2,1)S(1)}, u32[]{:S(2)}, u32[]{:S(2)}) collective-permute-start(bf16[128,1024]{1,0:T(8,128)(2,1)S(1)} %collective-permute-done.12.b2), channel_id=1, source_target_pairs={{0,1},{1,0},{2,3},{3,2},{4,5},{5,4},{6,7},{7,6},{8,9},{9,8},{10,11... | collective-permute-start | bytes 786440 | tf_op jit(solution)/shard_map/ppermute | solution.py:609
  54.5 1.0 %copy-start.3 = (bf16[256,1024]{1,0:T(8,128)(2,1)S(1)}, bf16[256,1024]{1,0:T(8,128)(2,1)}, u32[]{:S(2)}) copy-start(bf16[256,1024]{1,0:T(8,128)(2,1)} %po_ref) | copy-start | bytes 1572868
  54.5 1.0 %copy-start.8 = (f32[2,1024]{1,0:T(2,128)S(1)}, f32[2,1024]{1,0:T(2,128)}, u32[]{:S(2)}) copy-start(f32[2,1024]{1,0:T(2,128)} %c_ref.1) | copy-start | bytes 24580
  63.1 10.9 %collective-permute-start.17 = (bf16[288,256]{1,0:T(8,128)(2,1)S(1)}, bf16[288,256]{1,0:T(8,128)(2,1)S(1)}, u32[]{:S(2)}, u32[]{:S(2)}) collective-permute-start(bf16[288,256]{1,0:T(8,128)(2,1)S(1)} %get-tuple-element.98), channel_id=1, source_target_pairs={{0,4},{1,5},{2,6},{3,7},{4,8},{5,9},{6,10},{7,11},{8,12},{9,13},{1... | collective-permute-start | bytes 442376 | tf_op jit(solution)/shard_map/ppermute | solution.py:609
  63.1 10.8 %collective-permute-start.18 = (bf16[288,256]{1,0:T(8,128)(2,1)S(1)}, bf16[288,256]{1,0:T(8,128)(2,1)S(1)}, u32[]{:S(2)}, u32[]{:S(2)}) collective-permute-start(bf16[288,256]{1,0:T(8,128)(2,1)S(1)} %get-tuple-element.99), channel_id=1, source_target_pairs={{0,1},{1,0},{2,3},{3,2},{4,5},{5,4},{6,7},{7,6},{8,9},{9,8},{10,11... | collective-permute-start | bytes 442376 | tf_op jit(solution)/shard_map/ppermute | solution.py:609
  63.2 11.5 %collective-permute-start.19 = (bf16[288,256]{1,0:T(8,128)(2,1)S(1)}, bf16[288,256]{1,0:T(8,128)(2,1)S(1)}, u32[]{:S(2)}, u32[]{:S(2)}) collective-permute-start(bf16[288,256]{1,0:T(8,128)(2,1)S(1)} %get-tuple-element.100), channel_id=1, source_target_pairs={{0,5},{1,4},{2,7},{3,6},{4,9},{5,8},{6,11},{7,10},{8,13},{9,12},{1... | collective-permute-start | bytes 442376 | tf_op jit(solution)/shard_map/ppermute | solution.py:609
  68.3 4.1 %collective-permute-start.20 = (f32[2,1024]{1,0:T(2,128)S(1)}, f32[2,1024]{1,0:T(2,128)S(1)}, u32[]{:S(2)}, u32[]{:S(2)}) collective-permute-start(f32[2,1024]{1,0:T(2,128)S(1)} %shard_map.121), channel_id=1, source_target_pairs={{0,2},{1,3},{2,0},{3,1},{4,6},{5,7},{6,4},{7,5},{8,10},{9,11},{10,... | collective-permute-start | bytes 24584 | tf_op jit(solution)/shard_map/ppermute | solution.py:609
  72.4 4.3 %collective-permute-start.23 = (f32[2,1792]{1,0:T(2,128)S(1)}, f32[2,1792]{1,0:T(2,128)S(1)}, u32[]{:S(2)}, u32[]{:S(2)}) collective-permute-start(f32[2,1792]{1,0:T(2,128)S(1)} %pad_maximum_fusion), channel_id=1, source_target_pairs={{0,5},{1,4},{2,7},{3,6},{4,1},{5,0},{6,3},{7,2},{8,13},{9,12},{10,... | collective-permute-start | bytes 43016 | tf_op jit(solution)/shard_map/ppermute | solution.py:615
  73.1 3.5 %collective-permute-start.21 = (f32[2,1792]{1,0:T(2,128)S(1)}, f32[2,1792]{1,0:T(2,128)S(1)}, u32[]{:S(2)}, u32[]{:S(2)}) collective-permute-start(f32[2,1792]{1,0:T(2,128)S(1)} %pad_maximum_fusion), channel_id=1, source_target_pairs={{0,1},{1,0},{2,3},{3,2},{4,5},{5,4},{6,7},{7,6},{8,9},{9,8},{10,11... | collective-permute-start | bytes 43016 | tf_op jit(solution)/shard_map/ppermute | solution.py:609
  76.6 3.8 %collective-permute-start.22 = (f32[2,1792]{1,0:T(2,128)S(1)}, f32[2,1792]{1,0:T(2,128)S(1)}, u32[]{:S(2)}, u32[]{:S(2)}) collective-permute-start(f32[2,1792]{1,0:T(2,128)S(1)} %pad_maximum_fusion.1), channel_id=1, source_target_pairs={{0,4},{1,5},{2,6},{3,7},{4,0},{5,1},{6,2},{7,3},{8,12},{9,13},{10,... | collective-permute-start | bytes 43016 | tf_op jit(solution)/shard_map/ppermute | solution.py:615
  80.4 8.1 %collective-permute-start.25 = (f32[2,1792]{1,0:T(2,128)S(1)}, f32[2,1792]{1,0:T(2,128)S(1)}, u32[]{:S(2)}, u32[]{:S(2)}) collective-permute-start(f32[2,1792]{1,0:T(2,128)S(1)} %add_add_fusion.1), channel_id=1, source_target_pairs={{0,16},{1,17},{2,18},{3,19},{4,20},{5,21},{6,22},{7,23},{8,24},{9,... | collective-permute-start | bytes 43016 | tf_op jit(solution)/shard_map/ppermute | solution.py:615
  85.8 5.5 %collective-permute-start.26 = (f32[2,1792]{1,0:T(2,128)S(1)}, f32[2,1792]{1,0:T(2,128)S(1)}, u32[]{:S(2)}, u32[]{:S(2)}) collective-permute-start(f32[2,1792]{1,0:T(2,128)S(1)} %add_add_fusion.1), channel_id=1, source_target_pairs={{0,24},{1,25},{2,26},{3,27},{4,28},{5,29},{6,30},{7,31},{8,16},{9,... | collective-permute-start | bytes 43016 | tf_op jit(solution)/shard_map/ppermute | solution.py:615
  85.8 5.5 %collective-permute-start.24 = (f32[2,1792]{1,0:T(2,128)S(1)}, f32[2,1792]{1,0:T(2,128)S(1)}, u32[]{:S(2)}, u32[]{:S(2)}) collective-permute-start(f32[2,1792]{1,0:T(2,128)S(1)} %add_add_fusion.1), channel_id=1, source_target_pairs={{0,8},{1,9},{2,10},{3,11},{4,12},{5,13},{6,14},{7,15},{8,0},{9,1},... | collective-permute-start | bytes 43016 | tf_op jit(solution)/shard_map/ppermute | solution.py:615

commit v8 on v7

--- a/solution.py
+++ b/solution.py
@@ -661,14 +661,16 @@
     wc_own, b_own = clip_qkv(w3, c3)
     wc_peer, b_peer = clip_qkv(w3_peer, c3_peer)
     idk, idq = window_ids(place, region_ids, WLAT * lev * lon)
-    f_low, f_up_y, w1 = lax.optimization_barrier((f_low, f_up_y, w1))
+    f_low, f_up_y, w1, t_low, wc_own = lax.optimization_barrier(
+        (f_low, f_up_y, w1, t_raw[:, :half], wc_own)
+    )
     f_low_y = send(f_low, 0, 2)
-    t_low = send(after(t_raw, f_low)[:, :half], -1, 0)
+    t_low = send(t_low, -1, 0)
     t_own, t_away = split(place, t_raw, t_low)
     t_away = t_away.reshape(t_own.shape)
     t_1 = send(t_away, 0, 1)
-    f_low_y, t_own, t_away, slab, wc_own, wc_peer, idk, idq = lax.optimization_barrier(
-        (f_low_y, t_own, t_away, slab, wc_own, wc_peer, idk, idq)
+    f_low_y, t_own, t_away, slab, wc_peer, idk, idq = lax.optimization_barrier(
+        (f_low_y, t_own, t_away, slab, wc_peer, idk, idq)
     )
     x_0, x_2, x_away = split(place, f_raw, f_low, f_up_y, f_low_y)
     pieces = (x_0, x_2, send(x_away, 0, 1))

time: 92.9 us -> 89.9 us (0.968)
  Pallas kernels: 39.5 us -> 36.8 us
    pallas_call x2, Pallas kernels: 2.91 us -> 1.38 us  [clip_qkv(): pl.pallas_call(clip_qkv_kernel, out_shape=(jax.ShapeDtypeStruct((n, d, e)...]
    unnamed x24 -> x22, local copies, waits for them, and re-layouts: 3.06 us -> 4.48 us
    pallas_call x2, Pallas kernels: 5.02 us -> 3.62 us  [qkv_sums(): pl.pallas_call(functools.partial(qkv_sums_kernel, side), out_shape=jax.Sh...]
    ppermute x6, starting transfers between devices: 6.94 us -> 5.82 us  [swap(): return lax.ppermute(block, ('lat', 'tp'), route)]
    slice x1, local copies, waits for them, and re-layouts: 1.92 us -> 0.9 us  [local(): t_raw[:, :half]]
  transfers between devices with their start and end apart: 27 -> 27, of which waited for: 9 -> 7; matrix products, arithmetic and copies ran while one was open for 4% -> 3% of each run, Pallas kernels for 39% -> 37%
where the time goes in v8:
time: 89.9 us; the launch traced here: 89.6 us
  Pallas kernels  36.8 us (41%)
  starting transfers between devices  26.5 us (29%)
  waiting for transfers between devices  16.3 us (18%)
  local copies, waits for them, and re-layouts  8.23 us (9%)
  between operations  1.63 us (2%)
    ppermute x21, starting transfers between devices, send(): return lax.ppermute(block, ('lat', 'tp'), route)  20.7 us
    ppermute x21, waiting for transfers between devices, send(): return lax.ppermute(block, ('lat', 'tp'), route)  9.66 us
    pallas_call x1, Pallas kernels, forward(): pl.pallas_call(forward_kernel, out_shape=(jax.ShapeDtypeStruct((n, d), BF...  7.64 us
    ppermute x6, waiting for transfers between devices, swap(): return lax.ppermute(block, ('lat', 'tp'), route)  6.6 us
    pallas_call x2, Pallas kernels, backward(): pl.pallas_call(functools.partial(backward_kernel, group), out_shape=jax.S...  6.43 us
    ppermute x6, starting transfers between devices, swap(): return lax.ppermute(block, ('lat', 'tp'), route)  5.82 us
    unnamed x22, local copies, waits for them, and re-layouts  4.48 us
    pallas_call x2, Pallas kernels, qkv_sums(): pl.pallas_call(functools.partial(qkv_sums_kernel, side), out_shape=jax.Sh...  3.62 us
  transfers between devices with their start and end apart: 27, of which 7 were waited for; matrix products, arithmetic and copies ran while one was open for 3% of the time, Pallas kernels for 37%

profile of v8, /device:TPU:0, one launch (start us, length us, event | category | flops | bytes accessed | tf_op | source)
XLA Modules:
  0.0 89.6 jit_solution(2368699828251494001)
XLA Ops:
  0.6 0.0 copy-start
  0.6 1.0 %copy-done = bf16[42,2,12,256]{3,1,2,0:T(2,128)(2,1)S(1)} copy-done((bf16[42,2,12,256]{3,1,2,0:T(2,128)(2,1)S(1)}, bf16[42,2,12,256]{3,1,2,0:T(2,128)(2,1)}, u32[]{:S(2)}) %copy-start) | copy-done | bytes 516120
  1.7 0.9 shard_map.103
  2.6 0.5 collective-permute-start.7
  3.1 0.1 collective-permute-start.2
  3.2 6.0 %collective-permute-start = (bf16[42,6,2,256]{3,2,1,0:T(2,128)(2,1)}, bf16[42,6,2,256]{3,2,1,0:T(2,128)(2,1)}, u32[]{:S(2)}, u32[]{:S(2)}) collective-permute-start(bf16[42,6,2,256]{3,2,1,0:T(2,128)(2,1)} %get-tuple-element.59), channel_id=1, source_target_pairs={{0,28},{1,29},{2,30},{3,31},{4,0},{5,1},{6,2},{7,3},{8,4},{9,5},{1... | collective-permute-start | bytes 774152 | tf_op jit(solution)/shard_map/ppermute | solution.py:609
  9.1 1.5 %collective-permute-start.1 = (bf16[42,6,2,256]{3,2,1,0:T(2,128)(2,1)}, bf16[42,6,2,256]{3,2,1,0:T(2,128)(2,1)}, u32[]{:S(2)}, u32[]{:S(2)}) collective-permute-start(bf16[42,6,2,256]{3,2,1,0:T(2,128)(2,1)} %get-tuple-element.60), channel_id=1, source_target_pairs={{0,2},{1,3},{2,0},{3,1},{4,6},{5,7},{6,4},{7,5},{8,10},{9,11},{10,... | collective-permute-start | bytes 774152 | tf_op jit(solution)/shard_map/ppermute | solution.py:609
  10.6 0.0 collective-permute-start.5
  10.6 1.4 %collective-permute-done.5.c_ref = f32[3,2,256]{2,1,0:T(2,128)S(1)} collective-permute-done((f32[3,2,256]{2,1,0:T(2,128)}, f32[3,2,256]{2,1,0:T(2,128)S(1)}, u32[]{:S(2)}, u32[]{:S(2)}) %collective-permute-start.5) | collective-permute-done | bytes 6176 | tf_op jit(solution)/shard_map/ppermute | solution.py:609
  12.0 1.7 %constant_dynamic-slice_fusion = bf16[128,1024]{1,0:T(8,128)(2,1)} fusion(bf16[256,1024]{1,0:T(8,128)(2,1)} %po_ref, s32[]{:T(128)S(6)} %select_n.16), kind=kLoop, calls=%fused_computation.5 | loop fusion | bytes 524292 | tf_op jit(solution)/shard_map/dynamic_slice | solution.py:659
  13.7 0.5 collective-permute-start.6
  14.2 1.4 %copy-done.2 = bf16[1024,3,256]{2,0,1:T(8,128)(2,1)S(1)} copy-done((bf16[1024,3,256]{2,0,1:T(8,128)(2,1)S(1)}, bf16[1024,3,256]{2,0,1:T(8,128)(2,1)}, u32[]{:S(2)}) %copy-start.2) | copy-done | bytes 1572888
  15.6 0.7 copy-done.8
  16.3 0.7 shard_map.104
  17.0 1.2 %copy-done.9 = bf16[3,1024,256]{2,1,0:T(8,128)(2,1)} copy-done((bf16[3,1024,256]{2,1,0:T(8,128)(2,1)}, bf16[3,1024,256]{2,1,0:T(8,128)(2,1)S(1)}, u32[]{:S(2)}) %copy-start.9) | copy-done | bytes 1572888
  18.2 0.9 slice.12
  19.1 2.0 %collective-permute-start.4 = (bf16[42,6,2,256]{3,2,1,0:T(2,128)(2,1)}, bf16[42,6,2,256]{3,2,1,0:T(2,128)(2,1)}, u32[]{:S(2)}, u32[]{:S(2)}) collective-permute-start(bf16[42,6,2,256]{3,2,1,0:T(2,128)(2,1)} %slice.12), channel_id=1, source_target_pairs={{0,28},{1,29},{2,30},{3,31},{4,0},{5,1},{6,2},{7,3},{8,4},{9,5},{1... | collective-permute-start | bytes 774152 | tf_op jit(solution)/shard_map/ppermute | solution.py:609
  21.1 0.8 collective-permute-start.3
  22.5 0.1 pad_add_fusion.s_ref
  22.6 1.0 %shard_map.107 = (s32[576,1]{1,0:T(8,128)S(1)}, s32[4,1,288]{2,1,0:T(1,128)S(1)}) custom-call(s32[3]{0:T(128)S(1)} %pad_add_fusion.s_ref, s32[42,2,96]{2,1,0:T(2,128)S(1)} %copy-done.6), custom_call_target="tpu_custom_call" | custom-call | flops 1 | bytes 1 | tf_op jit(solution)/shard_map/pallas_call | solution.py:553
  23.6 3.8 %collective-permute-done.4.refs_1_ = bf16[42,6,2,256]{3,2,1,0:T(2,128)(2,1)} collective-permute-done((bf16[42,6,2,256]{3,2,1,0:T(2,128)(2,1)}, bf16[42,6,2,256]{3,2,1,0:T(2,128)(2,1)}, u32[]{:S(2)}, u32[]{:S(2)}) %collective-permute-start.4) | collective-permute-done | bytes 258080 | tf_op jit(solution)/shard_map/ppermute | solution.py:609
  27.5 1.4 %shard_map.105 = (bf16[576,256]{1,0:T(8,128)(2,1)S(1)}, bf16[1,576,256]{2,1,0:T(8,128)(2,1)S(1)}) custom-call(s32[3]{0:T(128)S(1)} %pad_add_fusion.s_ref, bf16[42,12,2,256]{3,2,1,0:T(2,128)(2,1)S(1)} %bitcast.16, bf16[42,6,2,256]{3,2,1,0:T(2,128)(2,1)} %collective-permute-done.4.refs_1_), custom_call_target="tpu_custom_call" | custom-call | flops 1 | bytes 1 | tf_op jit(solution)/shard_map/pallas_call | solution.py:497
  28.9 0.7 shard_map.106
  29.6 0.0 collective-permute-done.6.a2
  29.6 1.9 %shard_map.108 = (bf16[576,256]{1,0:T(8,128)(2,1)S(1)}, bf16[576,256]{1,0:T(8,128)(2,1)S(1)}, bf16[2,576,256]{2,1,0:T(8,128)(2,1)S(1)}) custom-call(s32[3]{0:T(128)S(1)} %pad_add_fusion.s_ref, bf16[42,12,2,256]{3,2,1,0:T(2,128)(2,1)S(1)} %bitcast.11, bf16[42,6,2,256]{3,2,1,0:T(2,128)(2,1)} %collective-permute-done.refs_1_, ...), custom_call_target="tpu_custom_call" | custom-call | flops 1 | bytes 1 | tf_op jit(solution)/shard_map/pallas_call | solution.py:497
  31.5 0.1 collective-permute-start.8
  31.6 0.5 collective-permute-start.9
  32.1 1.5 %collective-permute-start.10 = (bf16[576,256]{1,0:T(8,128)(2,1)S(1)}, bf16[576,256]{1,0:T(8,128)(2,1)S(1)}, u32[]{:S(2)}, u32[]{:S(2)}) collective-permute-start(bf16[576,256]{1,0:T(8,128)(2,1)S(1)} %get-tuple-element.77.refs_3_), channel_id=1, source_target_pairs={{0,2},{1,3},{2,0},{3,1},{4,6},{5,7},{6,4},{7,5},{8,10},{9,11},{10,... | collective-permute-start | bytes 884744 | tf_op jit(solution)/shard_map/ppermute | solution.py:609
  33.7 7.6 %shard_map.109 = (bf16[576,1024]{1,0:T(8,128)(2,1)S(1)}, bf16[6,576,256]{2,1,0:T(8,128)(2,1)S(1)}, bf16[288,512]{1,0:T(8,128)(2,1)S(1)}) custom-call(s32[1]{0:T(128)} %bitcast.2.t_ref, bf16[576,256]{1,0:T(8,128)(2,1)S(1)} %get-tuple-element.74.refs_0_, bf16[576,256]{1,0:T(8,128)(2,1)S(1)} %get-tuple-element.75.refs_1_, ...), custom_call_target="tpu_custom_call" | custom-call | flops 8000000000 | bytes 10000000 | tf_op jit(solution)/shard_map/pallas_call | solution.py:213
  41.3 1.0 %shard_map.110.p_ref = f32[8,144,288]{2,1,0:T(8,128)S(1)} custom-call(bf16[6,576,256]{2,1,0:T(8,128)(2,1)S(1)} %get-tuple-element.102.qkv_ref, s32[576,1]{1,0:T(8,128)S(1)} %get-tuple-element.81.refs_5_.idk_ref.refs_10_, s32[4,1,288]{2,1,0:T(1,128)S(1)} %get-tuple-element.82.refs_6_.idq_ref), custom_call_target="tpu_custom_call" | custom-call | flops 1 | bytes 1 | tf_op jit(solution)/shard_map/pallas_call | solution.py:326
  42.3 1.5 %collective-permute-start.14 = (bf16[288,512]{1,0:T(8,128)(2,1)S(1)}, bf16[288,512]{1,0:T(8,128)(2,1)S(1)}, u32[]{:S(2)}, u32[]{:S(2)}) collective-permute-start(bf16[288,512]{1,0:T(8,128)(2,1)S(1)} %get-tuple-element.86.refs_7_.a_ref), channel_id=1, source_target_pairs={{0,2},{1,3},{2,0},{3,1},{4,6},{5,7},{6,4},{7,5},{8,10},{9,11},{10,... | collective-permute-start | bytes 884744 | tf_op jit(solution)/shard_map/ppermute | solution.py:609
  43.9 3.5 %collective-permute-done.11.refs_6_ = bf16[576,256]{1,0:T(8,128)(2,1)S(1)} collective-permute-done((bf16[576,256]{1,0:T(8,128)(2,1)S(1)}, bf16[576,256]{1,0:T(8,128)(2,1)S(1)}, u32[]{:S(2)}, u32[]{:S(2)}) %collective-permute-start.11) | collective-permute-done | bytes 294944 | tf_op jit(solution)/shard_map/ppermute | solution.py:609
  47.3 2.7 %shard_map.111.refs_7_.b_ref = bf16[288,512]{1,0:T(8,128)(2,1)S(1)} custom-call(bf16[6,576,256]{2,1,0:T(8,128)(2,1)S(1)} %get-tuple-element.102.qkv_ref, s32[576,1]{1,0:T(8,128)S(1)} %get-tuple-element.81.refs_5_.idk_ref.refs_10_, s32[4,1,288]{2,1,0:T(1,128)S(1)} %get-tuple-element.82.refs_6_.idq_ref), custom_call_target="tpu_custom_call" | custom-call | flops 1 | bytes 1 | tf_op jit(solution)/shard_map/pallas_call | solution.py:200
  50.0 0.8 collective-permute-start.13
  50.8 1.3 %collective-permute-start.15 = (bf16[128,1024]{1,0:T(8,128)(2,1)S(1)}, bf16[128,1024]{1,0:T(8,128)(2,1)S(1)}, u32[]{:S(2)}, u32[]{:S(2)}) collective-permute-start(bf16[128,1024]{1,0:T(8,128)(2,1)S(1)} %collective-permute-done.6.a2), channel_id=1, source_target_pairs={{0,1},{1,0},{2,3},{3,2},{4,5},{5,4},{6,7},{7,6},{8,9},{9,8},{10,11... | collective-permute-start | bytes 786440 | tf_op jit(solution)/shard_map/ppermute | solution.py:609
  52.1 1.0 %shard_map.117.p_ref = f32[8,144,288]{2,1,0:T(8,128)S(1)} custom-call(bf16[6,576,256]{2,1,0:T(8,128)(2,1)S(1)} %get-tuple-element.102.qkv_ref, s32[576,1]{1,0:T(8,128)S(1)} %get-tuple-element.81.refs_5_.idk_ref.refs_10_, s32[4,1,288]{2,1,0:T(1,128)S(1)} %get-tuple-element.82.refs_6_.idq_ref), custom_call_target="tpu_custom_call" | custom-call | flops 1 | bytes 1 | tf_op jit(solution)/shard_map/pallas_call | solution.py:326
  53.1 0.0 copy-start.4
  53.1 0.0 copy-start.7
  53.1 0.8 shard_map.119
  54.0 0.1 copy-done.4
  54.2 1.6 %shard_map.112 = (bf16[1024,1024]{1,0:T(8,128)(2,1)S(1)}, f32[8,1024]{1,0:T(8,128)S(1)}) custom-call(s32[3]{0:T(128)S(1)} %pad_add_fusion.s_ref, bf16[256,1024]{1,0:T(8,128)(2,1)S(1)} %copy-done.4, bf16[256,1024]{1,0:T(8,128)(2,1)S(1)} %collective-permute-done.2.w1.pp_ref, bf16[128,1024]{1,0:T(8,128)(2,1)S(1)} %collective-permute-done.6.a2, ...), custom_call_target="tpu_custom_call" | custom-call | flops 1 | bytes 1 | tf_op jit(solution)/shard_map/pallas_call | solution.py:92
  55.7 1.0 %shard_map.113 = (bf16[144,256]{1,0:T(8,128)(2,1)S(1)}, bf16[144,256]{1,0:T(8,128)(2,1)S(1)}, bf16[144,256]{1,0:T(8,128)(2,1)S(1)}, bf16[144,256]{1,0:T(8,128)(2,1)S(1)}, bf16[288,1024]{1,0:T(8,128)(2,1)S(1)}) custom-call(s32[1]{0:T(128)} %bitcast.2.t_ref, bf16[576,256]{1,0:T(8,128)(2,1)S(1)} %get-tuple-element.74.refs_0_, ...), custom_call_target="tpu_custom_call" | custom-call | flops 1 | bytes 1 | tf_op jit(solution)/shard_map/pallas_call | solution.py:296
  56.7 3.2 %shard_map.114.g0_ref = bf16[6,288,256]{2,1,0:T(8,128)(2,1)S(1)} custom-call(bf16[288,1024]{1,0:T(8,128)(2,1)S(1)} %get-tuple-element.91.err_ref.e0_ref, bf16[1024,1024]{1,0:T(8,128)(2,1)S(1)} %get-tuple-element.90.refs_9_.wc_ref, bf16[6,576,256]{2,1,0:T(8,128)(2,1)S(1)} %get-tuple-element.102.qkv_ref, f32[8,144,288]{2,1,0:T(8,128)S(1)} %shard_map.110.p_ref), custom_call_target="tpu_custom_call" | custom-call | flops 1 | bytes 1 | tf_op jit(solution)/shard_map/pallas_call | solution.py:402
  59.9 0.1 collective-permute-done.13.refs_8_
  60.1 0.9 %shard_map.115 = (bf16[288,256]{1,0:T(8,128)(2,1)S(1)}, bf16[288,256]{1,0:T(8,128)(2,1)S(1)}, bf16[288,256]{1,0:T(8,128)(2,1)S(1)}, bf16[288,256]{1,0:T(8,128)(2,1)S(1)}, bf16[288,1024]{1,0:T(8,128)(2,1)S(1)}) custom-call(s32[1]{0:T(128)} %bitcast.2.t_ref, bf16[576,256]{1,0:T(8,128)(2,1)S(1)} %get-tuple-element.74.refs_0_, ...), custom_call_target="tpu_custom_call" | custom-call | flops 1 | bytes 1 | tf_op jit(solution)/shard_map/pallas_call | solution.py:296
  61.0 0.1 collective-permute-start.17
  61.1 0.5 collective-permute-start.18
  61.6 0.4 collective-permute-start.19
  61.9 3.2 %shard_map.118.g1_ref = bf16[6,288,256]{2,1,0:T(8,128)(2,1)S(1)} custom-call(bf16[288,1024]{1,0:T(8,128)(2,1)S(1)} %get-tuple-element.101.err_ref.e1_ref, bf16[1024,1024]{1,0:T(8,128)(2,1)S(1)} %get-tuple-element.90.refs_9_.wc_ref, bf16[6,576,256]{2,1,0:T(8,128)(2,1)S(1)} %get-tuple-element.102.qkv_ref, f32[8,144,288]{2,1,0:T(8,128)S(1)} %shard_map.117.p_ref), custom_call_target="tpu_custom_call" | custom-call | flops 8000000000 | bytes 10000000 | tf_op jit(solution)/shard_map/pallas_call | solution.py:402
  65.1 1.6 %shard_map.121 = f32[2,1024]{1,0:T(2,128)S(1)} custom-call(bf16[288,1024]{1,0:T(8,128)(2,1)S(1)} %get-tuple-element.91.err_ref.e0_ref, bf16[288,1024]{1,0:T(8,128)(2,1)S(1)} %get-tuple-element.101.err_ref.e1_ref, bf16[512,576]{1,0:T(8,128)(2,1)S(1)} %get-tuple-element.106.attn_t, bf16[256,1024]{1,0:T(8,128)(2,1)S(1)} %copy-done.4, ...), custom_call_target="tpu_custom_call" | custom-call | flops 1000000000 | bytes 3000000 | tf_op jit(solution)/shard_map/pallas_call | solution.py:359
  66.7 1.1 %collective-permute-start.20 = (f32[2,1024]{1,0:T(2,128)S(1)}, f32[2,1024]{1,0:T(2,128)S(1)}, u32[]{:S(2)}, u32[]{:S(2)}) collective-permute-start(f32[2,1024]{1,0:T(2,128)S(1)} %shard_map.121), channel_id=1, source_target_pairs={{0,2},{1,3},{2,0},{3,1},{4,6},{5,7},{6,4},{7,5},{8,10},{9,11},{10,... | collective-permute-start | bytes 24584 | tf_op jit(solution)/shard_map/ppermute | solution.py:609
  67.8 1.8 %shard_map.120 = f32[2,768]{1,0:T(2,128)S(1)} custom-call(bf16[6,288,256]{2,1,0:T(8,128)(2,1)S(1)} %shard_map.114.g0_ref, bf16[6,288,256]{2,1,0:T(8,128)(2,1)S(1)} %shard_map.118.g1_ref, bf16[1024,576]{1,0:T(8,128)(2,1)S(1)} %get-tuple-element.104.normed_t, bf16[3,1024,256]{2,1,0:T(8,128)(2,1)S(1)} %collective-permute-done.7.w_ref, ...), custom_call_target="tpu_custom_call" | custom-call | flops 8000000000 | bytes 10000000 | tf_op jit(solution)/shard_map/pallas_call | solution.py:429
  69.6 0.8 collective-permute-done.20
  70.5 0.6 collective-permute-start.23
  71.1 1.6 %collective-permute-start.21 = (f32[2,1792]{1,0:T(2,128)S(1)}, f32[2,1792]{1,0:T(2,128)S(1)}, u32[]{:S(2)}, u32[]{:S(2)}) collective-permute-start(f32[2,1792]{1,0:T(2,128)S(1)} %pad_maximum_fusion), channel_id=1, source_target_pairs={{0,1},{1,0},{2,3},{3,2},{4,5},{5,4},{6,7},{7,6},{8,9},{9,8},{10,11... | collective-permute-start | bytes 43016 | tf_op jit(solution)/shard_map/ppermute | solution.py:609
  72.8 1.8 %shard_map.122 = f32[2,768]{1,0:T(2,128)S(1)} custom-call(bf16[6,288,256]{2,1,0:T(8,128)(2,1)S(1)} %shard_map.114.g0_ref, bf16[6,288,256]{2,1,0:T(8,128)(2,1)S(1)} %shard_map.118.g1_ref, bf16[1024,576]{1,0:T(8,128)(2,1)S(1)} %get-tuple-element.104.normed_t, bf16[3,1024,256]{2,1,0:T(8,128)(2,1)S(1)} %bitcast.14, f32[3,8,256]{2,1,0:T(8,128)S(1)} %get-tuple-element.110.b_ref), custom_call_target="tpu_custom_call" | custom-call | flops 8000000000 | bytes 10000000 | tf_op jit(solution)/shard_map/pallas_call | solution.py:429
  74.6 0.1 collective-permute-start.22
  74.7 3.7 %collective-permute-done.22 = f32[2,1792]{1,0:T(2,128)S(1)} collective-permute-done((f32[2,1792]{1,0:T(2,128)S(1)}, f32[2,1792]{1,0:T(2,128)S(1)}, u32[]{:S(2)}, u32[]{:S(2)}) %collective-permute-start.22) | collective-permute-done | bytes 14368 | tf_op jit(solution)/shard_map/ppermute | solution.py:615
  78.4 4.5 %collective-permute-start.25 = (f32[2,1792]{1,0:T(2,128)S(1)}, f32[2,1792]{1,0:T(2,128)S(1)}, u32[]{:S(2)}, u32[]{:S(2)}) collective-permute-start(f32[2,1792]{1,0:T(2,128)S(1)} %add_add_fusion.1), channel_id=1, source_target_pairs={{0,16},{1,17},{2,18},{3,19},{4,20},{5,21},{6,22},{7,23},{8,24},{9,... | collective-permute-start | bytes 43016 | tf_op jit(solution)/shard_map/ppermute | solution.py:615
  82.9 0.6 collective-permute-start.24
  83.5 2.0 %shard_map.116 = bf16[42,12,2,256]{3,2,1,0:T(2,128)(2,1)} custom-call(s32[3]{0:T(128)S(1)} %pad_add_fusion.s_ref, bf16[288,256]{1,0:T(8,128)(2,1)S(1)} %get-tuple-element.97.a0, bf16[288,256]{1,0:T(8,128)(2,1)S(1)} %collective-permute-done.17.a1, bf16[288,256]{1,0:T(8,128)(2,1)S(1)} %collective-permute-done.18.b0, ...), custom_call_target="tpu_custom_call" | custom-call | flops 1 | bytes 1 | tf_op jit(solution)/shard_map/pallas_call | solution.py:592
  85.5 2.9 %collective-permute-done.26 = f32[2,1792]{1,0:T(2,128)S(1)} collective-permute-done((f32[2,1792]{1,0:T(2,128)S(1)}, f32[2,1792]{1,0:T(2,128)S(1)}, u32[]{:S(2)}, u32[]{:S(2)}) %collective-permute-start.26) | collective-permute-done | bytes 14368 | tf_op jit(solution)/shard_map/ppermute | solution.py:615
  88.4 0.6 slice.13
  89.0 0.6 slice.14
  (42 shorter events, 0.1 us)
Async XLA Ops:
  0.6 1.0 %copy-start = (bf16[42,2,12,256]{3,1,2,0:T(2,128)(2,1)S(1)}, bf16[42,2,12,256]{3,1,2,0:T(2,128)(2,1)}, u32[]{:S(2)}) copy-start(bf16[42,2,12,256]{3,1,2,0:T(2,128)(2,1)} %param.8) | copy-start | bytes 1548292
  1.7 16.5 %copy-start.5 = (bf16[42,2,12,256]{3,1,2,0:T(2,128)(2,1)S(1)}, bf16[42,2,12,256]{3,1,2,0:T(2,128)(2,1)}, u32[]{:S(2)}) copy-start(bf16[42,2,12,256]{3,1,2,0:T(2,128)(2,1)} %param.9) | copy-start | bytes 1548292
  1.7 20.9 %copy-start.6 = (s32[42,2,96]{2,1,0:T(2,128)S(1)}, s32[42,2,96]{2,1,0:T(2,128)}, u32[]{:S(2)}) copy-start(s32[42,2,96]{2,1,0:T(2,128)} %ids_ref.1) | copy-start | bytes 96772
  2.6 26.3 %collective-permute-start.7 = (bf16[3,1024,256]{2,1,0:T(8,128)(2,1)}, bf16[3,1024,256]{2,1,0:T(8,128)(2,1)S(1)}, u32[]{:S(2)}, u32[]{:S(2)}) collective-permute-start(bf16[3,1024,256]{2,1,0:T(8,128)(2,1)} %bitcast.12), channel_id=1, source_target_pairs={{0,1},{1,0},{2,3},{3,2},{4,5},{5,4},{6,7},{7,6},{8,9},{9,8},{10,11... | collective-permute-start | bytes 4718600 | tf_op jit(solution)/shard_map/ppermute | solution.py:609
  3.1 16.0 %collective-permute-start.2 = (bf16[256,1024]{1,0:T(8,128)(2,1)}, bf16[256,1024]{1,0:T(8,128)(2,1)S(1)}, u32[]{:S(2)}, u32[]{:S(2)}) collective-permute-start(bf16[256,1024]{1,0:T(8,128)(2,1)} %po_ref), channel_id=1, source_target_pairs={{0,1},{1,0},{2,3},{3,2},{4,5},{5,4},{6,7},{7,6},{8,9},{9,8},{10,11... | collective-permute-start | bytes 1572872 | tf_op jit(solution)/shard_map/ppermute | solution.py:609
  3.2 15.9 %collective-permute-start = (bf16[42,6,2,256]{3,2,1,0:T(2,128)(2,1)}, bf16[42,6,2,256]{3,2,1,0:T(2,128)(2,1)}, u32[]{:S(2)}, u32[]{:S(2)}) collective-permute-start(bf16[42,6,2,256]{3,2,1,0:T(2,128)(2,1)} %get-tuple-element.59), channel_id=1, source_target_pairs={{0,28},{1,29},{2,30},{3,31},{4,0},{5,1},{6,2},{7,3},{8,4},{9,5},{1... | collective-permute-start | bytes 774152 | tf_op jit(solution)/shard_map/ppermute | solution.py:609
  9.1 10.0 %collective-permute-start.1 = (bf16[42,6,2,256]{3,2,1,0:T(2,128)(2,1)}, bf16[42,6,2,256]{3,2,1,0:T(2,128)(2,1)}, u32[]{:S(2)}, u32[]{:S(2)}) collective-permute-start(bf16[42,6,2,256]{3,2,1,0:T(2,128)(2,1)} %get-tuple-element.60), channel_id=1, source_target_pairs={{0,2},{1,3},{2,0},{3,1},{4,6},{5,7},{6,4},{7,5},{8,10},{9,11},{10,... | collective-permute-start | bytes 774152 | tf_op jit(solution)/shard_map/ppermute | solution.py:609
  10.6 1.4 %collective-permute-start.5 = (f32[3,2,256]{2,1,0:T(2,128)}, f32[3,2,256]{2,1,0:T(2,128)S(1)}, u32[]{:S(2)}, u32[]{:S(2)}) collective-permute-start(f32[3,2,256]{2,1,0:T(2,128)} %bitcast.17), channel_id=1, source_target_pairs={{0,1},{1,0},{2,3},{3,2},{4,5},{5,4},{6,7},{7,6},{8,9},{9,8},{10,11... | collective-permute-start | bytes 18440 | tf_op jit(solution)/shard_map/ppermute | solution.py:609
  13.7 15.9 %collective-permute-start.6 = (bf16[128,1024]{1,0:T(8,128)(2,1)}, bf16[128,1024]{1,0:T(8,128)(2,1)S(1)}, u32[]{:S(2)}, u32[]{:S(2)}) collective-permute-start(bf16[128,1024]{1,0:T(8,128)(2,1)} %constant_dynamic-slice_fusion), channel_id=1, source_target_pairs={{0,2},{1,3},{2,0},{3,1},{4,6},{5,7},{6,4},{7,5},{8,10},{9,11},{10,... | collective-permute-start | bytes 786440 | tf_op jit(solution)/shard_map/ppermute | solution.py:609
  14.2 1.4 %copy-start.2 = (bf16[1024,3,256]{2,0,1:T(8,128)(2,1)S(1)}, bf16[1024,3,256]{2,0,1:T(8,128)(2,1)}, u32[]{:S(2)}) copy-start(bf16[1024,3,256]{2,0,1:T(8,128)(2,1)} %param.10) | copy-start | bytes 4718596
  15.6 0.7 copy-start.8
  17.0 1.2 %copy-start.9 = (bf16[3,1024,256]{2,1,0:T(8,128)(2,1)}, bf16[3,1024,256]{2,1,0:T(8,128)(2,1)S(1)}, u32[]{:S(2)}) copy-start(bf16[3,1024,256]{2,1,0:T(8,128)(2,1)S(1)} %get-tuple-element.79.refs_3_) | copy-start | bytes 4718596
  18.2 11.4 %copy-start.1 = (bf16[42,2,12,256]{3,1,2,0:T(2,128)(2,1)S(1)}, bf16[42,2,12,256]{3,1,2,0:T(2,128)(2,1)}, u32[]{:S(2)}) copy-start(bf16[42,2,12,256]{3,1,2,0:T(2,128)(2,1)} %param.8) | copy-start | bytes 1548292
  19.1 8.4 %collective-permute-start.4 = (bf16[42,6,2,256]{3,2,1,0:T(2,128)(2,1)}, bf16[42,6,2,256]{3,2,1,0:T(2,128)(2,1)}, u32[]{:S(2)}, u32[]{:S(2)}) collective-permute-start(bf16[42,6,2,256]{3,2,1,0:T(2,128)(2,1)} %slice.12), channel_id=1, source_target_pairs={{0,28},{1,29},{2,30},{3,31},{4,0},{5,1},{6,2},{7,3},{8,4},{9,5},{1... | collective-permute-start | bytes 774152 | tf_op jit(solution)/shard_map/ppermute | solution.py:609
  21.1 8.5 %collective-permute-start.3 = (bf16[42,6,2,256]{3,2,1,0:T(2,128)(2,1)}, bf16[42,6,2,256]{3,2,1,0:T(2,128)(2,1)}, u32[]{:S(2)}, u32[]{:S(2)}) collective-permute-start(bf16[42,6,2,256]{3,2,1,0:T(2,128)(2,1)} %collective-permute-done.refs_1_), channel_id=1, source_target_pairs={{0,2},{1,3},{2,0},{3,1},{4,6},{5,7},{6,4},{7,5},{8,10},{9,11},{10,... | collective-permute-start | bytes 774152 | tf_op jit(solution)/shard_map/ppermute | solution.py:609
  28.8 4.8 %copy-start.10 = (bf16[3,1024,256]{2,1,0:T(8,128)(2,1)S(1)}, bf16[3,1024,256]{2,1,0:T(8,128)(2,1)}, u32[]{:S(2)}) copy-start(bf16[3,1024,256]{2,1,0:T(8,128)(2,1)} %copy-done.9) | copy-start | bytes 4718596
  31.5 2.1 %collective-permute-start.8 = (bf16[2,576,256]{2,1,0:T(8,128)(2,1)S(1)}, bf16[2,576,256]{2,1,0:T(8,128)(2,1)S(1)}, u32[]{:S(2)}, u32[]{:S(2)}) collective-permute-start(bf16[2,576,256]{2,1,0:T(8,128)(2,1)S(1)} %get-tuple-element.76), channel_id=1, source_target_pairs={{0,1},{1,0},{2,3},{3,2},{4,5},{5,4},{6,7},{7,6},{8,9},{9,8},{10,11... | collective-permute-start | bytes 1769480 | tf_op jit(solution)/shard_map/ppermute | solution.py:609
  31.6 12.2 %collective-permute-start.9 = (bf16[576,256]{1,0:T(8,128)(2,1)S(1)}, bf16[576,256]{1,0:T(8,128)(2,1)S(1)}, u32[]{:S(2)}, u32[]{:S(2)}) collective-permute-start(bf16[576,256]{1,0:T(8,128)(2,1)S(1)} %bitcast.19), channel_id=1, source_target_pairs={{0,1},{1,0},{2,3},{3,2},{4,5},{5,4},{6,7},{7,6},{8,9},{9,8},{10,11... | collective-permute-start | bytes 884744 | tf_op jit(solution)/shard_map/ppermute | solution.py:609
  32.1 11.7 %collective-permute-start.10 = (bf16[576,256]{1,0:T(8,128)(2,1)S(1)}, bf16[576,256]{1,0:T(8,128)(2,1)S(1)}, u32[]{:S(2)}, u32[]{:S(2)}) collective-permute-start(bf16[576,256]{1,0:T(8,128)(2,1)S(1)} %get-tuple-element.77.refs_3_), channel_id=1, source_target_pairs={{0,2},{1,3},{2,0},{3,1},{4,6},{5,7},{6,4},{7,5},{8,10},{9,11},{10,... | collective-permute-start | bytes 884744 | tf_op jit(solution)/shard_map/ppermute | solution.py:609
  33.6 13.7 %collective-permute-start.11 = (bf16[576,256]{1,0:T(8,128)(2,1)S(1)}, bf16[576,256]{1,0:T(8,128)(2,1)S(1)}, u32[]{:S(2)}, u32[]{:S(2)}) collective-permute-start(bf16[576,256]{1,0:T(8,128)(2,1)S(1)} %bitcast.20), channel_id=1, source_target_pairs={{0,3},{1,2},{2,1},{3,0},{4,7},{5,6},{6,5},{7,4},{8,11},{9,10},{10,... | collective-permute-start | bytes 884744 | tf_op jit(solution)/shard_map/ppermute | solution.py:609
  33.6 10.2 %collective-permute-start.12 = (bf16[128,1024]{1,0:T(8,128)(2,1)S(1)}, bf16[128,1024]{1,0:T(8,128)(2,1)S(1)}, u32[]{:S(2)}, u32[]{:S(2)}) collective-permute-start(bf16[128,1024]{1,0:T(8,128)(2,1)S(1)} %collective-permute-done.6.a2), channel_id=1, source_target_pairs={{0,4},{1,5},{2,6},{3,7},{4,0},{5,1},{6,2},{7,3},{8,12},{9,13},{10,... | collective-permute-start | bytes 786440 | tf_op jit(solution)/shard_map/ppermute | solution.py:615
  42.3 13.4 %collective-permute-start.14 = (bf16[288,512]{1,0:T(8,128)(2,1)S(1)}, bf16[288,512]{1,0:T(8,128)(2,1)S(1)}, u32[]{:S(2)}, u32[]{:S(2)}) collective-permute-start(bf16[288,512]{1,0:T(8,128)(2,1)S(1)} %get-tuple-element.86.refs_7_.a_ref), channel_id=1, source_target_pairs={{0,2},{1,3},{2,0},{3,1},{4,6},{5,7},{6,4},{7,5},{8,10},{9,11},{10,... | collective-permute-start | bytes 884744 | tf_op jit(solution)/shard_map/ppermute | solution.py:609
  50.0 10.1 %collective-permute-start.13 = (bf16[288,512]{1,0:T(8,128)(2,1)S(1)}, bf16[288,512]{1,0:T(8,128)(2,1)S(1)}, u32[]{:S(2)}, u32[]{:S(2)}) collective-permute-start(bf16[288,512]{1,0:T(8,128)(2,1)S(1)} %shard_map.111.refs_7_.b_ref), channel_id=1, source_target_pairs={{0,2},{1,3},{2,0},{3,1},{4,6},{5,7},{6,4},{7,5},{8,10},{9,11},{10,... | collective-permute-start | bytes 884744 | tf_op jit(solution)/shard_map/ppermute | solution.py:609
  50.8 3.2 %collective-permute-start.15 = (bf16[128,1024]{1,0:T(8,128)(2,1)S(1)}, bf16[128,1024]{1,0:T(8,128)(2,1)S(1)}, u32[]{:S(2)}, u32[]{:S(2)}) collective-permute-start(bf16[128,1024]{1,0:T(8,128)(2,1)S(1)} %collective-permute-done.6.a2), channel_id=1, source_target_pairs={{0,1},{1,0},{2,3},{3,2},{4,5},{5,4},{6,7},{7,6},{8,9},{9,8},{10,11... | collective-permute-start | bytes 786440 | tf_op jit(solution)/shard_map/ppermute | solution.py:609
  52.1 1.9 %collective-permute-start.16 = (bf16[128,1024]{1,0:T(8,128)(2,1)S(1)}, bf16[128,1024]{1,0:T(8,128)(2,1)S(1)}, u32[]{:S(2)}, u32[]{:S(2)}) collective-permute-start(bf16[128,1024]{1,0:T(8,128)(2,1)S(1)} %collective-permute-done.12.b2), channel_id=1, source_target_pairs={{0,1},{1,0},{2,3},{3,2},{4,5},{5,4},{6,7},{7,6},{8,9},{9,8},{10,11... | collective-permute-start | bytes 786440 | tf_op jit(solution)/shard_map/ppermute | solution.py:609
  53.1 1.0 %copy-start.4 = (bf16[256,1024]{1,0:T(8,128)(2,1)S(1)}, bf16[256,1024]{1,0:T(8,128)(2,1)}, u32[]{:S(2)}) copy-start(bf16[256,1024]{1,0:T(8,128)(2,1)} %po_ref) | copy-start | bytes 1572868
  53.1 1.0 %copy-start.7 = (f32[2,1024]{1,0:T(2,128)S(1)}, f32[2,1024]{1,0:T(2,128)}, u32[]{:S(2)}) copy-start(f32[2,1024]{1,0:T(2,128)} %c_ref.1) | copy-start | bytes 24580
  61.0 11.7 %collective-permute-start.17 = (bf16[288,256]{1,0:T(8,128)(2,1)S(1)}, bf16[288,256]{1,0:T(8,128)(2,1)S(1)}, u32[]{:S(2)}, u32[]{:S(2)}) collective-permute-start(bf16[288,256]{1,0:T(8,128)(2,1)S(1)} %get-tuple-element.98), channel_id=1, source_target_pairs={{0,4},{1,5},{2,6},{3,7},{4,8},{5,9},{6,10},{7,11},{8,12},{9,13},{1... | collective-permute-start | bytes 442376 | tf_op jit(solution)/shard_map/ppermute | solution.py:609
  61.1 11.7 %collective-permute-start.18 = (bf16[288,256]{1,0:T(8,128)(2,1)S(1)}, bf16[288,256]{1,0:T(8,128)(2,1)S(1)}, u32[]{:S(2)}, u32[]{:S(2)}) collective-permute-start(bf16[288,256]{1,0:T(8,128)(2,1)S(1)} %get-tuple-element.99), channel_id=1, source_target_pairs={{0,1},{1,0},{2,3},{3,2},{4,5},{5,4},{6,7},{7,6},{8,9},{9,8},{10,11... | collective-permute-start | bytes 442376 | tf_op jit(solution)/shard_map/ppermute | solution.py:609
  61.6 11.2 %collective-permute-start.19 = (bf16[288,256]{1,0:T(8,128)(2,1)S(1)}, bf16[288,256]{1,0:T(8,128)(2,1)S(1)}, u32[]{:S(2)}, u32[]{:S(2)}) collective-permute-start(bf16[288,256]{1,0:T(8,128)(2,1)S(1)} %get-tuple-element.100), channel_id=1, source_target_pairs={{0,5},{1,4},{2,7},{3,6},{4,9},{5,8},{6,11},{7,10},{8,13},{9,12},{1... | collective-permute-start | bytes 442376 | tf_op jit(solution)/shard_map/ppermute | solution.py:609
  66.7 3.7 %collective-permute-start.20 = (f32[2,1024]{1,0:T(2,128)S(1)}, f32[2,1024]{1,0:T(2,128)S(1)}, u32[]{:S(2)}, u32[]{:S(2)}) collective-permute-start(f32[2,1024]{1,0:T(2,128)S(1)} %shard_map.121), channel_id=1, source_target_pairs={{0,2},{1,3},{2,0},{3,1},{4,6},{5,7},{6,4},{7,5},{8,10},{9,11},{10,... | collective-permute-start | bytes 24584 | tf_op jit(solution)/shard_map/ppermute | solution.py:609
  67.8 5.0 %copy-start.3 = (bf16[1024,3,256]{2,0,1:T(8,128)(2,1)S(1)}, bf16[1024,3,256]{2,0,1:T(8,128)(2,1)}, u32[]{:S(2)}) copy-start(bf16[1024,3,256]{2,0,1:T(8,128)(2,1)} %param.10) | copy-start | bytes 4718596
  70.5 4.2 %collective-permute-start.23 = (f32[2,1792]{1,0:T(2,128)S(1)}, f32[2,1792]{1,0:T(2,128)S(1)}, u32[]{:S(2)}, u32[]{:S(2)}) collective-permute-start(f32[2,1792]{1,0:T(2,128)S(1)} %pad_maximum_fusion), channel_id=1, source_target_pairs={{0,5},{1,4},{2,7},{3,6},{4,1},{5,0},{6,3},{7,2},{8,13},{9,12},{10,... | collective-permute-start | bytes 43016 | tf_op jit(solution)/shard_map/ppermute | solution.py:615
  71.1 3.6 %collective-permute-start.21 = (f32[2,1792]{1,0:T(2,128)S(1)}, f32[2,1792]{1,0:T(2,128)S(1)}, u32[]{:S(2)}, u32[]{:S(2)}) collective-permute-start(f32[2,1792]{1,0:T(2,128)S(1)} %pad_maximum_fusion), channel_id=1, source_target_pairs={{0,1},{1,0},{2,3},{3,2},{4,5},{5,4},{6,7},{7,6},{8,9},{9,8},{10,11... | collective-permute-start | bytes 43016 | tf_op jit(solution)/shard_map/ppermute | solution.py:609
  74.6 3.8 %collective-permute-start.22 = (f32[2,1792]{1,0:T(2,128)S(1)}, f32[2,1792]{1,0:T(2,128)S(1)}, u32[]{:S(2)}, u32[]{:S(2)}) collective-permute-start(f32[2,1792]{1,0:T(2,128)S(1)} %pad_maximum_fusion.1), channel_id=1, source_target_pairs={{0,4},{1,5},{2,6},{3,7},{4,0},{5,1},{6,2},{7,3},{8,12},{9,13},{10,... | collective-permute-start | bytes 43016 | tf_op jit(solution)/shard_map/ppermute | solution.py:615
  78.4 7.1 %collective-permute-start.25 = (f32[2,1792]{1,0:T(2,128)S(1)}, f32[2,1792]{1,0:T(2,128)S(1)}, u32[]{:S(2)}, u32[]{:S(2)}) collective-permute-start(f32[2,1792]{1,0:T(2,128)S(1)} %add_add_fusion.1), channel_id=1, source_target_pairs={{0,16},{1,17},{2,18},{3,19},{4,20},{5,21},{6,22},{7,23},{8,24},{9,... | collective-permute-start | bytes 43016 | tf_op jit(solution)/shard_map/ppermute | solution.py:615
  82.9 5.5 %collective-permute-start.26 = (f32[2,1792]{1,0:T(2,128)S(1)}, f32[2,1792]{1,0:T(2,128)S(1)}, u32[]{:S(2)}, u32[]{:S(2)}) collective-permute-start(f32[2,1792]{1,0:T(2,128)S(1)} %add_add_fusion.1), channel_id=1, source_target_pairs={{0,24},{1,25},{2,26},{3,27},{4,28},{5,29},{6,30},{7,31},{8,16},{9,... | collective-permute-start | bytes 43016 | tf_op jit(solution)/shard_map/ppermute | solution.py:615
  82.9 5.5 %collective-permute-start.24 = (f32[2,1792]{1,0:T(2,128)S(1)}, f32[2,1792]{1,0:T(2,128)S(1)}, u32[]{:S(2)}, u32[]{:S(2)}) collective-permute-start(f32[2,1792]{1,0:T(2,128)S(1)} %add_add_fusion.1), channel_id=1, source_target_pairs={{0,8},{1,9},{2,10},{3,11},{4,12},{5,13},{6,14},{7,15},{8,0},{9,1},... | collective-permute-start | bytes 43016 | tf_op jit(solution)/shard_map/ppermute | solution.py:615

commit v9 on v8

--- a/solution.py
+++ b/solution.py
@@ -648,21 +648,22 @@
     f_raw, t_raw = (jnp.transpose(block, (0, 2, 1, 3)) for block in (features, target))
     f_low, f_up = halves_of(f_raw)
     f_low, f_up, w_qkv, w_proj = lax.optimization_barrier((f_low, f_up, w_qkv, w_proj))
-    f_low, f_up_y = send(f_low, -1, 0), send(f_up, 0, 2)
+    f_up_y = send(f_up, 0, 2)
+    f_low = send(f_low, -1, 0)
 
     w3 = jnp.transpose(w_qkv, (1, 0, 2))
     c3 = jnp.transpose(qkv_clip, (1, 0, 2))
     w3_peer = send(w3, 0, 1)
     c3_peer = send(c3, 0, 1)
     share = w_proj.shape[0] // 2
-    slab = after(w_proj, c3_peer)
-    slab = send(lax.dynamic_slice_in_dim(slab, share * (sector % 2), share, 0), 0, 2)
     w1 = send(w_proj, 0, 1)
     wc_own, b_own = clip_qkv(w3, c3)
+    slab = after(w_proj, wc_own)
+    slab = send(lax.dynamic_slice_in_dim(slab, share * (sector % 2), share, 0), 0, 2)
     wc_peer, b_peer = clip_qkv(w3_peer, c3_peer)
     idk, idq = window_ids(place, region_ids, WLAT * lev * lon)
-    f_low, f_up_y, w1, t_low, wc_own = lax.optimization_barrier(
-        (f_low, f_up_y, w1, t_raw[:, :half], wc_own)
+    f_up_y, f_low, w1, t_low, wc_own = lax.optimization_barrier(
+        (f_up_y, f_low, w1, t_raw[:, :half], wc_own)
     )
     f_low_y = send(f_low, 0, 2)
     t_low = send(t_low, -1, 0)

time: 89.9 us -> 90.6 us (level)
  starting transfers between devices: 26.5 us -> 29 us
  waiting for transfers between devices: 16.3 us -> 14 us
  Pallas kernels: 36.8 us -> 38.4 us
  local copies, waits for them, and re-layouts: 8.23 us -> 7.14 us
    ppermute x6, starting transfers between devices: 5.82 us -> 8 us  [swap(): return lax.ppermute(block, ('lat', 'tp'), route)]
    ppermute x21, waiting for transfers between devices: 9.66 us -> 8.34 us  [send(): return lax.ppermute(block, ('lat', 'tp'), route)]
    pallas_call x1, Pallas kernels: 1.57 us -> 2.61 us  [proj_sums(): pl.pallas_call(proj_sums_kernel, out_shape=jax.ShapeDtypeStruct((2, errs[...]
    ppermute x6, waiting for transfers between devices: 6.6 us -> 5.65 us  [swap(): return lax.ppermute(block, ('lat', 'tp'), route)]
    dynamic_slice x1, local copies, waits for them, and re-layouts: 1.67 us -> 0.72 us  [local(): lax.dynamic_slice_in_dim(slab, share * (sector % 2), share, 0)]
    unnamed x22 -> x24, local copies, waits for them, and re-layouts: 4.48 us -> 4.34 us
  transfers between devices with their start and end apart: 27 -> 27, of which waited for: 7 -> 8; matrix products, arithmetic and copies ran while one was open for 3% -> 2% of each run, Pallas kernels for 37% -> 38%
where the time goes in v9:
time: 90.6 us; the launch traced here: 90.2 us
  Pallas kernels  38.4 us (42%)
  starting transfers between devices  29 us (32%)
  waiting for transfers between devices  14 us (15%)
  local copies, waits for them, and re-layouts  7.14 us (8%)
  between operations  1.6 us (2%)
    ppermute x21, starting transfers between devices, send(): return lax.ppermute(block, ('lat', 'tp'), route)  21 us
    ppermute x21, waiting for transfers between devices, send(): return lax.ppermute(block, ('lat', 'tp'), route)  8.34 us
    ppermute x6, starting transfers between devices, swap(): return lax.ppermute(block, ('lat', 'tp'), route)  8 us
    pallas_call x1, Pallas kernels, forward(): pl.pallas_call(forward_kernel, out_shape=(jax.ShapeDtypeStruct((n, d), BF...  7.62 us
    pallas_call x2, Pallas kernels, backward(): pl.pallas_call(functools.partial(backward_kernel, group), out_shape=jax.S...  6.42 us
    ppermute x6, waiting for transfers between devices, swap(): return lax.ppermute(block, ('lat', 'tp'), route)  5.65 us
    unnamed x24, local copies, waits for them, and re-layouts  4.34 us
    pallas_call x2, Pallas kernels, qkv_sums(): pl.pallas_call(functools.partial(qkv_sums_kernel, side), out_shape=jax.Sh...  3.61 us
  transfers between devices with their start and end apart: 27, of which 8 were waited for; matrix products, arithmetic and copies ran while one was open for 2% of the time, Pallas kernels for 38%

profile of v9, /device:TPU:0, one launch (start us, length us, event | category | flops | bytes accessed | tf_op | source)
XLA Modules:
  0.0 90.2 jit_solution(10058953671934269907)
XLA Ops:
  0.6 0.0 copy-start
  0.6 1.0 %copy-done = bf16[42,2,12,256]{3,1,2,0:T(2,128)(2,1)S(1)} copy-done((bf16[42,2,12,256]{3,1,2,0:T(2,128)(2,1)S(1)}, bf16[42,2,12,256]{3,1,2,0:T(2,128)(2,1)}, u32[]{:S(2)}) %copy-start) | copy-done | bytes 516120
  1.7 0.9 shard_map.103
  2.6 0.5 collective-permute-start.6
  3.1 0.1 collective-permute-start.2
  3.2 2.9 %collective-permute-start = (bf16[42,6,2,256]{3,2,1,0:T(2,128)(2,1)}, bf16[42,6,2,256]{3,2,1,0:T(2,128)(2,1)}, u32[]{:S(2)}, u32[]{:S(2)}) collective-permute-start(bf16[42,6,2,256]{3,2,1,0:T(2,128)(2,1)} %get-tuple-element.59), channel_id=1, source_target_pairs={{0,2},{1,3},{2,0},{3,1},{4,6},{5,7},{6,4},{7,5},{8,10},{9,11},{10,... | collective-permute-start | bytes 774152 | tf_op jit(solution)/shard_map/ppermute | solution.py:609
  6.1 4.5 %collective-permute-start.1 = (bf16[42,6,2,256]{3,2,1,0:T(2,128)(2,1)}, bf16[42,6,2,256]{3,2,1,0:T(2,128)(2,1)}, u32[]{:S(2)}, u32[]{:S(2)}) collective-permute-start(bf16[42,6,2,256]{3,2,1,0:T(2,128)(2,1)} %get-tuple-element.60), channel_id=1, source_target_pairs={{0,28},{1,29},{2,30},{3,31},{4,0},{5,1},{6,2},{7,3},{8,4},{9,5},{1... | collective-permute-start | bytes 774152 | tf_op jit(solution)/shard_map/ppermute | solution.py:609
  10.6 1.4 %copy-done.2 = bf16[1024,3,256]{2,0,1:T(8,128)(2,1)S(1)} copy-done((bf16[1024,3,256]{2,0,1:T(8,128)(2,1)S(1)}, bf16[1024,3,256]{2,0,1:T(8,128)(2,1)}, u32[]{:S(2)}) %copy-start.2) | copy-done | bytes 1572888
  12.0 0.7 copy-done.8
  12.7 0.7 shard_map.104
  13.4 1.2 %copy-done.10 = bf16[3,1024,256]{2,1,0:T(8,128)(2,1)} copy-done((bf16[3,1024,256]{2,1,0:T(8,128)(2,1)}, bf16[3,1024,256]{2,1,0:T(8,128)(2,1)S(1)}, u32[]{:S(2)}) %copy-start.10) | copy-done | bytes 1572888
  14.6 0.7 constant_dynamic-slice_fusion
  15.3 0.5 collective-permute-start.5
  15.8 0.9 slice.12
  16.7 4.8 %collective-permute-start.4 = (bf16[42,6,2,256]{3,2,1,0:T(2,128)(2,1)}, bf16[42,6,2,256]{3,2,1,0:T(2,128)(2,1)}, u32[]{:S(2)}, u32[]{:S(2)}) collective-permute-start(bf16[42,6,2,256]{3,2,1,0:T(2,128)(2,1)} %slice.12), channel_id=1, source_target_pairs={{0,28},{1,29},{2,30},{3,31},{4,0},{5,1},{6,2},{7,3},{8,4},{9,5},{1... | collective-permute-start | bytes 774152 | tf_op jit(solution)/shard_map/ppermute | solution.py:609
  21.6 0.5 collective-permute-start.3
  22.7 0.1 pad_add_fusion.s_ref
  22.8 1.0 %shard_map.107 = (s32[576,1]{1,0:T(8,128)S(1)}, s32[4,1,288]{2,1,0:T(1,128)S(1)}) custom-call(s32[3]{0:T(128)S(1)} %pad_add_fusion.s_ref, s32[42,2,96]{2,1,0:T(2,128)S(1)} %copy-done.6), custom_call_target="tpu_custom_call" | custom-call | flops 1 | bytes 1 | tf_op jit(solution)/shard_map/pallas_call | solution.py:553
  23.8 2.6 %collective-permute-done.4.refs_1_ = bf16[42,6,2,256]{3,2,1,0:T(2,128)(2,1)} collective-permute-done((bf16[42,6,2,256]{3,2,1,0:T(2,128)(2,1)}, bf16[42,6,2,256]{3,2,1,0:T(2,128)(2,1)}, u32[]{:S(2)}, u32[]{:S(2)}) %collective-permute-start.4) | collective-permute-done | bytes 258080 | tf_op jit(solution)/shard_map/ppermute | solution.py:609
  26.4 1.4 %shard_map.105 = (bf16[576,256]{1,0:T(8,128)(2,1)S(1)}, bf16[1,576,256]{2,1,0:T(8,128)(2,1)S(1)}) custom-call(s32[3]{0:T(128)S(1)} %pad_add_fusion.s_ref, bf16[42,12,2,256]{3,2,1,0:T(2,128)(2,1)S(1)} %bitcast.16, bf16[42,6,2,256]{3,2,1,0:T(2,128)(2,1)} %collective-permute-done.4.refs_1_), custom_call_target="tpu_custom_call" | custom-call | flops 1 | bytes 1 | tf_op jit(solution)/shard_map/pallas_call | solution.py:497
  27.9 0.7 shard_map.106
  28.6 0.3 collective-permute-done.3.refs_3_
  28.9 1.9 %shard_map.108 = (bf16[576,256]{1,0:T(8,128)(2,1)S(1)}, bf16[576,256]{1,0:T(8,128)(2,1)S(1)}, bf16[2,576,256]{2,1,0:T(8,128)(2,1)S(1)}) custom-call(s32[3]{0:T(128)S(1)} %pad_add_fusion.s_ref, bf16[42,12,2,256]{3,2,1,0:T(2,128)(2,1)S(1)} %bitcast.11, bf16[42,6,2,256]{3,2,1,0:T(2,128)(2,1)} %collective-permute-done.1.refs_1_, ...), custom_call_target="tpu_custom_call" | custom-call | flops 1 | bytes 1 | tf_op jit(solution)/shard_map/pallas_call | solution.py:497
  30.9 0.1 collective-permute-start.8
  30.9 0.5 collective-permute-start.9
  31.4 0.5 collective-permute-start.10
  31.9 0.9 %collective-permute-start.11 = (bf16[576,256]{1,0:T(8,128)(2,1)S(1)}, bf16[576,256]{1,0:T(8,128)(2,1)S(1)}, u32[]{:S(2)}, u32[]{:S(2)}) collective-permute-start(bf16[576,256]{1,0:T(8,128)(2,1)S(1)} %bitcast.20), channel_id=1, source_target_pairs={{0,3},{1,2},{2,1},{3,0},{4,7},{5,6},{6,5},{7,4},{8,11},{9,10},{10,... | collective-permute-start | bytes 884744 | tf_op jit(solution)/shard_map/ppermute | solution.py:609
  32.9 0.1 collective-permute-done.8.refs_2_
  32.9 7.6 %shard_map.109 = (bf16[576,1024]{1,0:T(8,128)(2,1)S(1)}, bf16[6,576,256]{2,1,0:T(8,128)(2,1)S(1)}, bf16[288,512]{1,0:T(8,128)(2,1)S(1)}) custom-call(s32[1]{0:T(128)} %bitcast.2.t_ref, bf16[576,256]{1,0:T(8,128)(2,1)S(1)} %get-tuple-element.74.refs_0_, bf16[576,256]{1,0:T(8,128)(2,1)S(1)} %get-tuple-element.75.refs_1_, ...), custom_call_target="tpu_custom_call" | custom-call | flops 8000000000 | bytes 10000000 | tf_op jit(solution)/shard_map/pallas_call | solution.py:213
  40.6 1.0 %shard_map.110.p_ref = f32[8,144,288]{2,1,0:T(8,128)S(1)} custom-call(bf16[6,576,256]{2,1,0:T(8,128)(2,1)S(1)} %get-tuple-element.102.qkv_ref, s32[576,1]{1,0:T(8,128)S(1)} %get-tuple-element.81.refs_5_.idk_ref.refs_10_, s32[4,1,288]{2,1,0:T(1,128)S(1)} %get-tuple-element.82.refs_6_.idq_ref), custom_call_target="tpu_custom_call" | custom-call | flops 1 | bytes 1 | tf_op jit(solution)/shard_map/pallas_call | solution.py:326
  41.6 0.6 collective-permute-start.14
  42.2 3.6 %collective-permute-done.11.refs_6_ = bf16[576,256]{1,0:T(8,128)(2,1)S(1)} collective-permute-done((bf16[576,256]{1,0:T(8,128)(2,1)S(1)}, bf16[576,256]{1,0:T(8,128)(2,1)S(1)}, u32[]{:S(2)}, u32[]{:S(2)}) %collective-permute-start.11) | collective-permute-done | bytes 294944 | tf_op jit(solution)/shard_map/ppermute | solution.py:609
  45.9 2.7 %shard_map.111.refs_7_.b_ref = bf16[288,512]{1,0:T(8,128)(2,1)S(1)} custom-call(bf16[6,576,256]{2,1,0:T(8,128)(2,1)S(1)} %get-tuple-element.102.qkv_ref, s32[576,1]{1,0:T(8,128)S(1)} %get-tuple-element.81.refs_5_.idk_ref.refs_10_, s32[4,1,288]{2,1,0:T(1,128)S(1)} %get-tuple-element.82.refs_6_.idq_ref), custom_call_target="tpu_custom_call" | custom-call | flops 1 | bytes 1 | tf_op jit(solution)/shard_map/pallas_call | solution.py:200
  48.5 1.4 %collective-permute-start.13 = (bf16[288,512]{1,0:T(8,128)(2,1)S(1)}, bf16[288,512]{1,0:T(8,128)(2,1)S(1)}, u32[]{:S(2)}, u32[]{:S(2)}) collective-permute-start(bf16[288,512]{1,0:T(8,128)(2,1)S(1)} %shard_map.111.refs_7_.b_ref), channel_id=1, source_target_pairs={{0,2},{1,3},{2,0},{3,1},{4,6},{5,7},{6,4},{7,5},{8,10},{9,11},{10,... | collective-permute-start | bytes 884744 | tf_op jit(solution)/shard_map/ppermute | solution.py:609
  49.9 0.5 collective-permute-start.15
  50.4 0.0 collective-permute-start.16
  50.4 1.0 %shard_map.117.p_ref = f32[8,144,288]{2,1,0:T(8,128)S(1)} custom-call(bf16[6,576,256]{2,1,0:T(8,128)(2,1)S(1)} %get-tuple-element.102.qkv_ref, s32[576,1]{1,0:T(8,128)S(1)} %get-tuple-element.81.refs_5_.idk_ref.refs_10_, s32[4,1,288]{2,1,0:T(1,128)S(1)} %get-tuple-element.82.refs_6_.idq_ref), custom_call_target="tpu_custom_call" | custom-call | flops 1 | bytes 1 | tf_op jit(solution)/shard_map/pallas_call | solution.py:326
  51.4 0.0 copy-start.7
  51.4 0.8 shard_map.119
  52.3 2.1 %shard_map.112 = (bf16[1024,1024]{1,0:T(8,128)(2,1)S(1)}, f32[8,1024]{1,0:T(8,128)S(1)}) custom-call(s32[3]{0:T(128)S(1)} %pad_add_fusion.s_ref, bf16[256,1024]{1,0:T(8,128)(2,1)S(1)} %copy-done.4, bf16[256,1024]{1,0:T(8,128)(2,1)} %collective-permute-done.2.w1.pp_ref, bf16[128,1024]{1,0:T(8,128)(2,1)S(1)} %collective-permute-done.5.a2, ...), custom_call_target="tpu_custom_call" | custom-call | flops 1 | bytes 1 | tf_op jit(solution)/shard_map/pallas_call | solution.py:92
  54.4 1.0 %shard_map.113 = (bf16[144,256]{1,0:T(8,128)(2,1)S(1)}, bf16[144,256]{1,0:T(8,128)(2,1)S(1)}, bf16[144,256]{1,0:T(8,128)(2,1)S(1)}, bf16[144,256]{1,0:T(8,128)(2,1)S(1)}, bf16[288,1024]{1,0:T(8,128)(2,1)S(1)}) custom-call(s32[1]{0:T(128)} %bitcast.2.t_ref, bf16[576,256]{1,0:T(8,128)(2,1)S(1)} %get-tuple-element.74.refs_0_, ...), custom_call_target="tpu_custom_call" | custom-call | flops 1 | bytes 1 | tf_op jit(solution)/shard_map/pallas_call | solution.py:296
  55.4 3.2 %shard_map.114.g0_ref = bf16[6,288,256]{2,1,0:T(8,128)(2,1)S(1)} custom-call(bf16[288,1024]{1,0:T(8,128)(2,1)S(1)} %get-tuple-element.91.err_ref.e0_ref, bf16[1024,1024]{1,0:T(8,128)(2,1)S(1)} %get-tuple-element.90.refs_9_.wc_ref, bf16[6,576,256]{2,1,0:T(8,128)(2,1)S(1)} %get-tuple-element.102.qkv_ref, f32[8,144,288]{2,1,0:T(8,128)S(1)} %shard_map.110.p_ref), custom_call_target="tpu_custom_call" | custom-call | flops 1 | bytes 1 | tf_op jit(solution)/shard_map/pallas_call | solution.py:402
  58.6 0.8 collective-permute-done.13.refs_8_
  59.4 1.0 %shard_map.115 = (bf16[288,256]{1,0:T(8,128)(2,1)S(1)}, bf16[288,256]{1,0:T(8,128)(2,1)S(1)}, bf16[288,256]{1,0:T(8,128)(2,1)S(1)}, bf16[288,256]{1,0:T(8,128)(2,1)S(1)}, bf16[288,1024]{1,0:T(8,128)(2,1)S(1)}) custom-call(s32[1]{0:T(128)} %bitcast.2.t_ref, bf16[576,256]{1,0:T(8,128)(2,1)S(1)} %get-tuple-element.74.refs_0_, ...), custom_call_target="tpu_custom_call" | custom-call | flops 1 | bytes 1 | tf_op jit(solution)/shard_map/pallas_call | solution.py:296
  60.4 0.1 collective-permute-start.17
  60.4 0.1 collective-permute-start.18
  60.5 0.2 collective-permute-start.19
  60.8 3.2 %shard_map.118.g1_ref = bf16[6,288,256]{2,1,0:T(8,128)(2,1)S(1)} custom-call(bf16[288,1024]{1,0:T(8,128)(2,1)S(1)} %get-tuple-element.101.err_ref.e1_ref, bf16[1024,1024]{1,0:T(8,128)(2,1)S(1)} %get-tuple-element.90.refs_9_.wc_ref, bf16[6,576,256]{2,1,0:T(8,128)(2,1)S(1)} %get-tuple-element.102.qkv_ref, f32[8,144,288]{2,1,0:T(8,128)S(1)} %shard_map.117.p_ref), custom_call_target="tpu_custom_call" | custom-call | flops 8000000000 | bytes 10000000 | tf_op jit(solution)/shard_map/pallas_call | solution.py:402
  64.0 2.6 %shard_map.121 = f32[2,1024]{1,0:T(2,128)S(1)} custom-call(bf16[288,1024]{1,0:T(8,128)(2,1)S(1)} %get-tuple-element.91.err_ref.e0_ref, bf16[288,1024]{1,0:T(8,128)(2,1)S(1)} %get-tuple-element.101.err_ref.e1_ref, bf16[512,576]{1,0:T(8,128)(2,1)S(1)} %get-tuple-element.106.attn_t, bf16[256,1024]{1,0:T(8,128)(2,1)S(1)} %copy-done.4, ...), custom_call_target="tpu_custom_call" | custom-call | flops 1000000000 | bytes 3000000 | tf_op jit(solution)/shard_map/pallas_call | solution.py:359
  66.6 1.1 %collective-permute-start.20 = (f32[2,1024]{1,0:T(2,128)S(1)}, f32[2,1024]{1,0:T(2,128)S(1)}, u32[]{:S(2)}, u32[]{:S(2)}) collective-permute-start(f32[2,1024]{1,0:T(2,128)S(1)} %shard_map.121), channel_id=1, source_target_pairs={{0,2},{1,3},{2,0},{3,1},{4,6},{5,7},{6,4},{7,5},{8,10},{9,11},{10,... | collective-permute-start | bytes 24584 | tf_op jit(solution)/shard_map/ppermute | solution.py:609
  67.6 1.8 %shard_map.120 = f32[2,768]{1,0:T(2,128)S(1)} custom-call(bf16[6,288,256]{2,1,0:T(8,128)(2,1)S(1)} %shard_map.114.g0_ref, bf16[6,288,256]{2,1,0:T(8,128)(2,1)S(1)} %shard_map.118.g1_ref, bf16[1024,576]{1,0:T(8,128)(2,1)S(1)} %get-tuple-element.104.normed_t, bf16[3,1024,256]{2,1,0:T(8,128)(2,1)S(1)} %collective-permute-done.6.w_ref, ...), custom_call_target="tpu_custom_call" | custom-call | flops 8000000000 | bytes 10000000 | tf_op jit(solution)/shard_map/pallas_call | solution.py:429
  69.5 0.8 collective-permute-done.20
  70.3 0.1 collective-permute-start.23
  70.4 1.1 %collective-permute-start.21 = (f32[2,1792]{1,0:T(2,128)S(1)}, f32[2,1792]{1,0:T(2,128)S(1)}, u32[]{:S(2)}, u32[]{:S(2)}) collective-permute-start(f32[2,1792]{1,0:T(2,128)S(1)} %pad_maximum_fusion), channel_id=1, source_target_pairs={{0,1},{1,0},{2,3},{3,2},{4,5},{5,4},{6,7},{7,6},{8,9},{9,8},{10,11... | collective-permute-start | bytes 43016 | tf_op jit(solution)/shard_map/ppermute | solution.py:609
  71.5 0.0 collective-permute-done.19.b1
  71.6 1.8 %shard_map.122 = f32[2,768]{1,0:T(2,128)S(1)} custom-call(bf16[6,288,256]{2,1,0:T(8,128)(2,1)S(1)} %shard_map.114.g0_ref, bf16[6,288,256]{2,1,0:T(8,128)(2,1)S(1)} %shard_map.118.g1_ref, bf16[1024,576]{1,0:T(8,128)(2,1)S(1)} %get-tuple-element.104.normed_t, bf16[3,1024,256]{2,1,0:T(8,128)(2,1)S(1)} %bitcast.14, f32[3,8,256]{2,1,0:T(8,128)S(1)} %get-tuple-element.110.b_ref), custom_call_target="tpu_custom_call" | custom-call | flops 8000000000 | bytes 10000000 | tf_op jit(solution)/shard_map/pallas_call | solution.py:429
  73.4 1.0 %collective-permute-start.22 = (f32[2,1792]{1,0:T(2,128)S(1)}, f32[2,1792]{1,0:T(2,128)S(1)}, u32[]{:S(2)}, u32[]{:S(2)}) collective-permute-start(f32[2,1792]{1,0:T(2,128)S(1)} %pad_maximum_fusion.1), channel_id=1, source_target_pairs={{0,4},{1,5},{2,6},{3,7},{4,0},{5,1},{6,2},{7,3},{8,12},{9,13},{10,... | collective-permute-start | bytes 43016 | tf_op jit(solution)/shard_map/ppermute | solution.py:615
  74.5 2.7 %collective-permute-done.22 = f32[2,1792]{1,0:T(2,128)S(1)} collective-permute-done((f32[2,1792]{1,0:T(2,128)S(1)}, f32[2,1792]{1,0:T(2,128)S(1)}, u32[]{:S(2)}, u32[]{:S(2)}) %collective-permute-start.22) | collective-permute-done | bytes 14368 | tf_op jit(solution)/shard_map/ppermute | solution.py:615
  77.2 6.2 %collective-permute-start.25 = (f32[2,1792]{1,0:T(2,128)S(1)}, f32[2,1792]{1,0:T(2,128)S(1)}, u32[]{:S(2)}, u32[]{:S(2)}) collective-permute-start(f32[2,1792]{1,0:T(2,128)S(1)} %add_add_fusion.1), channel_id=1, source_target_pairs={{0,16},{1,17},{2,18},{3,19},{4,20},{5,21},{6,22},{7,23},{8,24},{9,... | collective-permute-start | bytes 43016 | tf_op jit(solution)/shard_map/ppermute | solution.py:615
  83.4 0.6 collective-permute-start.24
  84.1 2.0 %shard_map.116 = bf16[42,12,2,256]{3,2,1,0:T(2,128)(2,1)} custom-call(s32[3]{0:T(128)S(1)} %pad_add_fusion.s_ref, bf16[288,256]{1,0:T(8,128)(2,1)S(1)} %get-tuple-element.97.a0, bf16[288,256]{1,0:T(8,128)(2,1)S(1)} %collective-permute-done.17.a1, bf16[288,256]{1,0:T(8,128)(2,1)S(1)} %collective-permute-done.18.b0, ...), custom_call_target="tpu_custom_call" | custom-call | flops 1 | bytes 1 | tf_op jit(solution)/shard_map/pallas_call | solution.py:592
  86.1 2.9 %collective-permute-done.26 = f32[2,1792]{1,0:T(2,128)S(1)} collective-permute-done((f32[2,1792]{1,0:T(2,128)S(1)}, f32[2,1792]{1,0:T(2,128)S(1)}, u32[]{:S(2)}, u32[]{:S(2)}) %collective-permute-start.26) | collective-permute-done | bytes 14368 | tf_op jit(solution)/shard_map/ppermute | solution.py:615
  89.0 0.6 slice.13
  89.6 0.6 slice.14
  (44 shorter events, 0.1 us)
Async XLA Ops:
  0.6 1.0 %copy-start = (bf16[42,2,12,256]{3,1,2,0:T(2,128)(2,1)S(1)}, bf16[42,2,12,256]{3,1,2,0:T(2,128)(2,1)}, u32[]{:S(2)}) copy-start(bf16[42,2,12,256]{3,1,2,0:T(2,128)(2,1)} %param.8) | copy-start | bytes 1548292
  1.7 14.2 %copy-start.5 = (bf16[42,2,12,256]{3,1,2,0:T(2,128)(2,1)S(1)}, bf16[42,2,12,256]{3,1,2,0:T(2,128)(2,1)}, u32[]{:S(2)}) copy-start(bf16[42,2,12,256]{3,1,2,0:T(2,128)(2,1)} %param.9) | copy-start | bytes 1548292
  1.7 20.4 %copy-start.9 = (f32[2,3,256]{2,0,1:T(2,128)S(1)}, f32[2,3,256]{2,0,1:T(2,128)}, u32[]{:S(2)}) copy-start(f32[2,3,256]{2,0,1:T(2,128)} %param.12) | copy-start | bytes 18436
  2.6 25.3 %collective-permute-start.6 = (bf16[3,1024,256]{2,1,0:T(8,128)(2,1)}, bf16[3,1024,256]{2,1,0:T(8,128)(2,1)S(1)}, u32[]{:S(2)}, u32[]{:S(2)}) collective-permute-start(bf16[3,1024,256]{2,1,0:T(8,128)(2,1)} %bitcast.12), channel_id=1, source_target_pairs={{0,1},{1,0},{2,3},{3,2},{4,5},{5,4},{6,7},{7,6},{8,9},{9,8},{10,11... | collective-permute-start | bytes 4718600 | tf_op jit(solution)/shard_map/ppermute | solution.py:609
  3.1 13.7 %collective-permute-start.2 = (bf16[256,1024]{1,0:T(8,128)(2,1)}, bf16[256,1024]{1,0:T(8,128)(2,1)}, u32[]{:S(2)}, u32[]{:S(2)}) collective-permute-start(bf16[256,1024]{1,0:T(8,128)(2,1)} %po_ref), channel_id=1, source_target_pairs={{0,1},{1,0},{2,3},{3,2},{4,5},{5,4},{6,7},{7,6},{8,9},{9,8},{10,11... | collective-permute-start | bytes 1572872 | tf_op jit(solution)/shard_map/ppermute | solution.py:609
  3.2 13.6 %collective-permute-start = (bf16[42,6,2,256]{3,2,1,0:T(2,128)(2,1)}, bf16[42,6,2,256]{3,2,1,0:T(2,128)(2,1)}, u32[]{:S(2)}, u32[]{:S(2)}) collective-permute-start(bf16[42,6,2,256]{3,2,1,0:T(2,128)(2,1)} %get-tuple-element.59), channel_id=1, source_target_pairs={{0,2},{1,3},{2,0},{3,1},{4,6},{5,7},{6,4},{7,5},{8,10},{9,11},{10,... | collective-permute-start | bytes 774152 | tf_op jit(solution)/shard_map/ppermute | solution.py:609
  6.1 10.6 %collective-permute-start.1 = (bf16[42,6,2,256]{3,2,1,0:T(2,128)(2,1)}, bf16[42,6,2,256]{3,2,1,0:T(2,128)(2,1)}, u32[]{:S(2)}, u32[]{:S(2)}) collective-permute-start(bf16[42,6,2,256]{3,2,1,0:T(2,128)(2,1)} %get-tuple-element.60), channel_id=1, source_target_pairs={{0,28},{1,29},{2,30},{3,31},{4,0},{5,1},{6,2},{7,3},{8,4},{9,5},{1... | collective-permute-start | bytes 774152 | tf_op jit(solution)/shard_map/ppermute | solution.py:609
  10.6 1.4 %copy-start.2 = (bf16[1024,3,256]{2,0,1:T(8,128)(2,1)S(1)}, bf16[1024,3,256]{2,0,1:T(8,128)(2,1)}, u32[]{:S(2)}) copy-start(bf16[1024,3,256]{2,0,1:T(8,128)(2,1)} %param.10) | copy-start | bytes 4718596
  12.0 0.7 copy-start.8
  12.7 1.9 %copy-start.4 = (bf16[256,1024]{1,0:T(8,128)(2,1)S(1)}, bf16[256,1024]{1,0:T(8,128)(2,1)}, u32[]{:S(2)}) copy-start(bf16[256,1024]{1,0:T(8,128)(2,1)} %po_ref) | copy-start | bytes 1572868
  12.7 10.1 %copy-start.6 = (s32[42,2,96]{2,1,0:T(2,128)S(1)}, s32[42,2,96]{2,1,0:T(2,128)}, u32[]{:S(2)}) copy-start(s32[42,2,96]{2,1,0:T(2,128)} %ids_ref.1) | copy-start | bytes 96772
  13.4 1.2 %copy-start.10 = (bf16[3,1024,256]{2,1,0:T(8,128)(2,1)}, bf16[3,1024,256]{2,1,0:T(8,128)(2,1)S(1)}, u32[]{:S(2)}) copy-start(bf16[3,1024,256]{2,1,0:T(8,128)(2,1)S(1)} %get-tuple-element.79.refs_3_) | copy-start | bytes 4718596
  15.3 13.6 %copy-start.1 = (bf16[42,2,12,256]{3,1,2,0:T(2,128)(2,1)S(1)}, bf16[42,2,12,256]{3,1,2,0:T(2,128)(2,1)}, u32[]{:S(2)}) copy-start(bf16[42,2,12,256]{3,1,2,0:T(2,128)(2,1)} %param.8) | copy-start | bytes 1548292
  15.3 13.2 %collective-permute-start.5 = (bf16[128,1024]{1,0:T(8,128)(2,1)}, bf16[128,1024]{1,0:T(8,128)(2,1)S(1)}, u32[]{:S(2)}, u32[]{:S(2)}) collective-permute-start(bf16[128,1024]{1,0:T(8,128)(2,1)} %constant_dynamic-slice_fusion), channel_id=1, source_target_pairs={{0,2},{1,3},{2,0},{3,1},{4,6},{5,7},{6,4},{7,5},{8,10},{9,11},{10,... | collective-permute-start | bytes 786440 | tf_op jit(solution)/shard_map/ppermute | solution.py:609
  16.7 9.7 %collective-permute-start.4 = (bf16[42,6,2,256]{3,2,1,0:T(2,128)(2,1)}, bf16[42,6,2,256]{3,2,1,0:T(2,128)(2,1)}, u32[]{:S(2)}, u32[]{:S(2)}) collective-permute-start(bf16[42,6,2,256]{3,2,1,0:T(2,128)(2,1)} %slice.12), channel_id=1, source_target_pairs={{0,28},{1,29},{2,30},{3,31},{4,0},{5,1},{6,2},{7,3},{8,4},{9,5},{1... | collective-permute-start | bytes 774152 | tf_op jit(solution)/shard_map/ppermute | solution.py:609
  21.6 7.3 %collective-permute-start.3 = (bf16[42,6,2,256]{3,2,1,0:T(2,128)(2,1)}, bf16[42,6,2,256]{3,2,1,0:T(2,128)(2,1)}, u32[]{:S(2)}, u32[]{:S(2)}) collective-permute-start(bf16[42,6,2,256]{3,2,1,0:T(2,128)(2,1)} %collective-permute-done.1.refs_1_), channel_id=1, source_target_pairs={{0,2},{1,3},{2,0},{3,1},{4,6},{5,7},{6,4},{7,5},{8,10},{9,11},{10,... | collective-permute-start | bytes 774152 | tf_op jit(solution)/shard_map/ppermute | solution.py:609
  22.1 5.8 %collective-permute-start.7 = (f32[3,2,256]{2,1,0:T(2,128)S(1)}, f32[3,2,256]{2,1,0:T(2,128)S(1)}, u32[]{:S(2)}, u32[]{:S(2)}) collective-permute-start(f32[3,2,256]{2,1,0:T(2,128)S(1)} %bitcast.18), channel_id=1, source_target_pairs={{0,1},{1,0},{2,3},{3,2},{4,5},{5,4},{6,7},{7,6},{8,9},{9,8},{10,11... | collective-permute-start | bytes 18440 | tf_op jit(solution)/shard_map/ppermute | solution.py:609
  27.8 5.1 %copy-start.11 = (bf16[3,1024,256]{2,1,0:T(8,128)(2,1)S(1)}, bf16[3,1024,256]{2,1,0:T(8,128)(2,1)}, u32[]{:S(2)}) copy-start(bf16[3,1024,256]{2,1,0:T(8,128)(2,1)} %copy-done.10) | copy-start | bytes 4718596
  30.9 2.1 %collective-permute-start.8 = (bf16[2,576,256]{2,1,0:T(8,128)(2,1)S(1)}, bf16[2,576,256]{2,1,0:T(8,128)(2,1)S(1)}, u32[]{:S(2)}, u32[]{:S(2)}) collective-permute-start(bf16[2,576,256]{2,1,0:T(8,128)(2,1)S(1)} %get-tuple-element.76), channel_id=1, source_target_pairs={{0,1},{1,0},{2,3},{3,2},{4,5},{5,4},{6,7},{7,6},{8,9},{9,8},{10,11... | collective-permute-start | bytes 1769480 | tf_op jit(solution)/shard_map/ppermute | solution.py:609
  30.9 11.3 %collective-permute-start.9 = (bf16[576,256]{1,0:T(8,128)(2,1)S(1)}, bf16[576,256]{1,0:T(8,128)(2,1)S(1)}, u32[]{:S(2)}, u32[]{:S(2)}) collective-permute-start(bf16[576,256]{1,0:T(8,128)(2,1)S(1)} %bitcast.19), channel_id=1, source_target_pairs={{0,1},{1,0},{2,3},{3,2},{4,5},{5,4},{6,7},{7,6},{8,9},{9,8},{10,11... | collective-permute-start | bytes 884744 | tf_op jit(solution)/shard_map/ppermute | solution.py:609
  31.4 10.8 %collective-permute-start.10 = (bf16[576,256]{1,0:T(8,128)(2,1)S(1)}, bf16[576,256]{1,0:T(8,128)(2,1)S(1)}, u32[]{:S(2)}, u32[]{:S(2)}) collective-permute-start(bf16[576,256]{1,0:T(8,128)(2,1)S(1)} %get-tuple-element.77.refs_3_), channel_id=1, source_target_pairs={{0,2},{1,3},{2,0},{3,1},{4,6},{5,7},{6,4},{7,5},{8,10},{9,11},{10,... | collective-permute-start | bytes 884744 | tf_op jit(solution)/shard_map/ppermute | solution.py:609
  31.9 13.9 %collective-permute-start.11 = (bf16[576,256]{1,0:T(8,128)(2,1)S(1)}, bf16[576,256]{1,0:T(8,128)(2,1)S(1)}, u32[]{:S(2)}, u32[]{:S(2)}) collective-permute-start(bf16[576,256]{1,0:T(8,128)(2,1)S(1)} %bitcast.20), channel_id=1, source_target_pairs={{0,3},{1,2},{2,1},{3,0},{4,7},{5,6},{6,5},{7,4},{8,11},{9,10},{10,... | collective-permute-start | bytes 884744 | tf_op jit(solution)/shard_map/ppermute | solution.py:609
  32.9 9.4 %collective-permute-start.12 = (bf16[128,1024]{1,0:T(8,128)(2,1)S(1)}, bf16[128,1024]{1,0:T(8,128)(2,1)S(1)}, u32[]{:S(2)}, u32[]{:S(2)}) collective-permute-start(bf16[128,1024]{1,0:T(8,128)(2,1)S(1)} %collective-permute-done.5.a2), channel_id=1, source_target_pairs={{0,4},{1,5},{2,6},{3,7},{4,0},{5,1},{6,2},{7,3},{8,12},{9,13},{10,... | collective-permute-start | bytes 786440 | tf_op jit(solution)/shard_map/ppermute | solution.py:615
  41.6 12.8 %collective-permute-start.14 = (bf16[288,512]{1,0:T(8,128)(2,1)S(1)}, bf16[288,512]{1,0:T(8,128)(2,1)S(1)}, u32[]{:S(2)}, u32[]{:S(2)}) collective-permute-start(bf16[288,512]{1,0:T(8,128)(2,1)S(1)} %get-tuple-element.86.refs_7_.a_ref), channel_id=1, source_target_pairs={{0,2},{1,3},{2,0},{3,1},{4,6},{5,7},{6,4},{7,5},{8,10},{9,11},{10,... | collective-permute-start | bytes 884744 | tf_op jit(solution)/shard_map/ppermute | solution.py:609
  48.5 10.8 %collective-permute-start.13 = (bf16[288,512]{1,0:T(8,128)(2,1)S(1)}, bf16[288,512]{1,0:T(8,128)(2,1)S(1)}, u32[]{:S(2)}, u32[]{:S(2)}) collective-permute-start(bf16[288,512]{1,0:T(8,128)(2,1)S(1)} %shard_map.111.refs_7_.b_ref), channel_id=1, source_target_pairs={{0,2},{1,3},{2,0},{3,1},{4,6},{5,7},{6,4},{7,5},{8,10},{9,11},{10,... | collective-permute-start | bytes 884744 | tf_op jit(solution)/shard_map/ppermute | solution.py:609
  49.9 2.4 %collective-permute-start.15 = (bf16[128,1024]{1,0:T(8,128)(2,1)S(1)}, bf16[128,1024]{1,0:T(8,128)(2,1)S(1)}, u32[]{:S(2)}, u32[]{:S(2)}) collective-permute-start(bf16[128,1024]{1,0:T(8,128)(2,1)S(1)} %collective-permute-done.5.a2), channel_id=1, source_target_pairs={{0,1},{1,0},{2,3},{3,2},{4,5},{5,4},{6,7},{7,6},{8,9},{9,8},{10,11... | collective-permute-start | bytes 786440 | tf_op jit(solution)/shard_map/ppermute | solution.py:609
  50.4 1.9 %collective-permute-start.16 = (bf16[128,1024]{1,0:T(8,128)(2,1)S(1)}, bf16[128,1024]{1,0:T(8,128)(2,1)S(1)}, u32[]{:S(2)}, u32[]{:S(2)}) collective-permute-start(bf16[128,1024]{1,0:T(8,128)(2,1)S(1)} %collective-permute-done.12.b2), channel_id=1, source_target_pairs={{0,1},{1,0},{2,3},{3,2},{4,5},{5,4},{6,7},{7,6},{8,9},{9,8},{10,11... | collective-permute-start | bytes 786440 | tf_op jit(solution)/shard_map/ppermute | solution.py:609
  51.4 0.9 copy-start.7
  60.4 11.2 %collective-permute-start.17 = (bf16[288,256]{1,0:T(8,128)(2,1)S(1)}, bf16[288,256]{1,0:T(8,128)(2,1)S(1)}, u32[]{:S(2)}, u32[]{:S(2)}) collective-permute-start(bf16[288,256]{1,0:T(8,128)(2,1)S(1)} %get-tuple-element.98), channel_id=1, source_target_pairs={{0,4},{1,5},{2,6},{3,7},{4,8},{5,9},{6,10},{7,11},{8,12},{9,13},{1... | collective-permute-start | bytes 442376 | tf_op jit(solution)/shard_map/ppermute | solution.py:609
  60.4 11.1 %collective-permute-start.18 = (bf16[288,256]{1,0:T(8,128)(2,1)S(1)}, bf16[288,256]{1,0:T(8,128)(2,1)S(1)}, u32[]{:S(2)}, u32[]{:S(2)}) collective-permute-start(bf16[288,256]{1,0:T(8,128)(2,1)S(1)} %get-tuple-element.99), channel_id=1, source_target_pairs={{0,1},{1,0},{2,3},{3,2},{4,5},{5,4},{6,7},{7,6},{8,9},{9,8},{10,11... | collective-permute-start | bytes 442376 | tf_op jit(solution)/shard_map/ppermute | solution.py:609
  60.5 11.1 %collective-permute-start.19 = (bf16[288,256]{1,0:T(8,128)(2,1)S(1)}, bf16[288,256]{1,0:T(8,128)(2,1)S(1)}, u32[]{:S(2)}, u32[]{:S(2)}) collective-permute-start(bf16[288,256]{1,0:T(8,128)(2,1)S(1)} %get-tuple-element.100), channel_id=1, source_target_pairs={{0,5},{1,4},{2,7},{3,6},{4,9},{5,8},{6,11},{7,10},{8,13},{9,12},{1... | collective-permute-start | bytes 442376 | tf_op jit(solution)/shard_map/ppermute | solution.py:609
  66.6 3.7 %collective-permute-start.20 = (f32[2,1024]{1,0:T(2,128)S(1)}, f32[2,1024]{1,0:T(2,128)S(1)}, u32[]{:S(2)}, u32[]{:S(2)}) collective-permute-start(f32[2,1024]{1,0:T(2,128)S(1)} %shard_map.121), channel_id=1, source_target_pairs={{0,2},{1,3},{2,0},{3,1},{4,6},{5,7},{6,4},{7,5},{8,10},{9,11},{10,... | collective-permute-start | bytes 24584 | tf_op jit(solution)/shard_map/ppermute | solution.py:609
  67.6 3.9 %copy-start.3 = (bf16[1024,3,256]{2,0,1:T(8,128)(2,1)S(1)}, bf16[1024,3,256]{2,0,1:T(8,128)(2,1)}, u32[]{:S(2)}) copy-start(bf16[1024,3,256]{2,0,1:T(8,128)(2,1)} %param.10) | copy-start | bytes 4718596
  70.3 4.1 %collective-permute-start.23 = (f32[2,1792]{1,0:T(2,128)S(1)}, f32[2,1792]{1,0:T(2,128)S(1)}, u32[]{:S(2)}, u32[]{:S(2)}) collective-permute-start(f32[2,1792]{1,0:T(2,128)S(1)} %pad_maximum_fusion), channel_id=1, source_target_pairs={{0,5},{1,4},{2,7},{3,6},{4,1},{5,0},{6,3},{7,2},{8,13},{9,12},{10,... | collective-permute-start | bytes 43016 | tf_op jit(solution)/shard_map/ppermute | solution.py:615
  70.4 4.1 %collective-permute-start.21 = (f32[2,1792]{1,0:T(2,128)S(1)}, f32[2,1792]{1,0:T(2,128)S(1)}, u32[]{:S(2)}, u32[]{:S(2)}) collective-permute-start(f32[2,1792]{1,0:T(2,128)S(1)} %pad_maximum_fusion), channel_id=1, source_target_pairs={{0,1},{1,0},{2,3},{3,2},{4,5},{5,4},{6,7},{7,6},{8,9},{9,8},{10,11... | collective-permute-start | bytes 43016 | tf_op jit(solution)/shard_map/ppermute | solution.py:609
  73.4 3.8 %collective-permute-start.22 = (f32[2,1792]{1,0:T(2,128)S(1)}, f32[2,1792]{1,0:T(2,128)S(1)}, u32[]{:S(2)}, u32[]{:S(2)}) collective-permute-start(f32[2,1792]{1,0:T(2,128)S(1)} %pad_maximum_fusion.1), channel_id=1, source_target_pairs={{0,4},{1,5},{2,6},{3,7},{4,0},{5,1},{6,2},{7,3},{8,12},{9,13},{10,... | collective-permute-start | bytes 43016 | tf_op jit(solution)/shard_map/ppermute | solution.py:615
  77.2 8.8 %collective-permute-start.25 = (f32[2,1792]{1,0:T(2,128)S(1)}, f32[2,1792]{1,0:T(2,128)S(1)}, u32[]{:S(2)}, u32[]{:S(2)}) collective-permute-start(f32[2,1792]{1,0:T(2,128)S(1)} %add_add_fusion.1), channel_id=1, source_target_pairs={{0,16},{1,17},{2,18},{3,19},{4,20},{5,21},{6,22},{7,23},{8,24},{9,... | collective-permute-start | bytes 43016 | tf_op jit(solution)/shard_map/ppermute | solution.py:615
  83.4 5.5 %collective-permute-start.26 = (f32[2,1792]{1,0:T(2,128)S(1)}, f32[2,1792]{1,0:T(2,128)S(1)}, u32[]{:S(2)}, u32[]{:S(2)}) collective-permute-start(f32[2,1792]{1,0:T(2,128)S(1)} %add_add_fusion.1), channel_id=1, source_target_pairs={{0,24},{1,25},{2,26},{3,27},{4,28},{5,29},{6,30},{7,31},{8,16},{9,... | collective-permute-start | bytes 43016 | tf_op jit(solution)/shard_map/ppermute | solution.py:615
  83.4 5.5 %collective-permute-start.24 = (f32[2,1792]{1,0:T(2,128)S(1)}, f32[2,1792]{1,0:T(2,128)S(1)}, u32[]{:S(2)}, u32[]{:S(2)}) collective-permute-start(f32[2,1792]{1,0:T(2,128)S(1)} %add_add_fusion.1), channel_id=1, source_target_pairs={{0,8},{1,9},{2,10},{3,11},{4,12},{5,13},{6,14},{7,15},{8,0},{9,1},... | collective-permute-start | bytes 43016 | tf_op jit(solution)/shard_map/ppermute | solution.py:615

commit v10 on v9

--- a/solution.py
+++ b/solution.py
@@ -667,16 +667,15 @@
     )
     f_low_y = send(f_low, 0, 2)
     t_low = send(t_low, -1, 0)
-    t_own, t_away = split(place, t_raw, t_low)
-    t_away = t_away.reshape(t_own.shape)
-    t_1 = send(t_away, 0, 1)
-    f_low_y, t_own, t_away, slab, wc_peer, idk, idq = lax.optimization_barrier(
-        (f_low_y, t_own, t_away, slab, wc_peer, idk, idq)
+    f_low_y, t_low, slab, wc_peer, idk, idq = lax.optimization_barrier(
+        (f_low_y, t_low, slab, wc_peer, idk, idq)
     )
     x_0, x_2, x_away = split(place, f_raw, f_low, f_up_y, f_low_y)
     pieces = (x_0, x_2, send(x_away, 0, 1))
 
-    targets = (t_own, t_1, send(t_own, 0, 2), send(t_away, 0, 3))
+    t_own, t_away = split(place, after(t_raw, x_0), t_low)
+    t_away = t_away.reshape(t_own.shape)
+    targets = (t_own, send(t_away, 0, 1), send(t_own, 0, 2), send(t_away, 0, 3))
     more = swap(slab, 1, 0)
 
     normed, qkv, attn_0 = forward(t_arr, pieces, wc_own, wc_peer, idk, idq)

time: 90.6 us -> 91 us (level)
  waiting for transfers between devices: 14 us -> 15.4 us
  starting transfers between devices: 29 us -> 28 us
    ppermute x21, waiting for transfers between devices: 8.34 us -> 10.5 us  [send(): return lax.ppermute(block, ('lat', 'tp'), route)]
    ppermute x21, starting transfers between devices: 21 us -> 19.9 us  [send(): return lax.ppermute(block, ('lat', 'tp'), route)]
  transfers between devices with their start and end apart: 27 -> 27, of which waited for: 8 -> 7; matrix products, arithmetic and copies ran while one was open for 2% -> 2% of each run, Pallas kernels for 38% -> 38%
where the time goes in v10:
time: 91 us; the launch traced here: 90.6 us
  Pallas kernels  38.4 us (42%)
  starting transfers between devices  28 us (31%)
  waiting for transfers between devices  15.4 us (17%)
  local copies, waits for them, and re-layouts  7.14 us (8%)
  between operations  1.6 us (2%)
    ppermute x21, starting transfers between devices, send(): return lax.ppermute(block, ('lat', 'tp'), route)  19.9 us
    ppermute x21, waiting for transfers between devices, send(): return lax.ppermute(block, ('lat', 'tp'), route)  10.5 us
    ppermute x6, starting transfers between devices, swap(): return lax.ppermute(block, ('lat', 'tp'), route)  8.09 us
    pallas_call x1, Pallas kernels, forward(): pl.pallas_call(forward_kernel, out_shape=(jax.ShapeDtypeStruct((n, d), BF...  7.63 us
    pallas_call x2, Pallas kernels, backward(): pl.pallas_call(functools.partial(backward_kernel, group), out_shape=jax.S...  6.41 us
    ppermute x6, waiting for transfers between devices, swap(): return lax.ppermute(block, ('lat', 'tp'), route)  4.97 us
    unnamed x24, local copies, waits for them, and re-layouts  4.34 us
    pallas_call x2, Pallas kernels, qkv_sums(): pl.pallas_call(functools.partial(qkv_sums_kernel, side), out_shape=jax.Sh...  3.62 us
  transfers between devices with their start and end apart: 27, of which 7 were waited for; matrix products, arithmetic and copies ran while one was open for 2% of the time, Pallas kernels for 38%

profile of v10, /device:TPU:0, one launch (start us, length us, event | category | flops | bytes accessed | tf_op | source)
XLA Modules:
  0.0 90.6 jit_solution(7820657521481875735)
XLA Ops:
  0.6 0.0 copy-start
  0.6 1.0 %copy-done = bf16[42,2,12,256]{3,1,2,0:T(2,128)(2,1)S(1)} copy-done((bf16[42,2,12,256]{3,1,2,0:T(2,128)(2,1)S(1)}, bf16[42,2,12,256]{3,1,2,0:T(2,128)(2,1)}, u32[]{:S(2)}) %copy-start) | copy-done | bytes 516120
  1.7 0.9 shard_map.103
  2.6 0.5 collective-permute-start.6
  3.1 0.1 collective-permute-start.2
  3.2 2.9 %collective-permute-start = (bf16[42,6,2,256]{3,2,1,0:T(2,128)(2,1)}, bf16[42,6,2,256]{3,2,1,0:T(2,128)(2,1)}, u32[]{:S(2)}, u32[]{:S(2)}) collective-permute-start(bf16[42,6,2,256]{3,2,1,0:T(2,128)(2,1)} %get-tuple-element.59), channel_id=1, source_target_pairs={{0,2},{1,3},{2,0},{3,1},{4,6},{5,7},{6,4},{7,5},{8,10},{9,11},{10,... | collective-permute-start | bytes 774152 | tf_op jit(solution)/shard_map/ppermute | solution.py:609
  6.1 4.5 %collective-permute-start.1 = (bf16[42,6,2,256]{3,2,1,0:T(2,128)(2,1)}, bf16[42,6,2,256]{3,2,1,0:T(2,128)(2,1)}, u32[]{:S(2)}, u32[]{:S(2)}) collective-permute-start(bf16[42,6,2,256]{3,2,1,0:T(2,128)(2,1)} %get-tuple-element.60), channel_id=1, source_target_pairs={{0,28},{1,29},{2,30},{3,31},{4,0},{5,1},{6,2},{7,3},{8,4},{9,5},{1... | collective-permute-start | bytes 774152 | tf_op jit(solution)/shard_map/ppermute | solution.py:609
  10.6 1.4 %copy-done.2 = bf16[1024,3,256]{2,0,1:T(8,128)(2,1)S(1)} copy-done((bf16[1024,3,256]{2,0,1:T(8,128)(2,1)S(1)}, bf16[1024,3,256]{2,0,1:T(8,128)(2,1)}, u32[]{:S(2)}) %copy-start.2) | copy-done | bytes 1572888
  12.0 0.7 copy-done.8
  12.7 0.7 shard_map.104
  13.4 1.2 %copy-done.10 = bf16[3,1024,256]{2,1,0:T(8,128)(2,1)} copy-done((bf16[3,1024,256]{2,1,0:T(8,128)(2,1)}, bf16[3,1024,256]{2,1,0:T(8,128)(2,1)S(1)}, u32[]{:S(2)}) %copy-start.10) | copy-done | bytes 1572888
  14.6 0.7 constant_dynamic-slice_fusion
  15.3 0.5 collective-permute-start.5
  15.8 0.9 slice.12
  16.7 0.0 collective-permute-done.1.refs_1_
  16.7 0.0 collective-permute-done.2.w1.pp_ref
  16.7 1.6 %collective-permute-start.3 = (bf16[42,6,2,256]{3,2,1,0:T(2,128)(2,1)}, bf16[42,6,2,256]{3,2,1,0:T(2,128)(2,1)}, u32[]{:S(2)}, u32[]{:S(2)}) collective-permute-start(bf16[42,6,2,256]{3,2,1,0:T(2,128)(2,1)} %collective-permute-done.1.refs_1_), channel_id=1, source_target_pairs={{0,2},{1,3},{2,0},{3,1},{4,6},{5,7},{6,4},{7,5},{8,10},{9,11},{10,... | collective-permute-start | bytes 774152 | tf_op jit(solution)/shard_map/ppermute | solution.py:609
  18.3 3.7 %collective-permute-start.4 = (bf16[42,6,2,256]{3,2,1,0:T(2,128)(2,1)}, bf16[42,6,2,256]{3,2,1,0:T(2,128)(2,1)}, u32[]{:S(2)}, u32[]{:S(2)}) collective-permute-start(bf16[42,6,2,256]{3,2,1,0:T(2,128)(2,1)} %slice.12), channel_id=1, source_target_pairs={{0,28},{1,29},{2,30},{3,31},{4,0},{5,1},{6,2},{7,3},{8,4},{9,5},{1... | collective-permute-start | bytes 774152 | tf_op jit(solution)/shard_map/ppermute | solution.py:609
  22.1 0.0 collective-permute-start.7
  22.7 0.1 pad_add_fusion.s_ref
  22.8 1.0 %shard_map.106 = (s32[576,1]{1,0:T(8,128)S(1)}, s32[4,1,288]{2,1,0:T(1,128)S(1)}) custom-call(s32[3]{0:T(128)S(1)} %pad_add_fusion.s_ref, s32[42,2,96]{2,1,0:T(2,128)S(1)} %copy-done.6), custom_call_target="tpu_custom_call" | custom-call | flops 1 | bytes 1 | tf_op jit(solution)/shard_map/pallas_call | solution.py:553
  23.9 0.7 shard_map.105
  24.6 0.2 collective-permute-done.5.a2
  24.8 4.1 %collective-permute-done.3.refs_3_ = bf16[42,6,2,256]{3,2,1,0:T(2,128)(2,1)} collective-permute-done((bf16[42,6,2,256]{3,2,1,0:T(2,128)(2,1)}, bf16[42,6,2,256]{3,2,1,0:T(2,128)(2,1)}, u32[]{:S(2)}, u32[]{:S(2)}) %collective-permute-start.3) | collective-permute-done | bytes 258080 | tf_op jit(solution)/shard_map/ppermute | solution.py:609
  28.9 1.9 %shard_map.107 = (bf16[576,256]{1,0:T(8,128)(2,1)S(1)}, bf16[576,256]{1,0:T(8,128)(2,1)S(1)}, bf16[2,576,256]{2,1,0:T(8,128)(2,1)S(1)}) custom-call(s32[3]{0:T(128)S(1)} %pad_add_fusion.s_ref, bf16[42,12,2,256]{3,2,1,0:T(2,128)(2,1)S(1)} %bitcast.11, bf16[42,6,2,256]{3,2,1,0:T(2,128)(2,1)} %collective-permute-done.1.refs_1_, ...), custom_call_target="tpu_custom_call" | custom-call | flops 1 | bytes 1 | tf_op jit(solution)/shard_map/pallas_call | solution.py:497
  30.9 0.1 collective-permute-start.8
  30.9 1.4 %shard_map.108 = (bf16[576,256]{1,0:T(8,128)(2,1)S(1)}, bf16[1,576,256]{2,1,0:T(8,128)(2,1)S(1)}) custom-call(s32[3]{0:T(128)S(1)} %pad_add_fusion.s_ref, bf16[42,12,2,256]{3,2,1,0:T(2,128)(2,1)S(1)} %bitcast.16, bf16[42,6,2,256]{3,2,1,0:T(2,128)(2,1)} %collective-permute-done.4.refs_1_), custom_call_target="tpu_custom_call" | custom-call | flops 1 | bytes 1 | tf_op jit(solution)/shard_map/pallas_call | solution.py:497
  32.3 0.6 collective-permute-start.9
  32.9 0.2 collective-permute-start.11
  33.1 1.5 %collective-permute-start.10 = (bf16[576,256]{1,0:T(8,128)(2,1)S(1)}, bf16[576,256]{1,0:T(8,128)(2,1)S(1)}, u32[]{:S(2)}, u32[]{:S(2)}) collective-permute-start(bf16[576,256]{1,0:T(8,128)(2,1)S(1)} %get-tuple-element.77.refs_3_), channel_id=1, source_target_pairs={{0,2},{1,3},{2,0},{3,1},{4,6},{5,7},{6,4},{7,5},{8,10},{9,11},{10,... | collective-permute-start | bytes 884744 | tf_op jit(solution)/shard_map/ppermute | solution.py:609
  34.6 7.6 %shard_map.109 = (bf16[576,1024]{1,0:T(8,128)(2,1)S(1)}, bf16[6,576,256]{2,1,0:T(8,128)(2,1)S(1)}, bf16[288,512]{1,0:T(8,128)(2,1)S(1)}) custom-call(s32[1]{0:T(128)} %bitcast.2.t_ref, bf16[576,256]{1,0:T(8,128)(2,1)S(1)} %get-tuple-element.72.refs_0_, bf16[576,256]{1,0:T(8,128)(2,1)S(1)} %get-tuple-element.73.refs_1_, ...), custom_call_target="tpu_custom_call" | custom-call | flops 8000000000 | bytes 10000000 | tf_op jit(solution)/shard_map/pallas_call | solution.py:213
  42.3 1.0 %shard_map.110.p_ref = f32[8,144,288]{2,1,0:T(8,128)S(1)} custom-call(bf16[6,576,256]{2,1,0:T(8,128)(2,1)S(1)} %get-tuple-element.102.qkv_ref, s32[576,1]{1,0:T(8,128)S(1)} %get-tuple-element.81.refs_5_.idk_ref.refs_10_, s32[4,1,288]{2,1,0:T(1,128)S(1)} %get-tuple-element.82.refs_6_.idq_ref), custom_call_target="tpu_custom_call" | custom-call | flops 1 | bytes 1 | tf_op jit(solution)/shard_map/pallas_call | solution.py:326
  43.3 0.6 collective-permute-start.14
  43.9 4.9 %collective-permute-done.10.refs_5_ = bf16[576,256]{1,0:T(8,128)(2,1)S(1)} collective-permute-done((bf16[576,256]{1,0:T(8,128)(2,1)S(1)}, bf16[576,256]{1,0:T(8,128)(2,1)S(1)}, u32[]{:S(2)}, u32[]{:S(2)}) %collective-permute-start.10) | collective-permute-done | bytes 294944 | tf_op jit(solution)/shard_map/ppermute | solution.py:609
  48.8 2.7 %shard_map.111.refs_7_.b_ref = bf16[288,512]{1,0:T(8,128)(2,1)S(1)} custom-call(bf16[6,576,256]{2,1,0:T(8,128)(2,1)S(1)} %get-tuple-element.102.qkv_ref, s32[576,1]{1,0:T(8,128)S(1)} %get-tuple-element.81.refs_5_.idk_ref.refs_10_, s32[4,1,288]{2,1,0:T(1,128)S(1)} %get-tuple-element.82.refs_6_.idq_ref), custom_call_target="tpu_custom_call" | custom-call | flops 1 | bytes 1 | tf_op jit(solution)/shard_map/pallas_call | solution.py:200
  51.5 0.6 collective-permute-start.13
  52.0 0.5 collective-permute-start.16
  52.5 1.0 %shard_map.117.p_ref = f32[8,144,288]{2,1,0:T(8,128)S(1)} custom-call(bf16[6,576,256]{2,1,0:T(8,128)(2,1)S(1)} %get-tuple-element.102.qkv_ref, s32[576,1]{1,0:T(8,128)S(1)} %get-tuple-element.81.refs_5_.idk_ref.refs_10_, s32[4,1,288]{2,1,0:T(1,128)S(1)} %get-tuple-element.82.refs_6_.idq_ref), custom_call_target="tpu_custom_call" | custom-call | flops 1 | bytes 1 | tf_op jit(solution)/shard_map/pallas_call | solution.py:326
  53.6 0.0 copy-start.7
  53.6 0.8 shard_map.119
  54.5 2.1 %shard_map.112 = (bf16[1024,1024]{1,0:T(8,128)(2,1)S(1)}, f32[8,1024]{1,0:T(8,128)S(1)}) custom-call(s32[3]{0:T(128)S(1)} %pad_add_fusion.s_ref, bf16[256,1024]{1,0:T(8,128)(2,1)S(1)} %copy-done.4, bf16[256,1024]{1,0:T(8,128)(2,1)} %collective-permute-done.2.w1.pp_ref, bf16[128,1024]{1,0:T(8,128)(2,1)S(1)} %collective-permute-done.5.a2, ...), custom_call_target="tpu_custom_call" | custom-call | flops 1 | bytes 1 | tf_op jit(solution)/shard_map/pallas_call | solution.py:92
  56.5 1.0 %shard_map.113 = (bf16[144,256]{1,0:T(8,128)(2,1)S(1)}, bf16[144,256]{1,0:T(8,128)(2,1)S(1)}, bf16[144,256]{1,0:T(8,128)(2,1)S(1)}, bf16[144,256]{1,0:T(8,128)(2,1)S(1)}, bf16[288,1024]{1,0:T(8,128)(2,1)S(1)}) custom-call(s32[1]{0:T(128)} %bitcast.2.t_ref, bf16[576,256]{1,0:T(8,128)(2,1)S(1)} %get-tuple-element.72.refs_0_, ...), custom_call_target="tpu_custom_call" | custom-call | flops 1 | bytes 1 | tf_op jit(solution)/shard_map/pallas_call | solution.py:296
  57.5 3.2 %shard_map.114.g0_ref = bf16[6,288,256]{2,1,0:T(8,128)(2,1)S(1)} custom-call(bf16[288,1024]{1,0:T(8,128)(2,1)S(1)} %get-tuple-element.91.err_ref.e0_ref, bf16[1024,1024]{1,0:T(8,128)(2,1)S(1)} %get-tuple-element.90.refs_9_.wc_ref, bf16[6,576,256]{2,1,0:T(8,128)(2,1)S(1)} %get-tuple-element.102.qkv_ref, f32[8,144,288]{2,1,0:T(8,128)S(1)} %shard_map.110.p_ref), custom_call_target="tpu_custom_call" | custom-call | flops 1 | bytes 1 | tf_op jit(solution)/shard_map/pallas_call | solution.py:402
  60.7 0.4 collective-permute-done.13.refs_8_
  61.2 1.0 %shard_map.115 = (bf16[288,256]{1,0:T(8,128)(2,1)S(1)}, bf16[288,256]{1,0:T(8,128)(2,1)S(1)}, bf16[288,256]{1,0:T(8,128)(2,1)S(1)}, bf16[288,256]{1,0:T(8,128)(2,1)S(1)}, bf16[288,1024]{1,0:T(8,128)(2,1)S(1)}) custom-call(s32[1]{0:T(128)} %bitcast.2.t_ref, bf16[576,256]{1,0:T(8,128)(2,1)S(1)} %get-tuple-element.72.refs_0_, ...), custom_call_target="tpu_custom_call" | custom-call | flops 1 | bytes 1 | tf_op jit(solution)/shard_map/pallas_call | solution.py:296
  62.1 0.1 collective-permute-start.17
  62.2 0.1 collective-permute-start.18
  62.3 0.2 collective-permute-start.19
  62.5 3.2 %shard_map.118.g1_ref = bf16[6,288,256]{2,1,0:T(8,128)(2,1)S(1)} custom-call(bf16[288,1024]{1,0:T(8,128)(2,1)S(1)} %get-tuple-element.101.err_ref.e1_ref, bf16[1024,1024]{1,0:T(8,128)(2,1)S(1)} %get-tuple-element.90.refs_9_.wc_ref, bf16[6,576,256]{2,1,0:T(8,128)(2,1)S(1)} %get-tuple-element.102.qkv_ref, f32[8,144,288]{2,1,0:T(8,128)S(1)} %shard_map.117.p_ref), custom_call_target="tpu_custom_call" | custom-call | flops 8000000000 | bytes 10000000 | tf_op jit(solution)/shard_map/pallas_call | solution.py:402
  65.7 2.6 %shard_map.121 = f32[2,1024]{1,0:T(2,128)S(1)} custom-call(bf16[288,1024]{1,0:T(8,128)(2,1)S(1)} %get-tuple-element.91.err_ref.e0_ref, bf16[288,1024]{1,0:T(8,128)(2,1)S(1)} %get-tuple-element.101.err_ref.e1_ref, bf16[512,576]{1,0:T(8,128)(2,1)S(1)} %get-tuple-element.106.attn_t, bf16[256,1024]{1,0:T(8,128)(2,1)S(1)} %copy-done.4, ...), custom_call_target="tpu_custom_call" | custom-call | flops 1000000000 | bytes 3000000 | tf_op jit(solution)/shard_map/pallas_call | solution.py:359
  68.4 1.2 %collective-permute-start.20 = (f32[2,1024]{1,0:T(2,128)S(1)}, f32[2,1024]{1,0:T(2,128)S(1)}, u32[]{:S(2)}, u32[]{:S(2)}) collective-permute-start(f32[2,1024]{1,0:T(2,128)S(1)} %shard_map.121), channel_id=1, source_target_pairs={{0,2},{1,3},{2,0},{3,1},{4,6},{5,7},{6,4},{7,5},{8,10},{9,11},{10,... | collective-permute-start | bytes 24584 | tf_op jit(solution)/shard_map/ppermute | solution.py:609
  69.5 1.8 %shard_map.120 = f32[2,768]{1,0:T(2,128)S(1)} custom-call(bf16[6,288,256]{2,1,0:T(8,128)(2,1)S(1)} %shard_map.114.g0_ref, bf16[6,288,256]{2,1,0:T(8,128)(2,1)S(1)} %shard_map.118.g1_ref, bf16[1024,576]{1,0:T(8,128)(2,1)S(1)} %get-tuple-element.104.normed_t, bf16[3,1024,256]{2,1,0:T(8,128)(2,1)S(1)} %collective-permute-done.6.w_ref, ...), custom_call_target="tpu_custom_call" | custom-call | flops 8000000000 | bytes 10000000 | tf_op jit(solution)/shard_map/pallas_call | solution.py:429
  71.3 0.7 collective-permute-done.20
  72.1 0.1 collective-permute-start.23
  72.2 0.4 collective-permute-start.21
  72.6 1.8 %shard_map.122 = f32[2,768]{1,0:T(2,128)S(1)} custom-call(bf16[6,288,256]{2,1,0:T(8,128)(2,1)S(1)} %shard_map.114.g0_ref, bf16[6,288,256]{2,1,0:T(8,128)(2,1)S(1)} %shard_map.118.g1_ref, bf16[1024,576]{1,0:T(8,128)(2,1)S(1)} %get-tuple-element.104.normed_t, bf16[3,1024,256]{2,1,0:T(8,128)(2,1)S(1)} %bitcast.14, f32[3,8,256]{2,1,0:T(8,128)S(1)} %get-tuple-element.110.b_ref), custom_call_target="tpu_custom_call" | custom-call | flops 8000000000 | bytes 10000000 | tf_op jit(solution)/shard_map/pallas_call | solution.py:429
  74.4 1.8 %collective-permute-start.22 = (f32[2,1792]{1,0:T(2,128)S(1)}, f32[2,1792]{1,0:T(2,128)S(1)}, u32[]{:S(2)}, u32[]{:S(2)}) collective-permute-start(f32[2,1792]{1,0:T(2,128)S(1)} %pad_maximum_fusion.1), channel_id=1, source_target_pairs={{0,4},{1,5},{2,6},{3,7},{4,0},{5,1},{6,2},{7,3},{8,12},{9,13},{10,... | collective-permute-start | bytes 43016 | tf_op jit(solution)/shard_map/ppermute | solution.py:615
  76.2 2.1 %collective-permute-done.22 = f32[2,1792]{1,0:T(2,128)S(1)} collective-permute-done((f32[2,1792]{1,0:T(2,128)S(1)}, f32[2,1792]{1,0:T(2,128)S(1)}, u32[]{:S(2)}, u32[]{:S(2)}) %collective-permute-start.22) | collective-permute-done | bytes 14368 | tf_op jit(solution)/shard_map/ppermute | solution.py:615
  78.3 5.6 %collective-permute-start.25 = (f32[2,1792]{1,0:T(2,128)S(1)}, f32[2,1792]{1,0:T(2,128)S(1)}, u32[]{:S(2)}, u32[]{:S(2)}) collective-permute-start(f32[2,1792]{1,0:T(2,128)S(1)} %add_add_fusion.1), channel_id=1, source_target_pairs={{0,16},{1,17},{2,18},{3,19},{4,20},{5,21},{6,22},{7,23},{8,24},{9,... | collective-permute-start | bytes 43016 | tf_op jit(solution)/shard_map/ppermute | solution.py:615
  83.9 0.6 collective-permute-start.24
  84.5 2.0 %shard_map.116 = bf16[42,12,2,256]{3,2,1,0:T(2,128)(2,1)} custom-call(s32[3]{0:T(128)S(1)} %pad_add_fusion.s_ref, bf16[288,256]{1,0:T(8,128)(2,1)S(1)} %get-tuple-element.97.a0, bf16[288,256]{1,0:T(8,128)(2,1)S(1)} %collective-permute-done.17.a1, bf16[288,256]{1,0:T(8,128)(2,1)S(1)} %collective-permute-done.18.b0, ...), custom_call_target="tpu_custom_call" | custom-call | flops 1 | bytes 1 | tf_op jit(solution)/shard_map/pallas_call | solution.py:592
  86.5 2.9 %collective-permute-done.26 = f32[2,1792]{1,0:T(2,128)S(1)} collective-permute-done((f32[2,1792]{1,0:T(2,128)S(1)}, f32[2,1792]{1,0:T(2,128)S(1)}, u32[]{:S(2)}, u32[]{:S(2)}) %collective-permute-start.26) | collective-permute-done | bytes 14368 | tf_op jit(solution)/shard_map/ppermute | solution.py:615
  89.4 0.6 slice.13
  90.0 0.6 slice.14
  (44 shorter events, 0.1 us)
Async XLA Ops:
  0.6 1.0 %copy-start = (bf16[42,2,12,256]{3,1,2,0:T(2,128)(2,1)S(1)}, bf16[42,2,12,256]{3,1,2,0:T(2,128)(2,1)}, u32[]{:S(2)}) copy-start(bf16[42,2,12,256]{3,1,2,0:T(2,128)(2,1)} %param.8) | copy-start | bytes 1548292
  1.7 14.2 %copy-start.5 = (bf16[42,2,12,256]{3,1,2,0:T(2,128)(2,1)S(1)}, bf16[42,2,12,256]{3,1,2,0:T(2,128)(2,1)}, u32[]{:S(2)}) copy-start(bf16[42,2,12,256]{3,1,2,0:T(2,128)(2,1)} %param.9) | copy-start | bytes 1548292
  1.7 20.4 %copy-start.9 = (f32[2,3,256]{2,0,1:T(2,128)S(1)}, f32[2,3,256]{2,0,1:T(2,128)}, u32[]{:S(2)}) copy-start(f32[2,3,256]{2,0,1:T(2,128)} %param.12) | copy-start | bytes 18436
  2.6 21.3 %collective-permute-start.6 = (bf16[3,1024,256]{2,1,0:T(8,128)(2,1)}, bf16[3,1024,256]{2,1,0:T(8,128)(2,1)S(1)}, u32[]{:S(2)}, u32[]{:S(2)}) collective-permute-start(bf16[3,1024,256]{2,1,0:T(8,128)(2,1)} %bitcast.12), channel_id=1, source_target_pairs={{0,1},{1,0},{2,3},{3,2},{4,5},{5,4},{6,7},{7,6},{8,9},{9,8},{10,11... | collective-permute-start | bytes 4718600 | tf_op jit(solution)/shard_map/ppermute | solution.py:609
  3.1 13.7 %collective-permute-start.2 = (bf16[256,1024]{1,0:T(8,128)(2,1)}, bf16[256,1024]{1,0:T(8,128)(2,1)}, u32[]{:S(2)}, u32[]{:S(2)}) collective-permute-start(bf16[256,1024]{1,0:T(8,128)(2,1)} %po_ref), channel_id=1, source_target_pairs={{0,1},{1,0},{2,3},{3,2},{4,5},{5,4},{6,7},{7,6},{8,9},{9,8},{10,11... | collective-permute-start | bytes 1572872 | tf_op jit(solution)/shard_map/ppermute | solution.py:609
  3.2 13.6 %collective-permute-start = (bf16[42,6,2,256]{3,2,1,0:T(2,128)(2,1)}, bf16[42,6,2,256]{3,2,1,0:T(2,128)(2,1)}, u32[]{:S(2)}, u32[]{:S(2)}) collective-permute-start(bf16[42,6,2,256]{3,2,1,0:T(2,128)(2,1)} %get-tuple-element.59), channel_id=1, source_target_pairs={{0,2},{1,3},{2,0},{3,1},{4,6},{5,7},{6,4},{7,5},{8,10},{9,11},{10,... | collective-permute-start | bytes 774152 | tf_op jit(solution)/shard_map/ppermute | solution.py:609
  6.1 10.6 %collective-permute-start.1 = (bf16[42,6,2,256]{3,2,1,0:T(2,128)(2,1)}, bf16[42,6,2,256]{3,2,1,0:T(2,128)(2,1)}, u32[]{:S(2)}, u32[]{:S(2)}) collective-permute-start(bf16[42,6,2,256]{3,2,1,0:T(2,128)(2,1)} %get-tuple-element.60), channel_id=1, source_target_pairs={{0,28},{1,29},{2,30},{3,31},{4,0},{5,1},{6,2},{7,3},{8,4},{9,5},{1... | collective-permute-start | bytes 774152 | tf_op jit(solution)/shard_map/ppermute | solution.py:609
  10.6 1.4 %copy-start.2 = (bf16[1024,3,256]{2,0,1:T(8,128)(2,1)S(1)}, bf16[1024,3,256]{2,0,1:T(8,128)(2,1)}, u32[]{:S(2)}) copy-start(bf16[1024,3,256]{2,0,1:T(8,128)(2,1)} %param.10) | copy-start | bytes 4718596
  12.0 0.7 copy-start.8
  12.7 1.9 %copy-start.4 = (bf16[256,1024]{1,0:T(8,128)(2,1)S(1)}, bf16[256,1024]{1,0:T(8,128)(2,1)}, u32[]{:S(2)}) copy-start(bf16[256,1024]{1,0:T(8,128)(2,1)} %po_ref) | copy-start | bytes 1572868
  12.7 10.1 %copy-start.6 = (s32[42,2,96]{2,1,0:T(2,128)S(1)}, s32[42,2,96]{2,1,0:T(2,128)}, u32[]{:S(2)}) copy-start(s32[42,2,96]{2,1,0:T(2,128)} %ids_ref.1) | copy-start | bytes 96772
  13.4 1.2 %copy-start.10 = (bf16[3,1024,256]{2,1,0:T(8,128)(2,1)}, bf16[3,1024,256]{2,1,0:T(8,128)(2,1)S(1)}, u32[]{:S(2)}) copy-start(bf16[3,1024,256]{2,1,0:T(8,128)(2,1)S(1)} %get-tuple-element.79.refs_3_) | copy-start | bytes 4718596
  14.6 14.3 %copy-start.1 = (bf16[42,2,12,256]{3,1,2,0:T(2,128)(2,1)S(1)}, bf16[42,2,12,256]{3,1,2,0:T(2,128)(2,1)}, u32[]{:S(2)}) copy-start(bf16[42,2,12,256]{3,1,2,0:T(2,128)(2,1)} %param.8) | copy-start | bytes 1548292
  15.3 9.5 %collective-permute-start.5 = (bf16[128,1024]{1,0:T(8,128)(2,1)}, bf16[128,1024]{1,0:T(8,128)(2,1)S(1)}, u32[]{:S(2)}, u32[]{:S(2)}) collective-permute-start(bf16[128,1024]{1,0:T(8,128)(2,1)} %constant_dynamic-slice_fusion), channel_id=1, source_target_pairs={{0,2},{1,3},{2,0},{3,1},{4,6},{5,7},{6,4},{7,5},{8,10},{9,11},{10,... | collective-permute-start | bytes 786440 | tf_op jit(solution)/shard_map/ppermute | solution.py:609
  16.7 12.2 %collective-permute-start.3 = (bf16[42,6,2,256]{3,2,1,0:T(2,128)(2,1)}, bf16[42,6,2,256]{3,2,1,0:T(2,128)(2,1)}, u32[]{:S(2)}, u32[]{:S(2)}) collective-permute-start(bf16[42,6,2,256]{3,2,1,0:T(2,128)(2,1)} %collective-permute-done.1.refs_1_), channel_id=1, source_target_pairs={{0,2},{1,3},{2,0},{3,1},{4,6},{5,7},{6,4},{7,5},{8,10},{9,11},{10,... | collective-permute-start | bytes 774152 | tf_op jit(solution)/shard_map/ppermute | solution.py:609
  18.3 10.6 %collective-permute-start.4 = (bf16[42,6,2,256]{3,2,1,0:T(2,128)(2,1)}, bf16[42,6,2,256]{3,2,1,0:T(2,128)(2,1)}, u32[]{:S(2)}, u32[]{:S(2)}) collective-permute-start(bf16[42,6,2,256]{3,2,1,0:T(2,128)(2,1)} %slice.12), channel_id=1, source_target_pairs={{0,28},{1,29},{2,30},{3,31},{4,0},{5,1},{6,2},{7,3},{8,4},{9,5},{1... | collective-permute-start | bytes 774152 | tf_op jit(solution)/shard_map/ppermute | solution.py:609
  22.1 1.8 %collective-permute-start.7 = (f32[3,2,256]{2,1,0:T(2,128)S(1)}, f32[3,2,256]{2,1,0:T(2,128)S(1)}, u32[]{:S(2)}, u32[]{:S(2)}) collective-permute-start(f32[3,2,256]{2,1,0:T(2,128)S(1)} %bitcast.18), channel_id=1, source_target_pairs={{0,1},{1,0},{2,3},{3,2},{4,5},{5,4},{6,7},{7,6},{8,9},{9,8},{10,11... | collective-permute-start | bytes 18440 | tf_op jit(solution)/shard_map/ppermute | solution.py:609
  23.8 10.8 %copy-start.11 = (bf16[3,1024,256]{2,1,0:T(8,128)(2,1)S(1)}, bf16[3,1024,256]{2,1,0:T(8,128)(2,1)}, u32[]{:S(2)}) copy-start(bf16[3,1024,256]{2,1,0:T(8,128)(2,1)} %copy-done.10) | copy-start | bytes 4718596
  30.9 3.7 %collective-permute-start.8 = (bf16[2,576,256]{2,1,0:T(8,128)(2,1)S(1)}, bf16[2,576,256]{2,1,0:T(8,128)(2,1)S(1)}, u32[]{:S(2)}, u32[]{:S(2)}) collective-permute-start(bf16[2,576,256]{2,1,0:T(8,128)(2,1)S(1)} %get-tuple-element.74), channel_id=1, source_target_pairs={{0,1},{1,0},{2,3},{3,2},{4,5},{5,4},{6,7},{7,6},{8,9},{9,8},{10,11... | collective-permute-start | bytes 1769480 | tf_op jit(solution)/shard_map/ppermute | solution.py:609
  32.3 11.5 %collective-permute-start.9 = (bf16[576,256]{1,0:T(8,128)(2,1)S(1)}, bf16[576,256]{1,0:T(8,128)(2,1)S(1)}, u32[]{:S(2)}, u32[]{:S(2)}) collective-permute-start(bf16[576,256]{1,0:T(8,128)(2,1)S(1)} %bitcast.19), channel_id=1, source_target_pairs={{0,1},{1,0},{2,3},{3,2},{4,5},{5,4},{6,7},{7,6},{8,9},{9,8},{10,11... | collective-permute-start | bytes 884744 | tf_op jit(solution)/shard_map/ppermute | solution.py:609
  32.9 15.9 %collective-permute-start.11 = (bf16[576,256]{1,0:T(8,128)(2,1)S(1)}, bf16[576,256]{1,0:T(8,128)(2,1)S(1)}, u32[]{:S(2)}, u32[]{:S(2)}) collective-permute-start(bf16[576,256]{1,0:T(8,128)(2,1)S(1)} %bitcast.20), channel_id=1, source_target_pairs={{0,3},{1,2},{2,1},{3,0},{4,7},{5,6},{6,5},{7,4},{8,11},{9,10},{10,... | collective-permute-start | bytes 884744 | tf_op jit(solution)/shard_map/ppermute | solution.py:609
  33.1 15.7 %collective-permute-start.10 = (bf16[576,256]{1,0:T(8,128)(2,1)S(1)}, bf16[576,256]{1,0:T(8,128)(2,1)S(1)}, u32[]{:S(2)}, u32[]{:S(2)}) collective-permute-start(bf16[576,256]{1,0:T(8,128)(2,1)S(1)} %get-tuple-element.77.refs_3_), channel_id=1, source_target_pairs={{0,2},{1,3},{2,0},{3,1},{4,6},{5,7},{6,4},{7,5},{8,10},{9,11},{10,... | collective-permute-start | bytes 884744 | tf_op jit(solution)/shard_map/ppermute | solution.py:609
  34.6 9.3 %collective-permute-start.12 = (bf16[128,1024]{1,0:T(8,128)(2,1)S(1)}, bf16[128,1024]{1,0:T(8,128)(2,1)S(1)}, u32[]{:S(2)}, u32[]{:S(2)}) collective-permute-start(bf16[128,1024]{1,0:T(8,128)(2,1)S(1)} %collective-permute-done.5.a2), channel_id=1, source_target_pairs={{0,4},{1,5},{2,6},{3,7},{4,0},{5,1},{6,2},{7,3},{8,12},{9,13},{10,... | collective-permute-start | bytes 786440 | tf_op jit(solution)/shard_map/ppermute | solution.py:615
  43.3 13.3 %collective-permute-start.14 = (bf16[288,512]{1,0:T(8,128)(2,1)S(1)}, bf16[288,512]{1,0:T(8,128)(2,1)S(1)}, u32[]{:S(2)}, u32[]{:S(2)}) collective-permute-start(bf16[288,512]{1,0:T(8,128)(2,1)S(1)} %get-tuple-element.86.refs_7_.a_ref), channel_id=1, source_target_pairs={{0,2},{1,3},{2,0},{3,1},{4,6},{5,7},{6,4},{7,5},{8,10},{9,11},{10,... | collective-permute-start | bytes 884744 | tf_op jit(solution)/shard_map/ppermute | solution.py:609
  51.5 9.7 %collective-permute-start.13 = (bf16[288,512]{1,0:T(8,128)(2,1)S(1)}, bf16[288,512]{1,0:T(8,128)(2,1)S(1)}, u32[]{:S(2)}, u32[]{:S(2)}) collective-permute-start(bf16[288,512]{1,0:T(8,128)(2,1)S(1)} %shard_map.111.refs_7_.b_ref), channel_id=1, source_target_pairs={{0,2},{1,3},{2,0},{3,1},{4,6},{5,7},{6,4},{7,5},{8,10},{9,11},{10,... | collective-permute-start | bytes 884744 | tf_op jit(solution)/shard_map/ppermute | solution.py:609
  52.0 2.4 %collective-permute-start.15 = (bf16[128,1024]{1,0:T(8,128)(2,1)S(1)}, bf16[128,1024]{1,0:T(8,128)(2,1)S(1)}, u32[]{:S(2)}, u32[]{:S(2)}) collective-permute-start(bf16[128,1024]{1,0:T(8,128)(2,1)S(1)} %collective-permute-done.5.a2), channel_id=1, source_target_pairs={{0,1},{1,0},{2,3},{3,2},{4,5},{5,4},{6,7},{7,6},{8,9},{9,8},{10,11... | collective-permute-start | bytes 786440 | tf_op jit(solution)/shard_map/ppermute | solution.py:609
  52.0 2.4 %collective-permute-start.16 = (bf16[128,1024]{1,0:T(8,128)(2,1)S(1)}, bf16[128,1024]{1,0:T(8,128)(2,1)S(1)}, u32[]{:S(2)}, u32[]{:S(2)}) collective-permute-start(bf16[128,1024]{1,0:T(8,128)(2,1)S(1)} %collective-permute-done.12.b2), channel_id=1, source_target_pairs={{0,1},{1,0},{2,3},{3,2},{4,5},{5,4},{6,7},{7,6},{8,9},{9,8},{10,11... | collective-permute-start | bytes 786440 | tf_op jit(solution)/shard_map/ppermute | solution.py:609
  53.6 0.9 copy-start.7
  62.1 10.5 %collective-permute-start.17 = (bf16[288,256]{1,0:T(8,128)(2,1)S(1)}, bf16[288,256]{1,0:T(8,128)(2,1)S(1)}, u32[]{:S(2)}, u32[]{:S(2)}) collective-permute-start(bf16[288,256]{1,0:T(8,128)(2,1)S(1)} %get-tuple-element.98), channel_id=1, source_target_pairs={{0,4},{1,5},{2,6},{3,7},{4,8},{5,9},{6,10},{7,11},{8,12},{9,13},{1... | collective-permute-start | bytes 442376 | tf_op jit(solution)/shard_map/ppermute | solution.py:609
  62.2 10.4 %collective-permute-start.18 = (bf16[288,256]{1,0:T(8,128)(2,1)S(1)}, bf16[288,256]{1,0:T(8,128)(2,1)S(1)}, u32[]{:S(2)}, u32[]{:S(2)}) collective-permute-start(bf16[288,256]{1,0:T(8,128)(2,1)S(1)} %get-tuple-element.99), channel_id=1, source_target_pairs={{0,1},{1,0},{2,3},{3,2},{4,5},{5,4},{6,7},{7,6},{8,9},{9,8},{10,11... | collective-permute-start | bytes 442376 | tf_op jit(solution)/shard_map/ppermute | solution.py:609
  62.3 10.3 %collective-permute-start.19 = (bf16[288,256]{1,0:T(8,128)(2,1)S(1)}, bf16[288,256]{1,0:T(8,128)(2,1)S(1)}, u32[]{:S(2)}, u32[]{:S(2)}) collective-permute-start(bf16[288,256]{1,0:T(8,128)(2,1)S(1)} %get-tuple-element.100), channel_id=1, source_target_pairs={{0,5},{1,4},{2,7},{3,6},{4,9},{5,8},{6,11},{7,10},{8,13},{9,12},{1... | collective-permute-start | bytes 442376 | tf_op jit(solution)/shard_map/ppermute | solution.py:609
  68.4 3.7 %collective-permute-start.20 = (f32[2,1024]{1,0:T(2,128)S(1)}, f32[2,1024]{1,0:T(2,128)S(1)}, u32[]{:S(2)}, u32[]{:S(2)}) collective-permute-start(f32[2,1024]{1,0:T(2,128)S(1)} %shard_map.121), channel_id=1, source_target_pairs={{0,2},{1,3},{2,0},{3,1},{4,6},{5,7},{6,4},{7,5},{8,10},{9,11},{10,... | collective-permute-start | bytes 24584 | tf_op jit(solution)/shard_map/ppermute | solution.py:609
  69.5 3.1 %copy-start.3 = (bf16[1024,3,256]{2,0,1:T(8,128)(2,1)S(1)}, bf16[1024,3,256]{2,0,1:T(8,128)(2,1)}, u32[]{:S(2)}) copy-start(bf16[1024,3,256]{2,0,1:T(8,128)(2,1)} %param.10) | copy-start | bytes 4718596
  72.1 4.1 %collective-permute-start.23 = (f32[2,1792]{1,0:T(2,128)S(1)}, f32[2,1792]{1,0:T(2,128)S(1)}, u32[]{:S(2)}, u32[]{:S(2)}) collective-permute-start(f32[2,1792]{1,0:T(2,128)S(1)} %pad_maximum_fusion), channel_id=1, source_target_pairs={{0,5},{1,4},{2,7},{3,6},{4,1},{5,0},{6,3},{7,2},{8,13},{9,12},{10,... | collective-permute-start | bytes 43016 | tf_op jit(solution)/shard_map/ppermute | solution.py:615
  72.2 4.1 %collective-permute-start.21 = (f32[2,1792]{1,0:T(2,128)S(1)}, f32[2,1792]{1,0:T(2,128)S(1)}, u32[]{:S(2)}, u32[]{:S(2)}) collective-permute-start(f32[2,1792]{1,0:T(2,128)S(1)} %pad_maximum_fusion), channel_id=1, source_target_pairs={{0,1},{1,0},{2,3},{3,2},{4,5},{5,4},{6,7},{7,6},{8,9},{9,8},{10,11... | collective-permute-start | bytes 43016 | tf_op jit(solution)/shard_map/ppermute | solution.py:609
  74.4 3.8 %collective-permute-start.22 = (f32[2,1792]{1,0:T(2,128)S(1)}, f32[2,1792]{1,0:T(2,128)S(1)}, u32[]{:S(2)}, u32[]{:S(2)}) collective-permute-start(f32[2,1792]{1,0:T(2,128)S(1)} %pad_maximum_fusion.1), channel_id=1, source_target_pairs={{0,4},{1,5},{2,6},{3,7},{4,0},{5,1},{6,2},{7,3},{8,12},{9,13},{10,... | collective-permute-start | bytes 43016 | tf_op jit(solution)/shard_map/ppermute | solution.py:615
  78.3 8.2 %collective-permute-start.25 = (f32[2,1792]{1,0:T(2,128)S(1)}, f32[2,1792]{1,0:T(2,128)S(1)}, u32[]{:S(2)}, u32[]{:S(2)}) collective-permute-start(f32[2,1792]{1,0:T(2,128)S(1)} %add_add_fusion.1), channel_id=1, source_target_pairs={{0,16},{1,17},{2,18},{3,19},{4,20},{5,21},{6,22},{7,23},{8,24},{9,... | collective-permute-start | bytes 43016 | tf_op jit(solution)/shard_map/ppermute | solution.py:615
  83.9 5.5 %collective-permute-start.26 = (f32[2,1792]{1,0:T(2,128)S(1)}, f32[2,1792]{1,0:T(2,128)S(1)}, u32[]{:S(2)}, u32[]{:S(2)}) collective-permute-start(f32[2,1792]{1,0:T(2,128)S(1)} %add_add_fusion.1), channel_id=1, source_target_pairs={{0,24},{1,25},{2,26},{3,27},{4,28},{5,29},{6,30},{7,31},{8,16},{9,... | collective-permute-start | bytes 43016 | tf_op jit(solution)/shard_map/ppermute | solution.py:615
  83.9 5.5 %collective-permute-start.24 = (f32[2,1792]{1,0:T(2,128)S(1)}, f32[2,1792]{1,0:T(2,128)S(1)}, u32[]{:S(2)}, u32[]{:S(2)}) collective-permute-start(f32[2,1792]{1,0:T(2,128)S(1)} %add_add_fusion.1), channel_id=1, source_target_pairs={{0,8},{1,9},{2,10},{3,11},{4,12},{5,13},{6,14},{7,15},{8,0},{9,1},... | collective-permute-start | bytes 43016 | tf_op jit(solution)/shard_map/ppermute | solution.py:615

commit v11 on v10

--- a/solution.py
+++ b/solution.py
@@ -658,29 +658,28 @@
     share = w_proj.shape[0] // 2
     w1 = send(w_proj, 0, 1)
     wc_own, b_own = clip_qkv(w3, c3)
-    slab = after(w_proj, wc_own)
-    slab = send(lax.dynamic_slice_in_dim(slab, share * (sector % 2), share, 0), 0, 2)
+    slab = lax.dynamic_slice_in_dim(after(w_proj, wc_own), share * (sector % 2), share, 0)
     wc_peer, b_peer = clip_qkv(w3_peer, c3_peer)
     idk, idq = window_ids(place, region_ids, WLAT * lev * lon)
-    f_up_y, f_low, w1, t_low, wc_own = lax.optimization_barrier(
-        (f_up_y, f_low, w1, t_raw[:, :half], wc_own)
+    f_up_y, f_low, w1, t_low, slab, wc_own = lax.optimization_barrier(
+        (f_up_y, f_low, w1, t_raw[:, :half], slab, wc_own)
     )
     f_low_y = send(f_low, 0, 2)
     t_low = send(t_low, -1, 0)
-    f_low_y, t_low, slab, wc_peer, idk, idq = lax.optimization_barrier(
-        (f_low_y, t_low, slab, wc_peer, idk, idq)
-    )
+    f_low_y, t_low, wc_peer, idk, idq = lax.optimization_barrier((f_low_y, t_low, wc_peer, idk, idq))
+    slab = send(slab, 0, 2)
     x_0, x_2, x_away = split(place, f_raw, f_low, f_up_y, f_low_y)
     pieces = (x_0, x_2, send(x_away, 0, 1))
 
     t_own, t_away = split(place, after(t_raw, x_0), t_low)
     t_away = t_away.reshape(t_own.shape)
     targets = (t_own, send(t_away, 0, 1), send(t_own, 0, 2), send(t_away, 0, 3))
-    more = swap(slab, 1, 0)
 
     normed, qkv, attn_0 = forward(t_arr, pieces, wc_own, wc_peer, idk, idq)
     other_0 = send(attn_0, 0, 2)
     probs_0 = probs_of(0, qkv, idk, idq)
+    slab = after(slab, probs_0)
+    more = swap(slab, 1, 0)
     attn_1 = last_windows(after(qkv, probs_0, *targets, more), idk, idq)
     slab_3, more_3 = send(after(slab, attn_1), 0, 1), send(after(more, attn_1), 0, 1)
     pc, pb = clip_proj(place, [w_proj, w1, slab, more, slab_3, more_3], proj_clip)

time: 91 us -> 94.8 us (1.042)
  waiting for transfers between devices: 15.4 us -> 17.4 us
  starting transfers between devices: 28 us -> 29.5 us
    ppermute x21, starting transfers between devices: 19.9 us -> 22.3 us  [send(): return lax.ppermute(block, ('lat', 'tp'), route)]
    ppermute x6, waiting for transfers between devices: 4.97 us -> 6.16 us  [swap(): return lax.ppermute(block, ('lat', 'tp'), route)]
    unnamed x24 -> x30, local copies, waits for them, and re-layouts: 4.34 us -> 5.04 us
  transfers between devices with their start and end apart: 27 -> 27, of which waited for: 7 -> 7; matrix products, arithmetic and copies ran while one was open for 2% -> 2% of each run, Pallas kernels for 38% -> 36%
where the time goes in v11:
time: 94.8 us; the launch traced here: 94.4 us
  Pallas kernels  37.8 us (40%)
  starting transfers between devices  29.5 us (31%)
  waiting for transfers between devices  17.4 us (18%)
  local copies, waits for them, and re-layouts  7.83 us (8%)
  between operations  1.63 us (2%)
    ppermute x21, starting transfers between devices, send(): return lax.ppermute(block, ('lat', 'tp'), route)  22.3 us
    ppermute x21, waiting for transfers between devices, send(): return lax.ppermute(block, ('lat', 'tp'), route)  11.3 us
    pallas_call x1, Pallas kernels, forward(): pl.pallas_call(forward_kernel, out_shape=(jax.ShapeDtypeStruct((n, d), BF...  7.61 us
    ppermute x6, starting transfers between devices, swap(): return lax.ppermute(block, ('lat', 'tp'), route)  7.27 us
    pallas_call x2, Pallas kernels, backward(): pl.pallas_call(functools.partial(backward_kernel, group), out_shape=jax.S...  6.42 us
    ppermute x6, waiting for transfers between devices, swap(): return lax.ppermute(block, ('lat', 'tp'), route)  6.16 us
    unnamed x30, local copies, waits for them, and re-layouts  5.04 us
    pallas_call x2, Pallas kernels, qkv_sums(): pl.pallas_call(functools.partial(qkv_sums_kernel, side), out_shape=jax.Sh...  3.66 us
  transfers between devices with their start and end apart: 27, of which 7 were waited for; matrix products, arithmetic and copies ran while one was open for 2% of the time, Pallas kernels for 36%

profile of v11, /device:TPU:0, one launch (start us, length us, event | category | flops | bytes accessed | tf_op | source)
XLA Modules:
  0.0 94.4 jit_solution(3373925508462759947)
XLA Ops:
  0.6 0.0 copy-start
  0.6 1.0 %copy-done = bf16[42,2,12,256]{3,1,2,0:T(2,128)(2,1)S(1)} copy-done((bf16[42,2,12,256]{3,1,2,0:T(2,128)(2,1)S(1)}, bf16[42,2,12,256]{3,1,2,0:T(2,128)(2,1)}, u32[]{:S(2)}) %copy-start) | copy-done | bytes 516120
  1.7 0.9 shard_map.103
  2.5 0.5 collective-permute-start.5
  3.1 0.1 collective-permute-start.2
  3.1 2.9 %collective-permute-start = (bf16[42,6,2,256]{3,2,1,0:T(2,128)(2,1)}, bf16[42,6,2,256]{3,2,1,0:T(2,128)(2,1)S(1)}, u32[]{:S(2)}, u32[]{:S(2)}) collective-permute-start(bf16[42,6,2,256]{3,2,1,0:T(2,128)(2,1)} %get-tuple-element.60), channel_id=1, source_target_pairs={{0,2},{1,3},{2,0},{3,1},{4,6},{5,7},{6,4},{7,5},{8,10},{9,11},{10,... | collective-permute-start | bytes 774152 | tf_op jit(solution)/shard_map/ppermute | solution.py:609
  6.1 4.5 %collective-permute-start.1 = (bf16[42,6,2,256]{3,2,1,0:T(2,128)(2,1)}, bf16[42,6,2,256]{3,2,1,0:T(2,128)(2,1)}, u32[]{:S(2)}, u32[]{:S(2)}) collective-permute-start(bf16[42,6,2,256]{3,2,1,0:T(2,128)(2,1)} %get-tuple-element.61), channel_id=1, source_target_pairs={{0,28},{1,29},{2,30},{3,31},{4,0},{5,1},{6,2},{7,3},{8,4},{9,5},{1... | collective-permute-start | bytes 774152 | tf_op jit(solution)/shard_map/ppermute | solution.py:609
  10.6 1.4 %copy-done.2 = bf16[1024,3,256]{2,0,1:T(8,128)(2,1)S(1)} copy-done((bf16[1024,3,256]{2,0,1:T(8,128)(2,1)S(1)}, bf16[1024,3,256]{2,0,1:T(8,128)(2,1)}, u32[]{:S(2)}) %copy-start.2) | copy-done | bytes 1572888
  12.0 0.7 copy-done.10
  12.7 0.7 shard_map.104
  13.4 1.2 %copy-done.12 = bf16[3,1024,256]{2,1,0:T(8,128)(2,1)} copy-done((bf16[3,1024,256]{2,1,0:T(8,128)(2,1)}, bf16[3,1024,256]{2,1,0:T(8,128)(2,1)S(1)}, u32[]{:S(2)}) %copy-start.12) | copy-done | bytes 1572888
  14.6 0.9 slice.12
  15.5 0.7 constant_dynamic-slice_fusion
  16.2 0.7 copy-done.6
  16.9 0.5 collective-permute-start.3
  17.4 4.7 %collective-permute-start.4 = (bf16[42,6,2,256]{3,2,1,0:T(2,128)(2,1)}, bf16[42,6,2,256]{3,2,1,0:T(2,128)(2,1)S(1)}, u32[]{:S(2)}, u32[]{:S(2)}) collective-permute-start(bf16[42,6,2,256]{3,2,1,0:T(2,128)(2,1)} %slice.12), channel_id=1, source_target_pairs={{0,28},{1,29},{2,30},{3,31},{4,0},{5,1},{6,2},{7,3},{8,4},{9,5},{1... | collective-permute-start | bytes 774152 | tf_op jit(solution)/shard_map/ppermute | solution.py:609
  22.7 0.0 copy-start.14
  22.7 0.1 pad_add_fusion.s_ref
  22.8 1.0 %shard_map.106 = (s32[576,1]{1,0:T(8,128)S(1)}, s32[4,1,288]{2,1,0:T(1,128)S(1)}) custom-call(s32[3]{0:T(128)S(1)} %pad_add_fusion.s_ref, s32[42,2,96]{2,1,0:T(2,128)S(1)} %copy-done.8), custom_call_target="tpu_custom_call" | custom-call | flops 1 | bytes 1 | tf_op jit(solution)/shard_map/pallas_call | solution.py:553
  23.9 0.7 shard_map.105
  24.6 0.3 collective-permute-done.3.refs_3_
  24.9 1.8 %collective-permute-done.4.refs_1_ = bf16[42,6,2,256]{3,2,1,0:T(2,128)(2,1)S(1)} collective-permute-done((bf16[42,6,2,256]{3,2,1,0:T(2,128)(2,1)}, bf16[42,6,2,256]{3,2,1,0:T(2,128)(2,1)S(1)}, u32[]{:S(2)}, u32[]{:S(2)}) %collective-permute-start.4) | collective-permute-done | bytes 258080 | tf_op jit(solution)/shard_map/ppermute | solution.py:609
  26.7 1.8 %shard_map.107 = (bf16[576,256]{1,0:T(8,128)(2,1)S(1)}, bf16[576,256]{1,0:T(8,128)(2,1)S(1)}, bf16[2,576,256]{2,1,0:T(8,128)(2,1)S(1)}) custom-call(s32[3]{0:T(128)S(1)} %pad_add_fusion.s_ref, bf16[42,12,2,256]{3,2,1,0:T(2,128)(2,1)S(1)} %bitcast.11, bf16[42,6,2,256]{3,2,1,0:T(2,128)(2,1)} %collective-permute-done.1.refs_1_, ...), custom_call_target="tpu_custom_call" | custom-call | flops 1 | bytes 1 | tf_op jit(solution)/shard_map/pallas_call | solution.py:497
  28.5 0.1 collective-permute-start.7
  28.6 1.6 %collective-permute-start.11 = (bf16[128,1024]{1,0:T(8,128)(2,1)S(1)}, bf16[128,1024]{1,0:T(8,128)(2,1)S(1)}, u32[]{:S(2)}, u32[]{:S(2)}) collective-permute-start(bf16[128,1024]{1,0:T(8,128)(2,1)S(1)} %copy-done.14), channel_id=1, source_target_pairs={{0,2},{1,3},{2,0},{3,1},{4,6},{5,7},{6,4},{7,5},{8,10},{9,11},{10,... | collective-permute-start | bytes 786440 | tf_op jit(solution)/shard_map/ppermute | solution.py:609
  30.2 1.0 %shard_map.108 = (bf16[576,256]{1,0:T(8,128)(2,1)S(1)}, bf16[1,576,256]{2,1,0:T(8,128)(2,1)S(1)}) custom-call(s32[3]{0:T(128)S(1)} %pad_add_fusion.s_ref, bf16[42,12,2,256]{3,2,1,0:T(2,128)(2,1)S(1)} %bitcast.16, bf16[42,6,2,256]{3,2,1,0:T(2,128)(2,1)S(1)} %collective-permute-done.4.refs_1_), custom_call_target="tpu_custom_call" | custom-call | flops 1 | bytes 1 | tf_op jit(solution)/shard_map/pallas_call | solution.py:497
  31.1 0.2 collective-permute-start.8
  31.4 0.5 collective-permute-start.10
  31.8 1.5 %collective-permute-start.9 = (bf16[576,256]{1,0:T(8,128)(2,1)S(1)}, bf16[576,256]{1,0:T(8,128)(2,1)S(1)}, u32[]{:S(2)}, u32[]{:S(2)}) collective-permute-start(bf16[576,256]{1,0:T(8,128)(2,1)S(1)} %get-tuple-element.78.refs_3_), channel_id=1, source_target_pairs={{0,2},{1,3},{2,0},{3,1},{4,6},{5,7},{6,4},{7,5},{8,10},{9,11},{10,... | collective-permute-start | bytes 884744 | tf_op jit(solution)/shard_map/ppermute | solution.py:609
  33.3 7.6 %shard_map.109 = (bf16[576,1024]{1,0:T(8,128)(2,1)S(1)}, bf16[6,576,256]{2,1,0:T(8,128)(2,1)S(1)}, bf16[288,512]{1,0:T(8,128)(2,1)S(1)}) custom-call(s32[1]{0:T(128)} %bitcast.2.t_ref, bf16[576,256]{1,0:T(8,128)(2,1)S(1)} %get-tuple-element.73.refs_0_, bf16[576,256]{1,0:T(8,128)(2,1)S(1)} %get-tuple-element.74.refs_1_, ...), custom_call_target="tpu_custom_call" | custom-call | flops 8000000000 | bytes 10000000 | tf_op jit(solution)/shard_map/pallas_call | solution.py:213
  41.0 1.0 %shard_map.110.p_ref = f32[8,144,288]{2,1,0:T(8,128)S(1)} custom-call(bf16[6,576,256]{2,1,0:T(8,128)(2,1)S(1)} %get-tuple-element.104.qkv_ref, s32[576,1]{1,0:T(8,128)S(1)} %get-tuple-element.82.refs_5_.idk_ref.refs_10_, s32[4,1,288]{2,1,0:T(1,128)S(1)} %get-tuple-element.83.refs_6_.idq_ref), custom_call_target="tpu_custom_call" | custom-call | flops 1 | bytes 1 | tf_op jit(solution)/shard_map/pallas_call | solution.py:326
  42.0 0.1 collective-permute-start.12
  42.1 0.6 collective-permute-start.14
  42.7 7.7 %collective-permute-done.9.refs_5_ = bf16[576,256]{1,0:T(8,128)(2,1)S(1)} collective-permute-done((bf16[576,256]{1,0:T(8,128)(2,1)S(1)}, bf16[576,256]{1,0:T(8,128)(2,1)S(1)}, u32[]{:S(2)}, u32[]{:S(2)}) %collective-permute-start.9) | collective-permute-done | bytes 294944 | tf_op jit(solution)/shard_map/ppermute | solution.py:609
  50.4 2.7 %shard_map.111.refs_7_.b_ref = bf16[288,512]{1,0:T(8,128)(2,1)S(1)} custom-call(bf16[6,576,256]{2,1,0:T(8,128)(2,1)S(1)} %get-tuple-element.104.qkv_ref, s32[576,1]{1,0:T(8,128)S(1)} %get-tuple-element.82.refs_5_.idk_ref.refs_10_, s32[4,1,288]{2,1,0:T(1,128)S(1)} %get-tuple-element.83.refs_6_.idq_ref), custom_call_target="tpu_custom_call" | custom-call | flops 1 | bytes 1 | tf_op jit(solution)/shard_map/pallas_call | solution.py:200
  53.1 1.6 %collective-permute-start.13 = (bf16[288,512]{1,0:T(8,128)(2,1)S(1)}, bf16[288,512]{1,0:T(8,128)(2,1)S(1)}, u32[]{:S(2)}, u32[]{:S(2)}) collective-permute-start(bf16[288,512]{1,0:T(8,128)(2,1)S(1)} %shard_map.111.refs_7_.b_ref), channel_id=1, source_target_pairs={{0,2},{1,3},{2,0},{3,1},{4,6},{5,7},{6,4},{7,5},{8,10},{9,11},{10,... | collective-permute-start | bytes 884744 | tf_op jit(solution)/shard_map/ppermute | solution.py:609
  54.7 0.5 collective-permute-start.16
  55.2 1.0 %shard_map.117.p_ref = f32[8,144,288]{2,1,0:T(8,128)S(1)} custom-call(bf16[6,576,256]{2,1,0:T(8,128)(2,1)S(1)} %get-tuple-element.104.qkv_ref, s32[576,1]{1,0:T(8,128)S(1)} %get-tuple-element.82.refs_5_.idk_ref.refs_10_, s32[4,1,288]{2,1,0:T(1,128)S(1)} %get-tuple-element.83.refs_6_.idq_ref), custom_call_target="tpu_custom_call" | custom-call | flops 1 | bytes 1 | tf_op jit(solution)/shard_map/pallas_call | solution.py:326
  56.2 0.0 copy-start.9
  56.2 0.8 shard_map.119
  57.1 2.1 %shard_map.112 = (bf16[1024,1024]{1,0:T(8,128)(2,1)S(1)}, f32[8,1024]{1,0:T(8,128)S(1)}) custom-call(s32[3]{0:T(128)S(1)} %pad_add_fusion.s_ref, bf16[256,1024]{1,0:T(8,128)(2,1)S(1)} %copy-done.4, bf16[256,1024]{1,0:T(8,128)(2,1)} %collective-permute-done.2.w1.pp_ref, bf16[128,1024]{1,0:T(8,128)(2,1)S(1)} %collective-permute-done.11.a2, ...), custom_call_target="tpu_custom_call" | custom-call | flops 1 | bytes 1 | tf_op jit(solution)/shard_map/pallas_call | solution.py:92
  59.2 1.0 %shard_map.113 = (bf16[144,256]{1,0:T(8,128)(2,1)S(1)}, bf16[144,256]{1,0:T(8,128)(2,1)S(1)}, bf16[144,256]{1,0:T(8,128)(2,1)S(1)}, bf16[144,256]{1,0:T(8,128)(2,1)S(1)}, bf16[288,1024]{1,0:T(8,128)(2,1)S(1)}) custom-call(s32[1]{0:T(128)} %bitcast.2.t_ref, bf16[576,256]{1,0:T(8,128)(2,1)S(1)} %get-tuple-element.73.refs_0_, ...), custom_call_target="tpu_custom_call" | custom-call | flops 1 | bytes 1 | tf_op jit(solution)/shard_map/pallas_call | solution.py:296
  60.1 3.2 %shard_map.114.g0_ref = bf16[6,288,256]{2,1,0:T(8,128)(2,1)S(1)} custom-call(bf16[288,1024]{1,0:T(8,128)(2,1)S(1)} %get-tuple-element.93.err_ref.e0_ref, bf16[1024,1024]{1,0:T(8,128)(2,1)S(1)} %get-tuple-element.92.refs_9_.wc_ref, bf16[6,576,256]{2,1,0:T(8,128)(2,1)S(1)} %get-tuple-element.104.qkv_ref, f32[8,144,288]{2,1,0:T(8,128)S(1)} %shard_map.110.p_ref), custom_call_target="tpu_custom_call" | custom-call | flops 1 | bytes 1 | tf_op jit(solution)/shard_map/pallas_call | solution.py:402
  63.4 1.0 %shard_map.115 = (bf16[288,256]{1,0:T(8,128)(2,1)S(1)}, bf16[288,256]{1,0:T(8,128)(2,1)S(1)}, bf16[288,256]{1,0:T(8,128)(2,1)S(1)}, bf16[288,256]{1,0:T(8,128)(2,1)S(1)}, bf16[288,1024]{1,0:T(8,128)(2,1)S(1)}) custom-call(s32[1]{0:T(128)} %bitcast.2.t_ref, bf16[576,256]{1,0:T(8,128)(2,1)S(1)} %get-tuple-element.73.refs_0_, ...), custom_call_target="tpu_custom_call" | custom-call | flops 1 | bytes 1 | tf_op jit(solution)/shard_map/pallas_call | solution.py:296
  64.3 0.1 collective-permute-start.17
  64.4 0.1 collective-permute-start.18
  64.5 0.2 collective-permute-start.19
  64.7 3.2 %shard_map.118.g1_ref = bf16[6,288,256]{2,1,0:T(8,128)(2,1)S(1)} custom-call(bf16[288,1024]{1,0:T(8,128)(2,1)S(1)} %get-tuple-element.103.err_ref.e1_ref, bf16[1024,1024]{1,0:T(8,128)(2,1)S(1)} %get-tuple-element.92.refs_9_.wc_ref, bf16[6,576,256]{2,1,0:T(8,128)(2,1)S(1)} %get-tuple-element.104.qkv_ref, f32[8,144,288]{2,1,0:T(8,128)S(1)} %shard_map.117.p_ref), custom_call_target="tpu_custom_call" | custom-call | flops 8000000000 | bytes 10000000 | tf_op jit(solution)/shard_map/pallas_call | solution.py:402
  67.9 2.6 %shard_map.121 = f32[2,1024]{1,0:T(2,128)S(1)} custom-call(bf16[288,1024]{1,0:T(8,128)(2,1)S(1)} %get-tuple-element.93.err_ref.e0_ref, bf16[288,1024]{1,0:T(8,128)(2,1)S(1)} %get-tuple-element.103.err_ref.e1_ref, bf16[512,576]{1,0:T(8,128)(2,1)S(1)} %get-tuple-element.108.attn_t, bf16[256,1024]{1,0:T(8,128)(2,1)S(1)} %copy-done.4, ...), custom_call_target="tpu_custom_call" | custom-call | flops 1000000000 | bytes 3000000 | tf_op jit(solution)/shard_map/pallas_call | solution.py:359
  70.6 0.8 collective-permute-start.20
  71.3 1.8 %shard_map.120 = f32[2,768]{1,0:T(2,128)S(1)} custom-call(bf16[6,288,256]{2,1,0:T(8,128)(2,1)S(1)} %shard_map.114.g0_ref, bf16[6,288,256]{2,1,0:T(8,128)(2,1)S(1)} %shard_map.118.g1_ref, bf16[1024,576]{1,0:T(8,128)(2,1)S(1)} %get-tuple-element.106.normed_t, bf16[3,1024,256]{2,1,0:T(8,128)(2,1)S(1)} %collective-permute-done.5.w_ref, ...), custom_call_target="tpu_custom_call" | custom-call | flops 8000000000 | bytes 10000000 | tf_op jit(solution)/shard_map/pallas_call | solution.py:429
  73.2 1.1 %collective-permute-done.20 = f32[2,1024]{1,0:T(2,128)S(1)} collective-permute-done((f32[2,1024]{1,0:T(2,128)S(1)}, f32[2,1024]{1,0:T(2,128)S(1)}, u32[]{:S(2)}, u32[]{:S(2)}) %collective-permute-start.20) | collective-permute-done | bytes 8224 | tf_op jit(solution)/shard_map/ppermute | solution.py:609
  74.3 0.1 collective-permute-start.23
  74.4 1.4 %collective-permute-start.21 = (f32[2,1792]{1,0:T(2,128)S(1)}, f32[2,1792]{1,0:T(2,128)S(1)}, u32[]{:S(2)}, u32[]{:S(2)}) collective-permute-start(f32[2,1792]{1,0:T(2,128)S(1)} %pad_maximum_fusion), channel_id=1, source_target_pairs={{0,1},{1,0},{2,3},{3,2},{4,5},{5,4},{6,7},{7,6},{8,9},{9,8},{10,11... | collective-permute-start | bytes 43016 | tf_op jit(solution)/shard_map/ppermute | solution.py:609
  75.7 0.3 collective-permute-done.19.b1
  76.1 1.8 %shard_map.122 = f32[2,768]{1,0:T(2,128)S(1)} custom-call(bf16[6,288,256]{2,1,0:T(8,128)(2,1)S(1)} %shard_map.114.g0_ref, bf16[6,288,256]{2,1,0:T(8,128)(2,1)S(1)} %shard_map.118.g1_ref, bf16[1024,576]{1,0:T(8,128)(2,1)S(1)} %get-tuple-element.106.normed_t, bf16[3,1024,256]{2,1,0:T(8,128)(2,1)S(1)} %bitcast.14, f32[3,8,256]{2,1,0:T(8,128)S(1)} %get-tuple-element.112.b_ref), custom_call_target="tpu_custom_call" | custom-call | flops 8000000000 | bytes 10000000 | tf_op jit(solution)/shard_map/pallas_call | solution.py:429
  77.9 0.5 collective-permute-start.22
  78.4 3.2 %collective-permute-done.22 = f32[2,1792]{1,0:T(2,128)S(1)} collective-permute-done((f32[2,1792]{1,0:T(2,128)S(1)}, f32[2,1792]{1,0:T(2,128)S(1)}, u32[]{:S(2)}, u32[]{:S(2)}) %collective-permute-start.22) | collective-permute-done | bytes 14368 | tf_op jit(solution)/shard_map/ppermute | solution.py:615
  81.7 6.0 %collective-permute-start.25 = (f32[2,1792]{1,0:T(2,128)S(1)}, f32[2,1792]{1,0:T(2,128)S(1)}, u32[]{:S(2)}, u32[]{:S(2)}) collective-permute-start(f32[2,1792]{1,0:T(2,128)S(1)} %add_add_fusion.1), channel_id=1, source_target_pairs={{0,16},{1,17},{2,18},{3,19},{4,20},{5,21},{6,22},{7,23},{8,24},{9,... | collective-permute-start | bytes 43016 | tf_op jit(solution)/shard_map/ppermute | solution.py:615
  87.7 0.6 collective-permute-start.24
  88.3 2.0 %shard_map.116 = bf16[42,12,2,256]{3,2,1,0:T(2,128)(2,1)} custom-call(s32[3]{0:T(128)S(1)} %pad_add_fusion.s_ref, bf16[288,256]{1,0:T(8,128)(2,1)S(1)} %get-tuple-element.99.a0, bf16[288,256]{1,0:T(8,128)(2,1)S(1)} %collective-permute-done.17.a1, bf16[288,256]{1,0:T(8,128)(2,1)S(1)} %collective-permute-done.18.b0, ...), custom_call_target="tpu_custom_call" | custom-call | flops 1 | bytes 1 | tf_op jit(solution)/shard_map/pallas_call | solution.py:592
  90.3 2.9 %collective-permute-done.26 = f32[2,1792]{1,0:T(2,128)S(1)} collective-permute-done((f32[2,1792]{1,0:T(2,128)S(1)}, f32[2,1792]{1,0:T(2,128)S(1)}, u32[]{:S(2)}, u32[]{:S(2)}) %collective-permute-start.26) | collective-permute-done | bytes 14368 | tf_op jit(solution)/shard_map/ppermute | solution.py:615
  93.2 0.6 slice.13
  93.8 0.6 slice.14
  (50 shorter events, 0.2 us)
Async XLA Ops:
  0.6 1.0 %copy-start = (bf16[42,2,12,256]{3,1,2,0:T(2,128)(2,1)S(1)}, bf16[42,2,12,256]{3,1,2,0:T(2,128)(2,1)}, u32[]{:S(2)}) copy-start(bf16[42,2,12,256]{3,1,2,0:T(2,128)(2,1)} %param.8) | copy-start | bytes 1548292
  1.7 12.9 %copy-start.5 = (bf16[42,2,12,256]{3,1,2,0:T(2,128)(2,1)S(1)}, bf16[42,2,12,256]{3,1,2,0:T(2,128)(2,1)}, u32[]{:S(2)}) copy-start(bf16[42,2,12,256]{3,1,2,0:T(2,128)(2,1)} %param.9) | copy-start | bytes 1548292
  1.7 20.4 %copy-start.11 = (f32[2,3,256]{2,0,1:T(2,128)S(1)}, f32[2,3,256]{2,0,1:T(2,128)}, u32[]{:S(2)}) copy-start(f32[2,3,256]{2,0,1:T(2,128)} %param.12) | copy-start | bytes 18436
  2.5 21.3 %collective-permute-start.5 = (bf16[3,1024,256]{2,1,0:T(8,128)(2,1)}, bf16[3,1024,256]{2,1,0:T(8,128)(2,1)S(1)}, u32[]{:S(2)}, u32[]{:S(2)}) collective-permute-start(bf16[3,1024,256]{2,1,0:T(8,128)(2,1)} %bitcast.12), channel_id=1, source_target_pairs={{0,1},{1,0},{2,3},{3,2},{4,5},{5,4},{6,7},{7,6},{8,9},{9,8},{10,11... | collective-permute-start | bytes 4718600 | tf_op jit(solution)/shard_map/ppermute | solution.py:609
  3.1 13.8 %collective-permute-start.2 = (bf16[256,1024]{1,0:T(8,128)(2,1)}, bf16[256,1024]{1,0:T(8,128)(2,1)}, u32[]{:S(2)}, u32[]{:S(2)}) collective-permute-start(bf16[256,1024]{1,0:T(8,128)(2,1)} %po_ref), channel_id=1, source_target_pairs={{0,1},{1,0},{2,3},{3,2},{4,5},{5,4},{6,7},{7,6},{8,9},{9,8},{10,11... | collective-permute-start | bytes 1572872 | tf_op jit(solution)/shard_map/ppermute | solution.py:609
  3.1 13.1 %collective-permute-start = (bf16[42,6,2,256]{3,2,1,0:T(2,128)(2,1)}, bf16[42,6,2,256]{3,2,1,0:T(2,128)(2,1)S(1)}, u32[]{:S(2)}, u32[]{:S(2)}) collective-permute-start(bf16[42,6,2,256]{3,2,1,0:T(2,128)(2,1)} %get-tuple-element.60), channel_id=1, source_target_pairs={{0,2},{1,3},{2,0},{3,1},{4,6},{5,7},{6,4},{7,5},{8,10},{9,11},{10,... | collective-permute-start | bytes 774152 | tf_op jit(solution)/shard_map/ppermute | solution.py:609
  6.1 10.8 %collective-permute-start.1 = (bf16[42,6,2,256]{3,2,1,0:T(2,128)(2,1)}, bf16[42,6,2,256]{3,2,1,0:T(2,128)(2,1)}, u32[]{:S(2)}, u32[]{:S(2)}) collective-permute-start(bf16[42,6,2,256]{3,2,1,0:T(2,128)(2,1)} %get-tuple-element.61), channel_id=1, source_target_pairs={{0,28},{1,29},{2,30},{3,31},{4,0},{5,1},{6,2},{7,3},{8,4},{9,5},{1... | collective-permute-start | bytes 774152 | tf_op jit(solution)/shard_map/ppermute | solution.py:609
  10.6 1.4 %copy-start.2 = (bf16[1024,3,256]{2,0,1:T(8,128)(2,1)S(1)}, bf16[1024,3,256]{2,0,1:T(8,128)(2,1)}, u32[]{:S(2)}) copy-start(bf16[1024,3,256]{2,0,1:T(8,128)(2,1)} %param.10) | copy-start | bytes 4718596
  12.0 0.7 copy-start.10
  12.7 2.8 %copy-start.4 = (bf16[256,1024]{1,0:T(8,128)(2,1)S(1)}, bf16[256,1024]{1,0:T(8,128)(2,1)}, u32[]{:S(2)}) copy-start(bf16[256,1024]{1,0:T(8,128)(2,1)} %po_ref) | copy-start | bytes 1572868
  12.7 10.1 %copy-start.8 = (s32[42,2,96]{2,1,0:T(2,128)S(1)}, s32[42,2,96]{2,1,0:T(2,128)}, u32[]{:S(2)}) copy-start(s32[42,2,96]{2,1,0:T(2,128)} %ids_ref.1) | copy-start | bytes 96772
  13.4 1.2 %copy-start.12 = (bf16[3,1024,256]{2,1,0:T(8,128)(2,1)}, bf16[3,1024,256]{2,1,0:T(8,128)(2,1)S(1)}, u32[]{:S(2)}) copy-start(bf16[3,1024,256]{2,1,0:T(8,128)(2,1)S(1)} %get-tuple-element.80.refs_3_) | copy-start | bytes 4718596
  14.6 12.1 %copy-start.1 = (bf16[42,2,12,256]{3,1,2,0:T(2,128)(2,1)S(1)}, bf16[42,2,12,256]{3,1,2,0:T(2,128)(2,1)}, u32[]{:S(2)}) copy-start(bf16[42,2,12,256]{3,1,2,0:T(2,128)(2,1)} %param.8) | copy-start | bytes 1548292
  16.2 0.7 copy-start.6
  16.9 8.0 %collective-permute-start.3 = (bf16[42,6,2,256]{3,2,1,0:T(2,128)(2,1)}, bf16[42,6,2,256]{3,2,1,0:T(2,128)(2,1)}, u32[]{:S(2)}, u32[]{:S(2)}) collective-permute-start(bf16[42,6,2,256]{3,2,1,0:T(2,128)(2,1)} %collective-permute-done.1.refs_1_), channel_id=1, source_target_pairs={{0,2},{1,3},{2,0},{3,1},{4,6},{5,7},{6,4},{7,5},{8,10},{9,11},{10,... | collective-permute-start | bytes 774152 | tf_op jit(solution)/shard_map/ppermute | solution.py:609
  17.4 9.2 %collective-permute-start.4 = (bf16[42,6,2,256]{3,2,1,0:T(2,128)(2,1)}, bf16[42,6,2,256]{3,2,1,0:T(2,128)(2,1)S(1)}, u32[]{:S(2)}, u32[]{:S(2)}) collective-permute-start(bf16[42,6,2,256]{3,2,1,0:T(2,128)(2,1)} %slice.12), channel_id=1, source_target_pairs={{0,28},{1,29},{2,30},{3,31},{4,0},{5,1},{6,2},{7,3},{8,4},{9,5},{1... | collective-permute-start | bytes 774152 | tf_op jit(solution)/shard_map/ppermute | solution.py:609
  22.1 1.8 %collective-permute-start.6 = (f32[3,2,256]{2,1,0:T(2,128)S(1)}, f32[3,2,256]{2,1,0:T(2,128)S(1)}, u32[]{:S(2)}, u32[]{:S(2)}) collective-permute-start(f32[3,2,256]{2,1,0:T(2,128)S(1)} %bitcast.18), channel_id=1, source_target_pairs={{0,1},{1,0},{2,3},{3,2},{4,5},{5,4},{6,7},{7,6},{8,9},{9,8},{10,11... | collective-permute-start | bytes 18440 | tf_op jit(solution)/shard_map/ppermute | solution.py:609
  22.7 3.9 %copy-start.7 = (bf16[42,6,2,256]{3,2,1,0:T(2,128)(2,1)S(1)}, bf16[42,6,2,256]{3,2,1,0:T(2,128)(2,1)}, u32[]{:S(2)}) copy-start(bf16[42,6,2,256]{3,2,1,0:T(2,128)(2,1)} %copy-done.6) | copy-start | bytes 774148
  22.7 5.8 %copy-start.14 = (bf16[128,1024]{1,0:T(8,128)(2,1)S(1)}, bf16[128,1024]{1,0:T(8,128)(2,1)}, u32[]{:S(2)}) copy-start(bf16[128,1024]{1,0:T(8,128)(2,1)} %constant_dynamic-slice_fusion) | copy-start | bytes 786436
  23.9 9.5 %copy-start.13 = (bf16[3,1024,256]{2,1,0:T(8,128)(2,1)S(1)}, bf16[3,1024,256]{2,1,0:T(8,128)(2,1)}, u32[]{:S(2)}) copy-start(bf16[3,1024,256]{2,1,0:T(8,128)(2,1)} %copy-done.12) | copy-start | bytes 4718596
  28.5 4.9 %collective-permute-start.7 = (bf16[2,576,256]{2,1,0:T(8,128)(2,1)S(1)}, bf16[2,576,256]{2,1,0:T(8,128)(2,1)S(1)}, u32[]{:S(2)}, u32[]{:S(2)}) collective-permute-start(bf16[2,576,256]{2,1,0:T(8,128)(2,1)S(1)} %get-tuple-element.75), channel_id=1, source_target_pairs={{0,1},{1,0},{2,3},{3,2},{4,5},{5,4},{6,7},{7,6},{8,9},{9,8},{10,11... | collective-permute-start | bytes 1769480 | tf_op jit(solution)/shard_map/ppermute | solution.py:609
  28.6 13.4 %collective-permute-start.11 = (bf16[128,1024]{1,0:T(8,128)(2,1)S(1)}, bf16[128,1024]{1,0:T(8,128)(2,1)S(1)}, u32[]{:S(2)}, u32[]{:S(2)}) collective-permute-start(bf16[128,1024]{1,0:T(8,128)(2,1)S(1)} %copy-done.14), channel_id=1, source_target_pairs={{0,2},{1,3},{2,0},{3,1},{4,6},{5,7},{6,4},{7,5},{8,10},{9,11},{10,... | collective-permute-start | bytes 786440 | tf_op jit(solution)/shard_map/ppermute | solution.py:609
  31.1 11.5 %collective-permute-start.8 = (bf16[576,256]{1,0:T(8,128)(2,1)S(1)}, bf16[576,256]{1,0:T(8,128)(2,1)S(1)}, u32[]{:S(2)}, u32[]{:S(2)}) collective-permute-start(bf16[576,256]{1,0:T(8,128)(2,1)S(1)} %bitcast.19), channel_id=1, source_target_pairs={{0,1},{1,0},{2,3},{3,2},{4,5},{5,4},{6,7},{7,6},{8,9},{9,8},{10,11... | collective-permute-start | bytes 884744 | tf_op jit(solution)/shard_map/ppermute | solution.py:609
  31.4 19.0 %collective-permute-start.10 = (bf16[576,256]{1,0:T(8,128)(2,1)S(1)}, bf16[576,256]{1,0:T(8,128)(2,1)S(1)}, u32[]{:S(2)}, u32[]{:S(2)}) collective-permute-start(bf16[576,256]{1,0:T(8,128)(2,1)S(1)} %bitcast.20), channel_id=1, source_target_pairs={{0,3},{1,2},{2,1},{3,0},{4,7},{5,6},{6,5},{7,4},{8,11},{9,10},{10,... | collective-permute-start | bytes 884744 | tf_op jit(solution)/shard_map/ppermute | solution.py:609
  31.8 18.6 %collective-permute-start.9 = (bf16[576,256]{1,0:T(8,128)(2,1)S(1)}, bf16[576,256]{1,0:T(8,128)(2,1)S(1)}, u32[]{:S(2)}, u32[]{:S(2)}) collective-permute-start(bf16[576,256]{1,0:T(8,128)(2,1)S(1)} %get-tuple-element.78.refs_3_), channel_id=1, source_target_pairs={{0,2},{1,3},{2,0},{3,1},{4,6},{5,7},{6,4},{7,5},{8,10},{9,11},{10,... | collective-permute-start | bytes 884744 | tf_op jit(solution)/shard_map/ppermute | solution.py:609
  42.0 8.4 %collective-permute-start.12 = (bf16[128,1024]{1,0:T(8,128)(2,1)S(1)}, bf16[128,1024]{1,0:T(8,128)(2,1)S(1)}, u32[]{:S(2)}, u32[]{:S(2)}) collective-permute-start(bf16[128,1024]{1,0:T(8,128)(2,1)S(1)} %collective-permute-done.11.a2), channel_id=1, source_target_pairs={{0,4},{1,5},{2,6},{3,7},{4,0},{5,1},{6,2},{7,3},{8,12},{9,13},{10,... | collective-permute-start | bytes 786440 | tf_op jit(solution)/shard_map/ppermute | solution.py:615
  42.1 17.1 %collective-permute-start.14 = (bf16[288,512]{1,0:T(8,128)(2,1)S(1)}, bf16[288,512]{1,0:T(8,128)(2,1)S(1)}, u32[]{:S(2)}, u32[]{:S(2)}) collective-permute-start(bf16[288,512]{1,0:T(8,128)(2,1)S(1)} %get-tuple-element.88.refs_7_.a_ref), channel_id=1, source_target_pairs={{0,2},{1,3},{2,0},{3,1},{4,6},{5,7},{6,4},{7,5},{8,10},{9,11},{10,... | collective-permute-start | bytes 884744 | tf_op jit(solution)/shard_map/ppermute | solution.py:609
  53.1 10.3 %collective-permute-start.13 = (bf16[288,512]{1,0:T(8,128)(2,1)S(1)}, bf16[288,512]{1,0:T(8,128)(2,1)S(1)}, u32[]{:S(2)}, u32[]{:S(2)}) collective-permute-start(bf16[288,512]{1,0:T(8,128)(2,1)S(1)} %shard_map.111.refs_7_.b_ref), channel_id=1, source_target_pairs={{0,2},{1,3},{2,0},{3,1},{4,6},{5,7},{6,4},{7,5},{8,10},{9,11},{10,... | collective-permute-start | bytes 884744 | tf_op jit(solution)/shard_map/ppermute | solution.py:609
  54.7 2.4 %collective-permute-start.15 = (bf16[128,1024]{1,0:T(8,128)(2,1)S(1)}, bf16[128,1024]{1,0:T(8,128)(2,1)S(1)}, u32[]{:S(2)}, u32[]{:S(2)}) collective-permute-start(bf16[128,1024]{1,0:T(8,128)(2,1)S(1)} %collective-permute-done.11.a2), channel_id=1, source_target_pairs={{0,1},{1,0},{2,3},{3,2},{4,5},{5,4},{6,7},{7,6},{8,9},{9,8},{10,11... | collective-permute-start | bytes 786440 | tf_op jit(solution)/shard_map/ppermute | solution.py:609
  54.7 2.4 %collective-permute-start.16 = (bf16[128,1024]{1,0:T(8,128)(2,1)S(1)}, bf16[128,1024]{1,0:T(8,128)(2,1)S(1)}, u32[]{:S(2)}, u32[]{:S(2)}) collective-permute-start(bf16[128,1024]{1,0:T(8,128)(2,1)S(1)} %collective-permute-done.12.b2), channel_id=1, source_target_pairs={{0,1},{1,0},{2,3},{3,2},{4,5},{5,4},{6,7},{7,6},{8,9},{9,8},{10,11... | collective-permute-start | bytes 786440 | tf_op jit(solution)/shard_map/ppermute | solution.py:609
  56.2 0.9 copy-start.9
  64.3 11.4 %collective-permute-start.17 = (bf16[288,256]{1,0:T(8,128)(2,1)S(1)}, bf16[288,256]{1,0:T(8,128)(2,1)S(1)}, u32[]{:S(2)}, u32[]{:S(2)}) collective-permute-start(bf16[288,256]{1,0:T(8,128)(2,1)S(1)} %get-tuple-element.100), channel_id=1, source_target_pairs={{0,4},{1,5},{2,6},{3,7},{4,8},{5,9},{6,10},{7,11},{8,12},{9,13},{1... | collective-permute-start | bytes 442376 | tf_op jit(solution)/shard_map/ppermute | solution.py:609
  64.4 11.3 %collective-permute-start.18 = (bf16[288,256]{1,0:T(8,128)(2,1)S(1)}, bf16[288,256]{1,0:T(8,128)(2,1)S(1)}, u32[]{:S(2)}, u32[]{:S(2)}) collective-permute-start(bf16[288,256]{1,0:T(8,128)(2,1)S(1)} %get-tuple-element.101), channel_id=1, source_target_pairs={{0,1},{1,0},{2,3},{3,2},{4,5},{5,4},{6,7},{7,6},{8,9},{9,8},{10,11... | collective-permute-start | bytes 442376 | tf_op jit(solution)/shard_map/ppermute | solution.py:609
  64.5 11.6 %collective-permute-start.19 = (bf16[288,256]{1,0:T(8,128)(2,1)S(1)}, bf16[288,256]{1,0:T(8,128)(2,1)S(1)}, u32[]{:S(2)}, u32[]{:S(2)}) collective-permute-start(bf16[288,256]{1,0:T(8,128)(2,1)S(1)} %get-tuple-element.102), channel_id=1, source_target_pairs={{0,5},{1,4},{2,7},{3,6},{4,9},{5,8},{6,11},{7,10},{8,13},{9,12},{1... | collective-permute-start | bytes 442376 | tf_op jit(solution)/shard_map/ppermute | solution.py:609
  70.6 3.7 %collective-permute-start.20 = (f32[2,1024]{1,0:T(2,128)S(1)}, f32[2,1024]{1,0:T(2,128)S(1)}, u32[]{:S(2)}, u32[]{:S(2)}) collective-permute-start(f32[2,1024]{1,0:T(2,128)S(1)} %shard_map.121), channel_id=1, source_target_pairs={{0,2},{1,3},{2,0},{3,1},{4,6},{5,7},{6,4},{7,5},{8,10},{9,11},{10,... | collective-permute-start | bytes 24584 | tf_op jit(solution)/shard_map/ppermute | solution.py:609
  71.3 4.7 %copy-start.3 = (bf16[1024,3,256]{2,0,1:T(8,128)(2,1)S(1)}, bf16[1024,3,256]{2,0,1:T(8,128)(2,1)}, u32[]{:S(2)}) copy-start(bf16[1024,3,256]{2,0,1:T(8,128)(2,1)} %param.10) | copy-start | bytes 4718596
  74.3 4.1 %collective-permute-start.23 = (f32[2,1792]{1,0:T(2,128)S(1)}, f32[2,1792]{1,0:T(2,128)S(1)}, u32[]{:S(2)}, u32[]{:S(2)}) collective-permute-start(f32[2,1792]{1,0:T(2,128)S(1)} %pad_maximum_fusion), channel_id=1, source_target_pairs={{0,5},{1,4},{2,7},{3,6},{4,1},{5,0},{6,3},{7,2},{8,13},{9,12},{10,... | collective-permute-start | bytes 43016 | tf_op jit(solution)/shard_map/ppermute | solution.py:615
  74.4 4.1 %collective-permute-start.21 = (f32[2,1792]{1,0:T(2,128)S(1)}, f32[2,1792]{1,0:T(2,128)S(1)}, u32[]{:S(2)}, u32[]{:S(2)}) collective-permute-start(f32[2,1792]{1,0:T(2,128)S(1)} %pad_maximum_fusion), channel_id=1, source_target_pairs={{0,1},{1,0},{2,3},{3,2},{4,5},{5,4},{6,7},{7,6},{8,9},{9,8},{10,11... | collective-permute-start | bytes 43016 | tf_op jit(solution)/shard_map/ppermute | solution.py:609
  77.9 3.8 %collective-permute-start.22 = (f32[2,1792]{1,0:T(2,128)S(1)}, f32[2,1792]{1,0:T(2,128)S(1)}, u32[]{:S(2)}, u32[]{:S(2)}) collective-permute-start(f32[2,1792]{1,0:T(2,128)S(1)} %pad_maximum_fusion.1), channel_id=1, source_target_pairs={{0,4},{1,5},{2,6},{3,7},{4,0},{5,1},{6,2},{7,3},{8,12},{9,13},{10,... | collective-permute-start | bytes 43016 | tf_op jit(solution)/shard_map/ppermute | solution.py:615
  81.7 8.6 %collective-permute-start.25 = (f32[2,1792]{1,0:T(2,128)S(1)}, f32[2,1792]{1,0:T(2,128)S(1)}, u32[]{:S(2)}, u32[]{:S(2)}) collective-permute-start(f32[2,1792]{1,0:T(2,128)S(1)} %add_add_fusion.1), channel_id=1, source_target_pairs={{0,16},{1,17},{2,18},{3,19},{4,20},{5,21},{6,22},{7,23},{8,24},{9,... | collective-permute-start | bytes 43016 | tf_op jit(solution)/shard_map/ppermute | solution.py:615
  87.7 5.5 %collective-permute-start.26 = (f32[2,1792]{1,0:T(2,128)S(1)}, f32[2,1792]{1,0:T(2,128)S(1)}, u32[]{:S(2)}, u32[]{:S(2)}) collective-permute-start(f32[2,1792]{1,0:T(2,128)S(1)} %add_add_fusion.1), channel_id=1, source_target_pairs={{0,24},{1,25},{2,26},{3,27},{4,28},{5,29},{6,30},{7,31},{8,16},{9,... | collective-permute-start | bytes 43016 | tf_op jit(solution)/shard_map/ppermute | solution.py:615
  87.7 5.5 %collective-permute-start.24 = (f32[2,1792]{1,0:T(2,128)S(1)}, f32[2,1792]{1,0:T(2,128)S(1)}, u32[]{:S(2)}, u32[]{:S(2)}) collective-permute-start(f32[2,1792]{1,0:T(2,128)S(1)} %add_add_fusion.1), channel_id=1, source_target_pairs={{0,8},{1,9},{2,10},{3,11},{4,12},{5,13},{6,14},{7,15},{8,0},{9,1},... | collective-permute-start | bytes 43016 | tf_op jit(solution)/shard_map/ppermute | solution.py:615

commit v12 on v8

--- a/solution.py
+++ b/solution.py
@@ -655,10 +655,10 @@
     w3_peer = send(w3, 0, 1)
     c3_peer = send(c3, 0, 1)
     share = w_proj.shape[0] // 2
-    slab = after(w_proj, c3_peer)
-    slab = send(lax.dynamic_slice_in_dim(slab, share * (sector % 2), share, 0), 0, 2)
     w1 = send(w_proj, 0, 1)
     wc_own, b_own = clip_qkv(w3, c3)
+    slab = after(w_proj, wc_own)
+    slab = send(lax.dynamic_slice_in_dim(slab, share * (sector % 2), share, 0), 0, 2)
     wc_peer, b_peer = clip_qkv(w3_peer, c3_peer)
     idk, idq = window_ids(place, region_ids, WLAT * lev * lon)
     f_low, f_up_y, w1, t_low, wc_own = lax.optimization_barrier(

time: 89.9 us -> 89.9 us (level)
  Pallas kernels: 36.8 us -> 38.4 us
  waiting for transfers between devices: 16.3 us -> 15.1 us
  local copies, waits for them, and re-layouts: 8.23 us -> 7.14 us
    ppermute x6, starting transfers between devices: 5.82 us -> 6.93 us  [swap(): return lax.ppermute(block, ('lat', 'tp'), route)]
    pallas_call x1, Pallas kernels: 1.57 us -> 2.61 us  [proj_sums(): pl.pallas_call(proj_sums_kernel, out_shape=jax.ShapeDtypeStruct((2, errs[...]
    dynamic_slice x1, local copies, waits for them, and re-layouts: 1.67 us -> 0.72 us  [local(): lax.dynamic_slice_in_dim(slab, share * (sector % 2), share, 0)]
    unnamed x22 -> x24, local copies, waits for them, and re-layouts: 4.48 us -> 4.34 us
  transfers between devices with their start and end apart: 27 -> 27, of which waited for: 7 -> 10; matrix products, arithmetic and copies ran while one was open for 3% -> 2% of each run, Pallas kernels for 37% -> 39%
where the time goes in v12:
time: 89.9 us; the launch traced here: 89.5 us
  Pallas kernels  38.4 us (43%)
  starting transfers between devices  27.2 us (30%)
  waiting for transfers between devices  15.1 us (17%)
  local copies, waits for them, and re-layouts  7.14 us (8%)
  between operations  1.58 us (2%)
    ppermute x21, starting transfers between devices, send(): return lax.ppermute(block, ('lat', 'tp'), route)  20.2 us
    ppermute x21, waiting for transfers between devices, send(): return lax.ppermute(block, ('lat', 'tp'), route)  9.29 us
    pallas_call x1, Pallas kernels, forward(): pl.pallas_call(forward_kernel, out_shape=(jax.ShapeDtypeStruct((n, d), BF...  7.62 us
    ppermute x6, starting transfers between devices, swap(): return lax.ppermute(block, ('lat', 'tp'), route)  6.93 us
    pallas_call x2, Pallas kernels, backward(): pl.pallas_call(functools.partial(backward_kernel, group), out_shape=jax.S...  6.42 us
    ppermute x6, waiting for transfers between devices, swap(): return lax.ppermute(block, ('lat', 'tp'), route)  5.82 us
    unnamed x24, local copies, waits for them, and re-layouts  4.34 us
    pallas_call x2, Pallas kernels, qkv_sums(): pl.pallas_call(functools.partial(qkv_sums_kernel, side), out_shape=jax.Sh...  3.61 us
  transfers between devices with their start and end apart: 27, of which 10 were waited for; matrix products, arithmetic and copies ran while one was open for 2% of the time, Pallas kernels for 39%

profile of v12, /device:TPU:0, one launch (start us, length us, event | category | flops | bytes accessed | tf_op | source)
XLA Modules:
  0.0 89.5 jit_solution(5378827017661624948)
XLA Ops:
  0.6 0.0 copy-start
  0.6 1.0 %copy-done = bf16[42,2,12,256]{3,1,2,0:T(2,128)(2,1)S(1)} copy-done((bf16[42,2,12,256]{3,1,2,0:T(2,128)(2,1)S(1)}, bf16[42,2,12,256]{3,1,2,0:T(2,128)(2,1)}, u32[]{:S(2)}) %copy-start) | copy-done | bytes 516120
  1.7 0.9 shard_map.103
  2.6 0.5 collective-permute-start.6
  3.1 0.1 collective-permute-start.2
  3.2 6.0 %collective-permute-start = (bf16[42,6,2,256]{3,2,1,0:T(2,128)(2,1)}, bf16[42,6,2,256]{3,2,1,0:T(2,128)(2,1)}, u32[]{:S(2)}, u32[]{:S(2)}) collective-permute-start(bf16[42,6,2,256]{3,2,1,0:T(2,128)(2,1)} %get-tuple-element.59), channel_id=1, source_target_pairs={{0,28},{1,29},{2,30},{3,31},{4,0},{5,1},{6,2},{7,3},{8,4},{9,5},{1... | collective-permute-start | bytes 774152 | tf_op jit(solution)/shard_map/ppermute | solution.py:609
  9.1 1.5 %collective-permute-start.1 = (bf16[42,6,2,256]{3,2,1,0:T(2,128)(2,1)}, bf16[42,6,2,256]{3,2,1,0:T(2,128)(2,1)}, u32[]{:S(2)}, u32[]{:S(2)}) collective-permute-start(bf16[42,6,2,256]{3,2,1,0:T(2,128)(2,1)} %get-tuple-element.60), channel_id=1, source_target_pairs={{0,2},{1,3},{2,0},{3,1},{4,6},{5,7},{6,4},{7,5},{8,10},{9,11},{10,... | collective-permute-start | bytes 774152 | tf_op jit(solution)/shard_map/ppermute | solution.py:609
  10.6 1.4 %copy-done.2 = bf16[1024,3,256]{2,0,1:T(8,128)(2,1)S(1)} copy-done((bf16[1024,3,256]{2,0,1:T(8,128)(2,1)S(1)}, bf16[1024,3,256]{2,0,1:T(8,128)(2,1)}, u32[]{:S(2)}) %copy-start.2) | copy-done | bytes 1572888
  12.0 0.7 copy-done.8
  12.7 0.7 shard_map.104
  13.4 1.2 %copy-done.10 = bf16[3,1024,256]{2,1,0:T(8,128)(2,1)} copy-done((bf16[3,1024,256]{2,1,0:T(8,128)(2,1)}, bf16[3,1024,256]{2,1,0:T(8,128)(2,1)S(1)}, u32[]{:S(2)}) %copy-start.10) | copy-done | bytes 1572888
  14.6 0.7 constant_dynamic-slice_fusion
  15.3 0.5 collective-permute-start.5
  15.8 0.9 slice.12
  16.7 0.6 collective-permute-done.1.refs_2_
  17.3 3.0 %collective-permute-start.4 = (bf16[42,6,2,256]{3,2,1,0:T(2,128)(2,1)}, bf16[42,6,2,256]{3,2,1,0:T(2,128)(2,1)}, u32[]{:S(2)}, u32[]{:S(2)}) collective-permute-start(bf16[42,6,2,256]{3,2,1,0:T(2,128)(2,1)} %slice.12), channel_id=1, source_target_pairs={{0,28},{1,29},{2,30},{3,31},{4,0},{5,1},{6,2},{7,3},{8,4},{9,5},{1... | collective-permute-start | bytes 774152 | tf_op jit(solution)/shard_map/ppermute | solution.py:609
  20.3 1.5 %collective-permute-start.3 = (bf16[42,6,2,256]{3,2,1,0:T(2,128)(2,1)}, bf16[42,6,2,256]{3,2,1,0:T(2,128)(2,1)}, u32[]{:S(2)}, u32[]{:S(2)}) collective-permute-start(bf16[42,6,2,256]{3,2,1,0:T(2,128)(2,1)} %collective-permute-done.refs_1_), channel_id=1, source_target_pairs={{0,2},{1,3},{2,0},{3,1},{4,6},{5,7},{6,4},{7,5},{8,10},{9,11},{10,... | collective-permute-start | bytes 774152 | tf_op jit(solution)/shard_map/ppermute | solution.py:609
  22.5 0.1 pad_add_fusion.s_ref
  22.6 1.0 %shard_map.107 = (s32[576,1]{1,0:T(8,128)S(1)}, s32[4,1,288]{2,1,0:T(1,128)S(1)}) custom-call(s32[3]{0:T(128)S(1)} %pad_add_fusion.s_ref, s32[42,2,96]{2,1,0:T(2,128)S(1)} %copy-done.6), custom_call_target="tpu_custom_call" | custom-call | flops 1 | bytes 1 | tf_op jit(solution)/shard_map/pallas_call | solution.py:553
  23.6 1.9 %collective-permute-done.4.refs_1_ = bf16[42,6,2,256]{3,2,1,0:T(2,128)(2,1)} collective-permute-done((bf16[42,6,2,256]{3,2,1,0:T(2,128)(2,1)}, bf16[42,6,2,256]{3,2,1,0:T(2,128)(2,1)}, u32[]{:S(2)}, u32[]{:S(2)}) %collective-permute-start.4) | collective-permute-done | bytes 258080 | tf_op jit(solution)/shard_map/ppermute | solution.py:609
  25.5 1.4 %shard_map.105 = (bf16[576,256]{1,0:T(8,128)(2,1)S(1)}, bf16[1,576,256]{2,1,0:T(8,128)(2,1)S(1)}) custom-call(s32[3]{0:T(128)S(1)} %pad_add_fusion.s_ref, bf16[42,12,2,256]{3,2,1,0:T(2,128)(2,1)S(1)} %bitcast.16, bf16[42,6,2,256]{3,2,1,0:T(2,128)(2,1)} %collective-permute-done.4.refs_1_), custom_call_target="tpu_custom_call" | custom-call | flops 1 | bytes 1 | tf_op jit(solution)/shard_map/pallas_call | solution.py:497
  26.9 0.7 shard_map.106
  27.7 1.3 %collective-permute-done.3.refs_3_ = bf16[42,6,2,256]{3,2,1,0:T(2,128)(2,1)} collective-permute-done((bf16[42,6,2,256]{3,2,1,0:T(2,128)(2,1)}, bf16[42,6,2,256]{3,2,1,0:T(2,128)(2,1)}, u32[]{:S(2)}, u32[]{:S(2)}) %collective-permute-start.3) | collective-permute-done | bytes 258080 | tf_op jit(solution)/shard_map/ppermute | solution.py:609
  28.9 1.9 %shard_map.108 = (bf16[576,256]{1,0:T(8,128)(2,1)S(1)}, bf16[576,256]{1,0:T(8,128)(2,1)S(1)}, bf16[2,576,256]{2,1,0:T(8,128)(2,1)S(1)}) custom-call(s32[3]{0:T(128)S(1)} %pad_add_fusion.s_ref, bf16[42,12,2,256]{3,2,1,0:T(2,128)(2,1)S(1)} %bitcast.11, bf16[42,6,2,256]{3,2,1,0:T(2,128)(2,1)} %collective-permute-done.refs_1_, ...), custom_call_target="tpu_custom_call" | custom-call | flops 1 | bytes 1 | tf_op jit(solution)/shard_map/pallas_call | solution.py:497
  30.9 0.1 collective-permute-start.8
  30.9 0.5 collective-permute-start.9
  31.4 1.1 %collective-permute-start.10 = (bf16[576,256]{1,0:T(8,128)(2,1)S(1)}, bf16[576,256]{1,0:T(8,128)(2,1)S(1)}, u32[]{:S(2)}, u32[]{:S(2)}) collective-permute-start(bf16[576,256]{1,0:T(8,128)(2,1)S(1)} %get-tuple-element.77.refs_3_), channel_id=1, source_target_pairs={{0,2},{1,3},{2,0},{3,1},{4,6},{5,7},{6,4},{7,5},{8,10},{9,11},{10,... | collective-permute-start | bytes 884744 | tf_op jit(solution)/shard_map/ppermute | solution.py:609
  32.5 0.3 collective-permute-start.11
  32.9 0.1 collective-permute-done.8.refs_2_
  32.9 7.6 %shard_map.109 = (bf16[576,1024]{1,0:T(8,128)(2,1)S(1)}, bf16[6,576,256]{2,1,0:T(8,128)(2,1)S(1)}, bf16[288,512]{1,0:T(8,128)(2,1)S(1)}) custom-call(s32[1]{0:T(128)} %bitcast.2.t_ref, bf16[576,256]{1,0:T(8,128)(2,1)S(1)} %get-tuple-element.74.refs_0_, bf16[576,256]{1,0:T(8,128)(2,1)S(1)} %get-tuple-element.75.refs_1_, ...), custom_call_target="tpu_custom_call" | custom-call | flops 8000000000 | bytes 10000000 | tf_op jit(solution)/shard_map/pallas_call | solution.py:213
  40.6 1.0 %shard_map.110.p_ref = f32[8,144,288]{2,1,0:T(8,128)S(1)} custom-call(bf16[6,576,256]{2,1,0:T(8,128)(2,1)S(1)} %get-tuple-element.102.qkv_ref, s32[576,1]{1,0:T(8,128)S(1)} %get-tuple-element.81.refs_5_.idk_ref.refs_10_, s32[4,1,288]{2,1,0:T(1,128)S(1)} %get-tuple-element.82.refs_6_.idq_ref), custom_call_target="tpu_custom_call" | custom-call | flops 1 | bytes 1 | tf_op jit(solution)/shard_map/pallas_call | solution.py:326
  41.6 1.2 %collective-permute-start.14 = (bf16[288,512]{1,0:T(8,128)(2,1)S(1)}, bf16[288,512]{1,0:T(8,128)(2,1)S(1)}, u32[]{:S(2)}, u32[]{:S(2)}) collective-permute-start(bf16[288,512]{1,0:T(8,128)(2,1)S(1)} %get-tuple-element.86.refs_7_.a_ref), channel_id=1, source_target_pairs={{0,2},{1,3},{2,0},{3,1},{4,6},{5,7},{6,4},{7,5},{8,10},{9,11},{10,... | collective-permute-start | bytes 884744 | tf_op jit(solution)/shard_map/ppermute | solution.py:609
  42.8 3.5 %collective-permute-done.11.refs_6_ = bf16[576,256]{1,0:T(8,128)(2,1)S(1)} collective-permute-done((bf16[576,256]{1,0:T(8,128)(2,1)S(1)}, bf16[576,256]{1,0:T(8,128)(2,1)S(1)}, u32[]{:S(2)}, u32[]{:S(2)}) %collective-permute-start.11) | collective-permute-done | bytes 294944 | tf_op jit(solution)/shard_map/ppermute | solution.py:609
  46.2 2.7 %shard_map.111.refs_7_.b_ref = bf16[288,512]{1,0:T(8,128)(2,1)S(1)} custom-call(bf16[6,576,256]{2,1,0:T(8,128)(2,1)S(1)} %get-tuple-element.102.qkv_ref, s32[576,1]{1,0:T(8,128)S(1)} %get-tuple-element.81.refs_5_.idk_ref.refs_10_, s32[4,1,288]{2,1,0:T(1,128)S(1)} %get-tuple-element.82.refs_6_.idq_ref), custom_call_target="tpu_custom_call" | custom-call | flops 1 | bytes 1 | tf_op jit(solution)/shard_map/pallas_call | solution.py:200
  48.9 1.0 %collective-permute-start.13 = (bf16[288,512]{1,0:T(8,128)(2,1)S(1)}, bf16[288,512]{1,0:T(8,128)(2,1)S(1)}, u32[]{:S(2)}, u32[]{:S(2)}) collective-permute-start(bf16[288,512]{1,0:T(8,128)(2,1)S(1)} %shard_map.111.refs_7_.b_ref), channel_id=1, source_target_pairs={{0,2},{1,3},{2,0},{3,1},{4,6},{5,7},{6,4},{7,5},{8,10},{9,11},{10,... | collective-permute-start | bytes 884744 | tf_op jit(solution)/shard_map/ppermute | solution.py:609
  49.9 1.1 %collective-permute-start.15 = (bf16[128,1024]{1,0:T(8,128)(2,1)S(1)}, bf16[128,1024]{1,0:T(8,128)(2,1)S(1)}, u32[]{:S(2)}, u32[]{:S(2)}) collective-permute-start(bf16[128,1024]{1,0:T(8,128)(2,1)S(1)} %collective-permute-done.5.a2), channel_id=1, source_target_pairs={{0,1},{1,0},{2,3},{3,2},{4,5},{5,4},{6,7},{7,6},{8,9},{9,8},{10,11... | collective-permute-start | bytes 786440 | tf_op jit(solution)/shard_map/ppermute | solution.py:609
  51.0 1.0 %shard_map.117.p_ref = f32[8,144,288]{2,1,0:T(8,128)S(1)} custom-call(bf16[6,576,256]{2,1,0:T(8,128)(2,1)S(1)} %get-tuple-element.102.qkv_ref, s32[576,1]{1,0:T(8,128)S(1)} %get-tuple-element.81.refs_5_.idk_ref.refs_10_, s32[4,1,288]{2,1,0:T(1,128)S(1)} %get-tuple-element.82.refs_6_.idq_ref), custom_call_target="tpu_custom_call" | custom-call | flops 1 | bytes 1 | tf_op jit(solution)/shard_map/pallas_call | solution.py:326
  52.0 0.0 copy-start.7
  52.0 0.8 shard_map.119
  52.9 2.1 %shard_map.112 = (bf16[1024,1024]{1,0:T(8,128)(2,1)S(1)}, f32[8,1024]{1,0:T(8,128)S(1)}) custom-call(s32[3]{0:T(128)S(1)} %pad_add_fusion.s_ref, bf16[256,1024]{1,0:T(8,128)(2,1)S(1)} %copy-done.4, bf16[256,1024]{1,0:T(8,128)(2,1)} %collective-permute-done.2.w1.pp_ref, bf16[128,1024]{1,0:T(8,128)(2,1)S(1)} %collective-permute-done.5.a2, ...), custom_call_target="tpu_custom_call" | custom-call | flops 1 | bytes 1 | tf_op jit(solution)/shard_map/pallas_call | solution.py:92
  55.0 1.0 %shard_map.113 = (bf16[144,256]{1,0:T(8,128)(2,1)S(1)}, bf16[144,256]{1,0:T(8,128)(2,1)S(1)}, bf16[144,256]{1,0:T(8,128)(2,1)S(1)}, bf16[144,256]{1,0:T(8,128)(2,1)S(1)}, bf16[288,1024]{1,0:T(8,128)(2,1)S(1)}) custom-call(s32[1]{0:T(128)} %bitcast.2.t_ref, bf16[576,256]{1,0:T(8,128)(2,1)S(1)} %get-tuple-element.74.refs_0_, ...), custom_call_target="tpu_custom_call" | custom-call | flops 1 | bytes 1 | tf_op jit(solution)/shard_map/pallas_call | solution.py:296
  56.0 3.2 %shard_map.114.g0_ref = bf16[6,288,256]{2,1,0:T(8,128)(2,1)S(1)} custom-call(bf16[288,1024]{1,0:T(8,128)(2,1)S(1)} %get-tuple-element.91.err_ref.e0_ref, bf16[1024,1024]{1,0:T(8,128)(2,1)S(1)} %get-tuple-element.90.refs_9_.wc_ref, bf16[6,576,256]{2,1,0:T(8,128)(2,1)S(1)} %get-tuple-element.102.qkv_ref, f32[8,144,288]{2,1,0:T(8,128)S(1)} %shard_map.110.p_ref), custom_call_target="tpu_custom_call" | custom-call | flops 1 | bytes 1 | tf_op jit(solution)/shard_map/pallas_call | solution.py:402
  59.2 0.2 collective-permute-done.13.refs_8_
  59.4 1.0 %shard_map.115 = (bf16[288,256]{1,0:T(8,128)(2,1)S(1)}, bf16[288,256]{1,0:T(8,128)(2,1)S(1)}, bf16[288,256]{1,0:T(8,128)(2,1)S(1)}, bf16[288,256]{1,0:T(8,128)(2,1)S(1)}, bf16[288,1024]{1,0:T(8,128)(2,1)S(1)}) custom-call(s32[1]{0:T(128)} %bitcast.2.t_ref, bf16[576,256]{1,0:T(8,128)(2,1)S(1)} %get-tuple-element.74.refs_0_, ...), custom_call_target="tpu_custom_call" | custom-call | flops 1 | bytes 1 | tf_op jit(solution)/shard_map/pallas_call | solution.py:296
  60.4 0.1 collective-permute-start.17
  60.4 0.4 collective-permute-start.18
  60.8 0.0 collective-permute-start.19
  60.8 3.2 %shard_map.118.g1_ref = bf16[6,288,256]{2,1,0:T(8,128)(2,1)S(1)} custom-call(bf16[288,1024]{1,0:T(8,128)(2,1)S(1)} %get-tuple-element.101.err_ref.e1_ref, bf16[1024,1024]{1,0:T(8,128)(2,1)S(1)} %get-tuple-element.90.refs_9_.wc_ref, bf16[6,576,256]{2,1,0:T(8,128)(2,1)S(1)} %get-tuple-element.102.qkv_ref, f32[8,144,288]{2,1,0:T(8,128)S(1)} %shard_map.117.p_ref), custom_call_target="tpu_custom_call" | custom-call | flops 8000000000 | bytes 10000000 | tf_op jit(solution)/shard_map/pallas_call | solution.py:402
  64.1 2.6 %shard_map.121 = f32[2,1024]{1,0:T(2,128)S(1)} custom-call(bf16[288,1024]{1,0:T(8,128)(2,1)S(1)} %get-tuple-element.91.err_ref.e0_ref, bf16[288,1024]{1,0:T(8,128)(2,1)S(1)} %get-tuple-element.101.err_ref.e1_ref, bf16[512,576]{1,0:T(8,128)(2,1)S(1)} %get-tuple-element.106.attn_t, bf16[256,1024]{1,0:T(8,128)(2,1)S(1)} %copy-done.4, ...), custom_call_target="tpu_custom_call" | custom-call | flops 1000000000 | bytes 3000000 | tf_op jit(solution)/shard_map/pallas_call | solution.py:359
  66.7 1.1 %collective-permute-start.20 = (f32[2,1024]{1,0:T(2,128)S(1)}, f32[2,1024]{1,0:T(2,128)S(1)}, u32[]{:S(2)}, u32[]{:S(2)}) collective-permute-start(f32[2,1024]{1,0:T(2,128)S(1)} %shard_map.121), channel_id=1, source_target_pairs={{0,2},{1,3},{2,0},{3,1},{4,6},{5,7},{6,4},{7,5},{8,10},{9,11},{10,... | collective-permute-start | bytes 24584 | tf_op jit(solution)/shard_map/ppermute | solution.py:609
  67.7 1.8 %shard_map.120 = f32[2,768]{1,0:T(2,128)S(1)} custom-call(bf16[6,288,256]{2,1,0:T(8,128)(2,1)S(1)} %shard_map.114.g0_ref, bf16[6,288,256]{2,1,0:T(8,128)(2,1)S(1)} %shard_map.118.g1_ref, bf16[1024,576]{1,0:T(8,128)(2,1)S(1)} %get-tuple-element.104.normed_t, bf16[3,1024,256]{2,1,0:T(8,128)(2,1)S(1)} %collective-permute-done.6.w_ref, ...), custom_call_target="tpu_custom_call" | custom-call | flops 8000000000 | bytes 10000000 | tf_op jit(solution)/shard_map/pallas_call | solution.py:429
  69.5 0.8 collective-permute-done.20
  70.4 0.1 collective-permute-start.23
  70.5 0.4 collective-permute-start.21
  70.9 0.9 %collective-permute-done.19.b1 = bf16[288,256]{1,0:T(8,128)(2,1)S(1)} collective-permute-done((bf16[288,256]{1,0:T(8,128)(2,1)S(1)}, bf16[288,256]{1,0:T(8,128)(2,1)S(1)}, u32[]{:S(2)}, u32[]{:S(2)}) %collective-permute-start.19) | collective-permute-done | bytes 147488 | tf_op jit(solution)/shard_map/ppermute | solution.py:609
  71.8 1.8 %shard_map.122 = f32[2,768]{1,0:T(2,128)S(1)} custom-call(bf16[6,288,256]{2,1,0:T(8,128)(2,1)S(1)} %shard_map.114.g0_ref, bf16[6,288,256]{2,1,0:T(8,128)(2,1)S(1)} %shard_map.118.g1_ref, bf16[1024,576]{1,0:T(8,128)(2,1)S(1)} %get-tuple-element.104.normed_t, bf16[3,1024,256]{2,1,0:T(8,128)(2,1)S(1)} %bitcast.14, f32[3,8,256]{2,1,0:T(8,128)S(1)} %get-tuple-element.110.b_ref), custom_call_target="tpu_custom_call" | custom-call | flops 8000000000 | bytes 10000000 | tf_op jit(solution)/shard_map/pallas_call | solution.py:429
  73.6 0.9 %collective-permute-start.22 = (f32[2,1792]{1,0:T(2,128)S(1)}, f32[2,1792]{1,0:T(2,128)S(1)}, u32[]{:S(2)}, u32[]{:S(2)}) collective-permute-start(f32[2,1792]{1,0:T(2,128)S(1)} %pad_maximum_fusion.1), channel_id=1, source_target_pairs={{0,4},{1,5},{2,6},{3,7},{4,0},{5,1},{6,2},{7,3},{8,12},{9,13},{10,... | collective-permute-start | bytes 43016 | tf_op jit(solution)/shard_map/ppermute | solution.py:615
  74.5 2.9 %collective-permute-done.22 = f32[2,1792]{1,0:T(2,128)S(1)} collective-permute-done((f32[2,1792]{1,0:T(2,128)S(1)}, f32[2,1792]{1,0:T(2,128)S(1)}, u32[]{:S(2)}, u32[]{:S(2)}) %collective-permute-start.22) | collective-permute-done | bytes 14368 | tf_op jit(solution)/shard_map/ppermute | solution.py:615
  77.5 5.3 %collective-permute-start.25 = (f32[2,1792]{1,0:T(2,128)S(1)}, f32[2,1792]{1,0:T(2,128)S(1)}, u32[]{:S(2)}, u32[]{:S(2)}) collective-permute-start(f32[2,1792]{1,0:T(2,128)S(1)} %add_add_fusion.1), channel_id=1, source_target_pairs={{0,16},{1,17},{2,18},{3,19},{4,20},{5,21},{6,22},{7,23},{8,24},{9,... | collective-permute-start | bytes 43016 | tf_op jit(solution)/shard_map/ppermute | solution.py:615
  82.8 0.6 collective-permute-start.24
  83.4 2.0 %shard_map.116 = bf16[42,12,2,256]{3,2,1,0:T(2,128)(2,1)} custom-call(s32[3]{0:T(128)S(1)} %pad_add_fusion.s_ref, bf16[288,256]{1,0:T(8,128)(2,1)S(1)} %get-tuple-element.97.a0, bf16[288,256]{1,0:T(8,128)(2,1)S(1)} %collective-permute-done.17.a1, bf16[288,256]{1,0:T(8,128)(2,1)S(1)} %collective-permute-done.18.b0, ...), custom_call_target="tpu_custom_call" | custom-call | flops 1 | bytes 1 | tf_op jit(solution)/shard_map/pallas_call | solution.py:592
  85.4 2.9 %collective-permute-done.26 = f32[2,1792]{1,0:T(2,128)S(1)} collective-permute-done((f32[2,1792]{1,0:T(2,128)S(1)}, f32[2,1792]{1,0:T(2,128)S(1)}, u32[]{:S(2)}, u32[]{:S(2)}) %collective-permute-start.26) | collective-permute-done | bytes 14368 | tf_op jit(solution)/shard_map/ppermute | solution.py:615
  88.3 0.6 slice.13
  88.9 0.6 slice.14
  (44 shorter events, 0.1 us)
Async XLA Ops:
  0.6 1.0 %copy-start = (bf16[42,2,12,256]{3,1,2,0:T(2,128)(2,1)S(1)}, bf16[42,2,12,256]{3,1,2,0:T(2,128)(2,1)}, u32[]{:S(2)}) copy-start(bf16[42,2,12,256]{3,1,2,0:T(2,128)(2,1)} %param.8) | copy-start | bytes 1548292
  1.7 14.2 %copy-start.5 = (bf16[42,2,12,256]{3,1,2,0:T(2,128)(2,1)S(1)}, bf16[42,2,12,256]{3,1,2,0:T(2,128)(2,1)}, u32[]{:S(2)}) copy-start(bf16[42,2,12,256]{3,1,2,0:T(2,128)(2,1)} %param.9) | copy-start | bytes 1548292
  1.7 20.2 %copy-start.9 = (f32[2,3,256]{2,0,1:T(2,128)S(1)}, f32[2,3,256]{2,0,1:T(2,128)}, u32[]{:S(2)}) copy-start(f32[2,3,256]{2,0,1:T(2,128)} %param.12) | copy-start | bytes 18436
  2.6 24.4 %collective-permute-start.6 = (bf16[3,1024,256]{2,1,0:T(8,128)(2,1)}, bf16[3,1024,256]{2,1,0:T(8,128)(2,1)S(1)}, u32[]{:S(2)}, u32[]{:S(2)}) collective-permute-start(bf16[3,1024,256]{2,1,0:T(8,128)(2,1)} %bitcast.12), channel_id=1, source_target_pairs={{0,1},{1,0},{2,3},{3,2},{4,5},{5,4},{6,7},{7,6},{8,9},{9,8},{10,11... | collective-permute-start | bytes 4718600 | tf_op jit(solution)/shard_map/ppermute | solution.py:609
  3.1 14.3 %collective-permute-start.2 = (bf16[256,1024]{1,0:T(8,128)(2,1)}, bf16[256,1024]{1,0:T(8,128)(2,1)}, u32[]{:S(2)}, u32[]{:S(2)}) collective-permute-start(bf16[256,1024]{1,0:T(8,128)(2,1)} %po_ref), channel_id=1, source_target_pairs={{0,1},{1,0},{2,3},{3,2},{4,5},{5,4},{6,7},{7,6},{8,9},{9,8},{10,11... | collective-permute-start | bytes 1572872 | tf_op jit(solution)/shard_map/ppermute | solution.py:609
  3.2 13.6 %collective-permute-start = (bf16[42,6,2,256]{3,2,1,0:T(2,128)(2,1)}, bf16[42,6,2,256]{3,2,1,0:T(2,128)(2,1)}, u32[]{:S(2)}, u32[]{:S(2)}) collective-permute-start(bf16[42,6,2,256]{3,2,1,0:T(2,128)(2,1)} %get-tuple-element.59), channel_id=1, source_target_pairs={{0,28},{1,29},{2,30},{3,31},{4,0},{5,1},{6,2},{7,3},{8,4},{9,5},{1... | collective-permute-start | bytes 774152 | tf_op jit(solution)/shard_map/ppermute | solution.py:609
  9.1 8.2 %collective-permute-start.1 = (bf16[42,6,2,256]{3,2,1,0:T(2,128)(2,1)}, bf16[42,6,2,256]{3,2,1,0:T(2,128)(2,1)}, u32[]{:S(2)}, u32[]{:S(2)}) collective-permute-start(bf16[42,6,2,256]{3,2,1,0:T(2,128)(2,1)} %get-tuple-element.60), channel_id=1, source_target_pairs={{0,2},{1,3},{2,0},{3,1},{4,6},{5,7},{6,4},{7,5},{8,10},{9,11},{10,... | collective-permute-start | bytes 774152 | tf_op jit(solution)/shard_map/ppermute | solution.py:609
  10.6 1.4 %copy-start.2 = (bf16[1024,3,256]{2,0,1:T(8,128)(2,1)S(1)}, bf16[1024,3,256]{2,0,1:T(8,128)(2,1)}, u32[]{:S(2)}) copy-start(bf16[1024,3,256]{2,0,1:T(8,128)(2,1)} %param.10) | copy-start | bytes 4718596
  12.0 0.7 copy-start.8
  12.7 1.9 %copy-start.4 = (bf16[256,1024]{1,0:T(8,128)(2,1)S(1)}, bf16[256,1024]{1,0:T(8,128)(2,1)}, u32[]{:S(2)}) copy-start(bf16[256,1024]{1,0:T(8,128)(2,1)} %po_ref) | copy-start | bytes 1572868
  12.7 9.9 %copy-start.6 = (s32[42,2,96]{2,1,0:T(2,128)S(1)}, s32[42,2,96]{2,1,0:T(2,128)}, u32[]{:S(2)}) copy-start(s32[42,2,96]{2,1,0:T(2,128)} %ids_ref.1) | copy-start | bytes 96772
  13.4 1.2 %copy-start.10 = (bf16[3,1024,256]{2,1,0:T(8,128)(2,1)}, bf16[3,1024,256]{2,1,0:T(8,128)(2,1)S(1)}, u32[]{:S(2)}) copy-start(bf16[3,1024,256]{2,1,0:T(8,128)(2,1)S(1)} %get-tuple-element.79.refs_3_) | copy-start | bytes 4718596
  15.3 13.6 %copy-start.1 = (bf16[42,2,12,256]{3,1,2,0:T(2,128)(2,1)S(1)}, bf16[42,2,12,256]{3,1,2,0:T(2,128)(2,1)}, u32[]{:S(2)}) copy-start(bf16[42,2,12,256]{3,1,2,0:T(2,128)(2,1)} %param.8) | copy-start | bytes 1548292
  15.3 12.3 %collective-permute-start.5 = (bf16[128,1024]{1,0:T(8,128)(2,1)}, bf16[128,1024]{1,0:T(8,128)(2,1)S(1)}, u32[]{:S(2)}, u32[]{:S(2)}) collective-permute-start(bf16[128,1024]{1,0:T(8,128)(2,1)} %constant_dynamic-slice_fusion), channel_id=1, source_target_pairs={{0,2},{1,3},{2,0},{3,1},{4,6},{5,7},{6,4},{7,5},{8,10},{9,11},{10,... | collective-permute-start | bytes 786440 | tf_op jit(solution)/shard_map/ppermute | solution.py:609
  17.3 8.2 %collective-permute-start.4 = (bf16[42,6,2,256]{3,2,1,0:T(2,128)(2,1)}, bf16[42,6,2,256]{3,2,1,0:T(2,128)(2,1)}, u32[]{:S(2)}, u32[]{:S(2)}) collective-permute-start(bf16[42,6,2,256]{3,2,1,0:T(2,128)(2,1)} %slice.12), channel_id=1, source_target_pairs={{0,28},{1,29},{2,30},{3,31},{4,0},{5,1},{6,2},{7,3},{8,4},{9,5},{1... | collective-permute-start | bytes 774152 | tf_op jit(solution)/shard_map/ppermute | solution.py:609
  20.3 8.6 %collective-permute-start.3 = (bf16[42,6,2,256]{3,2,1,0:T(2,128)(2,1)}, bf16[42,6,2,256]{3,2,1,0:T(2,128)(2,1)}, u32[]{:S(2)}, u32[]{:S(2)}) collective-permute-start(bf16[42,6,2,256]{3,2,1,0:T(2,128)(2,1)} %collective-permute-done.refs_1_), channel_id=1, source_target_pairs={{0,2},{1,3},{2,0},{3,1},{4,6},{5,7},{6,4},{7,5},{8,10},{9,11},{10,... | collective-permute-start | bytes 774152 | tf_op jit(solution)/shard_map/ppermute | solution.py:609
  21.9 5.1 %collective-permute-start.7 = (f32[3,2,256]{2,1,0:T(2,128)S(1)}, f32[3,2,256]{2,1,0:T(2,128)S(1)}, u32[]{:S(2)}, u32[]{:S(2)}) collective-permute-start(f32[3,2,256]{2,1,0:T(2,128)S(1)} %bitcast.18), channel_id=1, source_target_pairs={{0,1},{1,0},{2,3},{3,2},{4,5},{5,4},{6,7},{7,6},{8,9},{9,8},{10,11... | collective-permute-start | bytes 18440 | tf_op jit(solution)/shard_map/ppermute | solution.py:609
  26.9 6.0 %copy-start.11 = (bf16[3,1024,256]{2,1,0:T(8,128)(2,1)S(1)}, bf16[3,1024,256]{2,1,0:T(8,128)(2,1)}, u32[]{:S(2)}) copy-start(bf16[3,1024,256]{2,1,0:T(8,128)(2,1)} %copy-done.10) | copy-start | bytes 4718596
  30.9 2.1 %collective-permute-start.8 = (bf16[2,576,256]{2,1,0:T(8,128)(2,1)S(1)}, bf16[2,576,256]{2,1,0:T(8,128)(2,1)S(1)}, u32[]{:S(2)}, u32[]{:S(2)}) collective-permute-start(bf16[2,576,256]{2,1,0:T(8,128)(2,1)S(1)} %get-tuple-element.76), channel_id=1, source_target_pairs={{0,1},{1,0},{2,3},{3,2},{4,5},{5,4},{6,7},{7,6},{8,9},{9,8},{10,11... | collective-permute-start | bytes 1769480 | tf_op jit(solution)/shard_map/ppermute | solution.py:609
  30.9 11.8 %collective-permute-start.9 = (bf16[576,256]{1,0:T(8,128)(2,1)S(1)}, bf16[576,256]{1,0:T(8,128)(2,1)S(1)}, u32[]{:S(2)}, u32[]{:S(2)}) collective-permute-start(bf16[576,256]{1,0:T(8,128)(2,1)S(1)} %bitcast.19), channel_id=1, source_target_pairs={{0,1},{1,0},{2,3},{3,2},{4,5},{5,4},{6,7},{7,6},{8,9},{9,8},{10,11... | collective-permute-start | bytes 884744 | tf_op jit(solution)/shard_map/ppermute | solution.py:609
  31.4 11.3 %collective-permute-start.10 = (bf16[576,256]{1,0:T(8,128)(2,1)S(1)}, bf16[576,256]{1,0:T(8,128)(2,1)S(1)}, u32[]{:S(2)}, u32[]{:S(2)}) collective-permute-start(bf16[576,256]{1,0:T(8,128)(2,1)S(1)} %get-tuple-element.77.refs_3_), channel_id=1, source_target_pairs={{0,2},{1,3},{2,0},{3,1},{4,6},{5,7},{6,4},{7,5},{8,10},{9,11},{10,... | collective-permute-start | bytes 884744 | tf_op jit(solution)/shard_map/ppermute | solution.py:609
  32.5 13.7 %collective-permute-start.11 = (bf16[576,256]{1,0:T(8,128)(2,1)S(1)}, bf16[576,256]{1,0:T(8,128)(2,1)S(1)}, u32[]{:S(2)}, u32[]{:S(2)}) collective-permute-start(bf16[576,256]{1,0:T(8,128)(2,1)S(1)} %bitcast.20), channel_id=1, source_target_pairs={{0,3},{1,2},{2,1},{3,0},{4,7},{5,6},{6,5},{7,4},{8,11},{9,10},{10,... | collective-permute-start | bytes 884744 | tf_op jit(solution)/shard_map/ppermute | solution.py:609
  32.9 9.9 %collective-permute-start.12 = (bf16[128,1024]{1,0:T(8,128)(2,1)S(1)}, bf16[128,1024]{1,0:T(8,128)(2,1)S(1)}, u32[]{:S(2)}, u32[]{:S(2)}) collective-permute-start(bf16[128,1024]{1,0:T(8,128)(2,1)S(1)} %collective-permute-done.5.a2), channel_id=1, source_target_pairs={{0,4},{1,5},{2,6},{3,7},{4,0},{5,1},{6,2},{7,3},{8,12},{9,13},{10,... | collective-permute-start | bytes 786440 | tf_op jit(solution)/shard_map/ppermute | solution.py:615
  41.6 13.4 %collective-permute-start.14 = (bf16[288,512]{1,0:T(8,128)(2,1)S(1)}, bf16[288,512]{1,0:T(8,128)(2,1)S(1)}, u32[]{:S(2)}, u32[]{:S(2)}) collective-permute-start(bf16[288,512]{1,0:T(8,128)(2,1)S(1)} %get-tuple-element.86.refs_7_.a_ref), channel_id=1, source_target_pairs={{0,2},{1,3},{2,0},{3,1},{4,6},{5,7},{6,4},{7,5},{8,10},{9,11},{10,... | collective-permute-start | bytes 884744 | tf_op jit(solution)/shard_map/ppermute | solution.py:609
  48.9 10.5 %collective-permute-start.13 = (bf16[288,512]{1,0:T(8,128)(2,1)S(1)}, bf16[288,512]{1,0:T(8,128)(2,1)S(1)}, u32[]{:S(2)}, u32[]{:S(2)}) collective-permute-start(bf16[288,512]{1,0:T(8,128)(2,1)S(1)} %shard_map.111.refs_7_.b_ref), channel_id=1, source_target_pairs={{0,2},{1,3},{2,0},{3,1},{4,6},{5,7},{6,4},{7,5},{8,10},{9,11},{10,... | collective-permute-start | bytes 884744 | tf_op jit(solution)/shard_map/ppermute | solution.py:609
  49.9 3.0 %collective-permute-start.15 = (bf16[128,1024]{1,0:T(8,128)(2,1)S(1)}, bf16[128,1024]{1,0:T(8,128)(2,1)S(1)}, u32[]{:S(2)}, u32[]{:S(2)}) collective-permute-start(bf16[128,1024]{1,0:T(8,128)(2,1)S(1)} %collective-permute-done.5.a2), channel_id=1, source_target_pairs={{0,1},{1,0},{2,3},{3,2},{4,5},{5,4},{6,7},{7,6},{8,9},{9,8},{10,11... | collective-permute-start | bytes 786440 | tf_op jit(solution)/shard_map/ppermute | solution.py:609
  51.0 1.9 %collective-permute-start.16 = (bf16[128,1024]{1,0:T(8,128)(2,1)S(1)}, bf16[128,1024]{1,0:T(8,128)(2,1)S(1)}, u32[]{:S(2)}, u32[]{:S(2)}) collective-permute-start(bf16[128,1024]{1,0:T(8,128)(2,1)S(1)} %collective-permute-done.12.b2), channel_id=1, source_target_pairs={{0,1},{1,0},{2,3},{3,2},{4,5},{5,4},{6,7},{7,6},{8,9},{9,8},{10,11... | collective-permute-start | bytes 786440 | tf_op jit(solution)/shard_map/ppermute | solution.py:609
  52.0 0.9 copy-start.7
  60.4 10.5 %collective-permute-start.17 = (bf16[288,256]{1,0:T(8,128)(2,1)S(1)}, bf16[288,256]{1,0:T(8,128)(2,1)S(1)}, u32[]{:S(2)}, u32[]{:S(2)}) collective-permute-start(bf16[288,256]{1,0:T(8,128)(2,1)S(1)} %get-tuple-element.98), channel_id=1, source_target_pairs={{0,4},{1,5},{2,6},{3,7},{4,8},{5,9},{6,10},{7,11},{8,12},{9,13},{1... | collective-permute-start | bytes 442376 | tf_op jit(solution)/shard_map/ppermute | solution.py:609
  60.4 10.4 %collective-permute-start.18 = (bf16[288,256]{1,0:T(8,128)(2,1)S(1)}, bf16[288,256]{1,0:T(8,128)(2,1)S(1)}, u32[]{:S(2)}, u32[]{:S(2)}) collective-permute-start(bf16[288,256]{1,0:T(8,128)(2,1)S(1)} %get-tuple-element.99), channel_id=1, source_target_pairs={{0,1},{1,0},{2,3},{3,2},{4,5},{5,4},{6,7},{7,6},{8,9},{9,8},{10,11... | collective-permute-start | bytes 442376 | tf_op jit(solution)/shard_map/ppermute | solution.py:609
  60.8 11.0 %collective-permute-start.19 = (bf16[288,256]{1,0:T(8,128)(2,1)S(1)}, bf16[288,256]{1,0:T(8,128)(2,1)S(1)}, u32[]{:S(2)}, u32[]{:S(2)}) collective-permute-start(bf16[288,256]{1,0:T(8,128)(2,1)S(1)} %get-tuple-element.100), channel_id=1, source_target_pairs={{0,5},{1,4},{2,7},{3,6},{4,9},{5,8},{6,11},{7,10},{8,13},{9,12},{1... | collective-permute-start | bytes 442376 | tf_op jit(solution)/shard_map/ppermute | solution.py:609
  66.7 3.7 %collective-permute-start.20 = (f32[2,1024]{1,0:T(2,128)S(1)}, f32[2,1024]{1,0:T(2,128)S(1)}, u32[]{:S(2)}, u32[]{:S(2)}) collective-permute-start(f32[2,1024]{1,0:T(2,128)S(1)} %shard_map.121), channel_id=1, source_target_pairs={{0,2},{1,3},{2,0},{3,1},{4,6},{5,7},{6,4},{7,5},{8,10},{9,11},{10,... | collective-permute-start | bytes 24584 | tf_op jit(solution)/shard_map/ppermute | solution.py:609
  67.7 4.1 %copy-start.3 = (bf16[1024,3,256]{2,0,1:T(8,128)(2,1)S(1)}, bf16[1024,3,256]{2,0,1:T(8,128)(2,1)}, u32[]{:S(2)}) copy-start(bf16[1024,3,256]{2,0,1:T(8,128)(2,1)} %param.10) | copy-start | bytes 4718596
  70.4 4.1 %collective-permute-start.23 = (f32[2,1792]{1,0:T(2,128)S(1)}, f32[2,1792]{1,0:T(2,128)S(1)}, u32[]{:S(2)}, u32[]{:S(2)}) collective-permute-start(f32[2,1792]{1,0:T(2,128)S(1)} %pad_maximum_fusion), channel_id=1, source_target_pairs={{0,5},{1,4},{2,7},{3,6},{4,1},{5,0},{6,3},{7,2},{8,13},{9,12},{10,... | collective-permute-start | bytes 43016 | tf_op jit(solution)/shard_map/ppermute | solution.py:615
  70.5 4.1 %collective-permute-start.21 = (f32[2,1792]{1,0:T(2,128)S(1)}, f32[2,1792]{1,0:T(2,128)S(1)}, u32[]{:S(2)}, u32[]{:S(2)}) collective-permute-start(f32[2,1792]{1,0:T(2,128)S(1)} %pad_maximum_fusion), channel_id=1, source_target_pairs={{0,1},{1,0},{2,3},{3,2},{4,5},{5,4},{6,7},{7,6},{8,9},{9,8},{10,11... | collective-permute-start | bytes 43016 | tf_op jit(solution)/shard_map/ppermute | solution.py:609
  73.6 3.8 %collective-permute-start.22 = (f32[2,1792]{1,0:T(2,128)S(1)}, f32[2,1792]{1,0:T(2,128)S(1)}, u32[]{:S(2)}, u32[]{:S(2)}) collective-permute-start(f32[2,1792]{1,0:T(2,128)S(1)} %pad_maximum_fusion.1), channel_id=1, source_target_pairs={{0,4},{1,5},{2,6},{3,7},{4,0},{5,1},{6,2},{7,3},{8,12},{9,13},{10,... | collective-permute-start | bytes 43016 | tf_op jit(solution)/shard_map/ppermute | solution.py:615
  77.5 7.9 %collective-permute-start.25 = (f32[2,1792]{1,0:T(2,128)S(1)}, f32[2,1792]{1,0:T(2,128)S(1)}, u32[]{:S(2)}, u32[]{:S(2)}) collective-permute-start(f32[2,1792]{1,0:T(2,128)S(1)} %add_add_fusion.1), channel_id=1, source_target_pairs={{0,16},{1,17},{2,18},{3,19},{4,20},{5,21},{6,22},{7,23},{8,24},{9,... | collective-permute-start | bytes 43016 | tf_op jit(solution)/shard_map/ppermute | solution.py:615
  82.8 5.5 %collective-permute-start.26 = (f32[2,1792]{1,0:T(2,128)S(1)}, f32[2,1792]{1,0:T(2,128)S(1)}, u32[]{:S(2)}, u32[]{:S(2)}) collective-permute-start(f32[2,1792]{1,0:T(2,128)S(1)} %add_add_fusion.1), channel_id=1, source_target_pairs={{0,24},{1,25},{2,26},{3,27},{4,28},{5,29},{6,30},{7,31},{8,16},{9,... | collective-permute-start | bytes 43016 | tf_op jit(solution)/shard_map/ppermute | solution.py:615
  82.8 5.5 %collective-permute-start.24 = (f32[2,1792]{1,0:T(2,128)S(1)}, f32[2,1792]{1,0:T(2,128)S(1)}, u32[]{:S(2)}, u32[]{:S(2)}) collective-permute-start(f32[2,1792]{1,0:T(2,128)S(1)} %add_add_fusion.1), channel_id=1, source_target_pairs={{0,8},{1,9},{2,10},{3,11},{4,12},{5,13},{6,14},{7,15},{8,0},{9,1},... | collective-permute-start | bytes 43016 | tf_op jit(solution)/shard_map/ppermute | solution.py:615
